TPU v7x, 32 devices: a whole 2x2x4 slice. The times are simulated.
32 devices in a mesh: grp: 2 (over y), tgt: 4 (over z), qry: 2 (over x), rep: 2 (over core).
Axes of the slice: x: 2, y: 2, z: 4, core: 2. Of those that a mesh axis runs over, the one named last changes fastest.
Arguments:
- query_res: bfloat16 [16, 256, 1280], P(('grp', 'tgt', 'qry'), None, 'rep'), parts along dimension 0, may hold values from -100 to 100
- target_res: bfloat16 [16, 128, 1280], P(('grp', 'tgt'), None, 'rep'), parts along dimension 0, may hold values from -50 to 50
- target_len: int32 [16], P('grp'), parts along dimension 0, may hold values from 64 to 128
- hits: int32 [16, 28], P(('grp', 'tgt', 'qry')), parts along dimension 0, may hold values from 0 to 7, as said below
- sharpness: float32 [16], P(('grp', 'tgt', 'qry')), parts along dimension 0, may hold values from 0.4 to 30
- query_pool: float32 [16, 1280], P(('grp', 'tgt', 'qry')), parts along dimension 0, may hold values from -41 to 41
- target_pool: float32 [16, 1280], P(('grp', 'tgt')), parts along dimension 0, may hold values from -5.1 to 5.1
Outputs:
- profile: bfloat16 [16, 256, 1280], P(('grp', 'tgt', 'qry'), None, 'rep'), parts along dimension 0
- posterior: float32 [16, 8], P(('grp', 'tgt', 'qry')), parts along dimension 0
There are 2 independent parts, one for each index of `grp`. A program takes and returns all parts, laid end to end along the dimension named above; each array names one. Nothing has to cross between parts.
Inputs may be any that keep to these rules, and one draw needn't show every extreme that they name: Each row lists 28 ids of targets hit by that query; ids may repeat. Target t is held by index t // 2 of tgt. In each aligned block of 1 row (the queries of one device), at most 14 hits name targets held by one index of tgt, and in every block some index is named exactly 14 times.
All inputs are finite; a program needn't handle non-finite values.
Results may differ from a plain program's by a relative error of at most 0.0051.
Values may be sent and summed in bfloat16 or wider, within the bound.
No kernel may reach another device: no remote copies, remote signals or barrier semaphores. Data moves between devices by JAX's collectives and lax.ppermute only.
A program may use at most 64 MiB of HBM per device.

v0:
```python
import math

import jax
import jax.numpy as jnp
from jax import lax
from jax.sharding import PartitionSpec as P


def softmax_rows(logits):
    highest = jnp.max(logits, axis=-1, keepdims=True)
    raised = jnp.exp(logits - highest)
    return raised / jnp.sum(raised, axis=-1, keepdims=True)


def weigh_alignment(similar, lengths, sharpness, hit_weight):
    target_rows = similar.shape[-1]
    inside = jnp.arange(target_rows)[None, None, None, :] < lengths[:, :, None, None]
    counted = lengths[:, :, None, None].astype(jnp.float32)
    row_mean = jnp.sum(jnp.where(inside, similar, 0.0), axis=-1, keepdims=True) / counted
    row_diff = similar - row_mean
    row_var = jnp.sum(jnp.where(inside, row_diff * row_diff, 0.0), axis=-1, keepdims=True) / counted
    row_score = row_diff / jnp.sqrt(row_var + 1e-05)
    column_mean = jnp.mean(similar, axis=2, keepdims=True)
    column_diff = similar - column_mean
    column_var = jnp.mean(column_diff * column_diff, axis=2, keepdims=True)
    column_score = column_diff / jnp.sqrt(column_var + 1e-05)
    scores = sharpness[:, None, None, None] * (0.5 * (row_score + column_score))
    scores = jnp.where(inside, scores, -jnp.inf)
    alignment = softmax_rows(scores)
    return (hit_weight[:, :, None, None] * alignment).astype(jnp.bfloat16)


def plan_slots(flat_hits, owned_targets, tgt_count, capacity):
    owners = flat_hits // owned_targets
    local_ids = flat_hits % owned_targets
    matched = owners[:, None] == jnp.arange(tgt_count)[None, :]
    earlier = jnp.cumsum(matched.astype(jnp.int32), axis=0) - 1
    rank_in = jnp.sum(jnp.where(matched, earlier, 0), axis=1)
    slot_of = owners * capacity + rank_in
    placed = slot_of[:, None] == jnp.arange(tgt_count * capacity)[None, :]
    wanted = jnp.sum(jnp.where(placed, local_ids[:, None], 0), axis=0).reshape(tgt_count, capacity)
    return (wanted, slot_of)


def fetch_shares(target_res, flat_hits, capacity):
    tgt_count = lax.axis_size("tgt")
    owned_targets, target_rows, width = target_res.shape
    wanted, slot_of = plan_slots(flat_hits, owned_targets, tgt_count, capacity)
    requested = lax.all_to_all(wanted, "tgt", split_axis=0, concat_axis=0, tiled=True)
    outgoing = jnp.take(target_res, requested.reshape(tgt_count * capacity), axis=0)
    outgoing = outgoing.reshape(tgt_count, capacity, target_rows, width)
    arrived = lax.all_to_all(outgoing, "tgt", split_axis=0, concat_axis=0, tiled=True)
    return jnp.take(arrived.reshape(tgt_count * capacity, target_rows, width), slot_of, axis=0)


def per_device(query_res, target_res, target_len, hits, sharpness, query_pool, target_pool):
    tgt_count = lax.axis_size("tgt")
    query_count = query_res.shape[0]
    target_rows = target_res.shape[1]
    hit_count = hits.shape[1]
    pair_count = query_count * hit_count
    model_width = query_pool.shape[1]
    capacity = max(2, (2 * pair_count + tgt_count - 1) // tgt_count)
    library = lax.all_gather(target_pool, "tgt", axis=0, tiled=True)
    logits = jnp.dot(query_pool, library.T, precision=lax.Precision.HIGHEST) / math.sqrt(
        model_width
    )
    posterior = softmax_rows(logits)
    matches = hits[:, :, None] == jnp.arange(library.shape[0])[None, None, :]
    hit_weight = softmax_rows(jnp.sum(jnp.where(matches, logits[:, None, :], 0.0), axis=-1))
    lengths = jnp.sum(jnp.where(matches, target_len[None, None, :], 0), axis=-1)
    half_width = query_res.shape[2]
    chosen = fetch_shares(target_res, hits.reshape(pair_count), capacity)
    chosen = chosen.reshape(query_count, hit_count, target_rows, half_width)
    partial_sim = jnp.einsum(
        "qid,qhjd->qhij", query_res, chosen, preferred_element_type=jnp.float32
    ) / math.sqrt(model_width)
    similar = lax.psum(partial_sim, "rep")
    weighted = weigh_alignment(similar, lengths, sharpness, hit_weight)
    profile = jnp.einsum("qhij,qhjd->qid", weighted, chosen, preferred_element_type=jnp.float32)
    return (profile.astype(jnp.bfloat16), posterior)


def solution(mesh):
    placed = (
        P(("grp", "tgt", "qry"), None, "rep"),
        P(("grp", "tgt"), None, "rep"),
        P("grp"),
        P(("grp", "tgt", "qry"), None),
        P(("grp", "tgt", "qry")),
        P(("grp", "tgt", "qry"), None),
        P(("grp", "tgt"), None),
    )
    return jax.shard_map(
        per_device,
        mesh=mesh,
        in_specs=placed,
        out_specs=(P(("grp", "tgt", "qry"), None, "rep"), P(("grp", "tgt", "qry"), None)),
        check_vma=False,
    )
```

profile of v0, /device:TPU:0, one launch (start us, length us, event | category | flops | bytes accessed | tf_op | source)
XLA Modules:
  0.0 294.1 jit_solution(2259610699213316530)
XLA Ops:
  7.2 0.7 and_select_fusion.2
  8.4 11.7 %all_to_all.14 = s32[4,1,14]{2,1,0:T(1,128)S(1)} all-to-all(s32[4,1,14]{2,1,0:T(1,128)S(1)} %bitcast.73), channel_id=1, replica_groups=mesh['grp'=2,'tgt'=4,'qry'=2,'rep'=2] {'tgt'}, dimensions={0} | all-to-all | bytes 448 | tf_op jit(solution)/shard_map/all_to_all | solution.py:49
  20.1 0.5 broadcast.489
  20.6 0.7 reduce.19
  21.4 6.0 %gather_fusion = bf16[56,128,640]{2,1,0:T(8,128)(2,1)} fusion(bf16[2,128,640]{2,1,0:T(8,128)(2,1)S(1)} %copy-done, s32[1024]{0:T(1024)S(1)} %pad_clamp_fusion.1), kind=kCustom, calls=%fused_computation | custom fusion | bytes 18350304 | tf_op jit(solution)/shard_map/jit(_take)/gather | solution.py:50
  27.4 8.2 %broadcast_select_fusion = bf16[4,14,128,640]{3,2,1,0:T(8,128)(2,1)} fusion(bf16[4,14,128,640]{3,2,1,0:T(8,128)(2,1)} %bitcast.68, pred[4,14]{1,0:T(4,128)(4,1)S(1)} %compare_and_fusion), kind=kLoop, calls=%fused_computation.2 | loop fusion | flops 4587520 | bytes 18350136 | tf_op jit(solution)/shard_map/jit(_take)/select_n | solution.py:50
  35.6 5.9 %all-to-all-start.1 = ((bf16[4,14,128,640]{3,2,1,0:T(8,128)(2,1)}), bf16[4,14,128,640]{3,2,1,0:T(8,128)(2,1)}, u32[]{:S(2)}, u32[]{:S(2)}) async-start(bf16[4,14,128,640]{3,2,1,0:T(8,128)(2,1)} %broadcast_select_fusion), calls=%async_computation.1 | async-start | bytes 18350080 | tf_op jit(solution)/shard_map/all_to_all | solution.py:52
  41.6 198.7 %all-to-all-done.1 = bf16[4,14,128,640]{3,2,1,0:T(8,128)(2,1)} async-done(((bf16[4,14,128,640]{3,2,1,0:T(8,128)(2,1)}), bf16[4,14,128,640]{3,2,1,0:T(8,128)(2,1)}, u32[]{:S(2)}, u32[]{:S(2)}) %all-to-all-start.1) | async-done | bytes 9175072 | tf_op jit(solution)/shard_map/all_to_all | solution.py:52
  240.2 7.1 %gather_fusion.1 = bf16[28,128,640]{2,1,0:T(8,128)(2,1)} fusion(bf16[56,128,640]{2,1,0:T(8,128)(2,1)} %bitcast.7, s32[1024]{0:T(1024)S(1)} %pad_clamp_fusion), kind=kCustom, calls=%fused_computation.1 | custom fusion | bytes 9175152 | tf_op jit(solution)/shard_map/jit(_take)/gather | solution.py:53
  247.4 5.8 %multiply_bitcast_fusion = f32[1,28,256,128]{2,3,1,0:T(8,128)} fusion(bf16[28,128,640]{2,1,0:T(8,128)(2,1)} %gather_fusion.1, pred[28]{0:T(512)(128)(4,1)S(1)} %get-tuple-element.8, bf16[1,256,640]{2,1,0:T(8,128)(2,1)S(1)} %copy-done.4), kind=kOutput, calls=%fused_computation.10 | convolution fusion | flops 1177616384 | bytes 8585244 | tf_op jit(solution)/shard_map/qid,qhjd->qhij/dot_general | solution.py:75
  253.2 0.6 copy-done.5
  254.6 13.1 %all-gather = f32[4,2,1280]{2,1,0:T(2,128)S(1)} all-gather(f32[1,2,1280]{2,1,0:T(2,128)S(1)} %bitcast.72), channel_id=1, replica_groups=mesh['grp'=2,'tgt'=4,'qry'=2,'rep'=2] {'tgt'}, dimensions={0}, use_global_device_ids=true | all-gather | bytes 51200 | tf_op jit(solution)/shard_map/all_gather | solution.py:64
  267.8 0.9 fusion.25
  268.7 0.6 reduce_max.27
  269.3 1.3 fusion.22
  270.6 1.3 fusion.23
  271.9 1.3 broadcast_divide_fusion.1
  273.2 1.8 divide_bitcast_fusion
  275.1 1.6 all-reduce.2.cloned.1.call-done
  276.7 2.9 select_reduce_fusion.1
  279.8 2.0 select_reduce_fusion
  282.0 2.1 fusion.24
  284.1 0.6 fusion
  284.8 2.5 fusion.11
  (41 shorter events, 1.3 us)
Async XLA Ops:
  7.2 14.2 %copy-start = (bf16[2,128,640]{2,1,0:T(8,128)(2,1)S(1)}, bf16[2,128,640]{2,1,0:T(8,128)(2,1)}, u32[]{:S(2)}) copy-start(bf16[2,128,640]{2,1,0:T(8,128)(2,1)} %param.8) | copy-start | bytes 983044
  35.6 6.0 %copy-start.6 = (s32[1,28]{1,0:T(1,128)S(1)}, s32[1,28]{1,0:T(1,128)}, u32[]{:S(2)}) copy-start(s32[1,28]{1,0:T(1,128)} %param.10) | copy-start | bytes 340
  35.6 204.7 %all-to-all-start.1 = ((bf16[4,14,128,640]{3,2,1,0:T(8,128)(2,1)}), bf16[4,14,128,640]{3,2,1,0:T(8,128)(2,1)}, u32[]{:S(2)}, u32[]{:S(2)}) async-start(bf16[4,14,128,640]{3,2,1,0:T(8,128)(2,1)} %broadcast_select_fusion), calls=%async_computation.1 | async-start | bytes 18350080 | tf_op jit(solution)/shard_map/all_to_all | solution.py:52
  41.5 235.2 %all-reduce.2.cloned.1.call-start = ((), (), s32[]{:S(2)}) async-start(), calls=%async_computation.2 | async-start | bytes 7340032 | tf_op jit(solution)/shard_map/psum | solution.py:78
  240.2 7.1 %copy-start.4 = (bf16[1,256,640]{2,1,0:T(8,128)(2,1)S(1)}, bf16[1,256,640]{2,1,0:T(8,128)(2,1)}, u32[]{:S(2)}) copy-start(bf16[1,256,640]{2,1,0:T(8,128)(2,1)} %param.7) | copy-start | bytes 983044
  253.2 0.7 copy-start.5
  253.2 1.4 copy-start.2
  253.2 14.6 %copy-start.3 = (f32[1,1280]{1,0:T(1,128)S(1)}, f32[1,1280]{1,0:T(1,128)}, u32[]{:S(2)}) copy-start(f32[1,1280]{1,0:T(1,128)} %param.12) | copy-start | bytes 15364
  276.7 3.1 %copy-start.1 = (f32[1,28,256,128]{2,3,1,0:T(8,128)S(1)}, f32[1,28,256,128]{2,3,1,0:T(8,128)}, u32[]{:S(2)}) copy-start(f32[1,28,256,128]{2,3,1,0:T(8,128)} %all-reduce.2.cloned.1.call-done) | copy-start | bytes 11010052
  282.0 2.8 slice-start
  282.0 2.8 slice-start.1
Sparse Core Ops, SparseCore 0:
  253.3 23.3 all-reduce.1
where the time goes:
time: 295 us; the launch traced here: 294 us
  waiting for transfers between devices  200 us (68%)
  blocking collectives  24.8 us (8%)
  other arithmetic  24.4 us (8%)
  between operations  14.9 us (5%)
  local copies, waits for them, and re-layouts  14.7 us (5%)
  matrix products  9.14 us (3%)
  starting transfers between devices  5.93 us (2%)
    all_to_all x1, waiting for transfers between devices, fetch_shares(): lax.all_to_all(outgoing, 'tgt', split_axis=0, concat_axis=0, tiled=True)  199 us
    all_gather x1, blocking collectives, per_device(): library = lax.all_gather(target_pool, 'tgt', axis=0, tiled=True)  13.1 us
    all_to_all x1, blocking collectives, fetch_shares(): lax.all_to_all(wanted, 'tgt', split_axis=0, concat_axis=0, tiled=True)  11.7 us
    select_n x2, other arithmetic, fetch_shares(): jnp.take(target_res, requested.reshape(tgt_count * capacity), axis=0)  8.18 us
    gather x1, local copies, waits for them, and re-layouts, fetch_shares(): jnp.take(arrived.reshape(tgt_count * capacity, target_rows, width), slot_...  7.13 us
    gather x1, local copies, waits for them, and re-layouts, fetch_shares(): jnp.take(target_res, requested.reshape(tgt_count * capacity), axis=0)  6.03 us
  transfers between devices with their start and end apart: 2, of which 2 were waited for; matrix products, arithmetic and copies ran while one was open for 3% of the time, Pallas kernels for 0%

commit v1 on v0

--- a/solution.py
+++ b/solution.py
@@ -1,9 +1,14 @@
+import functools
 import math
 
 import jax
 import jax.numpy as jnp
 from jax import lax
+from jax.experimental import pallas as pl
+from jax.experimental.pallas import tpu as pltpu
 from jax.sharding import PartitionSpec as P
+
+VMEM_BYTES = 48 * 1024 * 1024
 
 
 def softmax_rows(logits):
@@ -53,7 +58,7 @@
     return jnp.take(arrived.reshape(tgt_count * capacity, target_rows, width), slot_of, axis=0)
 
 
-def per_device(query_res, target_res, target_len, hits, sharpness, query_pool, target_pool):
+def per_device_by_hit(query_res, target_res, target_len, hits, sharpness, query_pool, target_pool):
     tgt_count = lax.axis_size("tgt")
     query_count = query_res.shape[0]
     target_rows = target_res.shape[1]
@@ -81,6 +86,150 @@
     return (profile.astype(jnp.bfloat16), posterior)
 
 
+def partial_kernel(*refs):
+    query, blocks, out = refs[0], refs[1:-1], refs[-1]
+    rows = 0
+    for block in blocks:
+        out[:, rows : rows + block.shape[0]] = lax.dot_general(
+            query[...], block[...], (((1,), (1,)), ((), ())), preferred_element_type=jnp.float32
+        )
+        rows += block.shape[0]
+
+
+def partial_similar(query, blocks):
+    rows = sum(block.shape[0] for block in blocks)
+    cost = pl.CostEstimate(
+        flops=2 * query.shape[0] * rows * query.shape[1],
+        bytes_accessed=2 * (query.size + rows * query.shape[1]) + 4 * query.shape[0] * rows,
+        transcendentals=0,
+    )
+    return pl.pallas_call(
+        partial_kernel,
+        out_shape=jax.ShapeDtypeStruct((query.shape[0], rows), jnp.float32),
+        cost_estimate=cost,
+        compiler_params=pltpu.CompilerParams(vmem_limit_bytes=VMEM_BYTES),
+    )(query, *blocks)
+
+
+def align_kernel(groups, target_rows, target_count, *refs):
+    slot_ref, len_ref, sharp_ref, hits_ref, pool_ref = refs[:5]
+    libs = refs[5 : 5 + groups]
+    mine = refs[5 + groups : 5 + 2 * groups]
+    other = refs[5 + 2 * groups : 5 + 3 * groups]
+    blocks = refs[5 + 3 * groups : 5 + 3 * groups + target_count]
+    profile_ref, posterior_ref, weight_ref = refs[5 + 3 * groups + target_count :]
+    width = pool_ref.shape[1]
+    scale = 1.0 / math.sqrt(width)
+    owned = target_count // groups
+
+    pool = pool_ref[...]
+    logits = []
+    for group in range(groups):
+        products = jnp.sum(libs[group][...] * pool, axis=1, keepdims=True) * scale
+        logits += [products[a : a + 1, :] for a in range(owned)]
+    lane = lax.broadcasted_iota(jnp.int32, (1, target_count), 1)
+    ordered = jnp.zeros((1, target_count), jnp.float32)
+    for s in range(target_count):
+        ordered = jnp.where(lane == slot_ref[s], logits[s], ordered)
+    raised = jnp.exp(ordered - jnp.max(ordered, axis=1, keepdims=True))
+    posterior_ref[...] = raised / jnp.sum(raised, axis=1, keepdims=True)
+
+    hits = hits_ref[...]
+    counts = [
+        jnp.sum(jnp.where(hits == slot_ref[s], 1.0, 0.0), axis=1, keepdims=True)
+        for s in range(target_count)
+    ]
+    shown = [jnp.where(c > 0.0, l, -jnp.inf) for c, l in zip(counts, logits)]
+    highest = functools.reduce(jnp.maximum, shown)
+    parts = [c * jnp.exp(l - highest) for c, l in zip(counts, shown)]
+    total = functools.reduce(jnp.add, parts)
+
+    half_sharp = 0.5 * sharp_ref[0]
+    column = lax.broadcasted_iota(jnp.int32, (1, target_rows), 1)
+    for s in range(target_count):
+        at = pl.ds((s % owned) * target_rows, target_rows)
+        similar = (mine[s // owned][:, at] + other[s // owned][:, at]) * scale
+        length = len_ref[slot_ref[s]]
+        inside = column < length
+        fraction = 1.0 / length.astype(jnp.float32)
+        row_mean = jnp.sum(jnp.where(inside, similar, 0.0), axis=1, keepdims=True) * fraction
+        row_diff = similar - row_mean
+        row_var = (
+            jnp.sum(jnp.where(inside, row_diff * row_diff, 0.0), axis=1, keepdims=True) * fraction
+        )
+        column_mean = jnp.mean(similar, axis=0, keepdims=True)
+        column_diff = similar - column_mean
+        column_var = jnp.mean(column_diff * column_diff, axis=0, keepdims=True)
+        scores = row_diff * (half_sharp * lax.rsqrt(row_var + 1e-05)) + column_diff * (
+            half_sharp * lax.rsqrt(column_var + 1e-05)
+        )
+        scores = jnp.where(inside, scores, -jnp.inf)
+        raised = jnp.exp(scores - jnp.max(scores, axis=1, keepdims=True))
+        weight = (parts[s] / total) / jnp.sum(raised, axis=1, keepdims=True)
+        weight_ref[:, pl.ds(s * target_rows, target_rows)] = (raised * weight).astype(jnp.bfloat16)
+
+    acc = None
+    for s in range(target_count):
+        term = jnp.dot(
+            weight_ref[:, pl.ds(s * target_rows, target_rows)],
+            blocks[s][...],
+            preferred_element_type=jnp.float32,
+        )
+        acc = term if acc is None else acc + term
+    profile_ref[...] = acc.astype(jnp.bfloat16)
+
+
+def per_device_by_target(
+    query_res, target_res, target_len, hits, sharpness, query_pool, target_pool
+):
+    groups = lax.axis_size("tgt")
+    owned, target_rows, width = target_res.shape
+    target_count = groups * owned
+    query = query_res[0]
+    at_tgt, at_qry = lax.axis_index("tgt"), lax.axis_index("qry")
+    swap = [(0, 1), (1, 0)]
+
+    def from_peer(array, k):
+        return lax.ppermute(array, "tgt", [(i, i ^ k) for i in range(groups)])
+
+    share = lax.dynamic_index_in_dim(target_res, at_qry, 0, keepdims=False)
+    direct = [from_peer(share, k) for k in range(1, groups)]
+    libs = [target_pool] + [from_peer(target_pool, k) for k in range(1, groups)]
+    libs = [libs[0]] + [jnp.where(at_qry == 0, lib, lib[::-1]) for lib in libs[1:]]
+    blocks = [[target_res[0], target_res[1]]]
+    slots = [at_tgt * owned, at_tgt * owned + 1]
+    for k in range(1, groups):
+        blocks.append([direct[k - 1], lax.ppermute(direct[k - 1], "qry", swap)])
+        base = (at_tgt ^ k) * owned
+        slots += [base + at_qry, base + 1 - at_qry]
+    mine = [partial_similar(query, pair) for pair in blocks]
+    other = [lax.ppermute(m, "rep", swap) for m in mine]
+    slots = jnp.stack(slots).astype(jnp.int32)
+
+    flat_blocks = [block for pair in blocks for block in pair]
+    smem = pl.BlockSpec(memory_space=pltpu.SMEM)
+    vmem = pl.BlockSpec(memory_space=pltpu.VMEM)
+    operands = [slots, target_len, sharpness, hits, query_pool, *libs, *mine, *other, *flat_blocks]
+    rows = query.shape[0]
+    profile, posterior = pl.pallas_call(
+        functools.partial(align_kernel, groups, target_rows, target_count),
+        out_shape=(
+            jax.ShapeDtypeStruct((rows, width), jnp.bfloat16),
+            jax.ShapeDtypeStruct((1, target_count), jnp.float32),
+        ),
+        in_specs=[smem] * 3 + [vmem] * (len(operands) - 3),
+        out_specs=(vmem, vmem),
+        scratch_shapes=[pltpu.VMEM((rows, target_count * target_rows), jnp.bfloat16)],
+        cost_estimate=pl.CostEstimate(
+            flops=2 * rows * width * target_count * target_rows,
+            bytes_accessed=4 * 1024 * 1024,
+            transcendentals=rows * target_count * target_rows,
+        ),
+        compiler_params=pltpu.CompilerParams(vmem_limit_bytes=VMEM_BYTES),
+    )(*operands)
+    return (profile[None], posterior)
+
+
 def solution(mesh):
     placed = (
         P(("grp", "tgt", "qry"), None, "rep"),
@@ -91,6 +240,19 @@
         P(("grp", "tgt", "qry"), None),
         P(("grp", "tgt"), None),
     )
+    groups = mesh.shape["tgt"]
+
+    def per_device(*arrays):
+        query_res, target_res, _, hits = arrays[:4]
+        few = (
+            query_res.shape[0] == 1
+            and groups * target_res.shape[0] <= hits.shape[1]
+            and target_res.shape[0] == mesh.shape["qry"] == 2
+            and mesh.shape["rep"] == 2
+            and groups & (groups - 1) == 0
+        )
+        return (per_device_by_target if few else per_device_by_hit)(*arrays)
+
     return jax.shard_map(
         per_device,
         mesh=mesh,

time: 295 us -> 38.3 us (0.13)
  waiting for transfers between devices: 200 us -> 14.7 us
  blocking collectives: 24.8 us -> 0 us
  other arithmetic: 24.4 us -> 0.02 us
  between operations: 14.9 us -> 1.49 us
  local copies, waits for them, and re-layouts: 14.7 us -> 2.06 us
  matrix products: 9.14 us -> 0 us
  starting transfers between devices: 5.93 us -> 14.3 us
  Pallas kernels: 0 us -> 5.55 us
    all_to_all x1 -> x0, waiting for transfers between devices: 199 us -> none  [fetch_shares(): lax.all_to_all(outgoing, 'tgt', split_axis=0, concat_axis=0, tiled=True)]
    ppermute x0 -> x13, waiting for transfers between devices: none -> 14.7 us  [the longest x6 8.33 us: from_peer(): return lax.ppermute(array, 'tgt', [(i, i ^ k) for i in range(groups)])]
    ppermute x0 -> x13, starting transfers between devices: none -> 14.3 us  [the longest x6 10.3 us: from_peer(): return lax.ppermute(array, 'tgt', [(i, i ^ k) for i in range(groups)])]
    gather x2 -> x0, local copies, waits for them, and re-layouts: 13.2 us -> none  [the longest x1 7.13 us: fetch_shares(): jnp.take(arrived.reshape(tgt_count * capacity, target_rows, width), slot_...]
    all_gather x1 -> x0, blocking collectives: 13.1 us -> none  [per_device(): library = lax.all_gather(target_pool, 'tgt', axis=0, tiled=True)]
    all_to_all x1 -> x0, blocking collectives: 11.7 us -> none  [fetch_shares(): lax.all_to_all(wanted, 'tgt', split_axis=0, concat_axis=0, tiled=True)]
    dot_general x3 -> x0, matrix products: 9.14 us -> none  [the longest x1 5.79 us: per_device(): jnp.einsum('qid,qhjd->qhij', query_res, chosen, preferred_element_type=jn...]
    select_n x4 -> x3, other arithmetic: 8.91 us -> 0.02 us  [per_device_by_target(): jnp.where(at_qry == 0, lib, lib[::-1])]
  transfers between devices with their start and end apart: 2 -> 13, of which waited for: 2 -> 5; matrix products, arithmetic and copies ran while one was open for 3% -> 5% of each run, Pallas kernels for 0% -> 3%
where the time goes in v1:
time: 38.3 us; the launch traced here: 38.2 us
  waiting for transfers between devices  14.7 us (38%)
  starting transfers between devices  14.3 us (37%)
  Pallas kernels  5.55 us (14%)
  local copies, waits for them, and re-layouts  2.06 us (5%)
  between operations  1.49 us (4%)
    ppermute x6, starting transfers between devices, from_peer(): return lax.ppermute(array, 'tgt', [(i, i ^ k) for i in range(groups)])  10.3 us
    ppermute x6, waiting for transfers between devices, from_peer(): return lax.ppermute(array, 'tgt', [(i, i ^ k) for i in range(groups)])  8.33 us
    ppermute x3, waiting for transfers between devices, per_device_by_target(): blocks.append([direct[k - 1], lax.ppermute(direct[k - 1], 'qry', swap)])  4.9 us
    pallas_call x1, Pallas kernels, per_device_by_target(): pl.pallas_call(functools.partial(align_kernel, groups, target_rows, targe...  4.24 us
    ppermute x3, starting transfers between devices, per_device_by_target(): blocks.append([direct[k - 1], lax.ppermute(direct[k - 1], 'qry', swap)])  3.78 us
    ppermute x4, waiting for transfers between devices, per_device_by_target(): other = [lax.ppermute(m, 'rep', swap) for m in mine]  1.48 us
    pallas_call x4, Pallas kernels, partial_similar(): pl.pallas_call(partial_kernel, out_shape=jax.ShapeDtypeStruct((query.shap...  1.31 us
    squeeze x1, local copies, waits for them, and re-layouts, per_device_by_target(): share = lax.dynamic_index_in_dim(target_res, at_qry, 0, keepdims=False)  1.16 us
  transfers between devices with their start and end apart: 13, of which 5 were waited for; matrix products, arithmetic and copies ran while one was open for 5% of the time, Pallas kernels for 3%

profile of v1, /device:TPU:0, one launch (start us, length us, event | category | flops | bytes accessed | tf_op | source)
XLA Modules:
  0.0 38.2 jit_solution(16515599867372677788)
XLA Ops:
  0.6 4.1 %collective-permute-start.1 = (f32[2,1280]{1,0:T(2,128)}, f32[2,1280]{1,0:T(2,128)S(1)}, u32[]{:S(2)}, u32[]{:S(2)}) collective-permute-start(f32[2,1280]{1,0:T(2,128)} %refs_5_.1), channel_id=1, source_target_pairs={{0,8},{4,12},{8,0},{12,4},{1,9},{5,13},{9,1},{13,5},{2,10},{6,14},... | collective-permute-start | bytes 30728 | tf_op jit(solution)/shard_map/ppermute | solution.py:193
  4.7 1.6 %collective-permute-start = (f32[2,1280]{1,0:T(2,128)}, f32[2,1280]{1,0:T(2,128)S(1)}, u32[]{:S(2)}, u32[]{:S(2)}) collective-permute-start(f32[2,1280]{1,0:T(2,128)} %refs_5_.1), channel_id=1, source_target_pairs={{0,4},{4,0},{8,12},{12,8},{1,5},{5,1},{9,13},{13,9},{2,6},{6,2},{1... | collective-permute-start | bytes 30728 | tf_op jit(solution)/shard_map/ppermute | solution.py:193
  6.3 1.2 %dynamic-slice_bitcast_fusion = (bf16[128,640]{1,0:T(8,128)(2,1)S(1)}, bf16[128,640]{1,0:T(8,128)(2,1)S(1)}, bf16[128,640]{1,0:T(8,128)(2,1)S(1)}) fusion(bf16[2,128,640]{2,1,0:T(8,128)(2,1)} %param.8, s32[]{:T(128)S(6)} %select_n.24), kind=kLoop, calls=%fused_computation | loop fusion | bytes 983044 | tf_op jit(solution)/shard_map/jit(dynamic_index_in_dim)/squeeze | solution.py:195
  7.5 3.9 %collective-permute-start.7 = (bf16[128,640]{1,0:T(8,128)(2,1)S(1)}, bf16[128,640]{1,0:T(8,128)(2,1)S(1)}, u32[]{:S(2)}, u32[]{:S(2)}) collective-permute-start(bf16[128,640]{1,0:T(8,128)(2,1)S(1)} %get-tuple-element.6), channel_id=1, source_target_pairs={{0,12},{4,8},{8,4},{12,0},{1,13},{5,9},{9,5},{13,1},{2,14},{6,10},... | collective-permute-start | bytes 491528 | tf_op jit(solution)/shard_map/ppermute | solution.py:193
  12.0 0.1 stack.35.refs_0_
  12.1 0.3 shard_map.86.refs_9_
  12.5 0.7 %collective-permute-start.3 = (bf16[128,640]{1,0:T(8,128)(2,1)S(1)}, bf16[128,640]{1,0:T(8,128)(2,1)S(1)}, u32[]{:S(2)}, u32[]{:S(2)}) collective-permute-start(bf16[128,640]{1,0:T(8,128)(2,1)S(1)} %get-tuple-element.6), channel_id=1, source_target_pairs={{0,4},{4,0},{8,12},{12,8},{1,5},{5,1},{9,13},{13,9},{2,6},{6,2},{1... | collective-permute-start | bytes 491528 | tf_op jit(solution)/shard_map/ppermute | solution.py:193
  13.2 0.2 rev.10
  13.4 0.1 collective-permute-start.9
  13.5 0.3 rev.9
  13.8 2.7 %collective-permute-done.7.refs_1_.refs_23_ = bf16[128,640]{1,0:T(8,128)(2,1)S(1)} collective-permute-done((bf16[128,640]{1,0:T(8,128)(2,1)S(1)}, bf16[128,640]{1,0:T(8,128)(2,1)S(1)}, u32[]{:S(2)}, u32[]{:S(2)}) %collective-permute-start.7) | collective-permute-done | bytes 163872 | tf_op jit(solution)/shard_map/ppermute | solution.py:193
  16.5 1.8 %collective-permute-start.8 = (bf16[128,640]{1,0:T(8,128)(2,1)S(1)}, bf16[128,640]{1,0:T(8,128)(2,1)S(1)}, u32[]{:S(2)}, u32[]{:S(2)}) collective-permute-start(bf16[128,640]{1,0:T(8,128)(2,1)S(1)} %collective-permute-done.7.refs_1_.refs_23_), channel_id=1, source_target_pairs={{0,2},{2,0},{1,3},{3,1},{4,6},{6,4},{5,7},{7,5},{8,10},{10,8},{9,1... | collective-permute-start | bytes 491528 | tf_op jit(solution)/shard_map/ppermute | solution.py:202
  18.3 5.6 %collective-permute-done.5.refs_1_.refs_21_ = bf16[128,640]{1,0:T(8,128)(2,1)S(1)} collective-permute-done((bf16[128,640]{1,0:T(8,128)(2,1)S(1)}, bf16[128,640]{1,0:T(8,128)(2,1)S(1)}, u32[]{:S(2)}, u32[]{:S(2)}) %collective-permute-start.5) | collective-permute-done | bytes 163872 | tf_op jit(solution)/shard_map/ppermute | solution.py:193
  23.9 1.5 %collective-permute-start.6 = (bf16[128,640]{1,0:T(8,128)(2,1)S(1)}, bf16[128,640]{1,0:T(8,128)(2,1)S(1)}, u32[]{:S(2)}, u32[]{:S(2)}) collective-permute-start(bf16[128,640]{1,0:T(8,128)(2,1)S(1)} %collective-permute-done.5.refs_1_.refs_21_), channel_id=1, source_target_pairs={{0,2},{2,0},{1,3},{3,1},{4,6},{6,4},{5,7},{7,5},{8,10},{10,8},{9,1... | collective-permute-start | bytes 491528 | tf_op jit(solution)/shard_map/ppermute | solution.py:202
  25.4 0.5 %collective-permute-start.4 = (bf16[128,640]{1,0:T(8,128)(2,1)S(1)}, bf16[128,640]{1,0:T(8,128)(2,1)S(1)}, u32[]{:S(2)}, u32[]{:S(2)}) collective-permute-start(bf16[128,640]{1,0:T(8,128)(2,1)S(1)} %collective-permute-done.3.refs_1_.refs_19_), channel_id=1, source_target_pairs={{0,2},{2,0},{1,3},{3,1},{4,6},{6,4},{5,7},{7,5},{8,10},{10,8},{9,1... | collective-permute-start | bytes 491528 | tf_op jit(solution)/shard_map/ppermute | solution.py:202
  25.9 0.3 rev.11
  26.2 0.3 shard_map.89.refs_12_
  26.6 3.6 %collective-permute-done.6.refs_2_.refs_22_ = bf16[128,640]{1,0:T(8,128)(2,1)S(1)} collective-permute-done((bf16[128,640]{1,0:T(8,128)(2,1)S(1)}, bf16[128,640]{1,0:T(8,128)(2,1)S(1)}, u32[]{:S(2)}, u32[]{:S(2)}) %collective-permute-start.6) | collective-permute-done | bytes 163872 | tf_op jit(solution)/shard_map/ppermute | solution.py:202
  30.2 0.3 shard_map.88.refs_11_
  30.5 0.1 collective-permute-start.11
  30.6 1.3 %collective-permute-done.4.refs_2_.refs_20_ = bf16[128,640]{1,0:T(8,128)(2,1)S(1)} collective-permute-done((bf16[128,640]{1,0:T(8,128)(2,1)S(1)}, bf16[128,640]{1,0:T(8,128)(2,1)S(1)}, u32[]{:S(2)}, u32[]{:S(2)}) %collective-permute-start.4) | collective-permute-done | bytes 163872 | tf_op jit(solution)/shard_map/ppermute | solution.py:202
  31.9 0.3 shard_map.87.refs_10_
  32.4 1.5 %collective-permute-done.10.refs_14_ = f32[256,256]{1,0:T(8,128)S(1)} collective-permute-done((f32[256,256]{1,0:T(8,128)S(1)}, f32[256,256]{1,0:T(8,128)S(1)}, u32[]{:S(2)}, u32[]{:S(2)}) %collective-permute-start.10) | collective-permute-done | bytes 262176 | tf_op jit(solution)/shard_map/ppermute | solution.py:206
  33.9 4.2 %shard_map.90 = (bf16[256,640]{1,0:T(8,128)(2,1)}, f32[1,8]{1,0:T(1,128)}) custom-call(s32[8]{0:T(128)S(1)} %stack.35.refs_0_, s32[8]{0:T(128)S(1)} %copy-done.3, f32[1]{0:T(128)S(6)} %copy.9.refs_2_, s32[1,28]{1,0:T(1,128)S(1)} %copy-done.4, f32[1,1280]{1,0:T(1,128)S(1)} %copy-done.2, f32[2,1280]{1,0:T(2,128)S(1)} %copy-done.1, ...), custom_call_target="tpu_custom_call" | custom-call | flops 335544320 | bytes 4194304 | tf_op jit(solution)/shard_map/pallas_call | solution.py:214
  (25 shorter events, 0.2 us)
Async XLA Ops:
  0.6 11.8 %collective-permute-start.1 = (f32[2,1280]{1,0:T(2,128)}, f32[2,1280]{1,0:T(2,128)S(1)}, u32[]{:S(2)}, u32[]{:S(2)}) collective-permute-start(f32[2,1280]{1,0:T(2,128)} %refs_5_.1), channel_id=1, source_target_pairs={{0,8},{4,12},{8,0},{12,4},{1,9},{5,13},{9,1},{13,5},{2,10},{6,14},... | collective-permute-start | bytes 30728 | tf_op jit(solution)/shard_map/ppermute | solution.py:193
  4.7 8.7 %collective-permute-start = (f32[2,1280]{1,0:T(2,128)}, f32[2,1280]{1,0:T(2,128)S(1)}, u32[]{:S(2)}, u32[]{:S(2)}) collective-permute-start(f32[2,1280]{1,0:T(2,128)} %refs_5_.1), channel_id=1, source_target_pairs={{0,4},{4,0},{8,12},{12,8},{1,5},{5,1},{9,13},{13,9},{2,6},{6,2},{1... | collective-permute-start | bytes 30728 | tf_op jit(solution)/shard_map/ppermute | solution.py:193
  6.3 19.6 %collective-permute-start.2 = (f32[2,1280]{1,0:T(2,128)}, f32[2,1280]{1,0:T(2,128)S(1)}, u32[]{:S(2)}, u32[]{:S(2)}) collective-permute-start(f32[2,1280]{1,0:T(2,128)} %refs_5_.1), channel_id=1, source_target_pairs={{0,12},{4,8},{8,4},{12,0},{1,13},{5,9},{9,5},{13,1},{2,14},{6,10},... | collective-permute-start | bytes 30728 | tf_op jit(solution)/shard_map/ppermute | solution.py:193
  6.3 5.8 %copy-start = (bf16[1,256,640]{2,1,0:T(8,128)(2,1)S(1)}, bf16[1,256,640]{2,1,0:T(8,128)(2,1)}, u32[]{:S(2)}) copy-start(bf16[1,256,640]{2,1,0:T(8,128)(2,1)} %param.7) | copy-start | bytes 983044
  7.5 9.1 %collective-permute-start.7 = (bf16[128,640]{1,0:T(8,128)(2,1)S(1)}, bf16[128,640]{1,0:T(8,128)(2,1)S(1)}, u32[]{:S(2)}, u32[]{:S(2)}) collective-permute-start(bf16[128,640]{1,0:T(8,128)(2,1)S(1)} %get-tuple-element.6), channel_id=1, source_target_pairs={{0,12},{4,8},{8,4},{12,0},{1,13},{5,9},{9,5},{13,1},{2,14},{6,10},... | collective-permute-start | bytes 491528 | tf_op jit(solution)/shard_map/ppermute | solution.py:193
  11.4 12.5 %collective-permute-start.5 = (bf16[128,640]{1,0:T(8,128)(2,1)S(1)}, bf16[128,640]{1,0:T(8,128)(2,1)S(1)}, u32[]{:S(2)}, u32[]{:S(2)}) collective-permute-start(bf16[128,640]{1,0:T(8,128)(2,1)S(1)} %get-tuple-element.6), channel_id=1, source_target_pairs={{0,8},{4,12},{8,0},{12,4},{1,9},{5,13},{9,1},{13,5},{2,10},{6,14},... | collective-permute-start | bytes 491528 | tf_op jit(solution)/shard_map/ppermute | solution.py:193
  12.5 12.9 %collective-permute-start.3 = (bf16[128,640]{1,0:T(8,128)(2,1)S(1)}, bf16[128,640]{1,0:T(8,128)(2,1)S(1)}, u32[]{:S(2)}, u32[]{:S(2)}) collective-permute-start(bf16[128,640]{1,0:T(8,128)(2,1)S(1)} %get-tuple-element.6), channel_id=1, source_target_pairs={{0,4},{4,0},{8,12},{12,8},{1,5},{5,1},{9,13},{13,9},{2,6},{6,2},{1... | collective-permute-start | bytes 491528 | tf_op jit(solution)/shard_map/ppermute | solution.py:193
  13.4 19.0 %collective-permute-start.9 = (f32[256,256]{1,0:T(8,128)S(1)}, f32[256,256]{1,0:T(8,128)S(1)}, u32[]{:S(2)}, u32[]{:S(2)}) collective-permute-start(f32[256,256]{1,0:T(8,128)S(1)} %shard_map.86.refs_9_), channel_id=1, source_target_pairs={{0,1},{1,0},{2,3},{3,2},{4,5},{5,4},{6,7},{7,6},{8,9},{9,8},{10,11... | collective-permute-start | bytes 786440 | tf_op jit(solution)/shard_map/ppermute | solution.py:206
  16.5 9.6 %collective-permute-start.8 = (bf16[128,640]{1,0:T(8,128)(2,1)S(1)}, bf16[128,640]{1,0:T(8,128)(2,1)S(1)}, u32[]{:S(2)}, u32[]{:S(2)}) collective-permute-start(bf16[128,640]{1,0:T(8,128)(2,1)S(1)} %collective-permute-done.7.refs_1_.refs_23_), channel_id=1, source_target_pairs={{0,2},{2,0},{1,3},{3,1},{4,6},{6,4},{5,7},{7,5},{8,10},{10,8},{9,1... | collective-permute-start | bytes 491528 | tf_op jit(solution)/shard_map/ppermute | solution.py:202
  23.9 6.3 %collective-permute-start.6 = (bf16[128,640]{1,0:T(8,128)(2,1)S(1)}, bf16[128,640]{1,0:T(8,128)(2,1)S(1)}, u32[]{:S(2)}, u32[]{:S(2)}) collective-permute-start(bf16[128,640]{1,0:T(8,128)(2,1)S(1)} %collective-permute-done.5.refs_1_.refs_21_), channel_id=1, source_target_pairs={{0,2},{2,0},{1,3},{3,1},{4,6},{6,4},{5,7},{7,5},{8,10},{10,8},{9,1... | collective-permute-start | bytes 491528 | tf_op jit(solution)/shard_map/ppermute | solution.py:202
  25.4 6.6 %collective-permute-start.4 = (bf16[128,640]{1,0:T(8,128)(2,1)S(1)}, bf16[128,640]{1,0:T(8,128)(2,1)S(1)}, u32[]{:S(2)}, u32[]{:S(2)}) collective-permute-start(bf16[128,640]{1,0:T(8,128)(2,1)S(1)} %collective-permute-done.3.refs_1_.refs_19_), channel_id=1, source_target_pairs={{0,2},{2,0},{1,3},{3,1},{4,6},{6,4},{5,7},{7,5},{8,10},{10,8},{9,1... | collective-permute-start | bytes 491528 | tf_op jit(solution)/shard_map/ppermute | solution.py:202
  26.5 5.9 %collective-permute-start.12 = (f32[256,256]{1,0:T(8,128)S(1)}, f32[256,256]{1,0:T(8,128)S(1)}, u32[]{:S(2)}, u32[]{:S(2)}) collective-permute-start(f32[256,256]{1,0:T(8,128)S(1)} %shard_map.89.refs_12_), channel_id=1, source_target_pairs={{0,1},{1,0},{2,3},{3,2},{4,5},{5,4},{6,7},{7,6},{8,9},{9,8},{10,11... | collective-permute-start | bytes 786440 | tf_op jit(solution)/shard_map/ppermute | solution.py:206
  30.5 1.9 %collective-permute-start.11 = (f32[256,256]{1,0:T(8,128)S(1)}, f32[256,256]{1,0:T(8,128)S(1)}, u32[]{:S(2)}, u32[]{:S(2)}) collective-permute-start(f32[256,256]{1,0:T(8,128)S(1)} %shard_map.88.refs_11_), channel_id=1, source_target_pairs={{0,1},{1,0},{2,3},{3,2},{4,5},{5,4},{6,7},{7,6},{8,9},{9,8},{10,11... | collective-permute-start | bytes 786440 | tf_op jit(solution)/shard_map/ppermute | solution.py:206
  32.3 1.7 %copy-start.1 = (f32[2,1280]{1,0:T(2,128)S(1)}, f32[2,1280]{1,0:T(2,128)}, u32[]{:S(2)}) copy-start(f32[2,1280]{1,0:T(2,128)} %refs_5_.1) | copy-start | bytes 30724
  32.3 1.6 %copy-start.2 = (f32[1,1280]{1,0:T(1,128)S(1)}, f32[1,1280]{1,0:T(1,128)}, u32[]{:S(2)}) copy-start(f32[1,1280]{1,0:T(1,128)} %refs_4_.1) | copy-start | bytes 15364
  32.3 1.6 %copy-start.3 = (s32[8]{0:T(128)S(1)}, s32[8]{0:T(128)}, u32[]{:S(2)}) copy-start(s32[8]{0:T(128)} %refs_1_.1) | copy-start | bytes 100
  32.3 1.6 %copy-start.4 = (s32[1,28]{1,0:T(1,128)S(1)}, s32[1,28]{1,0:T(1,128)}, u32[]{:S(2)}) copy-start(s32[1,28]{1,0:T(1,128)} %refs_3_.1) | copy-start | bytes 340
  32.3 1.6 %collective-permute-start.10 = (f32[256,256]{1,0:T(8,128)S(1)}, f32[256,256]{1,0:T(8,128)S(1)}, u32[]{:S(2)}, u32[]{:S(2)}) collective-permute-start(f32[256,256]{1,0:T(8,128)S(1)} %shard_map.87.refs_10_), channel_id=1, source_target_pairs={{0,1},{1,0},{2,3},{3,2},{4,5},{5,4},{6,7},{7,6},{8,9},{9,8},{10,11... | collective-permute-start | bytes 786440 | tf_op jit(solution)/shard_map/ppermute | solution.py:206

commit v2 on v0

--- a/solution.py
+++ b/solution.py
@@ -1,9 +1,14 @@
+import functools
 import math
 
 import jax
 import jax.numpy as jnp
 from jax import lax
+from jax.experimental import pallas as pl
+from jax.experimental.pallas import tpu as pltpu
 from jax.sharding import PartitionSpec as P
+
+VMEM_BYTES = 48 * 1024 * 1024
 
 
 def softmax_rows(logits):
@@ -53,7 +58,7 @@
     return jnp.take(arrived.reshape(tgt_count * capacity, target_rows, width), slot_of, axis=0)
 
 
-def per_device(query_res, target_res, target_len, hits, sharpness, query_pool, target_pool):
+def per_device_by_hit(query_res, target_res, target_len, hits, sharpness, query_pool, target_pool):
     tgt_count = lax.axis_size("tgt")
     query_count = query_res.shape[0]
     target_rows = target_res.shape[1]
@@ -81,6 +86,199 @@
     return (profile.astype(jnp.bfloat16), posterior)
 
 
+VMEM = pl.BlockSpec(memory_space=pltpu.VMEM)
+SMEM = pl.BlockSpec(memory_space=pltpu.SMEM)
+PARAMS = pltpu.CompilerParams(vmem_limit_bytes=VMEM_BYTES)
+
+
+def weigh_kernel(groups, slot_ref, hits_ref, pool_ref, *refs):
+    libs, (posterior_ref, weight_ref) = refs[:groups], refs[groups:]
+    owned, width = libs[0].shape
+    target_count = groups * owned
+    lane = lax.broadcasted_iota(jnp.int32, (1, target_count), 1)
+    pool, hits = pool_ref[...], hits_ref[...]
+    logits = jnp.zeros((1, target_count), jnp.float32)
+    counts = jnp.zeros((1, target_count), jnp.float32)
+    for group in range(groups):
+        products = jnp.sum(libs[group][...] * pool, axis=1, keepdims=True) / math.sqrt(width)
+        for a in range(owned):
+            logits = jnp.where(lane == slot_ref[group] * owned + a, products[a : a + 1, :], logits)
+    for t in range(target_count):
+        named = jnp.sum(jnp.where(hits == t, 1.0, 0.0), axis=1, keepdims=True)
+        counts = jnp.where(lane == t, named, counts)
+    raised = jnp.exp(logits - jnp.max(logits, axis=1, keepdims=True))
+    posterior_ref[...] = raised / jnp.sum(raised, axis=1, keepdims=True)
+    shown = jnp.where(counts > 0.0, logits, -jnp.inf)
+    parts = counts * jnp.exp(shown - jnp.max(shown, axis=1, keepdims=True))
+    weight_ref[...] = parts / jnp.sum(parts, axis=1, keepdims=True)
+
+
+def weigh_targets(slots, hits, pool, libs):
+    count = len(libs) * libs[0].shape[0]
+    shape = jax.ShapeDtypeStruct((1, count), jnp.float32)
+    return pl.pallas_call(
+        functools.partial(weigh_kernel, len(libs)),
+        out_shape=(shape, shape),
+        in_specs=[SMEM] + [VMEM] * (2 + len(libs)),
+        out_specs=(VMEM, VMEM),
+        cost_estimate=pl.CostEstimate(flops=65536, bytes_accessed=65536, transcendentals=64),
+        compiler_params=PARAMS,
+    )(slots, hits, pool, *libs)
+
+
+def partial_kernel(*refs):
+    query, blocks, out = refs[0], refs[1:-1], refs[-1]
+    rows = 0
+    for block in blocks:
+        out[:, rows : rows + block.shape[0]] = lax.dot_general(
+            query[...], block[...], (((1,), (1,)), ((), ())), preferred_element_type=jnp.float32
+        )
+        rows += block.shape[0]
+
+
+def partial_similar(query, blocks):
+    rows = sum(block.shape[0] for block in blocks)
+    cost = pl.CostEstimate(
+        flops=2 * query.shape[0] * rows * query.shape[1],
+        bytes_accessed=2 * (query.size + rows * query.shape[1]) + 4 * query.shape[0] * rows,
+        transcendentals=0,
+    )
+    return pl.pallas_call(
+        partial_kernel,
+        out_shape=jax.ShapeDtypeStruct((query.shape[0], rows), jnp.float32),
+        in_specs=[VMEM] * (1 + len(blocks)),
+        out_specs=VMEM,
+        cost_estimate=cost,
+        compiler_params=PARAMS,
+    )(query, *blocks)
+
+
+def align_kernel(model_width, parts, first, *refs):
+    slot_ref, len_ref, sharp_ref, weight_ref = refs[:4]
+    mine, other = refs[4 : 4 + parts], refs[4 + parts : 4 + 2 * parts]
+    blocks = refs[4 + 2 * parts : -2 if first else -3]
+    out_ref, align_ref = refs[-2:]
+    target_rows = blocks[0].shape[0]
+    scale = 1.0 / math.sqrt(model_width)
+    half_sharp = 0.5 * sharp_ref[0]
+    column = lax.broadcasted_iota(jnp.int32, (1, target_rows), 1)
+    weights = weight_ref[...]
+    lane = lax.broadcasted_iota(jnp.int32, weights.shape, 1)
+    acc = None if first else refs[-3][...]
+    places = [
+        (part, pl.ds(at, target_rows))
+        for part in range(parts)
+        for at in range(0, mine[part].shape[1], target_rows)
+    ]
+    for s, (part, at) in enumerate(places):
+        similar = (mine[part][:, at] + other[part][:, at]) * scale
+        length = len_ref[slot_ref[s]]
+        inside = column < length
+        fraction = 1.0 / length.astype(jnp.float32)
+        row_mean = jnp.sum(jnp.where(inside, similar, 0.0), axis=1, keepdims=True) * fraction
+        row_diff = similar - row_mean
+        row_var = (
+            jnp.sum(jnp.where(inside, row_diff * row_diff, 0.0), axis=1, keepdims=True) * fraction
+        )
+        column_mean = jnp.mean(similar, axis=0, keepdims=True)
+        column_diff = similar - column_mean
+        column_var = jnp.mean(column_diff * column_diff, axis=0, keepdims=True)
+        scores = row_diff * (half_sharp * lax.rsqrt(row_var + 1e-05)) + column_diff * (
+            half_sharp * lax.rsqrt(column_var + 1e-05)
+        )
+        scores = jnp.where(inside, scores, -jnp.inf)
+        raised = jnp.exp(scores - jnp.max(scores, axis=1, keepdims=True))
+        weight = jnp.sum(jnp.where(lane == slot_ref[s], weights, 0.0), axis=1, keepdims=True)
+        weight = weight / jnp.sum(raised, axis=1, keepdims=True)
+        align_ref[:, pl.ds(s * target_rows, target_rows)] = (raised * weight).astype(jnp.bfloat16)
+    for s, block in enumerate(blocks):
+        term = jnp.dot(
+            align_ref[:, pl.ds(s * target_rows, target_rows)],
+            block[...],
+            preferred_element_type=jnp.float32,
+        )
+        acc = term if acc is None else acc + term
+    out_ref[...] = acc.astype(out_ref.dtype)
+
+
+def add_aligned(common, weights, slots, mine, other, blocks, acc, dtype, model_width):
+    rows, width = mine[0].shape[0], blocks[0].shape[1]
+    target_rows = blocks[0].shape[0]
+    slots = jnp.stack(slots).astype(jnp.int32)
+    operands = [slots, *common, weights, *mine, *other, *blocks]
+    operands += [] if acc is None else [acc]
+    return pl.pallas_call(
+        functools.partial(align_kernel, model_width, len(mine), acc is None),
+        out_shape=jax.ShapeDtypeStruct((rows, width), dtype),
+        in_specs=[SMEM] * 3 + [VMEM] * (len(operands) - 3),
+        out_specs=VMEM,
+        scratch_shapes=[pltpu.VMEM((rows, len(blocks) * target_rows), jnp.bfloat16)],
+        cost_estimate=pl.CostEstimate(
+            flops=2 * rows * width * len(blocks) * target_rows,
+            bytes_accessed=len(blocks) * (8 * rows * target_rows + 2 * width * target_rows),
+            transcendentals=rows * len(blocks) * target_rows,
+        ),
+        compiler_params=PARAMS,
+    )(*operands)
+
+
+def per_device_by_target(
+    query_res, target_res, target_len, hits, sharpness, query_pool, target_pool
+):
+    model_width = query_pool.shape[1]
+    query = query_res[0]
+    at_tgt, at_qry = lax.axis_index("tgt"), lax.axis_index("qry")
+    swap = [(0, 1), (1, 0)]
+
+    def from_peer(array, k):
+        return lax.ppermute(array, "tgt", [(i, i ^ k) for i in range(4)])
+
+    def across(array, axis):
+        return lax.ppermute(array, axis, swap)
+
+    def after(array, *done):
+        return lax.optimization_barrier((array, *done))[0]
+
+    share = lax.dynamic_index_in_dim(target_res, at_qry, 0, keepdims=False)
+    far = from_peer(share, 2)
+    near = from_peer(target_res, 1)
+    own_blocks = [target_res[0], target_res[1]]
+    own = partial_similar(query, own_blocks)
+    own_other = across(own, "rep")
+    pool = after(target_pool, share)
+    libs = [pool, from_peer(pool, 1), from_peer(pool, 2), from_peer(after(pool, own_other), 3)]
+    far_rest = across(far, "qry")
+    last = from_peer(far, 1)
+    last_rest = across(last, "qry")
+
+    peers = jnp.stack([at_tgt ^ k for k in range(4)]).astype(jnp.int32)
+    posterior, weights = weigh_targets(peers, after(hits, far), query_pool, libs)
+    own_id, near_id, far_id, last_id = (2 * (at_tgt ^ k) for k in range(4))
+    common = (target_len, sharpness)
+
+    def aligned(slots, mine, other, blocks, acc, dtype=jnp.float32):
+        return add_aligned(
+            common, weights, slots, [mine], [other], blocks, acc, dtype, model_width
+        )
+
+    acc = aligned([own_id, own_id + 1], own, own_other, own_blocks, None)
+    one_blocks = [near[0], near[1], far, far_rest]
+    one = partial_similar(after(query, acc, last), one_blocks)
+    one_other = across(one, "rep")
+    two_blocks = [last]
+    two = partial_similar(query, two_blocks)
+    two_other = across(two, "rep")
+    slots = [near_id, near_id + 1, far_id + at_qry, far_id + 1 - at_qry]
+    acc = aligned(slots, after(one, two), one_other, one_blocks, acc)
+    three = partial_similar(after(query, acc), [last_rest])
+    three_other = across(three, "rep")
+    slots = [last_id + at_qry]
+    acc = aligned(slots, after(two, three), two_other, two_blocks, acc)
+    slots = [last_id + 1 - at_qry]
+    acc = aligned(slots, three, three_other, [last_rest], acc, jnp.bfloat16)
+    return (acc[None], posterior)
+
+
 def solution(mesh):
     placed = (
         P(("grp", "tgt", "qry"), None, "rep"),
@@ -91,6 +289,18 @@
         P(("grp", "tgt", "qry"), None),
         P(("grp", "tgt"), None),
     )
+    groups = mesh.shape["tgt"]
+
+    def per_device(*arrays):
+        query_res, target_res, _, hits = arrays[:4]
+        few = (
+            query_res.shape[0] == 1
+            and groups == 4 <= hits.shape[1] // target_res.shape[0]
+            and target_res.shape[0] == mesh.shape["qry"] == 2
+            and mesh.shape["rep"] == 2
+        )
+        return (per_device_by_target if few else per_device_by_hit)(*arrays)
+
     return jax.shard_map(
         per_device,
         mesh=mesh,

time: 295 us -> 36.8 us (0.12)
  waiting for transfers between devices: 200 us -> 8.79 us
  blocking collectives: 24.8 us -> 0 us
  other arithmetic: 24.4 us -> 0.23 us
  between operations: 14.9 us -> 1.45 us
  local copies, waits for them, and re-layouts: 14.7 us -> 4.28 us
  matrix products: 9.14 us -> 0 us
  Pallas kernels: 0 us -> 8.64 us
  starting transfers between devices: 5.93 us -> 13.2 us
    all_to_all x1 -> x0, waiting for transfers between devices: 199 us -> none  [fetch_shares(): lax.all_to_all(outgoing, 'tgt', split_axis=0, concat_axis=0, tiled=True)]
    ppermute x0 -> x12, starting transfers between devices: none -> 13.2 us  [the longest x6 9.68 us: from_peer(): return lax.ppermute(array, 'tgt', [(i, i ^ k) for i in range(4)])]
    gather x2 -> x0, local copies, waits for them, and re-layouts: 13.2 us -> none  [the longest x1 7.13 us: fetch_shares(): jnp.take(arrived.reshape(tgt_count * capacity, target_rows, width), slot_...]
    all_gather x1 -> x0, blocking collectives: 13.1 us -> none  [per_device(): library = lax.all_gather(target_pool, 'tgt', axis=0, tiled=True)]
    all_to_all x1 -> x0, blocking collectives: 11.7 us -> none  [fetch_shares(): lax.all_to_all(wanted, 'tgt', split_axis=0, concat_axis=0, tiled=True)]
    dot_general x3 -> x0, matrix products: 9.14 us -> none  [the longest x1 5.79 us: per_device(): jnp.einsum('qid,qhjd->qhij', query_res, chosen, preferred_element_type=jn...]
    select_n x4 -> x0, other arithmetic: 8.91 us -> none  [the longest x2 8.18 us: fetch_shares(): jnp.take(target_res, requested.reshape(tgt_count * capacity), axis=0)]
    ppermute x0 -> x12, waiting for transfers between devices: none -> 8.79 us  [the longest x6 7.68 us: from_peer(): return lax.ppermute(array, 'tgt', [(i, i ^ k) for i in range(4)])]
  transfers between devices with their start and end apart: 2 -> 12, of which waited for: 2 -> 5; matrix products, arithmetic and copies ran while one was open for 3% -> 1% of each run, Pallas kernels for 0% -> 17%
where the time goes in v2:
time: 36.8 us; the launch traced here: 36.6 us
  starting transfers between devices  13.2 us (36%)
  waiting for transfers between devices  8.79 us (24%)
  Pallas kernels  8.64 us (23%)
  local copies, waits for them, and re-layouts  4.28 us (12%)
  between operations  1.45 us (4%)
    ppermute x6, starting transfers between devices, from_peer(): return lax.ppermute(array, 'tgt', [(i, i ^ k) for i in range(4)])  9.68 us
    ppermute x6, waiting for transfers between devices, from_peer(): return lax.ppermute(array, 'tgt', [(i, i ^ k) for i in range(4)])  7.68 us
    pallas_call x4, Pallas kernels, add_aligned(): pl.pallas_call(functools.partial(align_kernel, model_width, len(mine), ac...  6 us
    ppermute x6, starting transfers between devices, across(): return lax.ppermute(array, axis, swap)  3.54 us
    unnamed x16, local copies, waits for them, and re-layouts  3.08 us
    pallas_call x1, Pallas kernels, weigh_targets(): pl.pallas_call(functools.partial(weigh_kernel, len(libs)), out_shape=(sha...  1.33 us
    pallas_call x4, Pallas kernels, partial_similar(): pl.pallas_call(partial_kernel, out_shape=jax.ShapeDtypeStruct((query.shap...  1.31 us
    squeeze x1, local copies, waits for them, and re-layouts, per_device_by_target(): own_blocks = [target_res[0], target_res[1]]  1.17 us
  transfers between devices with their start and end apart: 12, of which 5 were waited for; matrix products, arithmetic and copies ran while one was open for 1% of the time, Pallas kernels for 17%

profile of v2, /device:TPU:0, one launch (start us, length us, event | category | flops | bytes accessed | tf_op | source)
XLA Modules:
  0.0 36.6 jit_solution(2844728685518786872)
XLA Ops:
  0.6 1.2 %slice_bitcast_fusion.2 = (bf16[128,640]{1,0:T(8,128)(2,1)S(1)}, bf16[128,640]{1,0:T(8,128)(2,1)S(1)}, bf16[128,640]{1,0:T(8,128)(2,1)S(1)}) fusion(bf16[2,128,640]{2,1,0:T(8,128)(2,1)} %param.8, s32[]{:T(128)S(6)} %select_n.4), kind=kLoop, calls=%fused_computation.2 | loop fusion | bytes 983044 | tf_op jit(solution)/shard_map/squeeze | solution.py:245
  1.8 4.1 %collective-permute-start = (bf16[128,640]{1,0:T(8,128)(2,1)S(1)}, bf16[128,640]{1,0:T(8,128)(2,1)S(1)}, u32[]{:S(2)}, u32[]{:S(2)}) collective-permute-start(bf16[128,640]{1,0:T(8,128)(2,1)S(1)} %get-tuple-element.24), channel_id=1, source_target_pairs={{0,8},{4,12},{8,0},{12,4},{1,9},{5,13},{9,1},{13,5},{2,10},{6,14},... | collective-permute-start | bytes 491528 | tf_op jit(solution)/shard_map/ppermute | solution.py:234
  5.9 0.3 shard_map.86.refs_4_
  6.3 0.6 %copy-done.7 = bf16[2,128,640]{2,1,0:T(8,128)(2,1)S(1)} copy-done((bf16[2,128,640]{2,1,0:T(8,128)(2,1)S(1)}, bf16[2,128,640]{2,1,0:T(8,128)(2,1)}, u32[]{:S(2)}) %copy-start.7) | copy-done | bytes 327704
  6.9 1.6 %collective-permute-start.6 = (bf16[2,128,640]{2,1,0:T(8,128)(2,1)S(1)}, bf16[2,128,640]{2,1,0:T(8,128)(2,1)S(1)}, u32[]{:S(2)}, u32[]{:S(2)}) collective-permute-start(bf16[2,128,640]{2,1,0:T(8,128)(2,1)S(1)} %copy-done.7), channel_id=1, source_target_pairs={{0,4},{4,0},{8,12},{12,8},{1,5},{5,1},{9,13},{13,9},{2,6},{6,2},{1... | collective-permute-start | bytes 983048 | tf_op jit(solution)/shard_map/ppermute | solution.py:234
  8.5 0.4 %collective-permute-start.1 = (f32[2,1280]{1,0:T(2,128)S(1)}, f32[2,1280]{1,0:T(2,128)S(1)}, u32[]{:S(2)}, u32[]{:S(2)}) collective-permute-start(f32[2,1280]{1,0:T(2,128)S(1)} %copy-done.3), channel_id=1, source_target_pairs={{0,4},{4,0},{8,12},{12,8},{1,5},{5,1},{9,13},{13,9},{2,6},{6,2},{1... | collective-permute-start | bytes 30728 | tf_op jit(solution)/shard_map/ppermute | solution.py:234
  8.9 4.9 %collective-permute-done.refs_3_.refs_8_ = bf16[128,640]{1,0:T(8,128)(2,1)S(1)} collective-permute-done((bf16[128,640]{1,0:T(8,128)(2,1)S(1)}, bf16[128,640]{1,0:T(8,128)(2,1)S(1)}, u32[]{:S(2)}, u32[]{:S(2)}) %collective-permute-start) | collective-permute-done | bytes 163872 | tf_op jit(solution)/shard_map/ppermute | solution.py:234
  13.8 0.6 %collective-permute-start.5 = (bf16[128,640]{1,0:T(8,128)(2,1)S(1)}, bf16[128,640]{1,0:T(8,128)(2,1)S(1)}, u32[]{:S(2)}, u32[]{:S(2)}) collective-permute-start(bf16[128,640]{1,0:T(8,128)(2,1)S(1)} %collective-permute-done.refs_3_.refs_8_), channel_id=1, source_target_pairs={{0,4},{4,0},{8,12},{12,8},{1,5},{5,1},{9,13},{13,9},{2,6},{6,2},{1... | collective-permute-start | bytes 491528 | tf_op jit(solution)/shard_map/ppermute | solution.py:234
  14.6 2.9 %collective-permute-start.4 = (f32[2,1280]{1,0:T(2,128)S(1)}, f32[2,1280]{1,0:T(2,128)S(1)}, u32[]{:S(2)}, u32[]{:S(2)}) collective-permute-start(f32[2,1280]{1,0:T(2,128)S(1)} %copy-done.3), channel_id=1, source_target_pairs={{0,12},{4,8},{8,4},{12,0},{1,13},{5,9},{9,5},{13,1},{2,14},{6,10},... | collective-permute-start | bytes 30728 | tf_op jit(solution)/shard_map/ppermute | solution.py:234
  18.2 2.0 %collective-permute-done.1.refs_1_ = f32[2,1280]{1,0:T(2,128)S(1)} collective-permute-done((f32[2,1280]{1,0:T(2,128)S(1)}, f32[2,1280]{1,0:T(2,128)S(1)}, u32[]{:S(2)}, u32[]{:S(2)}) %collective-permute-start.1) | collective-permute-done | bytes 10272 | tf_op jit(solution)/shard_map/ppermute | solution.py:234
  20.1 1.5 %collective-permute-start.7 = (bf16[128,640]{1,0:T(8,128)(2,1)S(1)}, bf16[128,640]{1,0:T(8,128)(2,1)S(1)}, u32[]{:S(2)}, u32[]{:S(2)}) collective-permute-start(bf16[128,640]{1,0:T(8,128)(2,1)S(1)} %collective-permute-done.refs_3_.refs_8_), channel_id=1, source_target_pairs={{0,2},{2,0},{1,3},{3,1},{4,6},{6,4},{5,7},{7,5},{8,10},{10,8},{9,1... | collective-permute-start | bytes 491528 | tf_op jit(solution)/shard_map/ppermute | solution.py:237
  21.7 0.8 %collective-permute-done.4.refs_3_ = f32[2,1280]{1,0:T(2,128)S(1)} collective-permute-done((f32[2,1280]{1,0:T(2,128)S(1)}, f32[2,1280]{1,0:T(2,128)S(1)}, u32[]{:S(2)}, u32[]{:S(2)}) %collective-permute-start.4) | collective-permute-done | bytes 10272 | tf_op jit(solution)/shard_map/ppermute | solution.py:234
  22.5 1.3 %shard_map.87 = (f32[1,8]{1,0:T(1,128)}, f32[1,8]{1,0:T(1,128)S(1)}) custom-call(s32[4]{0:T(128)S(1)} %pad_add_fusion.slot_ref, s32[1,28]{1,0:T(1,128)S(1)} %copy-done.6, f32[1,1280]{1,0:T(1,128)S(1)} %copy-done.5, f32[2,1280]{1,0:T(2,128)S(1)} %copy-done.3, f32[2,1280]{1,0:T(2,128)S(1)} %collective-permute-done.1.refs_1_, ...), custom_call_target="tpu_custom_call" | custom-call | flops 65536 | bytes 65536 | tf_op jit(solution)/shard_map/pallas_call | solution.py:119
  23.9 0.7 %copy-done.4 = s32[8]{0:T(128)S(1)} copy-done((s32[8]{0:T(128)S(1)}, s32[8]{0:T(128)}, u32[]{:S(2)}) %copy-start.4) | copy-done | bytes 56
  24.5 1.3 %shard_map.88.refs_10_ = f32[256,640]{1,0:T(8,128)S(1)} custom-call(s32[2]{0:T(128)S(1)} %pad_add_fusion.2.refs_0_, s32[8]{0:T(128)S(1)} %copy-done.4, f32[1]{0:T(128)S(6)} %copy.9.refs_2_, f32[1,8]{1,0:T(1,128)S(1)} %get-tuple-element.14.refs_3_, f32[256,256]{1,0:T(8,128)S(1)} %shard_map.86.refs_4_, f32[256,256]{1,0:T(8,128)S(1)} %collective-permute-done.3.refs_5_, ...), custom_call_target="tpu_custom_call" | custom-call | flops 83886080 | bytes 851968 | tf_op jit(solution)/shard_map/pallas_call | solution.py:210
  25.9 0.5 %shard_map.89.refs_4_ = f32[256,512]{1,0:T(8,128)S(1)} custom-call(bf16[256,640]{1,0:T(8,128)(2,1)S(1)} %bitcast.25, bf16[128,640]{1,0:T(8,128)(2,1)S(1)} %get-tuple-element.21.refs_1_.refs_6_, bf16[128,640]{1,0:T(8,128)(2,1)S(1)} %get-tuple-element.20.refs_2_.refs_7_, bf16[128,640]{1,0:T(8,128)(2,1)S(1)} %collective-permute-done.refs_3_.refs_8_, ...), custom_call_target="tpu_custom_call" | custom-call | flops 167772160 | bytes 1507328 | tf_op jit(solution)/shard_map/pallas_call | solution.py:146
  26.5 1.6 %collective-permute-start.9 = (bf16[128,640]{1,0:T(8,128)(2,1)S(1)}, bf16[128,640]{1,0:T(8,128)(2,1)S(1)}, u32[]{:S(2)}, u32[]{:S(2)}) collective-permute-start(bf16[128,640]{1,0:T(8,128)(2,1)S(1)} %collective-permute-done.5.refs_1_.refs_6_), channel_id=1, source_target_pairs={{0,2},{2,0},{1,3},{3,1},{4,6},{6,4},{5,7},{7,5},{8,10},{10,8},{9,1... | collective-permute-start | bytes 491528 | tf_op jit(solution)/shard_map/ppermute | solution.py:237
  28.1 0.2 shard_map.90.refs_4_
  28.6 0.8 %copy-done.1 = f32[256,512]{1,0:T(8,128)} copy-done((f32[256,512]{1,0:T(8,128)}, f32[256,512]{1,0:T(8,128)S(1)}, u32[]{:S(2)}) %copy-start.1) | copy-done | bytes 524312
  29.4 1.0 %copy-done.2 = f32[256,512]{1,0:T(8,128)S(1)} copy-done((f32[256,512]{1,0:T(8,128)S(1)}, f32[256,512]{1,0:T(8,128)}, u32[]{:S(2)}) %copy-start.2) | copy-done | bytes 524312
  30.5 1.7 %shard_map.91.refs_7_ = f32[256,640]{1,0:T(8,128)S(1)} custom-call(s32[4]{0:T(128)S(1)} %pad_add_fusion.1.refs_0_, s32[8]{0:T(128)S(1)} %copy-done.4, f32[1]{0:T(128)S(6)} %copy.9.refs_2_, f32[1,8]{1,0:T(1,128)S(1)} %get-tuple-element.14.refs_3_, f32[256,512]{1,0:T(8,128)S(1)} %shard_map.89.refs_4_, f32[256,512]{1,0:T(8,128)S(1)} %copy-done.2, ...), custom_call_target="tpu_custom_call" | custom-call | flops 167772160 | bytes 1703936 | tf_op jit(solution)/shard_map/pallas_call | solution.py:210
  32.2 0.9 %collective-permute-done.9.refs_1_.refs_6_ = bf16[128,640]{1,0:T(8,128)(2,1)S(1)} collective-permute-done((bf16[128,640]{1,0:T(8,128)(2,1)S(1)}, bf16[128,640]{1,0:T(8,128)(2,1)S(1)}, u32[]{:S(2)}, u32[]{:S(2)}) %collective-permute-start.9) | collective-permute-done | bytes 163872 | tf_op jit(solution)/shard_map/ppermute | solution.py:237
  33.4 1.1 %shard_map.93.refs_7_ = f32[256,640]{1,0:T(8,128)S(1)} custom-call(s32[1]{0:T(128)} %bitcast.17.refs_0_, s32[8]{0:T(128)S(1)} %copy-done.4, f32[1]{0:T(128)S(6)} %copy.9.refs_2_, f32[1,8]{1,0:T(1,128)S(1)} %get-tuple-element.14.refs_3_, f32[256,128]{1,0:T(8,128)S(1)} %shard_map.90.refs_4_, f32[256,128]{1,0:T(8,128)S(1)} %collective-permute-done.11.refs_5_, ...), custom_call_target="tpu_custom_call" | custom-call | flops 41943040 | bytes 425984 | tf_op jit(solution)/shard_map/pallas_call | solution.py:210
  34.8 1.8 %shard_map.94 = bf16[256,640]{1,0:T(8,128)(2,1)} custom-call(s32[1]{0:T(128)} %bitcast.refs_0_, s32[8]{0:T(128)S(1)} %copy-done.4, f32[1]{0:T(128)S(6)} %copy.9.refs_2_, f32[1,8]{1,0:T(1,128)S(1)} %get-tuple-element.14.refs_3_, f32[256,128]{1,0:T(8,128)S(1)} %shard_map.92.refs_4_, f32[256,128]{1,0:T(8,128)S(1)} %collective-permute-done.10.refs_5_, ...), custom_call_target="tpu_custom_call" | custom-call | flops 41943040 | bytes 425984 | tf_op jit(solution)/shard_map/pallas_call | solution.py:210
  (30 shorter events, 1.2 us)
Async XLA Ops:
  0.6 5.3 %copy-start = (bf16[1,256,640]{2,1,0:T(8,128)(2,1)S(1)}, bf16[1,256,640]{2,1,0:T(8,128)(2,1)}, u32[]{:S(2)}) copy-start(bf16[1,256,640]{2,1,0:T(8,128)(2,1)} %param.7) | copy-start | bytes 983044
  1.8 12.0 %collective-permute-start = (bf16[128,640]{1,0:T(8,128)(2,1)S(1)}, bf16[128,640]{1,0:T(8,128)(2,1)S(1)}, u32[]{:S(2)}, u32[]{:S(2)}) collective-permute-start(bf16[128,640]{1,0:T(8,128)(2,1)S(1)} %get-tuple-element.24), channel_id=1, source_target_pairs={{0,8},{4,12},{8,0},{12,4},{1,9},{5,13},{9,1},{13,5},{2,10},{6,14},... | collective-permute-start | bytes 491528 | tf_op jit(solution)/shard_map/ppermute | solution.py:234
  5.9 1.0 %copy-start.7 = (bf16[2,128,640]{2,1,0:T(8,128)(2,1)S(1)}, bf16[2,128,640]{2,1,0:T(8,128)(2,1)}, u32[]{:S(2)}) copy-start(bf16[2,128,640]{2,1,0:T(8,128)(2,1)} %param.8) | copy-start | bytes 983044
  5.9 2.6 %copy-start.3 = (f32[2,1280]{1,0:T(2,128)S(1)}, f32[2,1280]{1,0:T(2,128)}, u32[]{:S(2)}) copy-start(f32[2,1280]{1,0:T(2,128)} %refs_0_) | copy-start | bytes 30724
  6.3 8.3 %collective-permute-start.3 = (f32[256,256]{1,0:T(8,128)S(1)}, f32[256,256]{1,0:T(8,128)S(1)}, u32[]{:S(2)}, u32[]{:S(2)}) collective-permute-start(f32[256,256]{1,0:T(8,128)S(1)} %shard_map.86.refs_4_), channel_id=1, source_target_pairs={{0,1},{1,0},{2,3},{3,2},{4,5},{5,4},{6,7},{7,6},{8,9},{9,8},{10,11... | collective-permute-start | bytes 786440 | tf_op jit(solution)/shard_map/ppermute | solution.py:237
  6.9 18.9 %collective-permute-start.6 = (bf16[2,128,640]{2,1,0:T(8,128)(2,1)S(1)}, bf16[2,128,640]{2,1,0:T(8,128)(2,1)S(1)}, u32[]{:S(2)}, u32[]{:S(2)}) collective-permute-start(bf16[2,128,640]{2,1,0:T(8,128)(2,1)S(1)} %copy-done.7), channel_id=1, source_target_pairs={{0,4},{4,0},{8,12},{12,8},{1,5},{5,1},{9,13},{13,9},{2,6},{6,2},{1... | collective-permute-start | bytes 983048 | tf_op jit(solution)/shard_map/ppermute | solution.py:234
  8.5 11.7 %collective-permute-start.1 = (f32[2,1280]{1,0:T(2,128)S(1)}, f32[2,1280]{1,0:T(2,128)S(1)}, u32[]{:S(2)}, u32[]{:S(2)}) collective-permute-start(f32[2,1280]{1,0:T(2,128)S(1)} %copy-done.3), channel_id=1, source_target_pairs={{0,4},{4,0},{8,12},{12,8},{1,5},{5,1},{9,13},{13,9},{2,6},{6,2},{1... | collective-permute-start | bytes 30728 | tf_op jit(solution)/shard_map/ppermute | solution.py:234
  8.9 12.8 %collective-permute-start.2 = (f32[2,1280]{1,0:T(2,128)S(1)}, f32[2,1280]{1,0:T(2,128)S(1)}, u32[]{:S(2)}, u32[]{:S(2)}) collective-permute-start(f32[2,1280]{1,0:T(2,128)S(1)} %copy-done.3), channel_id=1, source_target_pairs={{0,8},{4,12},{8,0},{12,4},{1,9},{5,13},{9,1},{13,5},{2,10},{6,14},... | collective-permute-start | bytes 30728 | tf_op jit(solution)/shard_map/ppermute | solution.py:234
  13.8 12.0 %collective-permute-start.5 = (bf16[128,640]{1,0:T(8,128)(2,1)S(1)}, bf16[128,640]{1,0:T(8,128)(2,1)S(1)}, u32[]{:S(2)}, u32[]{:S(2)}) collective-permute-start(bf16[128,640]{1,0:T(8,128)(2,1)S(1)} %collective-permute-done.refs_3_.refs_8_), channel_id=1, source_target_pairs={{0,4},{4,0},{8,12},{12,8},{1,5},{5,1},{9,13},{13,9},{2,6},{6,2},{1... | collective-permute-start | bytes 491528 | tf_op jit(solution)/shard_map/ppermute | solution.py:234
  14.6 8.0 %collective-permute-start.4 = (f32[2,1280]{1,0:T(2,128)S(1)}, f32[2,1280]{1,0:T(2,128)S(1)}, u32[]{:S(2)}, u32[]{:S(2)}) collective-permute-start(f32[2,1280]{1,0:T(2,128)S(1)} %copy-done.3), channel_id=1, source_target_pairs={{0,12},{4,8},{8,4},{12,0},{1,13},{5,9},{9,5},{13,1},{2,14},{6,10},... | collective-permute-start | bytes 30728 | tf_op jit(solution)/shard_map/ppermute | solution.py:234
  17.4 5.1 %copy-start.5 = (f32[1,1280]{1,0:T(1,128)S(1)}, f32[1,1280]{1,0:T(1,128)}, u32[]{:S(2)}) copy-start(f32[1,1280]{1,0:T(1,128)} %pool_ref.1) | copy-start | bytes 15364
  17.5 5.0 %copy-start.6 = (s32[1,28]{1,0:T(1,128)S(1)}, s32[1,28]{1,0:T(1,128)}, u32[]{:S(2)}) copy-start(s32[1,28]{1,0:T(1,128)} %hits_ref) | copy-start | bytes 340
  20.1 5.7 %collective-permute-start.7 = (bf16[128,640]{1,0:T(8,128)(2,1)S(1)}, bf16[128,640]{1,0:T(8,128)(2,1)S(1)}, u32[]{:S(2)}, u32[]{:S(2)}) collective-permute-start(bf16[128,640]{1,0:T(8,128)(2,1)S(1)} %collective-permute-done.refs_3_.refs_8_), channel_id=1, source_target_pairs={{0,2},{2,0},{1,3},{3,1},{4,6},{6,4},{5,7},{7,5},{8,10},{10,8},{9,1... | collective-permute-start | bytes 491528 | tf_op jit(solution)/shard_map/ppermute | solution.py:237
  23.9 0.7 %copy-start.4 = (s32[8]{0:T(128)S(1)}, s32[8]{0:T(128)}, u32[]{:S(2)}) copy-start(s32[8]{0:T(128)} %refs_1_.7) | copy-start | bytes 100
  26.4 2.2 %collective-permute-start.8 = (f32[256,512]{1,0:T(8,128)S(1)}, f32[256,512]{1,0:T(8,128)S(1)}, u32[]{:S(2)}, u32[]{:S(2)}) collective-permute-start(f32[256,512]{1,0:T(8,128)S(1)} %shard_map.89.refs_4_), channel_id=1, source_target_pairs={{0,1},{1,0},{2,3},{3,2},{4,5},{5,4},{6,7},{7,6},{8,9},{9,8},{10,11... | collective-permute-start | bytes 1572872 | tf_op jit(solution)/shard_map/ppermute | solution.py:237
  26.5 6.6 %collective-permute-start.9 = (bf16[128,640]{1,0:T(8,128)(2,1)S(1)}, bf16[128,640]{1,0:T(8,128)(2,1)S(1)}, u32[]{:S(2)}, u32[]{:S(2)}) collective-permute-start(bf16[128,640]{1,0:T(8,128)(2,1)S(1)} %collective-permute-done.5.refs_1_.refs_6_), channel_id=1, source_target_pairs={{0,2},{2,0},{1,3},{3,1},{4,6},{6,4},{5,7},{7,5},{8,10},{10,8},{9,1... | collective-permute-start | bytes 491528 | tf_op jit(solution)/shard_map/ppermute | solution.py:237
  28.4 5.1 %collective-permute-start.11 = (f32[256,128]{1,0:T(8,128)S(1)}, f32[256,128]{1,0:T(8,128)S(1)}, u32[]{:S(2)}, u32[]{:S(2)}) collective-permute-start(f32[256,128]{1,0:T(8,128)S(1)} %shard_map.90.refs_4_), channel_id=1, source_target_pairs={{0,1},{1,0},{2,3},{3,2},{4,5},{5,4},{6,7},{7,6},{8,9},{9,8},{10,11... | collective-permute-start | bytes 393224 | tf_op jit(solution)/shard_map/ppermute | solution.py:237
  28.6 0.8 %copy-start.1 = (f32[256,512]{1,0:T(8,128)}, f32[256,512]{1,0:T(8,128)S(1)}, u32[]{:S(2)}) copy-start(f32[256,512]{1,0:T(8,128)S(1)} %collective-permute-done.8.refs_5_) | copy-start | bytes 1572868
  29.4 1.0 %copy-start.2 = (f32[256,512]{1,0:T(8,128)S(1)}, f32[256,512]{1,0:T(8,128)}, u32[]{:S(2)}) copy-start(f32[256,512]{1,0:T(8,128)} %copy-done.1) | copy-start | bytes 1572868
  33.3 1.4 %collective-permute-start.10 = (f32[256,128]{1,0:T(8,128)S(1)}, f32[256,128]{1,0:T(8,128)S(1)}, u32[]{:S(2)}, u32[]{:S(2)}) collective-permute-start(f32[256,128]{1,0:T(8,128)S(1)} %shard_map.92.refs_4_), channel_id=1, source_target_pairs={{0,1},{1,0},{2,3},{3,2},{4,5},{5,4},{6,7},{7,6},{8,9},{9,8},{10,11... | collective-permute-start | bytes 393224 | tf_op jit(solution)/shard_map/ppermute | solution.py:237

commit v3 on v2

--- a/solution.py
+++ b/solution.py
@@ -8,7 +8,7 @@
 from jax.experimental.pallas import tpu as pltpu
 from jax.sharding import PartitionSpec as P
 
-VMEM_BYTES = 48 * 1024 * 1024
+VMEM_BYTES = 16 * 1024 * 1024
 
 
 def softmax_rows(logits):
@@ -239,43 +239,31 @@
     def after(array, *done):
         return lax.optimization_barrier((array, *done))[0]
 
-    share = lax.dynamic_index_in_dim(target_res, at_qry, 0, keepdims=False)
-    far = from_peer(share, 2)
-    near = from_peer(target_res, 1)
-    own_blocks = [target_res[0], target_res[1]]
-    own = partial_similar(query, own_blocks)
-    own_other = across(own, "rep")
+    share = lax.dynamic_index_in_dim(target_res, at_qry, 0, keepdims=True)
+    library = lax.all_gather(share, ("tgt", "qry"), axis=0, tiled=True)
     pool = after(target_pool, share)
-    libs = [pool, from_peer(pool, 1), from_peer(pool, 2), from_peer(after(pool, own_other), 3)]
-    far_rest = across(far, "qry")
-    last = from_peer(far, 1)
-    last_rest = across(last, "qry")
-
+    libs = [pool] + [from_peer(pool, k) for k in range(1, 4)]
     peers = jnp.stack([at_tgt ^ k for k in range(4)]).astype(jnp.int32)
-    posterior, weights = weigh_targets(peers, after(hits, far), query_pool, libs)
-    own_id, near_id, far_id, last_id = (2 * (at_tgt ^ k) for k in range(4))
+    posterior, weights = weigh_targets(peers, hits, query_pool, libs)
     common = (target_len, sharpness)
-
-    def aligned(slots, mine, other, blocks, acc, dtype=jnp.float32):
-        return add_aligned(
-            common, weights, slots, [mine], [other], blocks, acc, dtype, model_width
-        )
-
-    acc = aligned([own_id, own_id + 1], own, own_other, own_blocks, None)
-    one_blocks = [near[0], near[1], far, far_rest]
-    one = partial_similar(after(query, acc, last), one_blocks)
-    one_other = across(one, "rep")
-    two_blocks = [last]
-    two = partial_similar(query, two_blocks)
-    two_other = across(two, "rep")
-    slots = [near_id, near_id + 1, far_id + at_qry, far_id + 1 - at_qry]
-    acc = aligned(slots, after(one, two), one_other, one_blocks, acc)
-    three = partial_similar(after(query, acc), [last_rest])
-    three_other = across(three, "rep")
-    slots = [last_id + at_qry]
-    acc = aligned(slots, after(two, three), two_other, two_blocks, acc)
-    slots = [last_id + 1 - at_qry]
-    acc = aligned(slots, three, three_other, [last_rest], acc, jnp.bfloat16)
+    library, weights = lax.optimization_barrier((library, weights))
+
+    pairs = [[library[2 * g], library[2 * g + 1]] for g in range(4)]
+    mine = [partial_similar(query, pair) for pair in pairs]
+    other = [across(m, "rep") for m in mine]
+    acc = None
+    for cut in ((0, 1), (2, 3)):
+        acc = add_aligned(
+            common,
+            weights,
+            [jnp.int32(t) for g in cut for t in (2 * g, 2 * g + 1)],
+            [mine[g] for g in cut],
+            [other[g] for g in cut],
+            [block for g in cut for block in pairs[g]],
+            acc,
+            jnp.bfloat16 if cut[-1] == 3 else jnp.float32,
+            model_width,
+        )
     return (acc[None], posterior)
 
 

time: 36.8 us -> 71.8 us (1.95)
  waiting for transfers between devices: 8.79 us -> 37.5 us
  between operations: 1.45 us -> 14.8 us
  starting transfers between devices: 13.2 us -> 6.98 us
  Pallas kernels: 8.64 us -> 6.92 us
  local copies, waits for them, and re-layouts: 4.28 us -> 5.21 us
    all_gather x0 -> x1, waiting for transfers between devices: none -> 31.9 us  [per_device_by_target(): library = lax.all_gather(share, ('tgt', 'qry'), axis=0, tiled=True)]
    ppermute x6 -> x3, starting transfers between devices: 9.68 us -> 5.68 us  [from_peer(): return lax.ppermute(array, 'tgt', [(i, i ^ k) for i in range(4)])]
    ppermute x6 -> x4, starting transfers between devices: 3.54 us -> 1.26 us  [across(): return lax.ppermute(array, axis, swap)]
    ppermute x6 -> x3, waiting for transfers between devices: 7.68 us -> 5.6 us  [from_peer(): return lax.ppermute(array, 'tgt', [(i, i ^ k) for i in range(4)])]
    pallas_call x4 -> x2, Pallas kernels: 6 us -> 4.24 us  [add_aligned(): pl.pallas_call(functools.partial(align_kernel, model_width, len(mine), ac...]
    ppermute x6 -> x4, waiting for transfers between devices: 1.11 us -> 0.01 us  [across(): return lax.ppermute(array, axis, swap)]
    squeeze x2 -> x1, local copies, waits for them, and re-layouts: 1.2 us -> 1.54 us  [per_device_by_target(): pairs = [[library[2 * g], library[2 * g + 1]] for g in range(4)]]
    unnamed x16 -> x14, local copies, waits for them, and re-layouts: 3.08 us -> 2.99 us
  transfers between devices with their start and end apart: 12 -> 8, of which waited for: 5 -> 3; matrix products, arithmetic and copies ran while one was open for 1% -> 0% of each run, Pallas kernels for 17% -> 6%
where the time goes in v3:
time: 71.8 us; the launch traced here: 71.6 us
  waiting for transfers between devices  37.5 us (52%)
  between operations  14.8 us (21%)
  starting transfers between devices  6.98 us (10%)
  Pallas kernels  6.92 us (10%)
  local copies, waits for them, and re-layouts  5.21 us (7%)
    all_gather x1, waiting for transfers between devices, per_device_by_target(): library = lax.all_gather(share, ('tgt', 'qry'), axis=0, tiled=True)  31.9 us
    ppermute x3, starting transfers between devices, from_peer(): return lax.ppermute(array, 'tgt', [(i, i ^ k) for i in range(4)])  5.68 us
    ppermute x3, waiting for transfers between devices, from_peer(): return lax.ppermute(array, 'tgt', [(i, i ^ k) for i in range(4)])  5.6 us
    pallas_call x2, Pallas kernels, add_aligned(): pl.pallas_call(functools.partial(align_kernel, model_width, len(mine), ac...  4.24 us
    unnamed x14, local copies, waits for them, and re-layouts  2.99 us
    squeeze x1, local copies, waits for them, and re-layouts, per_device_by_target(): pairs = [[library[2 * g], library[2 * g + 1]] for g in range(4)]  1.54 us
  transfers between devices with their start and end apart: 8, of which 3 were waited for; matrix products, arithmetic and copies ran while one was open for 0% of the time, Pallas kernels for 6%

profile of v3, /device:TPU:0, one launch (start us, length us, event | category | flops | bytes accessed | tf_op | source)
XLA Modules:
  0.0 71.6 jit_solution(13393350694807425363)
XLA Ops:
  7.2 0.0 all-gather.2.cloned.1.call-start
  7.2 0.9 %copy-done = bf16[2,128,640]{2,1,0:T(8,128)(2,1)S(1)} copy-done((bf16[2,128,640]{2,1,0:T(8,128)(2,1)S(1)}, bf16[2,128,640]{2,1,0:T(8,128)(2,1)}, u32[]{:S(2)}) %copy-start) | copy-done | bytes 327704
  8.1 0.7 constant_dynamic-slice_fusion
  8.8 3.1 %collective-permute-start = (f32[2,1280]{1,0:T(2,128)}, f32[2,1280]{1,0:T(2,128)S(1)}, u32[]{:S(2)}, u32[]{:S(2)}) collective-permute-start(f32[2,1280]{1,0:T(2,128)} %refs_0_), channel_id=1, source_target_pairs={{0,4},{4,0},{8,12},{12,8},{1,5},{5,1},{9,13},{13,9},{2,6},{6,2},{1... | collective-permute-start | bytes 30728 | tf_op jit(solution)/shard_map/ppermute | solution.py:234
  11.9 2.6 %collective-permute-start.1 = (f32[2,1280]{1,0:T(2,128)}, f32[2,1280]{1,0:T(2,128)S(1)}, u32[]{:S(2)}, u32[]{:S(2)}) collective-permute-start(f32[2,1280]{1,0:T(2,128)} %refs_0_), channel_id=1, source_target_pairs={{0,8},{4,12},{8,0},{12,4},{1,9},{5,13},{9,1},{13,5},{2,10},{6,14},... | collective-permute-start | bytes 30728 | tf_op jit(solution)/shard_map/ppermute | solution.py:234
  14.5 0.1 pad_add_fusion.slot_ref
  14.6 2.1 %collective-permute-done.1.refs_2_ = f32[2,1280]{1,0:T(2,128)S(1)} collective-permute-done((f32[2,1280]{1,0:T(2,128)}, f32[2,1280]{1,0:T(2,128)S(1)}, u32[]{:S(2)}, u32[]{:S(2)}) %collective-permute-start.1) | collective-permute-done | bytes 10272 | tf_op jit(solution)/shard_map/ppermute | solution.py:234
  16.7 3.5 %collective-permute-done.2.refs_3_ = f32[2,1280]{1,0:T(2,128)S(1)} collective-permute-done((f32[2,1280]{1,0:T(2,128)}, f32[2,1280]{1,0:T(2,128)S(1)}, u32[]{:S(2)}, u32[]{:S(2)}) %collective-permute-start.2) | collective-permute-done | bytes 10272 | tf_op jit(solution)/shard_map/ppermute | solution.py:234
  20.2 0.7 copy-done.2
  20.9 0.7 copy-done.3
  21.6 0.7 copy-done.5
  22.3 1.3 %shard_map.86 = (f32[1,8]{1,0:T(1,128)}, f32[1,8]{1,0:T(1,128)S(1)}) custom-call(s32[4]{0:T(128)S(1)} %pad_add_fusion.slot_ref, s32[1,28]{1,0:T(1,128)S(1)} %copy-done.5, f32[1,1280]{1,0:T(1,128)S(1)} %copy-done.3, f32[2,1280]{1,0:T(2,128)S(1)} %copy-done.2, f32[2,1280]{1,0:T(2,128)S(1)} %collective-permute-done.refs_1_, ...), custom_call_target="tpu_custom_call" | custom-call | flops 65536 | bytes 65536 | tf_op jit(solution)/shard_map/pallas_call | solution.py:119
  23.6 31.9 %all-gather.2.cloned.1.call-done = bf16[8,128,640]{2,1,0:T(8,128)(2,1)} async-done(((bf16[1,128,640]{2,1,0:T(8,128)(2,1)}), bf16[8,128,640]{2,1,0:T(8,128)(2,1)}) %all-gather.2.cloned.1.call-update) | async-done | bytes 1310736 | tf_op jit(solution)/shard_map/all_gather | solution.py:243
  55.5 1.5 %slice_bitcast_fusion = (bf16[128,640]{1,0:T(8,128)(2,1)S(1)}, bf16[128,640]{1,0:T(8,128)(2,1)S(1)}, bf16[128,640]{1,0:T(8,128)(2,1)S(1)}, bf16[128,640]{1,0:T(8...) fusion(bf16[8,128,640]{2,1,0:T(8,128)(2,1)} %all-gather.2.clone, ...), kind=kLoop, calls=%fused_computation | loop fusion | bytes 2621440 | tf_op jit(solution)/shard_map/squeeze | solution.py:251
  57.1 0.3 shard_map.90.refs_5_
  57.4 0.1 collective-permute-start.6
  57.5 0.3 shard_map.89.refs_4_
  57.8 0.6 collective-permute-start.5
  58.4 0.3 shard_map.88.refs_5_
  58.7 0.1 collective-permute-start.4
  58.8 0.3 shard_map.87.refs_4_
  59.2 0.6 collective-permute-start.3
  60.4 1.8 %shard_map.91.refs_12_ = f32[256,640]{1,0:T(8,128)S(1)} custom-call(s32[4]{0:T(128)S(1)} %iota.3.refs_0_, s32[8]{0:T(128)S(1)} %copy-done.4, f32[1]{0:T(128)S(6)} %copy.9.refs_2_, f32[1,8]{1,0:T(1,128)S(1)} %get-tuple-element.9.refs_3_, f32[256,256]{1,0:T(8,128)S(1)} %shard_map.89.refs_4_, f32[256,256]{1,0:T(8,128)S(1)} %shard_map.90.refs_5_, ...), custom_call_target="tpu_custom_call" | custom-call | flops 167772160 | bytes 1703936 | tf_op jit(solution)/shard_map/pallas_call | solution.py:210
  62.2 2.5 %shard_map.92 = bf16[256,640]{1,0:T(8,128)(2,1)} custom-call(s32[4]{0:T(128)S(1)} %copy-done.6, s32[8]{0:T(128)S(1)} %copy-done.4, f32[1]{0:T(128)S(6)} %copy.9.refs_2_, f32[1,8]{1,0:T(1,128)S(1)} %get-tuple-element.9.refs_3_, f32[256,256]{1,0:T(8,128)S(1)} %shard_map.87.refs_4_, f32[256,256]{1,0:T(8,128)S(1)} %shard_map.88.refs_5_, ...), custom_call_target="tpu_custom_call" | custom-call | flops 167772160 | bytes 1703936 | tf_op jit(solution)/shard_map/pallas_call | solution.py:210
  (18 shorter events, 0.1 us)
Async XLA Ops:
  7.2 1.0 %copy-start = (bf16[2,128,640]{2,1,0:T(8,128)(2,1)S(1)}, bf16[2,128,640]{2,1,0:T(8,128)(2,1)}, u32[]{:S(2)}) copy-start(bf16[2,128,640]{2,1,0:T(8,128)(2,1)} %param.8) | copy-start | bytes 983044
  7.2 48.3 %all-gather.2.cloned.1.call-start = ((), (), s32[]{:S(2)}) async-start(), calls=%async_computation | async-start | bytes 1474560 | tf_op jit(solution)/shard_map/all_gather | solution.py:243
  8.8 5.8 %collective-permute-start = (f32[2,1280]{1,0:T(2,128)}, f32[2,1280]{1,0:T(2,128)S(1)}, u32[]{:S(2)}, u32[]{:S(2)}) collective-permute-start(f32[2,1280]{1,0:T(2,128)} %refs_0_), channel_id=1, source_target_pairs={{0,4},{4,0},{8,12},{12,8},{1,5},{5,1},{9,13},{13,9},{2,6},{6,2},{1... | collective-permute-start | bytes 30728 | tf_op jit(solution)/shard_map/ppermute | solution.py:234
  11.9 4.8 %collective-permute-start.1 = (f32[2,1280]{1,0:T(2,128)}, f32[2,1280]{1,0:T(2,128)S(1)}, u32[]{:S(2)}, u32[]{:S(2)}) collective-permute-start(f32[2,1280]{1,0:T(2,128)} %refs_0_), channel_id=1, source_target_pairs={{0,8},{4,12},{8,0},{12,4},{1,9},{5,13},{9,1},{13,5},{2,10},{6,14},... | collective-permute-start | bytes 30728 | tf_op jit(solution)/shard_map/ppermute | solution.py:234
  14.5 5.7 %collective-permute-start.2 = (f32[2,1280]{1,0:T(2,128)}, f32[2,1280]{1,0:T(2,128)S(1)}, u32[]{:S(2)}, u32[]{:S(2)}) collective-permute-start(f32[2,1280]{1,0:T(2,128)} %refs_0_), channel_id=1, source_target_pairs={{0,12},{4,8},{8,4},{12,0},{1,13},{5,9},{9,5},{13,1},{2,14},{6,10},... | collective-permute-start | bytes 30728 | tf_op jit(solution)/shard_map/ppermute | solution.py:234
  20.2 0.7 copy-start.2
  20.9 0.7 copy-start.3
  21.6 0.7 copy-start.5
  55.5 1.6 %copy-start.1 = (bf16[1,256,640]{2,1,0:T(8,128)(2,1)S(1)}, bf16[1,256,640]{2,1,0:T(8,128)(2,1)}, u32[]{:S(2)}) copy-start(bf16[1,256,640]{2,1,0:T(8,128)(2,1)} %param.7) | copy-start | bytes 983044
  57.4 3.0 %collective-permute-start.6 = (f32[256,256]{1,0:T(8,128)S(1)}, f32[256,256]{1,0:T(8,128)S(1)}, u32[]{:S(2)}, u32[]{:S(2)}) collective-permute-start(f32[256,256]{1,0:T(8,128)S(1)} %shard_map.90.refs_5_), channel_id=1, source_target_pairs={{0,1},{1,0},{2,3},{3,2},{4,5},{5,4},{6,7},{7,6},{8,9},{9,8},{10,11... | collective-permute-start | bytes 786440 | tf_op jit(solution)/shard_map/ppermute | solution.py:237
  57.5 2.9 %copy-start.4 = (s32[8]{0:T(128)S(1)}, s32[8]{0:T(128)}, u32[]{:S(2)}) copy-start(s32[8]{0:T(128)} %refs_1_.3) | copy-start | bytes 100
  57.8 2.6 %collective-permute-start.5 = (f32[256,256]{1,0:T(8,128)S(1)}, f32[256,256]{1,0:T(8,128)S(1)}, u32[]{:S(2)}, u32[]{:S(2)}) collective-permute-start(f32[256,256]{1,0:T(8,128)S(1)} %shard_map.89.refs_4_), channel_id=1, source_target_pairs={{0,1},{1,0},{2,3},{3,2},{4,5},{5,4},{6,7},{7,6},{8,9},{9,8},{10,11... | collective-permute-start | bytes 786440 | tf_op jit(solution)/shard_map/ppermute | solution.py:237
  58.7 3.4 %collective-permute-start.4 = (f32[256,256]{1,0:T(8,128)S(1)}, f32[256,256]{1,0:T(8,128)S(1)}, u32[]{:S(2)}, u32[]{:S(2)}) collective-permute-start(f32[256,256]{1,0:T(8,128)S(1)} %shard_map.88.refs_5_), channel_id=1, source_target_pairs={{0,1},{1,0},{2,3},{3,2},{4,5},{5,4},{6,7},{7,6},{8,9},{9,8},{10,11... | collective-permute-start | bytes 786440 | tf_op jit(solution)/shard_map/ppermute | solution.py:237
  59.2 3.0 %copy-start.6 = (s32[4]{0:T(128)S(1)}, s32[4]{0:T(128)}, u32[]{:S(2)}) copy-start(s32[4]{0:T(128)} %constant.8.clone.1.refs_0_) | copy-start | bytes 52
  59.2 3.0 %collective-permute-start.3 = (f32[256,256]{1,0:T(8,128)S(1)}, f32[256,256]{1,0:T(8,128)S(1)}, u32[]{:S(2)}, u32[]{:S(2)}) collective-permute-start(f32[256,256]{1,0:T(8,128)S(1)} %shard_map.87.refs_4_), channel_id=1, source_target_pairs={{0,1},{1,0},{2,3},{3,2},{4,5},{5,4},{6,7},{7,6},{8,9},{9,8},{10,11... | collective-permute-start | bytes 786440 | tf_op jit(solution)/shard_map/ppermute | solution.py:237
Sparse Core Ops, SparseCore 0:
  10.8 44.6 all-gather.1

commit v4 on v0

--- a/solution.py
+++ b/solution.py
@@ -1,9 +1,14 @@
+import functools
 import math
 
 import jax
 import jax.numpy as jnp
 from jax import lax
+from jax.experimental import pallas as pl
+from jax.experimental.pallas import tpu as pltpu
 from jax.sharding import PartitionSpec as P
+
+VMEM_BYTES = 16 * 1024 * 1024
 
 
 def softmax_rows(logits):
@@ -53,7 +58,7 @@
     return jnp.take(arrived.reshape(tgt_count * capacity, target_rows, width), slot_of, axis=0)
 
 
-def per_device(query_res, target_res, target_len, hits, sharpness, query_pool, target_pool):
+def per_device_by_hit(query_res, target_res, target_len, hits, sharpness, query_pool, target_pool):
     tgt_count = lax.axis_size("tgt")
     query_count = query_res.shape[0]
     target_rows = target_res.shape[1]
@@ -81,6 +86,197 @@
     return (profile.astype(jnp.bfloat16), posterior)
 
 
+VMEM = pl.BlockSpec(memory_space=pltpu.VMEM)
+
+
+def call_kernel(kernel, out_shape, *operands, scratch=(), flops=0):
+    return pl.pallas_call(
+        kernel,
+        out_shape=out_shape,
+        in_specs=[VMEM] * len(operands),
+        out_specs=jax.tree.map(lambda _: VMEM, out_shape),
+        scratch_shapes=scratch,
+        cost_estimate=pl.CostEstimate(flops=flops, bytes_accessed=0, transcendentals=0),
+        compiler_params=pltpu.CompilerParams(vmem_limit_bytes=VMEM_BYTES),
+    )(*operands)
+
+
+def weigh_kernel(slot_ref, len_ref, sharp_ref, hits_ref, pool_ref, owner_ref, *refs):
+    libs, (posterior_ref, table_ref) = refs[:-2], refs[-2:]
+    owned, width = libs[0].shape
+    target_count = len_ref.shape[1]
+    lane = lax.broadcasted_iota(jnp.int32, (1, target_count), 1)
+    pool, hits = pool_ref[...], hits_ref[...]
+    logits = jnp.zeros((1, target_count), jnp.float32)
+    counts = jnp.zeros((1, target_count), jnp.float32)
+    for at, lib in enumerate(libs):
+        products = jnp.sum(lib[...] * pool, axis=1, keepdims=True) / math.sqrt(width)
+        first = owner_ref[at : at + 1, :] * owned
+        for a in range(owned):
+            logits = jnp.where(lane == first + a, products[a : a + 1, :], logits)
+    for t in range(target_count):
+        named = jnp.sum(jnp.where(hits == t, 1.0, 0.0), axis=1, keepdims=True)
+        counts = jnp.where(lane == t, named, counts)
+    raised = jnp.exp(logits - jnp.max(logits, axis=1, keepdims=True))
+    posterior_ref[...] = raised / jnp.sum(raised, axis=1, keepdims=True)
+    shown = jnp.where(counts > 0.0, logits, -jnp.inf)
+    parts = counts * jnp.exp(shown - jnp.max(shown, axis=1, keepdims=True))
+    weights = parts / jnp.sum(parts, axis=1, keepdims=True)
+    matches = slot_ref[...] == lane
+    lengths = jnp.sum(
+        jnp.where(matches, len_ref[...].astype(jnp.float32), 0.0), axis=1, keepdims=True
+    )
+    weights = jnp.sum(jnp.where(matches, weights, 0.0), axis=1, keepdims=True)
+    rows = table_ref.shape[1:]
+    table_ref[0] = jnp.broadcast_to(lengths, rows)
+    table_ref[1] = jnp.broadcast_to(1.0 / lengths, rows)
+    table_ref[2] = jnp.broadcast_to(weights, rows)
+    table_ref[3] = jnp.broadcast_to(0.5 * sharp_ref[...], rows)
+
+
+def partial_kernel(*refs):
+    query, blocks, out = refs[0], refs[1:-1], refs[-1]
+    rows = 0
+    for block in blocks:
+        out[:, rows : rows + block.shape[0]] = lax.dot_general(
+            query[...], block[...], (((1,), (1,)), ((), ())), preferred_element_type=jnp.float32
+        )
+        rows += block.shape[0]
+
+
+def partial_similar(query, blocks):
+    rows = sum(block.shape[0] for block in blocks)
+    shape = jax.ShapeDtypeStruct((query.shape[0], rows), jnp.float32)
+    return call_kernel(partial_kernel, shape, query, *blocks)
+
+
+def align_kernel(model_width, slots, first, table_ref, mine, other, *refs):
+    blocks = refs[: len(slots)]
+    out_ref, align_ref = refs[-2:]
+    target_rows = blocks[0].shape[0]
+    scale = 1.0 / math.sqrt(model_width)
+    column = lax.broadcasted_iota(jnp.int32, (1, target_rows), 1).astype(jnp.float32)
+    acc = None if first else refs[-3][...]
+    for at, slot in enumerate(slots):
+        part = pl.ds(at * target_rows, target_rows)
+        similar = (mine[:, part] + other[:, part]) * scale
+        inside = column < table_ref[0, slot : slot + 1, :target_rows]
+        fraction = table_ref[1, slot : slot + 1, 0:1]
+        weight = table_ref[2, slot : slot + 1, 0:1]
+        half_sharp = table_ref[3, slot : slot + 1, 0:1]
+        row_mean = jnp.sum(jnp.where(inside, similar, 0.0), axis=1, keepdims=True) * fraction
+        row_diff = similar - row_mean
+        row_var = (
+            jnp.sum(jnp.where(inside, row_diff * row_diff, 0.0), axis=1, keepdims=True) * fraction
+        )
+        column_mean = jnp.mean(similar, axis=0, keepdims=True)
+        column_diff = similar - column_mean
+        column_var = jnp.mean(column_diff * column_diff, axis=0, keepdims=True)
+        scores = row_diff * (half_sharp * lax.rsqrt(row_var + 1e-05)) + column_diff * (
+            half_sharp * lax.rsqrt(column_var + 1e-05)
+        )
+        scores = jnp.where(inside, scores, -jnp.inf)
+        raised = jnp.exp(scores - jnp.max(scores, axis=1, keepdims=True))
+        weight = weight / jnp.sum(raised, axis=1, keepdims=True)
+        align_ref[:, part] = (raised * weight).astype(jnp.bfloat16)
+    for at, block in enumerate(blocks):
+        part = pl.ds(at * target_rows, target_rows)
+        term = jnp.dot(align_ref[:, part], block[...], preferred_element_type=jnp.float32)
+        acc = term if acc is None else acc + term
+    out_ref[...] = acc.astype(out_ref.dtype)
+
+
+def add_aligned(model_width, slots, table, mine, other, blocks, acc, dtype=jnp.float32):
+    rows, width = mine.shape[0], blocks[0].shape[1]
+    return call_kernel(
+        functools.partial(align_kernel, model_width, slots, acc is None),
+        jax.ShapeDtypeStruct((rows, width), dtype),
+        table,
+        mine,
+        other,
+        *blocks,
+        *([] if acc is None else [acc]),
+        scratch=[pltpu.VMEM(mine.shape, jnp.bfloat16)],
+    )
+
+
+def per_device_by_target(
+    query_res, target_res, target_len, hits, sharpness, query_pool, target_pool
+):
+    model_width = query_pool.shape[1]
+    target_rows = target_res.shape[1]
+    query = query_res[0]
+    at_tgt, at_qry, at_rep = (lax.axis_index(name) for name in ("tgt", "qry", "rep"))
+
+    def from_peer(array, k):
+        return lax.ppermute(array, "tgt", [(i, i ^ k) for i in range(4)])
+
+    def across(array, axis):
+        return lax.ppermute(array, axis, [(0, 1), (1, 0)])
+
+    def after(array, *done):
+        return lax.optimization_barrier((array, *done))[0]
+
+    split = [(2 * i + c, 2 * (i ^ (1 + c)) + c) for i in range(4) for c in range(2)]
+    pool_split = lax.ppermute(target_pool, ("tgt", "rep"), split)
+    pool_last = from_peer(target_pool, 3)
+    pool_other = across(pool_split, "rep")
+    owners = jnp.stack([at_tgt, at_tgt ^ (1 + at_rep), at_tgt ^ (2 - at_rep), at_tgt ^ 3])
+    libs = [target_pool, pool_split, pool_other, pool_last]
+
+    share = lax.dynamic_index_in_dim(target_res, at_qry, 0, keepdims=False)
+    rest = lax.dynamic_index_in_dim(target_res, 1 - at_qry, 0, keepdims=False)
+    share = after(share, pool_split, pool_last)
+    far = from_peer(share, 2)
+    near = from_peer(share, 1)
+
+    bases = [2 * (at_tgt ^ k) for k in range(4)]
+    slots = [bases[0], bases[0] + 1]
+    for base in bases[1:]:
+        slots += [base + at_qry, base + 1 - at_qry]
+    posterior, table = call_kernel(
+        weigh_kernel,
+        (
+            jax.ShapeDtypeStruct((1, len(slots)), jnp.float32),
+            jax.ShapeDtypeStruct((4, len(slots), target_rows), jnp.float32),
+        ),
+        jnp.stack(slots).astype(jnp.int32)[:, None],
+        target_len[None],
+        sharpness[None],
+        hits,
+        query_pool,
+        owners.astype(jnp.int32)[:, None],
+        *libs,
+    )
+
+    own_blocks = [target_res[0], target_res[1]]
+    own = partial_similar(after(query, share), own_blocks)
+    own_other = across(own, "rep")
+    acc = add_aligned(model_width, (0, 1), table, own, own_other, own_blocks, None)
+
+    far = after(far, acc)
+    near = after(near, far)
+    far_rest = across(far, "qry")
+    near_rest = across(near, "qry")
+    last = from_peer(far, 1)
+    last_rest = from_peer(after(rest, far), 3)
+
+    one = partial_similar(query, [far])
+    one_other = across(one, "rep")
+    acc = add_aligned(model_width, (4,), table, one, one_other, [far], acc)
+
+    blocks = [near, far_rest, near_rest]
+    two = partial_similar(after(query, acc), blocks)
+    two_other = across(two, "rep")
+    three = partial_similar(after(query, two), [last, last_rest])
+    three_other = across(three, "rep")
+    acc = add_aligned(model_width, (2, 5, 3), table, after(two, three), two_other, blocks, acc)
+    profile = add_aligned(
+        model_width, (6, 7), table, three, three_other, [last, last_rest], acc, jnp.bfloat16
+    )
+    return (profile[None], posterior)
+
+
 def solution(mesh):
     placed = (
         P(("grp", "tgt", "qry"), None, "rep"),
@@ -91,6 +287,18 @@
         P(("grp", "tgt", "qry"), None),
         P(("grp", "tgt"), None),
     )
+    groups = mesh.shape["tgt"]
+
+    def per_device(*arrays):
+        query_res, target_res, _, hits = arrays[:4]
+        few = (
+            query_res.shape[0] == 1
+            and groups == 4 <= hits.shape[1] // target_res.shape[0]
+            and target_res.shape[0] == mesh.shape["qry"] == 2
+            and mesh.shape["rep"] == 2
+        )
+        return (per_device_by_target if few else per_device_by_hit)(*arrays)
+
     return jax.shard_map(
         per_device,
         mesh=mesh,

time: 295 us -> 39.6 us (0.13)
  waiting for transfers between devices: 200 us -> 14.3 us
  blocking collectives: 24.8 us -> 0 us
  other arithmetic: 24.4 us -> 0.08 us
  between operations: 14.9 us -> 1.41 us
  local copies, waits for them, and re-layouts: 14.7 us -> 2.19 us
  matrix products: 9.14 us -> 0 us
  Pallas kernels: 0 us -> 8.81 us
  starting transfers between devices: 5.93 us -> 12.6 us
    all_to_all x1 -> x0, waiting for transfers between devices: 199 us -> none  [fetch_shares(): lax.all_to_all(outgoing, 'tgt', split_axis=0, concat_axis=0, tiled=True)]
    ppermute x0 -> x13, waiting for transfers between devices: none -> 14.3 us  [the longest x5 9.67 us: from_peer(): return lax.ppermute(array, 'tgt', [(i, i ^ k) for i in range(4)])]
    gather x2 -> x0, local copies, waits for them, and re-layouts: 13.2 us -> none  [the longest x1 7.13 us: fetch_shares(): jnp.take(arrived.reshape(tgt_count * capacity, target_rows, width), slot_...]
    all_gather x1 -> x0, blocking collectives: 13.1 us -> none  [per_device(): library = lax.all_gather(target_pool, 'tgt', axis=0, tiled=True)]
    ppermute x0 -> x13, starting transfers between devices: none -> 12.6 us  [the longest x5 7.22 us: from_peer(): return lax.ppermute(array, 'tgt', [(i, i ^ k) for i in range(4)])]
    all_to_all x1 -> x0, blocking collectives: 11.7 us -> none  [fetch_shares(): lax.all_to_all(wanted, 'tgt', split_axis=0, concat_axis=0, tiled=True)]
    dot_general x3 -> x0, matrix products: 9.14 us -> none  [the longest x1 5.79 us: per_device(): jnp.einsum('qid,qhjd->qhij', query_res, chosen, preferred_element_type=jn...]
    select_n x4 -> x0, other arithmetic: 8.91 us -> none  [the longest x2 8.18 us: fetch_shares(): jnp.take(target_res, requested.reshape(tgt_count * capacity), axis=0)]
  transfers between devices with their start and end apart: 2 -> 13, of which waited for: 2 -> 8; matrix products, arithmetic and copies ran while one was open for 3% -> 4% of each run, Pallas kernels for 0% -> 16%
where the time goes in v4:
time: 39.6 us; the launch traced here: 39.4 us
  waiting for transfers between devices  14.3 us (36%)
  starting transfers between devices  12.6 us (32%)
  Pallas kernels  8.81 us (22%)
  local copies, waits for them, and re-layouts  2.19 us (6%)
  between operations  1.41 us (4%)
    ppermute x5, waiting for transfers between devices, from_peer(): return lax.ppermute(array, 'tgt', [(i, i ^ k) for i in range(4)])  9.67 us
    pallas_call x9, Pallas kernels, call_kernel(): pl.pallas_call(kernel, out_shape=out_shape, in_specs=[VMEM] * len(operand...  8.81 us
    ppermute x5, starting transfers between devices, from_peer(): return lax.ppermute(array, 'tgt', [(i, i ^ k) for i in range(4)])  7.22 us
    ppermute x7, waiting for transfers between devices, across(): return lax.ppermute(array, axis, [(0, 1), (1, 0)])  4.64 us
    ppermute x1, starting transfers between devices, per_device_by_target(): pool_split = lax.ppermute(target_pool, ('tgt', 'rep'), split)  3.09 us
    ppermute x7, starting transfers between devices, across(): return lax.ppermute(array, axis, [(0, 1), (1, 0)])  2.31 us
    squeeze x1, local copies, waits for them, and re-layouts, per_device_by_target(): rest = lax.dynamic_index_in_dim(target_res, 1 - at_qry, 0, keepdims=False)  1.26 us
  transfers between devices with their start and end apart: 13, of which 8 were waited for; matrix products, arithmetic and copies ran while one was open for 4% of the time, Pallas kernels for 16%

profile of v4, /device:TPU:0, one launch (start us, length us, event | category | flops | bytes accessed | tf_op | source)
XLA Modules:
  0.0 39.4 jit_solution(11577026092039213309)
XLA Ops:
  0.6 3.1 %collective-permute-start = (f32[2,1280]{1,0:T(2,128)}, f32[2,1280]{1,0:T(2,128)S(1)}, u32[]{:S(2)}, u32[]{:S(2)}) collective-permute-start(f32[2,1280]{1,0:T(2,128)} %refs_0_.1), channel_id=1, source_target_pairs={{0,4},{1,9},{4,0},{5,13},{8,12},{9,1},{12,8},{13,5},{2,6},{3,11},{... | collective-permute-start | bytes 30728 | tf_op jit(solution)/shard_map/ppermute | solution.py:221
  3.7 2.5 %collective-permute-start.2 = (f32[2,1280]{1,0:T(2,128)}, f32[2,1280]{1,0:T(2,128)S(1)}, u32[]{:S(2)}, u32[]{:S(2)}) collective-permute-start(f32[2,1280]{1,0:T(2,128)} %refs_0_.1), channel_id=1, source_target_pairs={{0,12},{4,8},{8,4},{12,0},{1,13},{5,9},{9,5},{13,1},{2,14},{6,10},... | collective-permute-start | bytes 30728 | tf_op jit(solution)/shard_map/ppermute | solution.py:212
  6.2 1.3 %dynamic-slice_bitcast_fusion = (bf16[128,640]{1,0:T(8,128)(2,1)S(1)}, bf16[128,640]{1,0:T(8,128)(2,1)S(1)}, bf16[128,640]{1,0:T(8,128)(2,1)S(1)}, bf16[128,640]{1,0:T(8,128)(2,1)S(1)}) fusion(bf16[2,128,640]{2,1,0:T(8,128)(2,1)} %param.8, s32[]{:T(128)S(6)} %select_n.8, s32[]{:T(128)S(6)} %select_n.7), kind=kLoop, calls=%fused_computation | loop fusion | bytes 1310728 | tf_op jit(solution)/shard_map/jit(dynamic_index_in_dim)/squeeze | solution.py:228
  7.5 1.9 %collective-permute-done.2.refs_3_ = f32[2,1280]{1,0:T(2,128)S(1)} collective-permute-done((f32[2,1280]{1,0:T(2,128)}, f32[2,1280]{1,0:T(2,128)S(1)}, u32[]{:S(2)}, u32[]{:S(2)}) %collective-permute-start.2) | collective-permute-done | bytes 10272 | tf_op jit(solution)/shard_map/ppermute | solution.py:212
  9.4 0.3 shard_map.87.mine
  9.8 0.9 %collective-permute-start.3 = (bf16[128,640]{1,0:T(8,128)(2,1)S(1)}, bf16[128,640]{1,0:T(8,128)(2,1)S(1)}, u32[]{:S(2)}, u32[]{:S(2)}) collective-permute-start(bf16[128,640]{1,0:T(8,128)(2,1)S(1)} %get-tuple-element.13), channel_id=1, source_target_pairs={{0,8},{4,12},{8,0},{12,4},{1,9},{5,13},{9,1},{13,5},{2,10},{6,14},... | collective-permute-start | bytes 491528 | tf_op jit(solution)/shard_map/ppermute | solution.py:212
  10.7 2.2 %collective-permute-start.6 = (bf16[128,640]{1,0:T(8,128)(2,1)S(1)}, bf16[128,640]{1,0:T(8,128)(2,1)S(1)}, u32[]{:S(2)}, u32[]{:S(2)}) collective-permute-start(bf16[128,640]{1,0:T(8,128)(2,1)S(1)} %get-tuple-element.13), channel_id=1, source_target_pairs={{0,4},{4,0},{8,12},{12,8},{1,5},{5,1},{9,13},{13,9},{2,6},{6,2},{1... | collective-permute-start | bytes 491528 | tf_op jit(solution)/shard_map/ppermute | solution.py:212
  14.1 0.6 %copy-done.3 = s32[8]{0:T(128)S(1)} copy-done((s32[8]{0:T(128)S(1)}, s32[8]{0:T(128)}, u32[]{:S(2)}) %copy-start.3) | copy-done | bytes 56
  14.8 0.8 %shard_map.86 = (f32[1,8]{1,0:T(1,128)}, f32[4,8,128]{2,1,0:T(8,128)S(1)}) custom-call(s32[8,1]{1,0:T(8,128)S(1)} %copy.9.slot_ref, s32[1,8]{1,0:T(1,128)S(1)} %bitcast.32, f32[1,1]{1,0:T(1,128)} %bitcast.27.sharp_ref, s32[1,28]{1,0:T(1,128)S(1)} %copy-done.4, f32[1,1280]{1,0:T(1,128)S(1)} %copy-done.2, s32[4,1]{1,0:T(4,128)S(1)} %copy.10.owner_ref, ...), custom_call_target="tpu_custom_call" | custom-call | tf_op jit(solution)/shard_map/pallas_call | solution.py:93
  15.6 1.5 %shard_map.88.refs_1_ = f32[256,640]{1,0:T(8,128)S(1)} custom-call(f32[4,8,128]{2,1,0:T(8,128)S(1)} %get-tuple-element.12.table_ref, f32[256,256]{1,0:T(8,128)S(1)} %shard_map.87.mine, f32[256,256]{1,0:T(8,128)S(1)} %collective-permute-done.4.other, bf16[128,640]{1,0:T(8,128)(2,1)S(1)} %get-tuple-element.23.refs_1_.refs_0_, ...), custom_call_target="tpu_custom_call" | custom-call | tf_op jit(solution)/shard_map/pallas_call | solution.py:93
  17.1 3.7 %collective-permute-done.3.refs_1_.refs_0_ = bf16[128,640]{1,0:T(8,128)(2,1)S(1)} collective-permute-done((bf16[128,640]{1,0:T(8,128)(2,1)S(1)}, bf16[128,640]{1,0:T(8,128)(2,1)S(1)}, u32[]{:S(2)}, u32[]{:S(2)}) %collective-permute-start.3) | collective-permute-done | bytes 163872 | tf_op jit(solution)/shard_map/ppermute | solution.py:212
  20.9 1.5 %collective-permute-start.8 = (bf16[128,640]{1,0:T(8,128)(2,1)S(1)}, bf16[128,640]{1,0:T(8,128)(2,1)S(1)}, u32[]{:S(2)}, u32[]{:S(2)}) collective-permute-start(bf16[128,640]{1,0:T(8,128)(2,1)S(1)} %collective-permute-done.6.refs_1_.refs_0_), channel_id=1, source_target_pairs={{0,2},{2,0},{1,3},{3,1},{4,6},{6,4},{5,7},{7,5},{8,10},{10,8},{9,1... | collective-permute-start | bytes 491528 | tf_op jit(solution)/shard_map/ppermute | solution.py:215
  22.4 0.5 %collective-permute-start.7 = (bf16[128,640]{1,0:T(8,128)(2,1)S(1)}, bf16[128,640]{1,0:T(8,128)(2,1)S(1)}, u32[]{:S(2)}, u32[]{:S(2)}) collective-permute-start(bf16[128,640]{1,0:T(8,128)(2,1)S(1)} %collective-permute-done.3.refs_1_.refs_0_), channel_id=1, source_target_pairs={{0,2},{2,0},{1,3},{3,1},{4,6},{6,4},{5,7},{7,5},{8,10},{10,8},{9,1... | collective-permute-start | bytes 491528 | tf_op jit(solution)/shard_map/ppermute | solution.py:215
  23.0 0.2 shard_map.89.mine
  23.3 1.6 %collective-permute-start.10 = (bf16[128,640]{1,0:T(8,128)(2,1)S(1)}, bf16[128,640]{1,0:T(8,128)(2,1)S(1)}, u32[]{:S(2)}, u32[]{:S(2)}) collective-permute-start(bf16[128,640]{1,0:T(8,128)(2,1)S(1)} %get-tuple-element.19), channel_id=1, source_target_pairs={{0,12},{4,8},{8,4},{12,0},{1,13},{5,9},{9,5},{13,1},{2,14},{6,10},... | collective-permute-start | bytes 491528 | tf_op jit(solution)/shard_map/ppermute | solution.py:212
  25.0 1.0 %shard_map.90.refs_3_ = f32[256,640]{1,0:T(8,128)S(1)} custom-call(f32[4,8,128]{2,1,0:T(8,128)S(1)} %get-tuple-element.12.table_ref, f32[256,128]{1,0:T(8,128)S(1)} %shard_map.89.mine, f32[256,128]{1,0:T(8,128)S(1)} %collective-permute-done.5.other, bf16[128,640]{1,0:T(8,128)(2,1)S(1)} %collective-permute-done.3.refs_1_.refs_0_, ...), custom_call_target="tpu_custom_call" | custom-call | tf_op jit(solution)/shard_map/pallas_call | solution.py:93
  25.9 2.1 %collective-permute-done.8.refs_3_.refs_2_ = bf16[128,640]{1,0:T(8,128)(2,1)S(1)} collective-permute-done((bf16[128,640]{1,0:T(8,128)(2,1)S(1)}, bf16[128,640]{1,0:T(8,128)(2,1)S(1)}, u32[]{:S(2)}, u32[]{:S(2)}) %collective-permute-start.8) | collective-permute-done | bytes 163872 | tf_op jit(solution)/shard_map/ppermute | solution.py:215
  28.0 2.3 %collective-permute-done.7.refs_2_.refs_1_ = bf16[128,640]{1,0:T(8,128)(2,1)S(1)} collective-permute-done((bf16[128,640]{1,0:T(8,128)(2,1)S(1)}, bf16[128,640]{1,0:T(8,128)(2,1)S(1)}, u32[]{:S(2)}, u32[]{:S(2)}) %collective-permute-start.7) | collective-permute-done | bytes 163872 | tf_op jit(solution)/shard_map/ppermute | solution.py:215
  30.4 0.4 %shard_map.91.mine = f32[256,384]{1,0:T(8,128)S(1)} custom-call(bf16[256,640]{1,0:T(8,128)(2,1)S(1)} %bitcast.30, bf16[128,640]{1,0:T(8,128)(2,1)S(1)} %collective-permute-done.6.refs_1_.refs_0_, bf16[128,640]{1,0:T(8,128)(2,1)S(1)} %collective-permute-done.7.refs_2_.refs_1_, bf16[128,640]{1,0:T(8,128)(2,1)S(1)} %collective-permute-done.8.refs_3_.refs_2_), custom_call_target="tpu_custom_call" | custom-call | tf_op jit(solution)/shard_map/pallas_call | solution.py:93
  30.9 1.3 %collective-permute-done.10.refs_2_.refs_1_ = bf16[128,640]{1,0:T(8,128)(2,1)S(1)} collective-permute-done((bf16[128,640]{1,0:T(8,128)(2,1)S(1)}, bf16[128,640]{1,0:T(8,128)(2,1)S(1)}, u32[]{:S(2)}, u32[]{:S(2)}) %collective-permute-start.10) | collective-permute-done | bytes 163872 | tf_op jit(solution)/shard_map/ppermute | solution.py:212
  32.2 2.5 %collective-permute-done.9.refs_1_.refs_0_ = bf16[128,640]{1,0:T(8,128)(2,1)S(1)} collective-permute-done((bf16[128,640]{1,0:T(8,128)(2,1)S(1)}, bf16[128,640]{1,0:T(8,128)(2,1)S(1)}, u32[]{:S(2)}, u32[]{:S(2)}) %collective-permute-start.9) | collective-permute-done | bytes 163872 | tf_op jit(solution)/shard_map/ppermute | solution.py:212
  34.7 0.3 shard_map.92.mine
  35.2 2.1 %shard_map.93.refs_2_ = f32[256,640]{1,0:T(8,128)S(1)} custom-call(f32[4,8,128]{2,1,0:T(8,128)S(1)} %get-tuple-element.12.table_ref, f32[256,384]{1,0:T(8,128)S(1)} %shard_map.91.mine, f32[256,384]{1,0:T(8,128)S(1)} %collective-permute-done.12.other, bf16[128,640]{1,0:T(8,128)(2,1)S(1)} %collective-permute-done.6.refs_1_.refs_0_, ...), custom_call_target="tpu_custom_call" | custom-call | tf_op jit(solution)/shard_map/pallas_call | solution.py:93
  37.2 2.2 %shard_map.94 = bf16[256,640]{1,0:T(8,128)(2,1)} custom-call(f32[4,8,128]{2,1,0:T(8,128)S(1)} %get-tuple-element.12.table_ref, f32[256,256]{1,0:T(8,128)S(1)} %shard_map.92.mine, f32[256,256]{1,0:T(8,128)S(1)} %collective-permute-done.11.other, bf16[128,640]{1,0:T(8,128)(2,1)S(1)} %collective-permute-done.9.refs_1_.refs_0_, ...), custom_call_target="tpu_custom_call" | custom-call | tf_op jit(solution)/shard_map/pallas_call | solution.py:93
  (26 shorter events, 1.0 us)
Async XLA Ops:
  0.6 6.8 %collective-permute-start = (f32[2,1280]{1,0:T(2,128)}, f32[2,1280]{1,0:T(2,128)S(1)}, u32[]{:S(2)}, u32[]{:S(2)}) collective-permute-start(f32[2,1280]{1,0:T(2,128)} %refs_0_.1), channel_id=1, source_target_pairs={{0,4},{1,9},{4,0},{5,13},{8,12},{9,1},{12,8},{13,5},{2,6},{3,11},{... | collective-permute-start | bytes 30728 | tf_op jit(solution)/shard_map/ppermute | solution.py:221
  3.7 5.7 %collective-permute-start.2 = (f32[2,1280]{1,0:T(2,128)}, f32[2,1280]{1,0:T(2,128)S(1)}, u32[]{:S(2)}, u32[]{:S(2)}) collective-permute-start(f32[2,1280]{1,0:T(2,128)} %refs_0_.1), channel_id=1, source_target_pairs={{0,12},{4,8},{8,4},{12,0},{1,13},{5,9},{9,5},{13,1},{2,14},{6,10},... | collective-permute-start | bytes 30728 | tf_op jit(solution)/shard_map/ppermute | solution.py:212
  6.2 3.2 %copy-start = (bf16[1,256,640]{2,1,0:T(8,128)(2,1)S(1)}, bf16[1,256,640]{2,1,0:T(8,128)(2,1)}, u32[]{:S(2)}) copy-start(bf16[1,256,640]{2,1,0:T(8,128)(2,1)} %param.7) | copy-start | bytes 983044
  9.7 5.8 %collective-permute-start.4 = (f32[256,256]{1,0:T(8,128)S(1)}, f32[256,256]{1,0:T(8,128)S(1)}, u32[]{:S(2)}, u32[]{:S(2)}) collective-permute-start(f32[256,256]{1,0:T(8,128)S(1)} %shard_map.87.mine), channel_id=1, source_target_pairs={{0,1},{1,0},{2,3},{3,2},{4,5},{5,4},{6,7},{7,6},{8,9},{9,8},{10,11... | collective-permute-start | bytes 786440 | tf_op jit(solution)/shard_map/ppermute | solution.py:215
  9.8 10.9 %collective-permute-start.3 = (bf16[128,640]{1,0:T(8,128)(2,1)S(1)}, bf16[128,640]{1,0:T(8,128)(2,1)S(1)}, u32[]{:S(2)}, u32[]{:S(2)}) collective-permute-start(bf16[128,640]{1,0:T(8,128)(2,1)S(1)} %get-tuple-element.13), channel_id=1, source_target_pairs={{0,8},{4,12},{8,0},{12,4},{1,9},{5,13},{9,1},{13,5},{2,10},{6,14},... | collective-permute-start | bytes 491528 | tf_op jit(solution)/shard_map/ppermute | solution.py:212
  10.7 10.3 %collective-permute-start.6 = (bf16[128,640]{1,0:T(8,128)(2,1)S(1)}, bf16[128,640]{1,0:T(8,128)(2,1)S(1)}, u32[]{:S(2)}, u32[]{:S(2)}) collective-permute-start(bf16[128,640]{1,0:T(8,128)(2,1)S(1)} %get-tuple-element.13), channel_id=1, source_target_pairs={{0,4},{4,0},{8,12},{12,8},{1,5},{5,1},{9,13},{13,9},{2,6},{6,2},{1... | collective-permute-start | bytes 491528 | tf_op jit(solution)/shard_map/ppermute | solution.py:212
  12.9 1.2 %collective-permute-start.1 = (f32[2,1280]{1,0:T(2,128)S(1)}, f32[2,1280]{1,0:T(2,128)S(1)}, u32[]{:S(2)}, u32[]{:S(2)}) collective-permute-start(f32[2,1280]{1,0:T(2,128)S(1)} %collective-permute-done.refs_1_), channel_id=1, source_target_pairs={{0,1},{1,0},{2,3},{3,2},{4,5},{5,4},{6,7},{7,6},{8,9},{9,8},{10,11... | collective-permute-start | bytes 30728 | tf_op jit(solution)/shard_map/ppermute | solution.py:215
  13.0 1.1 %copy-start.1 = (f32[2,1280]{1,0:T(2,128)S(1)}, f32[2,1280]{1,0:T(2,128)}, u32[]{:S(2)}) copy-start(f32[2,1280]{1,0:T(2,128)} %refs_0_.1) | copy-start | bytes 30724
  13.2 0.9 %copy-start.2 = (f32[1,1280]{1,0:T(1,128)S(1)}, f32[1,1280]{1,0:T(1,128)}, u32[]{:S(2)}) copy-start(f32[1,1280]{1,0:T(1,128)} %pool_ref.1) | copy-start | bytes 15364
  14.1 0.7 %copy-start.3 = (s32[8]{0:T(128)S(1)}, s32[8]{0:T(128)}, u32[]{:S(2)}) copy-start(s32[8]{0:T(128)} %param.9) | copy-start | bytes 100
  14.1 0.7 %copy-start.4 = (s32[1,28]{1,0:T(1,128)S(1)}, s32[1,28]{1,0:T(1,128)}, u32[]{:S(2)}) copy-start(s32[1,28]{1,0:T(1,128)} %hits_ref.1) | copy-start | bytes 340
  20.9 7.1 %collective-permute-start.8 = (bf16[128,640]{1,0:T(8,128)(2,1)S(1)}, bf16[128,640]{1,0:T(8,128)(2,1)S(1)}, u32[]{:S(2)}, u32[]{:S(2)}) collective-permute-start(bf16[128,640]{1,0:T(8,128)(2,1)S(1)} %collective-permute-done.6.refs_1_.refs_0_), channel_id=1, source_target_pairs={{0,2},{2,0},{1,3},{3,1},{4,6},{6,4},{5,7},{7,5},{8,10},{10,8},{9,1... | collective-permute-start | bytes 491528 | tf_op jit(solution)/shard_map/ppermute | solution.py:215
  22.4 7.9 %collective-permute-start.7 = (bf16[128,640]{1,0:T(8,128)(2,1)S(1)}, bf16[128,640]{1,0:T(8,128)(2,1)S(1)}, u32[]{:S(2)}, u32[]{:S(2)}) collective-permute-start(bf16[128,640]{1,0:T(8,128)(2,1)S(1)} %collective-permute-done.3.refs_1_.refs_0_), channel_id=1, source_target_pairs={{0,2},{2,0},{1,3},{3,1},{4,6},{6,4},{5,7},{7,5},{8,10},{10,8},{9,1... | collective-permute-start | bytes 491528 | tf_op jit(solution)/shard_map/ppermute | solution.py:215
  23.2 1.7 %collective-permute-start.5 = (f32[256,128]{1,0:T(8,128)S(1)}, f32[256,128]{1,0:T(8,128)S(1)}, u32[]{:S(2)}, u32[]{:S(2)}) collective-permute-start(f32[256,128]{1,0:T(8,128)S(1)} %shard_map.89.mine), channel_id=1, source_target_pairs={{0,1},{1,0},{2,3},{3,2},{4,5},{5,4},{6,7},{7,6},{8,9},{9,8},{10,11... | collective-permute-start | bytes 393224 | tf_op jit(solution)/shard_map/ppermute | solution.py:215
  23.3 8.9 %collective-permute-start.10 = (bf16[128,640]{1,0:T(8,128)(2,1)S(1)}, bf16[128,640]{1,0:T(8,128)(2,1)S(1)}, u32[]{:S(2)}, u32[]{:S(2)}) collective-permute-start(bf16[128,640]{1,0:T(8,128)(2,1)S(1)} %get-tuple-element.19), channel_id=1, source_target_pairs={{0,12},{4,8},{8,4},{12,0},{1,13},{5,9},{9,5},{13,1},{2,14},{6,10},... | collective-permute-start | bytes 491528 | tf_op jit(solution)/shard_map/ppermute | solution.py:212
  25.0 9.8 %collective-permute-start.9 = (bf16[128,640]{1,0:T(8,128)(2,1)S(1)}, bf16[128,640]{1,0:T(8,128)(2,1)S(1)}, u32[]{:S(2)}, u32[]{:S(2)}) collective-permute-start(bf16[128,640]{1,0:T(8,128)(2,1)S(1)} %collective-permute-done.3.refs_1_.refs_0_), channel_id=1, source_target_pairs={{0,4},{4,0},{8,12},{12,8},{1,5},{5,1},{9,13},{13,9},{2,6},{6,2},{1... | collective-permute-start | bytes 491528 | tf_op jit(solution)/shard_map/ppermute | solution.py:212
  30.8 4.3 %collective-permute-start.12 = (f32[256,384]{1,0:T(8,128)S(1)}, f32[256,384]{1,0:T(8,128)S(1)}, u32[]{:S(2)}, u32[]{:S(2)}) collective-permute-start(f32[256,384]{1,0:T(8,128)S(1)} %shard_map.91.mine), channel_id=1, source_target_pairs={{0,1},{1,0},{2,3},{3,2},{4,5},{5,4},{6,7},{7,6},{8,9},{9,8},{10,11... | collective-permute-start | bytes 1179656 | tf_op jit(solution)/shard_map/ppermute | solution.py:215
  35.1 2.1 %collective-permute-start.11 = (f32[256,256]{1,0:T(8,128)S(1)}, f32[256,256]{1,0:T(8,128)S(1)}, u32[]{:S(2)}, u32[]{:S(2)}) collective-permute-start(f32[256,256]{1,0:T(8,128)S(1)} %shard_map.92.mine), channel_id=1, source_target_pairs={{0,1},{1,0},{2,3},{3,2},{4,5},{5,4},{6,7},{7,6},{8,9},{9,8},{10,11... | collective-permute-start | bytes 786440 | tf_op jit(solution)/shard_map/ppermute | solution.py:215

commit v5 on v4

--- a/solution.py
+++ b/solution.py
@@ -101,10 +101,10 @@
     )(*operands)
 
 
-def weigh_kernel(slot_ref, len_ref, sharp_ref, hits_ref, pool_ref, owner_ref, *refs):
-    libs, (posterior_ref, table_ref) = refs[:-2], refs[-2:]
+def weigh_kernel(slot_ref, hits_ref, pool_ref, owner_ref, *refs):
+    libs, (posterior_ref, weight_ref) = refs[:-2], refs[-2:]
     owned, width = libs[0].shape
-    target_count = len_ref.shape[1]
+    target_count = posterior_ref.shape[1]
     lane = lax.broadcasted_iota(jnp.int32, (1, target_count), 1)
     pool, hits = pool_ref[...], hits_ref[...]
     logits = jnp.zeros((1, target_count), jnp.float32)
@@ -122,16 +122,8 @@
     shown = jnp.where(counts > 0.0, logits, -jnp.inf)
     parts = counts * jnp.exp(shown - jnp.max(shown, axis=1, keepdims=True))
     weights = parts / jnp.sum(parts, axis=1, keepdims=True)
-    matches = slot_ref[...] == lane
-    lengths = jnp.sum(
-        jnp.where(matches, len_ref[...].astype(jnp.float32), 0.0), axis=1, keepdims=True
-    )
-    weights = jnp.sum(jnp.where(matches, weights, 0.0), axis=1, keepdims=True)
-    rows = table_ref.shape[1:]
-    table_ref[0] = jnp.broadcast_to(lengths, rows)
-    table_ref[1] = jnp.broadcast_to(1.0 / lengths, rows)
-    table_ref[2] = jnp.broadcast_to(weights, rows)
-    table_ref[3] = jnp.broadcast_to(0.5 * sharp_ref[...], rows)
+    weights = jnp.sum(jnp.where(slot_ref[...] == lane, weights, 0.0), axis=1, keepdims=True)
+    weight_ref[...] = jnp.broadcast_to(weights, weight_ref.shape)
 
 
 def partial_kernel(*refs):
@@ -150,54 +142,71 @@
     return call_kernel(partial_kernel, shape, query, *blocks)
 
 
-def align_kernel(model_width, slots, first, table_ref, mine, other, *refs):
-    blocks = refs[: len(slots)]
-    out_ref, align_ref = refs[-2:]
-    target_rows = blocks[0].shape[0]
+def align_block(similar, length, half_sharp):
+    column = lax.broadcasted_iota(jnp.int32, (1, similar.shape[1]), 1).astype(jnp.float32)
+    inside = column < length
+    fraction = 1.0 / length[:, 0:1]
+    row_mean = jnp.sum(jnp.where(inside, similar, 0.0), axis=1, keepdims=True) * fraction
+    row_diff = similar - row_mean
+    row_var = (
+        jnp.sum(jnp.where(inside, row_diff * row_diff, 0.0), axis=1, keepdims=True) * fraction
+    )
+    column_mean = jnp.mean(similar, axis=0, keepdims=True)
+    column_diff = similar - column_mean
+    column_var = jnp.mean(column_diff * column_diff, axis=0, keepdims=True)
+    scores = row_diff * (half_sharp * lax.rsqrt(row_var + 1e-05)) + column_diff * (
+        half_sharp * lax.rsqrt(column_var + 1e-05)
+    )
+    scores = jnp.where(inside, scores, -jnp.inf)
+    raised = jnp.exp(scores - jnp.max(scores, axis=1, keepdims=True))
+    return raised / jnp.sum(raised, axis=1, keepdims=True)
+
+
+def align_kernel(model_width, slots, len_ref, sharp_ref, mine, other, out_ref):
     scale = 1.0 / math.sqrt(model_width)
-    column = lax.broadcasted_iota(jnp.int32, (1, target_rows), 1).astype(jnp.float32)
-    acc = None if first else refs[-3][...]
+    rows = mine.shape[1] // len(slots)
     for at, slot in enumerate(slots):
-        part = pl.ds(at * target_rows, target_rows)
+        part = pl.ds(at * rows, rows)
         similar = (mine[:, part] + other[:, part]) * scale
-        inside = column < table_ref[0, slot : slot + 1, :target_rows]
-        fraction = table_ref[1, slot : slot + 1, 0:1]
-        weight = table_ref[2, slot : slot + 1, 0:1]
-        half_sharp = table_ref[3, slot : slot + 1, 0:1]
-        row_mean = jnp.sum(jnp.where(inside, similar, 0.0), axis=1, keepdims=True) * fraction
-        row_diff = similar - row_mean
-        row_var = (
-            jnp.sum(jnp.where(inside, row_diff * row_diff, 0.0), axis=1, keepdims=True) * fraction
-        )
-        column_mean = jnp.mean(similar, axis=0, keepdims=True)
-        column_diff = similar - column_mean
-        column_var = jnp.mean(column_diff * column_diff, axis=0, keepdims=True)
-        scores = row_diff * (half_sharp * lax.rsqrt(row_var + 1e-05)) + column_diff * (
-            half_sharp * lax.rsqrt(column_var + 1e-05)
-        )
-        scores = jnp.where(inside, scores, -jnp.inf)
-        raised = jnp.exp(scores - jnp.max(scores, axis=1, keepdims=True))
-        weight = weight / jnp.sum(raised, axis=1, keepdims=True)
-        align_ref[:, part] = (raised * weight).astype(jnp.bfloat16)
-    for at, block in enumerate(blocks):
-        part = pl.ds(at * target_rows, target_rows)
-        term = jnp.dot(align_ref[:, part], block[...], preferred_element_type=jnp.float32)
-        acc = term if acc is None else acc + term
-    out_ref[...] = acc.astype(out_ref.dtype)
-
-
-def add_aligned(model_width, slots, table, mine, other, blocks, acc, dtype=jnp.float32):
-    rows, width = mine.shape[0], blocks[0].shape[1]
+        alignment = align_block(similar, len_ref[slot : slot + 1, :rows], sharp_ref[:, 0:1])
+        out_ref[:, part] = alignment.astype(out_ref.dtype)
+
+
+def align(model_width, slots, lengths, half_sharp, mine, other):
     return call_kernel(
-        functools.partial(align_kernel, model_width, slots, acc is None),
-        jax.ShapeDtypeStruct((rows, width), dtype),
-        table,
+        functools.partial(align_kernel, model_width, slots),
+        jax.ShapeDtypeStruct(mine.shape, jnp.bfloat16),
+        lengths,
+        half_sharp,
         mine,
         other,
-        *blocks,
-        *([] if acc is None else [acc]),
-        scratch=[pltpu.VMEM(mine.shape, jnp.bfloat16)],
-    )
+    )
+
+
+def profile_kernel(groups, weight_ref, *refs):
+    aligned, blocks, out_ref = refs[: len(groups)], refs[len(groups) : -1], refs[-1]
+    rows = blocks[0].shape[0]
+    acc, at = None, 0
+    for group, slots in zip(aligned, groups):
+        for i, slot in enumerate(slots):
+            term = weight_ref[slot : slot + 1, 0:1] * jnp.dot(
+                group[:, i * rows : (i + 1) * rows],
+                blocks[at][...],
+                preferred_element_type=jnp.float32,
+            )
+            acc = term if acc is None else acc + term
+            at += 1
+    out_ref[...] = acc
+
+
+def last_kernel(model_width, slot, len_ref, sharp_ref, weight_ref, mine, other, block, acc, out_ref):
+    rows = block.shape[0]
+    similar = (mine[...] + other[...]) * (1.0 / math.sqrt(model_width))
+    alignment = align_block(similar, len_ref[slot : slot + 1, :rows], sharp_ref[:, 0:1])
+    term = weight_ref[slot : slot + 1, 0:1] * jnp.dot(
+        alignment.astype(jnp.bfloat16), block[...], preferred_element_type=jnp.float32
+    )
+    out_ref[...] = (acc[...] + term).astype(out_ref.dtype)
 
 
 def per_device_by_target(
@@ -217,16 +226,23 @@
     def after(array, *done):
         return lax.optimization_barrier((array, *done))[0]
 
-    split = [(2 * i + c, 2 * (i ^ (1 + c)) + c) for i in range(4) for c in range(2)]
-    pool_split = lax.ppermute(target_pool, ("tgt", "rep"), split)
-    pool_last = from_peer(target_pool, 3)
-    pool_other = across(pool_split, "rep")
-    owners = jnp.stack([at_tgt, at_tgt ^ (1 + at_rep), at_tgt ^ (2 - at_rep), at_tgt ^ 3])
-    libs = [target_pool, pool_split, pool_other, pool_last]
+    def asked(x, c):
+        return 2 * c + (1 - c) * (1 + 2 * x)
+
+    pairs = [
+        ((2 * i + x) * 2 + c, (2 * (i ^ asked(x, c)) + x) * 2 + c)
+        for i in range(4)
+        for x in range(2)
+        for c in range(2)
+    ]
+    pools = [lax.ppermute(target_pool, ("tgt", "qry", "rep"), pairs)]
+    owners = [at_tgt] + [
+        at_tgt ^ asked(x, c) for c in (at_rep, 1 - at_rep) for x in (at_qry, 1 - at_qry)
+    ]
+    owners = jnp.stack(owners)
 
     share = lax.dynamic_index_in_dim(target_res, at_qry, 0, keepdims=False)
     rest = lax.dynamic_index_in_dim(target_res, 1 - at_qry, 0, keepdims=False)
-    share = after(share, pool_split, pool_last)
     far = from_peer(share, 2)
     near = from_peer(share, 1)
 
@@ -234,45 +250,79 @@
     slots = [bases[0], bases[0] + 1]
     for base in bases[1:]:
         slots += [base + at_qry, base + 1 - at_qry]
-    posterior, table = call_kernel(
+    slots = jnp.stack(slots).astype(jnp.int32)[:, None]
+    named = slots == jnp.arange(len(target_len))[None]
+    lengths = jnp.sum(jnp.where(named, target_len[None], 0), axis=1, keepdims=True)
+    lengths = jnp.broadcast_to(lengths.astype(jnp.float32), (len(target_len), target_rows))
+    half_sharp = jnp.broadcast_to(0.5 * sharpness, (1, target_rows))
+
+    def aligned(slots, mine, other):
+        return align(model_width, slots, lengths, half_sharp, mine, other)
+
+    own_blocks = [target_res[0], target_res[1]]
+    own = partial_similar(after(query, pools[0]), own_blocks)
+    own_other = across(own, "rep")
+
+    far = after(far, pools[0])
+    near = after(near, far)
+    far = after(far, near)
+    zero = aligned((0, 1), after(own, far), own_other)
+    last = from_peer(far, 1)
+    far_rest = across(far, "qry")
+
+    near_rest = from_peer(after(rest, far), 1)
+
+    pools.append(across(pools[0], "qry"))
+    pools += [across(pool, "rep") for pool in pools]
+    last = after(last, *pools)
+    two_blocks = [near, far, far_rest]
+    two = partial_similar(after(query, zero, last), two_blocks)
+    two_other = across(two, "rep")
+    last = after(last, two)
+    last_rest = across(last, "qry")
+    two_aligned = aligned((2, 4, 5), two, two_other)
+
+    posterior, weights = call_kernel(
         weigh_kernel,
         (
-            jax.ShapeDtypeStruct((1, len(slots)), jnp.float32),
-            jax.ShapeDtypeStruct((4, len(slots), target_rows), jnp.float32),
+            jax.ShapeDtypeStruct((1, len(target_len)), jnp.float32),
+            jax.ShapeDtypeStruct((len(target_len), target_rows), jnp.float32),
         ),
-        jnp.stack(slots).astype(jnp.int32)[:, None],
-        target_len[None],
-        sharpness[None],
-        hits,
+        slots,
+        after(hits, two_aligned),
         query_pool,
         owners.astype(jnp.int32)[:, None],
-        *libs,
-    )
-
-    own_blocks = [target_res[0], target_res[1]]
-    own = partial_similar(after(query, share), own_blocks)
-    own_other = across(own, "rep")
-    acc = add_aligned(model_width, (0, 1), table, own, own_other, own_blocks, None)
-
-    far = after(far, acc)
-    near = after(near, far)
-    far_rest = across(far, "qry")
-    near_rest = across(near, "qry")
-    last = from_peer(far, 1)
-    last_rest = from_peer(after(rest, far), 3)
-
-    one = partial_similar(query, [far])
-    one_other = across(one, "rep")
-    acc = add_aligned(model_width, (4,), table, one, one_other, [far], acc)
-
-    blocks = [near, far_rest, near_rest]
-    two = partial_similar(after(query, acc), blocks)
-    two_other = across(two, "rep")
-    three = partial_similar(after(query, two), [last, last_rest])
+        target_pool,
+        *pools,
+    )
+
+    three_blocks = [last, near_rest]
+    three = partial_similar(after(query, *pools), three_blocks)
     three_other = across(three, "rep")
-    acc = add_aligned(model_width, (2, 5, 3), table, after(two, three), two_other, blocks, acc)
-    profile = add_aligned(
-        model_width, (6, 7), table, three, three_other, [last, last_rest], acc, jnp.bfloat16
+    four = partial_similar(after(query, three, weights), [last_rest])
+    four_other = across(four, "rep")
+    three_aligned = aligned((6, 3), after(three, four), three_other)
+    acc = call_kernel(
+        functools.partial(profile_kernel, ((0, 1), (2, 4, 5), (6, 3))),
+        jax.ShapeDtypeStruct(query.shape, jnp.float32),
+        weights,
+        zero,
+        two_aligned,
+        three_aligned,
+        *own_blocks,
+        *two_blocks,
+        *three_blocks,
+    )
+    profile = call_kernel(
+        functools.partial(last_kernel, model_width, 7),
+        jax.ShapeDtypeStruct(query.shape, jnp.bfloat16),
+        lengths,
+        half_sharp,
+        weights,
+        four,
+        four_other,
+        last_rest,
+        acc,
     )
     return (profile[None], posterior)
 

time: 39.6 us -> 38.7 us (0.977)
  Pallas kernels: 8.81 us -> 7.4 us
  starting transfers between devices: 12.6 us -> 13.8 us
  local copies, waits for them, and re-layouts: 2.19 us -> 1.7 us
  waiting for transfers between devices: 14.3 us -> 13.9 us
    ppermute x5 -> x4, waiting for transfers between devices: 9.67 us -> 3.35 us  [from_peer(): return lax.ppermute(array, 'tgt', [(i, i ^ k) for i in range(4)])]
    ppermute x1, waiting for transfers between devices: 0.01 us -> 6.2 us  [per_device_by_target(): pools = [lax.ppermute(target_pool, ('tgt', 'qry', 'rep'), pairs)]]
    ppermute x7 -> x9, starting transfers between devices: 2.31 us -> 5.04 us  [across(): return lax.ppermute(array, axis, [(0, 1), (1, 0)])]
    ppermute x1, starting transfers between devices: 3.09 us -> 0.45 us  [per_device_by_target(): pools = [lax.ppermute(target_pool, ('tgt', 'qry', 'rep'), pairs)]]
    pallas_call x9 -> x10, Pallas kernels: 8.81 us -> 7.4 us  [call_kernel(): pl.pallas_call(kernel, out_shape=out_shape, in_specs=[VMEM] * len(operand...]
    ppermute x5 -> x4, starting transfers between devices: 7.22 us -> 8.33 us  [from_peer(): return lax.ppermute(array, 'tgt', [(i, i ^ k) for i in range(4)])]
    unnamed x10, local copies, waits for them, and re-layouts: 0.67 us -> 0.02 us
    ppermute x7 -> x9, waiting for transfers between devices: 4.64 us -> 4.37 us  [across(): return lax.ppermute(array, axis, [(0, 1), (1, 0)])]
  transfers between devices with their start and end apart: 13 -> 14, of which waited for: 8 -> 3; matrix products, arithmetic and copies ran while one was open for 4% -> 2% of each run, Pallas kernels for 16% -> 14%
where the time goes in v5:
time: 38.7 us; the launch traced here: 38.5 us
  waiting for transfers between devices  13.9 us (36%)
  starting transfers between devices  13.8 us (36%)
  Pallas kernels  7.4 us (19%)
  local copies, waits for them, and re-layouts  1.7 us (4%)
  between operations  1.5 us (4%)
    ppermute x4, starting transfers between devices, from_peer(): return lax.ppermute(array, 'tgt', [(i, i ^ k) for i in range(4)])  8.33 us
    pallas_call x10, Pallas kernels, call_kernel(): pl.pallas_call(kernel, out_shape=out_shape, in_specs=[VMEM] * len(operand...  7.4 us
    ppermute x1, waiting for transfers between devices, per_device_by_target(): pools = [lax.ppermute(target_pool, ('tgt', 'qry', 'rep'), pairs)]  6.2 us
    ppermute x9, starting transfers between devices, across(): return lax.ppermute(array, axis, [(0, 1), (1, 0)])  5.04 us
    ppermute x9, waiting for transfers between devices, across(): return lax.ppermute(array, axis, [(0, 1), (1, 0)])  4.37 us
    ppermute x4, waiting for transfers between devices, from_peer(): return lax.ppermute(array, 'tgt', [(i, i ^ k) for i in range(4)])  3.35 us
    squeeze x1, local copies, waits for them, and re-layouts, per_device_by_target(): rest = lax.dynamic_index_in_dim(target_res, 1 - at_qry, 0, keepdims=False)  1.26 us
  transfers between devices with their start and end apart: 14, of which 3 were waited for; matrix products, arithmetic and copies ran while one was open for 2% of the time, Pallas kernels for 14%

profile of v5, /device:TPU:0, one launch (start us, length us, event | category | flops | bytes accessed | tf_op | source)
XLA Modules:
  0.0 38.5 jit_solution(7925790672205250845)
XLA Ops:
  0.7 1.3 %dynamic-slice_bitcast_fusion = (bf16[128,640]{1,0:T(8,128)(2,1)S(1)}, bf16[128,640]{1,0:T(8,128)(2,1)S(1)}, bf16[128,640]{1,0:T(8,128)(2,1)S(1)}, bf16[128,640]{1,0:T(8,128)(2,1)S(1)}) fusion(bf16[2,128,640]{2,1,0:T(8,128)(2,1)} %param.8, s32[]{:T(128)S(6)} %select_n.13, s32[]{:T(128)S(6)} %select_n.12), kind=kLoop, calls=%fused_computation | loop fusion | bytes 1310728 | tf_op jit(solution)/shard_map/jit(dynamic_index_in_dim)/squeeze | solution.py:245
  1.9 4.1 %collective-permute-start.1 = (bf16[128,640]{1,0:T(8,128)(2,1)S(1)}, bf16[128,640]{1,0:T(8,128)(2,1)S(1)}, u32[]{:S(2)}, u32[]{:S(2)}) collective-permute-start(bf16[128,640]{1,0:T(8,128)(2,1)S(1)} %get-tuple-element.35), channel_id=1, source_target_pairs={{0,8},{4,12},{8,0},{12,4},{1,9},{5,13},{9,1},{13,5},{2,10},{6,14},... | collective-permute-start | bytes 491528 | tf_op jit(solution)/shard_map/ppermute | solution.py:221
  6.0 1.6 %collective-permute-start.2 = (bf16[128,640]{1,0:T(8,128)(2,1)S(1)}, bf16[128,640]{1,0:T(8,128)(2,1)S(1)}, u32[]{:S(2)}, u32[]{:S(2)}) collective-permute-start(bf16[128,640]{1,0:T(8,128)(2,1)S(1)} %get-tuple-element.35), channel_id=1, source_target_pairs={{0,4},{4,0},{8,12},{12,8},{1,5},{5,1},{9,13},{13,9},{2,6},{6,2},{1... | collective-permute-start | bytes 491528 | tf_op jit(solution)/shard_map/ppermute | solution.py:221
  7.6 0.4 %collective-permute-start = (f32[2,1280]{1,0:T(2,128)S(1)}, f32[2,1280]{1,0:T(2,128)S(1)}, u32[]{:S(2)}, u32[]{:S(2)}) collective-permute-start(f32[2,1280]{1,0:T(2,128)S(1)} %copy-done.1), channel_id=1, source_target_pairs={{0,4},{1,9},{2,14},{3,11},{4,0},{5,13},{6,10},{7,15},{8,12},{9,1},... | collective-permute-start | bytes 30728 | tf_op jit(solution)/shard_map/ppermute | solution.py:238
  8.1 6.2 %collective-permute-done.refs_1_ = f32[2,1280]{1,0:T(2,128)S(1)} collective-permute-done((f32[2,1280]{1,0:T(2,128)S(1)}, f32[2,1280]{1,0:T(2,128)S(1)}, u32[]{:S(2)}, u32[]{:S(2)}) %collective-permute-start) | collective-permute-done | bytes 10272 | tf_op jit(solution)/shard_map/ppermute | solution.py:238
  14.3 0.3 shard_map.86.mine
  14.7 1.6 %collective-permute-start.4 = (bf16[128,640]{1,0:T(8,128)(2,1)S(1)}, bf16[128,640]{1,0:T(8,128)(2,1)S(1)}, u32[]{:S(2)}, u32[]{:S(2)}) collective-permute-start(bf16[128,640]{1,0:T(8,128)(2,1)S(1)} %collective-permute-done.1.refs_2_.refs_6_), channel_id=1, source_target_pairs={{0,4},{4,0},{8,12},{12,8},{1,5},{5,1},{9,13},{13,9},{2,6},{6,2},{1... | collective-permute-start | bytes 491528 | tf_op jit(solution)/shard_map/ppermute | solution.py:221
  16.2 0.9 %collective-permute-start.8 = (bf16[128,640]{1,0:T(8,128)(2,1)S(1)}, bf16[128,640]{1,0:T(8,128)(2,1)S(1)}, u32[]{:S(2)}, u32[]{:S(2)}) collective-permute-start(bf16[128,640]{1,0:T(8,128)(2,1)S(1)} %collective-permute-done.1.refs_2_.refs_6_), channel_id=1, source_target_pairs={{0,2},{2,0},{1,3},{3,1},{4,6},{6,4},{5,7},{7,5},{8,10},{10,8},{9,1... | collective-permute-start | bytes 491528 | tf_op jit(solution)/shard_map/ppermute | solution.py:224
  17.1 1.1 %collective-permute-start.5 = (f32[2,1280]{1,0:T(2,128)S(1)}, f32[2,1280]{1,0:T(2,128)S(1)}, u32[]{:S(2)}, u32[]{:S(2)}) collective-permute-start(f32[2,1280]{1,0:T(2,128)S(1)} %collective-permute-done.refs_1_), channel_id=1, source_target_pairs={{0,2},{2,0},{1,3},{3,1},{4,6},{6,4},{5,7},{7,5},{8,10},{10,8},{9,1... | collective-permute-start | bytes 30728 | tf_op jit(solution)/shard_map/ppermute | solution.py:224
  18.4 4.3 %collective-permute-done.5.refs_2_ = f32[2,1280]{1,0:T(2,128)S(1)} collective-permute-done((f32[2,1280]{1,0:T(2,128)S(1)}, f32[2,1280]{1,0:T(2,128)S(1)}, u32[]{:S(2)}, u32[]{:S(2)}) %collective-permute-start.5) | collective-permute-done | bytes 10272 | tf_op jit(solution)/shard_map/ppermute | solution.py:224
  23.6 0.8 %shard_map.87.refs_0_ = bf16[256,256]{1,0:T(8,128)(2,1)S(1)} custom-call(f32[8,128]{1,0:T(8,128)S(1)} %broadcast_in_dim.36.len_ref, f32[1,128]{1,0:T(1,128)S(1)} %broadcast_in_dim.37.sharp_ref, f32[256,256]{1,0:T(8,128)S(1)} %shard_map.86.mine, f32[256,256]{1,0:T(8,128)S(1)} %collective-permute-done.3.other), custom_call_target="tpu_custom_call" | custom-call | tf_op jit(solution)/shard_map/pallas_call | solution.py:93
  24.5 0.4 %shard_map.88.mine = f32[256,384]{1,0:T(8,128)S(1)} custom-call(bf16[256,640]{1,0:T(8,128)(2,1)S(1)} %bitcast.27, bf16[128,640]{1,0:T(8,128)(2,1)S(1)} %collective-permute-done.2.refs_1_.refs_5_, bf16[128,640]{1,0:T(8,128)(2,1)S(1)} %collective-permute-done.1.refs_2_.refs_6_, bf16[128,640]{1,0:T(8,128)(2,1)S(1)} %collective-permute-done.8.refs_3_.refs_7_), custom_call_target="tpu_custom_call" | custom-call | tf_op jit(solution)/shard_map/pallas_call | solution.py:93
  24.9 0.6 %collective-permute-start.9 = (f32[256,384]{1,0:T(8,128)S(1)}, f32[256,384]{1,0:T(8,128)S(1)}, u32[]{:S(2)}, u32[]{:S(2)}) collective-permute-start(f32[256,384]{1,0:T(8,128)S(1)} %shard_map.88.mine), channel_id=1, source_target_pairs={{0,1},{1,0},{2,3},{3,2},{4,5},{5,4},{6,7},{7,6},{8,9},{9,8},{10,11... | collective-permute-start | bytes 1179656 | tf_op jit(solution)/shard_map/ppermute | solution.py:224
  25.5 1.1 %collective-permute-start.10 = (bf16[128,640]{1,0:T(8,128)(2,1)S(1)}, bf16[128,640]{1,0:T(8,128)(2,1)S(1)}, u32[]{:S(2)}, u32[]{:S(2)}) collective-permute-start(bf16[128,640]{1,0:T(8,128)(2,1)S(1)} %get-tuple-element.28), channel_id=1, source_target_pairs={{0,4},{4,0},{8,12},{12,8},{1,5},{5,1},{9,13},{13,9},{2,6},{6,2},{1... | collective-permute-start | bytes 491528 | tf_op jit(solution)/shard_map/ppermute | solution.py:221
  26.6 1.7 %collective-permute-start.11 = (bf16[128,640]{1,0:T(8,128)(2,1)S(1)}, bf16[128,640]{1,0:T(8,128)(2,1)S(1)}, u32[]{:S(2)}, u32[]{:S(2)}) collective-permute-start(bf16[128,640]{1,0:T(8,128)(2,1)S(1)} %collective-permute-done.4.refs_1_.refs_8_), channel_id=1, source_target_pairs={{0,2},{2,0},{1,3},{3,1},{4,6},{6,4},{5,7},{7,5},{8,10},{10,8},{9,1... | collective-permute-start | bytes 491528 | tf_op jit(solution)/shard_map/ppermute | solution.py:224
  28.3 3.3 %collective-permute-done.10.refs_2_.refs_9_ = bf16[128,640]{1,0:T(8,128)(2,1)S(1)} collective-permute-done((bf16[128,640]{1,0:T(8,128)(2,1)S(1)}, bf16[128,640]{1,0:T(8,128)(2,1)S(1)}, u32[]{:S(2)}, u32[]{:S(2)}) %collective-permute-start.10) | collective-permute-done | bytes 163872 | tf_op jit(solution)/shard_map/ppermute | solution.py:221
  31.7 0.3 shard_map.91.mine
  32.4 1.2 %shard_map.89.refs_1_ = bf16[256,384]{1,0:T(8,128)(2,1)S(1)} custom-call(f32[8,128]{1,0:T(8,128)S(1)} %broadcast_in_dim.36.len_ref, f32[1,128]{1,0:T(1,128)S(1)} %broadcast_in_dim.37.sharp_ref, f32[256,384]{1,0:T(8,128)S(1)} %shard_map.88.mine, f32[256,384]{1,0:T(8,128)S(1)} %collective-permute-done.9.other), custom_call_target="tpu_custom_call" | custom-call | tf_op jit(solution)/shard_map/pallas_call | solution.py:93
  33.6 0.8 %shard_map.90 = (f32[1,8]{1,0:T(1,128)}, f32[8,128]{1,0:T(8,128)S(1)}) custom-call(s32[8,1]{1,0:T(8,128)S(1)} %copy.11.slot_ref, s32[1,28]{1,0:T(1,128)S(1)} %copy-done.3, f32[1,1280]{1,0:T(1,128)S(1)} %copy-done.2, s32[5,1]{1,0:T(8,128)S(1)} %copy.12.owner_ref, f32[2,1280]{1,0:T(2,128)S(1)} %copy-done.1, f32[2,1280]{1,0:T(2,128)S(1)} %collective-permute-done.refs_1_, ...), custom_call_target="tpu_custom_call" | custom-call | tf_op jit(solution)/shard_map/pallas_call | solution.py:93
  34.5 0.2 shard_map.92.mine
  34.7 0.5 %collective-permute-start.12 = (f32[256,128]{1,0:T(8,128)S(1)}, f32[256,128]{1,0:T(8,128)S(1)}, u32[]{:S(2)}, u32[]{:S(2)}) collective-permute-start(f32[256,128]{1,0:T(8,128)S(1)} %shard_map.92.mine), channel_id=1, source_target_pairs={{0,1},{1,0},{2,3},{3,2},{4,5},{5,4},{6,7},{7,6},{8,9},{9,8},{10,11... | collective-permute-start | bytes 393224 | tf_op jit(solution)/shard_map/ppermute | solution.py:224
  35.3 0.8 %shard_map.93.refs_2_ = bf16[256,256]{1,0:T(8,128)(2,1)S(1)} custom-call(f32[8,128]{1,0:T(8,128)S(1)} %broadcast_in_dim.36.len_ref, f32[1,128]{1,0:T(1,128)S(1)} %broadcast_in_dim.37.sharp_ref, f32[256,256]{1,0:T(8,128)S(1)} %shard_map.91.mine, f32[256,256]{1,0:T(8,128)S(1)} %collective-permute-done.13.other), custom_call_target="tpu_custom_call" | custom-call | tf_op jit(solution)/shard_map/pallas_call | solution.py:93
  36.1 0.8 %shard_map.94.acc = f32[256,640]{1,0:T(8,128)S(1)} custom-call(f32[8,128]{1,0:T(8,128)S(1)} %get-tuple-element.25.weight_ref, bf16[256,256]{1,0:T(8,128)(2,1)S(1)} %shard_map.87.refs_0_, bf16[256,384]{1,0:T(8,128)(2,1)S(1)} %shard_map.89.refs_1_, bf16[256,256]{1,0:T(8,128)(2,1)S(1)} %shard_map.93.refs_2_, ...), custom_call_target="tpu_custom_call" | custom-call | tf_op jit(solution)/shard_map/pallas_call | solution.py:93
  36.9 1.6 %shard_map.95 = bf16[256,640]{1,0:T(8,128)(2,1)} custom-call(f32[8,128]{1,0:T(8,128)S(1)} %broadcast_in_dim.36.len_ref, f32[1,128]{1,0:T(1,128)S(1)} %broadcast_in_dim.37.sharp_ref, f32[8,128]{1,0:T(8,128)S(1)} %get-tuple-element.25.weight_ref, f32[256,128]{1,0:T(8,128)S(1)} %shard_map.92.mine, f32[256,128]{1,0:T(8,128)S(1)} %collective-permute-done.12.other, ...), custom_call_target="tpu_custom_call" | custom-call | tf_op jit(solution)/shard_map/pallas_call | solution.py:93
  (33 shorter events, 0.8 us)
Async XLA Ops:
  0.6 7.0 %copy-start.1 = (f32[2,1280]{1,0:T(2,128)S(1)}, f32[2,1280]{1,0:T(2,128)}, u32[]{:S(2)}) copy-start(f32[2,1280]{1,0:T(2,128)} %refs_0_.1) | copy-start | bytes 30724
  0.6 13.6 %copy-start = (bf16[1,256,640]{2,1,0:T(8,128)(2,1)S(1)}, bf16[1,256,640]{2,1,0:T(8,128)(2,1)}, u32[]{:S(2)}) copy-start(bf16[1,256,640]{2,1,0:T(8,128)(2,1)} %param.7) | copy-start | bytes 983044
  1.9 12.7 %collective-permute-start.1 = (bf16[128,640]{1,0:T(8,128)(2,1)S(1)}, bf16[128,640]{1,0:T(8,128)(2,1)S(1)}, u32[]{:S(2)}, u32[]{:S(2)}) collective-permute-start(bf16[128,640]{1,0:T(8,128)(2,1)S(1)} %get-tuple-element.35), channel_id=1, source_target_pairs={{0,8},{4,12},{8,0},{12,4},{1,9},{5,13},{9,1},{13,5},{2,10},{6,14},... | collective-permute-start | bytes 491528 | tf_op jit(solution)/shard_map/ppermute | solution.py:221
  6.0 8.7 %collective-permute-start.2 = (bf16[128,640]{1,0:T(8,128)(2,1)S(1)}, bf16[128,640]{1,0:T(8,128)(2,1)S(1)}, u32[]{:S(2)}, u32[]{:S(2)}) collective-permute-start(bf16[128,640]{1,0:T(8,128)(2,1)S(1)} %get-tuple-element.35), channel_id=1, source_target_pairs={{0,4},{4,0},{8,12},{12,8},{1,5},{5,1},{9,13},{13,9},{2,6},{6,2},{1... | collective-permute-start | bytes 491528 | tf_op jit(solution)/shard_map/ppermute | solution.py:221
  7.6 6.6 %collective-permute-start = (f32[2,1280]{1,0:T(2,128)S(1)}, f32[2,1280]{1,0:T(2,128)S(1)}, u32[]{:S(2)}, u32[]{:S(2)}) collective-permute-start(f32[2,1280]{1,0:T(2,128)S(1)} %copy-done.1), channel_id=1, source_target_pairs={{0,4},{1,9},{2,14},{3,11},{4,0},{5,13},{6,10},{7,15},{8,12},{9,1},... | collective-permute-start | bytes 30728 | tf_op jit(solution)/shard_map/ppermute | solution.py:238
  14.6 9.0 %collective-permute-start.3 = (f32[256,256]{1,0:T(8,128)S(1)}, f32[256,256]{1,0:T(8,128)S(1)}, u32[]{:S(2)}, u32[]{:S(2)}) collective-permute-start(f32[256,256]{1,0:T(8,128)S(1)} %shard_map.86.mine), channel_id=1, source_target_pairs={{0,1},{1,0},{2,3},{3,2},{4,5},{5,4},{6,7},{7,6},{8,9},{9,8},{10,11... | collective-permute-start | bytes 786440 | tf_op jit(solution)/shard_map/ppermute | solution.py:224
  14.7 9.8 %collective-permute-start.4 = (bf16[128,640]{1,0:T(8,128)(2,1)S(1)}, bf16[128,640]{1,0:T(8,128)(2,1)S(1)}, u32[]{:S(2)}, u32[]{:S(2)}) collective-permute-start(bf16[128,640]{1,0:T(8,128)(2,1)S(1)} %collective-permute-done.1.refs_2_.refs_6_), channel_id=1, source_target_pairs={{0,4},{4,0},{8,12},{12,8},{1,5},{5,1},{9,13},{13,9},{2,6},{6,2},{1... | collective-permute-start | bytes 491528 | tf_op jit(solution)/shard_map/ppermute | solution.py:221
  16.2 8.2 %collective-permute-start.8 = (bf16[128,640]{1,0:T(8,128)(2,1)S(1)}, bf16[128,640]{1,0:T(8,128)(2,1)S(1)}, u32[]{:S(2)}, u32[]{:S(2)}) collective-permute-start(bf16[128,640]{1,0:T(8,128)(2,1)S(1)} %collective-permute-done.1.refs_2_.refs_6_), channel_id=1, source_target_pairs={{0,2},{2,0},{1,3},{3,1},{4,6},{6,4},{5,7},{7,5},{8,10},{10,8},{9,1... | collective-permute-start | bytes 491528 | tf_op jit(solution)/shard_map/ppermute | solution.py:224
  17.1 5.6 %collective-permute-start.5 = (f32[2,1280]{1,0:T(2,128)S(1)}, f32[2,1280]{1,0:T(2,128)S(1)}, u32[]{:S(2)}, u32[]{:S(2)}) collective-permute-start(f32[2,1280]{1,0:T(2,128)S(1)} %collective-permute-done.refs_1_), channel_id=1, source_target_pairs={{0,2},{2,0},{1,3},{3,1},{4,6},{6,4},{5,7},{7,5},{8,10},{10,8},{9,1... | collective-permute-start | bytes 30728 | tf_op jit(solution)/shard_map/ppermute | solution.py:224
  18.3 4.5 %copy-start.4 = (s32[8]{0:T(128)S(1)}, s32[8]{0:T(128)}, u32[]{:S(2)}) copy-start(s32[8]{0:T(128)} %param.9) | copy-start | bytes 100
  18.4 6.1 %collective-permute-start.6 = (f32[2,1280]{1,0:T(2,128)S(1)}, f32[2,1280]{1,0:T(2,128)S(1)}, u32[]{:S(2)}, u32[]{:S(2)}) collective-permute-start(f32[2,1280]{1,0:T(2,128)S(1)} %collective-permute-done.refs_1_), channel_id=1, source_target_pairs={{0,1},{1,0},{2,3},{3,2},{4,5},{5,4},{6,7},{7,6},{8,9},{9,8},{10,11... | collective-permute-start | bytes 30728 | tf_op jit(solution)/shard_map/ppermute | solution.py:224
  22.7 1.7 %collective-permute-start.7 = (f32[2,1280]{1,0:T(2,128)S(1)}, f32[2,1280]{1,0:T(2,128)S(1)}, u32[]{:S(2)}, u32[]{:S(2)}) collective-permute-start(f32[2,1280]{1,0:T(2,128)S(1)} %collective-permute-done.5.refs_2_), channel_id=1, source_target_pairs={{0,1},{1,0},{2,3},{3,2},{4,5},{5,4},{6,7},{7,6},{8,9},{9,8},{10,11... | collective-permute-start | bytes 30728 | tf_op jit(solution)/shard_map/ppermute | solution.py:224
  24.9 7.5 %collective-permute-start.9 = (f32[256,384]{1,0:T(8,128)S(1)}, f32[256,384]{1,0:T(8,128)S(1)}, u32[]{:S(2)}, u32[]{:S(2)}) collective-permute-start(f32[256,384]{1,0:T(8,128)S(1)} %shard_map.88.mine), channel_id=1, source_target_pairs={{0,1},{1,0},{2,3},{3,2},{4,5},{5,4},{6,7},{7,6},{8,9},{9,8},{10,11... | collective-permute-start | bytes 1179656 | tf_op jit(solution)/shard_map/ppermute | solution.py:224
  25.5 6.2 %collective-permute-start.10 = (bf16[128,640]{1,0:T(8,128)(2,1)S(1)}, bf16[128,640]{1,0:T(8,128)(2,1)S(1)}, u32[]{:S(2)}, u32[]{:S(2)}) collective-permute-start(bf16[128,640]{1,0:T(8,128)(2,1)S(1)} %get-tuple-element.28), channel_id=1, source_target_pairs={{0,4},{4,0},{8,12},{12,8},{1,5},{5,1},{9,13},{13,9},{2,6},{6,2},{1... | collective-permute-start | bytes 491528 | tf_op jit(solution)/shard_map/ppermute | solution.py:221
  26.6 7.9 %collective-permute-start.11 = (bf16[128,640]{1,0:T(8,128)(2,1)S(1)}, bf16[128,640]{1,0:T(8,128)(2,1)S(1)}, u32[]{:S(2)}, u32[]{:S(2)}) collective-permute-start(bf16[128,640]{1,0:T(8,128)(2,1)S(1)} %collective-permute-done.4.refs_1_.refs_8_), channel_id=1, source_target_pairs={{0,2},{2,0},{1,3},{3,1},{4,6},{6,4},{5,7},{7,5},{8,10},{10,8},{9,1... | collective-permute-start | bytes 491528 | tf_op jit(solution)/shard_map/ppermute | solution.py:224
  32.0 3.3 %collective-permute-start.13 = (f32[256,256]{1,0:T(8,128)S(1)}, f32[256,256]{1,0:T(8,128)S(1)}, u32[]{:S(2)}, u32[]{:S(2)}) collective-permute-start(f32[256,256]{1,0:T(8,128)S(1)} %shard_map.91.mine), channel_id=1, source_target_pairs={{0,1},{1,0},{2,3},{3,2},{4,5},{5,4},{6,7},{7,6},{8,9},{9,8},{10,11... | collective-permute-start | bytes 786440 | tf_op jit(solution)/shard_map/ppermute | solution.py:224
  32.4 1.3 %copy-start.2 = (f32[1,1280]{1,0:T(1,128)S(1)}, f32[1,1280]{1,0:T(1,128)}, u32[]{:S(2)}) copy-start(f32[1,1280]{1,0:T(1,128)} %pool_ref.1) | copy-start | bytes 15364
  32.4 1.3 %copy-start.3 = (s32[1,28]{1,0:T(1,128)S(1)}, s32[1,28]{1,0:T(1,128)}, u32[]{:S(2)}) copy-start(s32[1,28]{1,0:T(1,128)} %hits_ref) | copy-start | bytes 340
  34.7 2.2 %collective-permute-start.12 = (f32[256,128]{1,0:T(8,128)S(1)}, f32[256,128]{1,0:T(8,128)S(1)}, u32[]{:S(2)}, u32[]{:S(2)}) collective-permute-start(f32[256,128]{1,0:T(8,128)S(1)} %shard_map.92.mine), channel_id=1, source_target_pairs={{0,1},{1,0},{2,3},{3,2},{4,5},{5,4},{6,7},{7,6},{8,9},{9,8},{10,11... | collective-permute-start | bytes 393224 | tf_op jit(solution)/shard_map/ppermute | solution.py:224

commit v6 on v5

--- a/solution.py
+++ b/solution.py
@@ -226,20 +226,11 @@
     def after(array, *done):
         return lax.optimization_barrier((array, *done))[0]
 
-    def asked(x, c):
-        return 2 * c + (1 - c) * (1 + 2 * x)
-
-    pairs = [
-        ((2 * i + x) * 2 + c, (2 * (i ^ asked(x, c)) + x) * 2 + c)
-        for i in range(4)
-        for x in range(2)
-        for c in range(2)
-    ]
-    pools = [lax.ppermute(target_pool, ("tgt", "qry", "rep"), pairs)]
-    owners = [at_tgt] + [
-        at_tgt ^ asked(x, c) for c in (at_rep, 1 - at_rep) for x in (at_qry, 1 - at_qry)
-    ]
-    owners = jnp.stack(owners)
+    split = [(2 * i + c, 2 * (i ^ (1 + c)) + c) for i in range(4) for c in range(2)]
+    pool_split = lax.ppermute(target_pool, ("tgt", "rep"), split)
+    pool_last = from_peer(target_pool, 3)
+    pool_other = across(pool_split, "rep")
+    owners = jnp.stack([at_tgt, at_tgt ^ (1 + at_rep), at_tgt ^ (2 - at_rep), at_tgt ^ 3])
 
     share = lax.dynamic_index_in_dim(target_res, at_qry, 0, keepdims=False)
     rest = lax.dynamic_index_in_dim(target_res, 1 - at_qry, 0, keepdims=False)
@@ -259,28 +250,12 @@
     def aligned(slots, mine, other):
         return align(model_width, slots, lengths, half_sharp, mine, other)
 
-    own_blocks = [target_res[0], target_res[1]]
-    own = partial_similar(after(query, pools[0]), own_blocks)
-    own_other = across(own, "rep")
-
-    far = after(far, pools[0])
+    far = after(far, pool_split, pool_last)
     near = after(near, far)
     far = after(far, near)
-    zero = aligned((0, 1), after(own, far), own_other)
     last = from_peer(far, 1)
     far_rest = across(far, "qry")
-
     near_rest = from_peer(after(rest, far), 1)
-
-    pools.append(across(pools[0], "qry"))
-    pools += [across(pool, "rep") for pool in pools]
-    last = after(last, *pools)
-    two_blocks = [near, far, far_rest]
-    two = partial_similar(after(query, zero, last), two_blocks)
-    two_other = across(two, "rep")
-    last = after(last, two)
-    last_rest = across(last, "qry")
-    two_aligned = aligned((2, 4, 5), two, two_other)
 
     posterior, weights = call_kernel(
         weigh_kernel,
@@ -289,29 +264,41 @@
             jax.ShapeDtypeStruct((len(target_len), target_rows), jnp.float32),
         ),
         slots,
-        after(hits, two_aligned),
+        hits,
         query_pool,
         owners.astype(jnp.int32)[:, None],
         target_pool,
-        *pools,
-    )
-
-    three_blocks = [last, near_rest]
-    three = partial_similar(after(query, *pools), three_blocks)
+        pool_split,
+        pool_other,
+        pool_last,
+    )
+
+    one_blocks = [target_res[0], target_res[1], near, far]
+    one = partial_similar(query, one_blocks)
+    one_other = across(one, "rep")
+    one_aligned = aligned((0, 1, 2, 4), one, one_other)
+
+    last = after(last, weights, one_aligned)
+    last_rest = across(last, "qry")
+    three = partial_similar(query, [last])
     three_other = across(three, "rep")
-    four = partial_similar(after(query, three, weights), [last_rest])
+    three_aligned = aligned((6,), three, three_other)
+    four_blocks = [far_rest, near_rest]
+    four = partial_similar(after(query, three_aligned), four_blocks)
     four_other = across(four, "rep")
-    three_aligned = aligned((6, 3), after(three, four), three_other)
+    five = partial_similar(after(query, four), [last_rest])
+    five_other = across(five, "rep")
+    four_aligned = aligned((5, 3), after(four, five), four_other)
     acc = call_kernel(
-        functools.partial(profile_kernel, ((0, 1), (2, 4, 5), (6, 3))),
+        functools.partial(profile_kernel, ((0, 1, 2, 4), (6,), (5, 3))),
         jax.ShapeDtypeStruct(query.shape, jnp.float32),
         weights,
-        zero,
-        two_aligned,
+        one_aligned,
         three_aligned,
-        *own_blocks,
-        *two_blocks,
-        *three_blocks,
+        four_aligned,
+        *one_blocks,
+        last,
+        *four_blocks,
     )
     profile = call_kernel(
         functools.partial(last_kernel, model_width, 7),
@@ -319,8 +306,8 @@
         lengths,
         half_sharp,
         weights,
-        four,
-        four_other,
+        five,
+        five_other,
         last_rest,
         acc,
     )

time: 38.7 us -> 35 us (0.904)
  waiting for transfers between devices: 13.9 us -> 10.8 us
  starting transfers between devices: 13.8 us -> 12.3 us
  local copies, waits for them, and re-layouts: 1.7 us -> 2.26 us
    ppermute x4 -> x5, waiting for transfers between devices: 3.35 us -> 0.93 us  [from_peer(): return lax.ppermute(array, 'tgt', [(i, i ^ k) for i in range(4)])]
    ppermute x9 -> x7, starting transfers between devices: 5.04 us -> 3.04 us  [across(): return lax.ppermute(array, axis, [(0, 1), (1, 0)])]
    ppermute x1, waiting for transfers between devices: 6.2 us -> 4.96 us  [per_device_by_target(): pool_split = lax.ppermute(target_pool, ('tgt', 'rep'), split)]
    unnamed x10, local copies, waits for them, and re-layouts: 0.02 us -> 0.67 us
    ppermute x9 -> x7, waiting for transfers between devices: 4.37 us -> 4.93 us  [across(): return lax.ppermute(array, axis, [(0, 1), (1, 0)])]
    ppermute x4 -> x5, starting transfers between devices: 8.33 us -> 8.79 us  [from_peer(): return lax.ppermute(array, 'tgt', [(i, i ^ k) for i in range(4)])]
  transfers between devices with their start and end apart: 14 -> 13, of which waited for: 3 -> 4; matrix products, arithmetic and copies ran while one was open for 2% -> 2% of each run, Pallas kernels for 14% -> 16%
where the time goes in v6:
time: 35 us; the launch traced here: 34.7 us
  starting transfers between devices  12.3 us (35%)
  waiting for transfers between devices  10.8 us (31%)
  Pallas kernels  7.64 us (22%)
  local copies, waits for them, and re-layouts  2.26 us (6%)
  between operations  1.48 us (4%)
    ppermute x5, starting transfers between devices, from_peer(): return lax.ppermute(array, 'tgt', [(i, i ^ k) for i in range(4)])  8.79 us
    pallas_call x10, Pallas kernels, call_kernel(): pl.pallas_call(kernel, out_shape=out_shape, in_specs=[VMEM] * len(operand...  7.64 us
    ppermute x1, waiting for transfers between devices, per_device_by_target(): pool_split = lax.ppermute(target_pool, ('tgt', 'rep'), split)  4.96 us
    ppermute x7, waiting for transfers between devices, across(): return lax.ppermute(array, axis, [(0, 1), (1, 0)])  4.93 us
    ppermute x7, starting transfers between devices, across(): return lax.ppermute(array, axis, [(0, 1), (1, 0)])  3.04 us
    squeeze x1, local copies, waits for them, and re-layouts, per_device_by_target(): rest = lax.dynamic_index_in_dim(target_res, 1 - at_qry, 0, keepdims=False)  1.26 us
    ppermute x5, waiting for transfers between devices, from_peer(): return lax.ppermute(array, 'tgt', [(i, i ^ k) for i in range(4)])  0.93 us
  transfers between devices with their start and end apart: 13, of which 4 were waited for; matrix products, arithmetic and copies ran while one was open for 2% of the time, Pallas kernels for 16%

profile of v6, /device:TPU:0, one launch (start us, length us, event | category | flops | bytes accessed | tf_op | source)
XLA Modules:
  0.0 34.7 jit_solution(10126335362684781400)
XLA Ops:
  0.7 1.3 %dynamic-slice_bitcast_fusion = (bf16[128,640]{1,0:T(8,128)(2,1)S(1)}, bf16[128,640]{1,0:T(8,128)(2,1)S(1)}, bf16[128,640]{1,0:T(8,128)(2,1)S(1)}, bf16[128,640]{1,0:T(8,128)(2,1)S(1)}) fusion(bf16[2,128,640]{2,1,0:T(8,128)(2,1)} %param.8, s32[]{:T(128)S(6)} %select_n.13, s32[]{:T(128)S(6)} %select_n.12), kind=kLoop, calls=%fused_computation | loop fusion | bytes 1310728 | tf_op jit(solution)/shard_map/jit(dynamic_index_in_dim)/squeeze | solution.py:236
  1.9 4.1 %collective-permute-start.3 = (bf16[128,640]{1,0:T(8,128)(2,1)S(1)}, bf16[128,640]{1,0:T(8,128)(2,1)S(1)}, u32[]{:S(2)}, u32[]{:S(2)}) collective-permute-start(bf16[128,640]{1,0:T(8,128)(2,1)S(1)} %get-tuple-element.24), channel_id=1, source_target_pairs={{0,8},{4,12},{8,0},{12,4},{1,9},{5,13},{9,1},{13,5},{2,10},{6,14},... | collective-permute-start | bytes 491528 | tf_op jit(solution)/shard_map/ppermute | solution.py:221
  6.0 1.6 %collective-permute-start.4 = (bf16[128,640]{1,0:T(8,128)(2,1)S(1)}, bf16[128,640]{1,0:T(8,128)(2,1)S(1)}, u32[]{:S(2)}, u32[]{:S(2)}) collective-permute-start(bf16[128,640]{1,0:T(8,128)(2,1)S(1)} %get-tuple-element.24), channel_id=1, source_target_pairs={{0,4},{4,0},{8,12},{12,8},{1,5},{5,1},{9,13},{13,9},{2,6},{6,2},{1... | collective-permute-start | bytes 491528 | tf_op jit(solution)/shard_map/ppermute | solution.py:221
  7.6 0.4 %collective-permute-start = (f32[2,1280]{1,0:T(2,128)S(1)}, f32[2,1280]{1,0:T(2,128)S(1)}, u32[]{:S(2)}, u32[]{:S(2)}) collective-permute-start(f32[2,1280]{1,0:T(2,128)S(1)} %copy-done.1), channel_id=1, source_target_pairs={{0,4},{1,9},{4,0},{5,13},{8,12},{9,1},{12,8},{13,5},{2,6},{3,11},{... | collective-permute-start | bytes 30728 | tf_op jit(solution)/shard_map/ppermute | solution.py:230
  8.1 1.3 %collective-permute-start.2 = (f32[2,1280]{1,0:T(2,128)S(1)}, f32[2,1280]{1,0:T(2,128)S(1)}, u32[]{:S(2)}, u32[]{:S(2)}) collective-permute-start(f32[2,1280]{1,0:T(2,128)S(1)} %copy-done.1), channel_id=1, source_target_pairs={{0,12},{4,8},{8,4},{12,0},{1,13},{5,9},{9,5},{13,1},{2,14},{6,10},... | collective-permute-start | bytes 30728 | tf_op jit(solution)/shard_map/ppermute | solution.py:221
  9.4 5.0 %collective-permute-done.refs_1_ = f32[2,1280]{1,0:T(2,128)S(1)} collective-permute-done((f32[2,1280]{1,0:T(2,128)S(1)}, f32[2,1280]{1,0:T(2,128)S(1)}, u32[]{:S(2)}, u32[]{:S(2)}) %collective-permute-start) | collective-permute-done | bytes 10272 | tf_op jit(solution)/shard_map/ppermute | solution.py:230
  14.4 0.9 %collective-permute-done.2.refs_3_ = f32[2,1280]{1,0:T(2,128)S(1)} collective-permute-done((f32[2,1280]{1,0:T(2,128)S(1)}, f32[2,1280]{1,0:T(2,128)S(1)}, u32[]{:S(2)}, u32[]{:S(2)}) %collective-permute-start.2) | collective-permute-done | bytes 10272 | tf_op jit(solution)/shard_map/ppermute | solution.py:221
  15.3 0.5 %shard_map.87.mine = f32[256,512]{1,0:T(8,128)S(1)} custom-call(bf16[256,640]{1,0:T(8,128)(2,1)S(1)} %bitcast.26, bf16[128,640]{1,0:T(8,128)(2,1)S(1)} %get-tuple-element.23.refs_1_.refs_3_, bf16[128,640]{1,0:T(8,128)(2,1)S(1)} %get-tuple-element.25.refs_2_.refs_4_, bf16[128,640]{1,0:T(8,128)(2,1)S(1)} %collective-permute-done.4.refs_3_.refs_5_, ...), custom_call_target="tpu_custom_call" | custom-call | tf_op jit(solution)/shard_map/pallas_call | solution.py:93
  16.0 0.6 %collective-permute-start.5 = (bf16[128,640]{1,0:T(8,128)(2,1)S(1)}, bf16[128,640]{1,0:T(8,128)(2,1)S(1)}, u32[]{:S(2)}, u32[]{:S(2)}) collective-permute-start(bf16[128,640]{1,0:T(8,128)(2,1)S(1)} %collective-permute-done.3.refs_4_.refs_6_), channel_id=1, source_target_pairs={{0,4},{4,0},{8,12},{12,8},{1,5},{5,1},{9,13},{13,9},{2,6},{6,2},{1... | collective-permute-start | bytes 491528 | tf_op jit(solution)/shard_map/ppermute | solution.py:221
  16.8 0.5 %collective-permute-start.1 = (f32[2,1280]{1,0:T(2,128)S(1)}, f32[2,1280]{1,0:T(2,128)S(1)}, u32[]{:S(2)}, u32[]{:S(2)}) collective-permute-start(f32[2,1280]{1,0:T(2,128)S(1)} %collective-permute-done.refs_1_), channel_id=1, source_target_pairs={{0,1},{1,0},{2,3},{3,2},{4,5},{5,4},{6,7},{7,6},{8,9},{9,8},{10,11... | collective-permute-start | bytes 30728 | tf_op jit(solution)/shard_map/ppermute | solution.py:224
  17.3 1.5 %collective-permute-start.8 = (bf16[128,640]{1,0:T(8,128)(2,1)S(1)}, bf16[128,640]{1,0:T(8,128)(2,1)S(1)}, u32[]{:S(2)}, u32[]{:S(2)}) collective-permute-start(bf16[128,640]{1,0:T(8,128)(2,1)S(1)} %collective-permute-done.3.refs_4_.refs_6_), channel_id=1, source_target_pairs={{0,2},{2,0},{1,3},{3,1},{4,6},{6,4},{5,7},{7,5},{8,10},{10,8},{9,1... | collective-permute-start | bytes 491528 | tf_op jit(solution)/shard_map/ppermute | solution.py:224
  18.8 1.2 %collective-permute-start.9 = (bf16[128,640]{1,0:T(8,128)(2,1)S(1)}, bf16[128,640]{1,0:T(8,128)(2,1)S(1)}, u32[]{:S(2)}, u32[]{:S(2)}) collective-permute-start(bf16[128,640]{1,0:T(8,128)(2,1)S(1)} %get-tuple-element.18), channel_id=1, source_target_pairs={{0,4},{4,0},{8,12},{12,8},{1,5},{5,1},{9,13},{13,9},{2,6},{6,2},{1... | collective-permute-start | bytes 491528 | tf_op jit(solution)/shard_map/ppermute | solution.py:221
  20.9 0.5 %copy-done.2 = f32[1,1280]{1,0:T(1,128)S(1)} copy-done((f32[1,1280]{1,0:T(1,128)S(1)}, f32[1,1280]{1,0:T(1,128)}, u32[]{:S(2)}) %copy-start.2) | copy-done | bytes 5144
  21.5 0.8 %shard_map.86 = (f32[1,8]{1,0:T(1,128)}, f32[8,128]{1,0:T(8,128)S(1)}) custom-call(s32[8,1]{1,0:T(8,128)S(1)} %copy.11.slot_ref, s32[1,28]{1,0:T(1,128)S(1)} %copy-done.3, f32[1,1280]{1,0:T(1,128)S(1)} %copy-done.2, s32[4,1]{1,0:T(4,128)S(1)} %copy.12.owner_ref, f32[2,1280]{1,0:T(2,128)S(1)} %copy-done.1, f32[2,1280]{1,0:T(2,128)S(1)} %collective-permute-done.refs_1_, ...), custom_call_target="tpu_custom_call" | custom-call | tf_op jit(solution)/shard_map/pallas_call | solution.py:93
  22.4 1.7 %shard_map.88.refs_0_ = bf16[256,512]{1,0:T(8,128)(2,1)S(1)} custom-call(f32[8,128]{1,0:T(8,128)S(1)} %broadcast_in_dim.36.len_ref, f32[1,128]{1,0:T(1,128)S(1)} %broadcast_in_dim.37.sharp_ref, f32[256,512]{1,0:T(8,128)S(1)} %shard_map.87.mine, f32[256,512]{1,0:T(8,128)S(1)} %collective-permute-done.6.other), custom_call_target="tpu_custom_call" | custom-call | tf_op jit(solution)/shard_map/pallas_call | solution.py:93
  24.2 0.2 shard_map.89.mine
  24.5 0.6 %collective-permute-start.10 = (bf16[128,640]{1,0:T(8,128)(2,1)S(1)}, bf16[128,640]{1,0:T(8,128)(2,1)S(1)}, u32[]{:S(2)}, u32[]{:S(2)}) collective-permute-start(bf16[128,640]{1,0:T(8,128)(2,1)S(1)} %collective-permute-done.5.refs_1_.refs_7_), channel_id=1, source_target_pairs={{0,2},{2,0},{1,3},{3,1},{4,6},{6,4},{5,7},{7,5},{8,10},{10,8},{9,1... | collective-permute-start | bytes 491528 | tf_op jit(solution)/shard_map/ppermute | solution.py:224
  25.1 0.7 %collective-permute-done.7.other = f32[256,128]{1,0:T(8,128)S(1)} collective-permute-done((f32[256,128]{1,0:T(8,128)S(1)}, f32[256,128]{1,0:T(8,128)S(1)}, u32[]{:S(2)}, u32[]{:S(2)}) %collective-permute-start.7) | collective-permute-done | bytes 131104 | tf_op jit(solution)/shard_map/ppermute | solution.py:224
  25.8 0.5 %shard_map.90.refs_1_ = bf16[256,128]{1,0:T(8,128)(2,1)S(1)} custom-call(f32[8,128]{1,0:T(8,128)S(1)} %broadcast_in_dim.36.len_ref, f32[1,128]{1,0:T(1,128)S(1)} %broadcast_in_dim.37.sharp_ref, f32[256,128]{1,0:T(8,128)S(1)} %shard_map.89.mine, f32[256,128]{1,0:T(8,128)S(1)} %collective-permute-done.7.other), custom_call_target="tpu_custom_call" | custom-call | tf_op jit(solution)/shard_map/pallas_call | solution.py:93
  26.4 0.3 shard_map.91.mine
  26.9 4.2 %collective-permute-done.10.refs_1_.block = bf16[128,640]{1,0:T(8,128)(2,1)S(1)} collective-permute-done((bf16[128,640]{1,0:T(8,128)(2,1)S(1)}, bf16[128,640]{1,0:T(8,128)(2,1)S(1)}, u32[]{:S(2)}, u32[]{:S(2)}) %collective-permute-start.10) | collective-permute-done | bytes 163872 | tf_op jit(solution)/shard_map/ppermute | solution.py:224
  31.5 0.8 %shard_map.93.refs_2_ = bf16[256,256]{1,0:T(8,128)(2,1)S(1)} custom-call(f32[8,128]{1,0:T(8,128)S(1)} %broadcast_in_dim.36.len_ref, f32[1,128]{1,0:T(1,128)S(1)} %broadcast_in_dim.37.sharp_ref, f32[256,256]{1,0:T(8,128)S(1)} %shard_map.91.mine, f32[256,256]{1,0:T(8,128)S(1)} %collective-permute-done.12.other), custom_call_target="tpu_custom_call" | custom-call | tf_op jit(solution)/shard_map/pallas_call | solution.py:93
  32.3 0.8 %shard_map.94.acc = f32[256,640]{1,0:T(8,128)S(1)} custom-call(f32[8,128]{1,0:T(8,128)S(1)} %get-tuple-element.12.weight_ref, bf16[256,512]{1,0:T(8,128)(2,1)S(1)} %shard_map.88.refs_0_, bf16[256,128]{1,0:T(8,128)(2,1)S(1)} %shard_map.90.refs_1_, bf16[256,256]{1,0:T(8,128)(2,1)S(1)} %shard_map.93.refs_2_, ...), custom_call_target="tpu_custom_call" | custom-call | tf_op jit(solution)/shard_map/pallas_call | solution.py:93
  33.1 1.6 %shard_map.95 = bf16[256,640]{1,0:T(8,128)(2,1)} custom-call(f32[8,128]{1,0:T(8,128)S(1)} %broadcast_in_dim.36.len_ref, f32[1,128]{1,0:T(1,128)S(1)} %broadcast_in_dim.37.sharp_ref, f32[8,128]{1,0:T(8,128)S(1)} %get-tuple-element.12.weight_ref, f32[256,128]{1,0:T(8,128)S(1)} %shard_map.92.mine, f32[256,128]{1,0:T(8,128)S(1)} %collective-permute-done.11.other, ...), custom_call_target="tpu_custom_call" | custom-call | tf_op jit(solution)/shard_map/pallas_call | solution.py:93
  (31 shorter events, 1.5 us)
Async XLA Ops:
  0.6 7.0 %copy-start.1 = (f32[2,1280]{1,0:T(2,128)S(1)}, f32[2,1280]{1,0:T(2,128)}, u32[]{:S(2)}) copy-start(f32[2,1280]{1,0:T(2,128)} %refs_0_.1) | copy-start | bytes 30724
  0.6 14.6 %copy-start = (bf16[1,256,640]{2,1,0:T(8,128)(2,1)S(1)}, bf16[1,256,640]{2,1,0:T(8,128)(2,1)}, u32[]{:S(2)}) copy-start(bf16[1,256,640]{2,1,0:T(8,128)(2,1)} %param.7) | copy-start | bytes 983044
  1.9 13.4 %collective-permute-start.3 = (bf16[128,640]{1,0:T(8,128)(2,1)S(1)}, bf16[128,640]{1,0:T(8,128)(2,1)S(1)}, u32[]{:S(2)}, u32[]{:S(2)}) collective-permute-start(bf16[128,640]{1,0:T(8,128)(2,1)S(1)} %get-tuple-element.24), channel_id=1, source_target_pairs={{0,8},{4,12},{8,0},{12,4},{1,9},{5,13},{9,1},{13,5},{2,10},{6,14},... | collective-permute-start | bytes 491528 | tf_op jit(solution)/shard_map/ppermute | solution.py:221
  6.0 9.3 %collective-permute-start.4 = (bf16[128,640]{1,0:T(8,128)(2,1)S(1)}, bf16[128,640]{1,0:T(8,128)(2,1)S(1)}, u32[]{:S(2)}, u32[]{:S(2)}) collective-permute-start(bf16[128,640]{1,0:T(8,128)(2,1)S(1)} %get-tuple-element.24), channel_id=1, source_target_pairs={{0,4},{4,0},{8,12},{12,8},{1,5},{5,1},{9,13},{13,9},{2,6},{6,2},{1... | collective-permute-start | bytes 491528 | tf_op jit(solution)/shard_map/ppermute | solution.py:221
  7.6 6.8 %collective-permute-start = (f32[2,1280]{1,0:T(2,128)S(1)}, f32[2,1280]{1,0:T(2,128)S(1)}, u32[]{:S(2)}, u32[]{:S(2)}) collective-permute-start(f32[2,1280]{1,0:T(2,128)S(1)} %copy-done.1), channel_id=1, source_target_pairs={{0,4},{1,9},{4,0},{5,13},{8,12},{9,1},{12,8},{13,5},{2,6},{3,11},{... | collective-permute-start | bytes 30728 | tf_op jit(solution)/shard_map/ppermute | solution.py:230
  8.1 7.2 %collective-permute-start.2 = (f32[2,1280]{1,0:T(2,128)S(1)}, f32[2,1280]{1,0:T(2,128)S(1)}, u32[]{:S(2)}, u32[]{:S(2)}) collective-permute-start(f32[2,1280]{1,0:T(2,128)S(1)} %copy-done.1), channel_id=1, source_target_pairs={{0,12},{4,8},{8,4},{12,0},{1,13},{5,9},{9,5},{13,1},{2,14},{6,10},... | collective-permute-start | bytes 30728 | tf_op jit(solution)/shard_map/ppermute | solution.py:221
  15.8 6.6 %collective-permute-start.6 = (f32[256,512]{1,0:T(8,128)S(1)}, f32[256,512]{1,0:T(8,128)S(1)}, u32[]{:S(2)}, u32[]{:S(2)}) collective-permute-start(f32[256,512]{1,0:T(8,128)S(1)} %shard_map.87.mine), channel_id=1, source_target_pairs={{0,1},{1,0},{2,3},{3,2},{4,5},{5,4},{6,7},{7,6},{8,9},{9,8},{10,11... | collective-permute-start | bytes 1572872 | tf_op jit(solution)/shard_map/ppermute | solution.py:224
  15.9 0.7 %copy-start.4 = (s32[8]{0:T(128)S(1)}, s32[8]{0:T(128)}, u32[]{:S(2)}) copy-start(s32[8]{0:T(128)} %param.9) | copy-start | bytes 100
  16.0 8.2 %collective-permute-start.5 = (bf16[128,640]{1,0:T(8,128)(2,1)S(1)}, bf16[128,640]{1,0:T(8,128)(2,1)S(1)}, u32[]{:S(2)}, u32[]{:S(2)}) collective-permute-start(bf16[128,640]{1,0:T(8,128)(2,1)S(1)} %collective-permute-done.3.refs_4_.refs_6_), channel_id=1, source_target_pairs={{0,4},{4,0},{8,12},{12,8},{1,5},{5,1},{9,13},{13,9},{2,6},{6,2},{1... | collective-permute-start | bytes 491528 | tf_op jit(solution)/shard_map/ppermute | solution.py:221
  16.8 4.1 %collective-permute-start.1 = (f32[2,1280]{1,0:T(2,128)S(1)}, f32[2,1280]{1,0:T(2,128)S(1)}, u32[]{:S(2)}, u32[]{:S(2)}) collective-permute-start(f32[2,1280]{1,0:T(2,128)S(1)} %collective-permute-done.refs_1_), channel_id=1, source_target_pairs={{0,1},{1,0},{2,3},{3,2},{4,5},{5,4},{6,7},{7,6},{8,9},{9,8},{10,11... | collective-permute-start | bytes 30728 | tf_op jit(solution)/shard_map/ppermute | solution.py:224
  17.3 9.1 %collective-permute-start.8 = (bf16[128,640]{1,0:T(8,128)(2,1)S(1)}, bf16[128,640]{1,0:T(8,128)(2,1)S(1)}, u32[]{:S(2)}, u32[]{:S(2)}) collective-permute-start(bf16[128,640]{1,0:T(8,128)(2,1)S(1)} %collective-permute-done.3.refs_4_.refs_6_), channel_id=1, source_target_pairs={{0,2},{2,0},{1,3},{3,1},{4,6},{6,4},{5,7},{7,5},{8,10},{10,8},{9,1... | collective-permute-start | bytes 491528 | tf_op jit(solution)/shard_map/ppermute | solution.py:224
  18.8 7.6 %collective-permute-start.9 = (bf16[128,640]{1,0:T(8,128)(2,1)S(1)}, bf16[128,640]{1,0:T(8,128)(2,1)S(1)}, u32[]{:S(2)}, u32[]{:S(2)}) collective-permute-start(bf16[128,640]{1,0:T(8,128)(2,1)S(1)} %get-tuple-element.18), channel_id=1, source_target_pairs={{0,4},{4,0},{8,12},{12,8},{1,5},{5,1},{9,13},{13,9},{2,6},{6,2},{1... | collective-permute-start | bytes 491528 | tf_op jit(solution)/shard_map/ppermute | solution.py:221
  20.7 0.7 %copy-start.2 = (f32[1,1280]{1,0:T(1,128)S(1)}, f32[1,1280]{1,0:T(1,128)}, u32[]{:S(2)}) copy-start(f32[1,1280]{1,0:T(1,128)} %pool_ref.1) | copy-start | bytes 15364
  20.9 0.7 %copy-start.3 = (s32[1,28]{1,0:T(1,128)S(1)}, s32[1,28]{1,0:T(1,128)}, u32[]{:S(2)}) copy-start(s32[1,28]{1,0:T(1,128)} %hits_ref.1) | copy-start | bytes 340
  24.4 1.4 %collective-permute-start.7 = (f32[256,128]{1,0:T(8,128)S(1)}, f32[256,128]{1,0:T(8,128)S(1)}, u32[]{:S(2)}, u32[]{:S(2)}) collective-permute-start(f32[256,128]{1,0:T(8,128)S(1)} %shard_map.89.mine), channel_id=1, source_target_pairs={{0,1},{1,0},{2,3},{3,2},{4,5},{5,4},{6,7},{7,6},{8,9},{9,8},{10,11... | collective-permute-start | bytes 393224 | tf_op jit(solution)/shard_map/ppermute | solution.py:224
  24.5 6.6 %collective-permute-start.10 = (bf16[128,640]{1,0:T(8,128)(2,1)S(1)}, bf16[128,640]{1,0:T(8,128)(2,1)S(1)}, u32[]{:S(2)}, u32[]{:S(2)}) collective-permute-start(bf16[128,640]{1,0:T(8,128)(2,1)S(1)} %collective-permute-done.5.refs_1_.refs_7_), channel_id=1, source_target_pairs={{0,2},{2,0},{1,3},{3,1},{4,6},{6,4},{5,7},{7,5},{8,10},{10,8},{9,1... | collective-permute-start | bytes 491528 | tf_op jit(solution)/shard_map/ppermute | solution.py:224
  26.7 4.7 %collective-permute-start.12 = (f32[256,256]{1,0:T(8,128)S(1)}, f32[256,256]{1,0:T(8,128)S(1)}, u32[]{:S(2)}, u32[]{:S(2)}) collective-permute-start(f32[256,256]{1,0:T(8,128)S(1)} %shard_map.91.mine), channel_id=1, source_target_pairs={{0,1},{1,0},{2,3},{3,2},{4,5},{5,4},{6,7},{7,6},{8,9},{9,8},{10,11... | collective-permute-start | bytes 786440 | tf_op jit(solution)/shard_map/ppermute | solution.py:224
  31.4 1.7 %collective-permute-start.11 = (f32[256,128]{1,0:T(8,128)S(1)}, f32[256,128]{1,0:T(8,128)S(1)}, u32[]{:S(2)}, u32[]{:S(2)}) collective-permute-start(f32[256,128]{1,0:T(8,128)S(1)} %shard_map.92.mine), channel_id=1, source_target_pairs={{0,1},{1,0},{2,3},{3,2},{4,5},{5,4},{6,7},{7,6},{8,9},{9,8},{10,11... | collective-permute-start | bytes 393224 | tf_op jit(solution)/shard_map/ppermute | solution.py:224

commit v7 on v6

--- a/solution.py
+++ b/solution.py
@@ -99,6 +99,24 @@
         cost_estimate=pl.CostEstimate(flops=flops, bytes_accessed=0, transcendentals=0),
         compiler_params=pltpu.CompilerParams(vmem_limit_bytes=VMEM_BYTES),
     )(*operands)
+
+
+def share_kernel(at_ref, blocks_ref, out_ref, done):
+    copy = pltpu.make_async_copy(blocks_ref.at[at_ref[0]], out_ref, done)
+    copy.start()
+    copy.wait()
+
+
+def take_share(blocks, at):
+    return pl.pallas_call(
+        share_kernel,
+        out_shape=jax.ShapeDtypeStruct(blocks.shape[1:], blocks.dtype),
+        in_specs=[pl.BlockSpec(memory_space=pltpu.SMEM), pl.BlockSpec(memory_space=pl.ANY)],
+        out_specs=pl.BlockSpec(memory_space=pl.ANY),
+        scratch_shapes=[pltpu.SemaphoreType.DMA],
+        cost_estimate=pl.CostEstimate(flops=0, bytes_accessed=0, transcendentals=0),
+        compiler_params=pltpu.CompilerParams(vmem_limit_bytes=VMEM_BYTES),
+    )(at.astype(jnp.int32)[None], blocks)
 
 
 def weigh_kernel(slot_ref, hits_ref, pool_ref, owner_ref, *refs):
@@ -232,7 +250,7 @@
     pool_other = across(pool_split, "rep")
     owners = jnp.stack([at_tgt, at_tgt ^ (1 + at_rep), at_tgt ^ (2 - at_rep), at_tgt ^ 3])
 
-    share = lax.dynamic_index_in_dim(target_res, at_qry, 0, keepdims=False)
+    share = take_share(target_res, at_qry)
     rest = lax.dynamic_index_in_dim(target_res, 1 - at_qry, 0, keepdims=False)
     far = from_peer(share, 2)
     near = from_peer(share, 1)
@@ -257,6 +275,17 @@
     far_rest = across(far, "qry")
     near_rest = from_peer(after(rest, far), 1)
 
+    one_blocks = [target_res[0], target_res[1], near, far]
+    one = partial_similar(query, one_blocks)
+    one_other = across(one, "rep")
+
+    last_rest = across(last, "qry")
+    three = partial_similar(query, [last])
+    three_other = across(three, "rep")
+    three_aligned = aligned((6,), three, three_other)
+    four_blocks = [far_rest, near_rest]
+    four = partial_similar(after(query, three_aligned), four_blocks)
+    four_other = across(four, "rep")
     posterior, weights = call_kernel(
         weigh_kernel,
         (
@@ -264,7 +293,7 @@
             jax.ShapeDtypeStruct((len(target_len), target_rows), jnp.float32),
         ),
         slots,
-        hits,
+        after(hits, four),
         query_pool,
         owners.astype(jnp.int32)[:, None],
         target_pool,
@@ -272,21 +301,8 @@
         pool_other,
         pool_last,
     )
-
-    one_blocks = [target_res[0], target_res[1], near, far]
-    one = partial_similar(query, one_blocks)
-    one_other = across(one, "rep")
-    one_aligned = aligned((0, 1, 2, 4), one, one_other)
-
-    last = after(last, weights, one_aligned)
-    last_rest = across(last, "qry")
-    three = partial_similar(query, [last])
-    three_other = across(three, "rep")
-    three_aligned = aligned((6,), three, three_other)
-    four_blocks = [far_rest, near_rest]
-    four = partial_similar(after(query, three_aligned), four_blocks)
-    four_other = across(four, "rep")
-    five = partial_similar(after(query, four), [last_rest])
+    one_aligned = aligned((0, 1, 2, 4), after(one, four), one_other)
+    five = partial_similar(after(query, weights, one_aligned), [last_rest])
     five_other = across(five, "rep")
     four_aligned = aligned((5, 3), after(four, five), four_other)
     acc = call_kernel(

time: 35 us -> 37.1 us (1.060)
  waiting for transfers between devices: 10.8 us -> 12.4 us
  starting transfers between devices: 12.3 us -> 13.6 us
  local copies, waits for them, and re-layouts: 2.26 us -> 1.37 us
    ppermute x5, waiting for transfers between devices: 0.93 us -> 11.6 us  [from_peer(): return lax.ppermute(array, 'tgt', [(i, i ^ k) for i in range(4)])]
    ppermute x1, waiting for transfers between devices: 4.96 us -> 0.01 us  [per_device_by_target(): pool_split = lax.ppermute(target_pool, ('tgt', 'rep'), split)]
    ppermute x7, waiting for transfers between devices: 4.93 us -> 0.8 us  [across(): return lax.ppermute(array, axis, [(0, 1), (1, 0)])]
    ppermute x1, starting transfers between devices: 0.45 us -> 3.09 us  [per_device_by_target(): pool_split = lax.ppermute(target_pool, ('tgt', 'rep'), split)]
    ppermute x5, starting transfers between devices: 8.79 us -> 6.54 us  [from_peer(): return lax.ppermute(array, 'tgt', [(i, i ^ k) for i in range(4)])]
    squeeze x1, local copies, waits for them, and re-layouts: 1.26 us -> 0.04 us  [per_device_by_target(): one_blocks = [target_res[0], target_res[1], near, far]]
    ppermute x7, starting transfers between devices: 3.04 us -> 3.95 us  [across(): return lax.ppermute(array, axis, [(0, 1), (1, 0)])]
    unnamed x10 -> x14, local copies, waits for them, and re-layouts: 0.67 us -> 1 us
  transfers between devices with their start and end apart: 13 -> 13, of which waited for: 4 -> 4; matrix products, arithmetic and copies ran while one was open for 2% -> 2% of each run, Pallas kernels for 16% -> 15%
where the time goes in v7:
time: 37.1 us; the launch traced here: 37 us
  starting transfers between devices  13.6 us (37%)
  waiting for transfers between devices  12.4 us (33%)
  Pallas kernels  7.83 us (21%)
  between operations  1.48 us (4%)
  local copies, waits for them, and re-layouts  1.37 us (4%)
    ppermute x5, waiting for transfers between devices, from_peer(): return lax.ppermute(array, 'tgt', [(i, i ^ k) for i in range(4)])  11.6 us
    pallas_call x10, Pallas kernels, call_kernel(): pl.pallas_call(kernel, out_shape=out_shape, in_specs=[VMEM] * len(operand...  7.63 us
    ppermute x5, starting transfers between devices, from_peer(): return lax.ppermute(array, 'tgt', [(i, i ^ k) for i in range(4)])  6.54 us
    ppermute x7, starting transfers between devices, across(): return lax.ppermute(array, axis, [(0, 1), (1, 0)])  3.95 us
    ppermute x1, starting transfers between devices, per_device_by_target(): pool_split = lax.ppermute(target_pool, ('tgt', 'rep'), split)  3.09 us
    unnamed x14, local copies, waits for them, and re-layouts  1 us
    ppermute x7, waiting for transfers between devices, across(): return lax.ppermute(array, axis, [(0, 1), (1, 0)])  0.8 us
  transfers between devices with their start and end apart: 13, of which 4 were waited for; matrix products, arithmetic and copies ran while one was open for 2% of the time, Pallas kernels for 15%

profile of v7, /device:TPU:0, one launch (start us, length us, event | category | flops | bytes accessed | tf_op | source)
XLA Modules:
  0.0 37.0 jit_solution(1273631761576853195)
XLA Ops:
  0.6 3.1 %collective-permute-start.1 = (f32[2,1280]{1,0:T(2,128)}, f32[2,1280]{1,0:T(2,128)S(1)}, u32[]{:S(2)}, u32[]{:S(2)}) collective-permute-start(f32[2,1280]{1,0:T(2,128)} %refs_0_.1), channel_id=1, source_target_pairs={{0,4},{1,9},{4,0},{5,13},{8,12},{9,1},{12,8},{13,5},{2,6},{3,11},{... | collective-permute-start | bytes 30728 | tf_op jit(solution)/shard_map/ppermute | solution.py:248
  3.7 2.5 %collective-permute-start.2 = (f32[2,1280]{1,0:T(2,128)}, f32[2,1280]{1,0:T(2,128)S(1)}, u32[]{:S(2)}, u32[]{:S(2)}) collective-permute-start(f32[2,1280]{1,0:T(2,128)} %refs_0_.1), channel_id=1, source_target_pairs={{0,12},{4,8},{8,4},{12,0},{1,13},{5,9},{9,5},{13,1},{2,14},{6,10},... | collective-permute-start | bytes 30728 | tf_op jit(solution)/shard_map/ppermute | solution.py:239
  6.2 1.0 %copy-done.1 = bf16[2,128,640]{2,1,0:T(8,128)(2,1)S(1)} copy-done((bf16[2,128,640]{2,1,0:T(8,128)(2,1)S(1)}, bf16[2,128,640]{2,1,0:T(8,128)(2,1)}, u32[]{:S(2)}) %copy-start.1) | copy-done | bytes 327704
  7.6 1.8 %collective-permute-start.3 = (bf16[128,640]{1,0:T(8,128)(2,1)S(1)}, bf16[128,640]{1,0:T(8,128)(2,1)S(1)}, u32[]{:S(2)}, u32[]{:S(2)}) collective-permute-start(bf16[128,640]{1,0:T(8,128)(2,1)S(1)} %shard_map.86), channel_id=1, source_target_pairs={{0,4},{4,0},{8,12},{12,8},{1,5},{5,1},{9,13},{13,9},{2,6},{6,2},{1... | collective-permute-start | bytes 491528 | tf_op jit(solution)/shard_map/ppermute | solution.py:239
  9.4 7.7 %collective-permute-done.refs_4_.refs_6_ = bf16[128,640]{1,0:T(8,128)(2,1)S(1)} collective-permute-done((bf16[128,640]{1,0:T(8,128)(2,1)S(1)}, bf16[128,640]{1,0:T(8,128)(2,1)S(1)}, u32[]{:S(2)}, u32[]{:S(2)}) %collective-permute-start) | collective-permute-done | bytes 163872 | tf_op jit(solution)/shard_map/ppermute | solution.py:239
  17.1 0.5 %collective-permute-done.3.refs_3_.refs_5_ = bf16[128,640]{1,0:T(8,128)(2,1)S(1)} collective-permute-done((bf16[128,640]{1,0:T(8,128)(2,1)S(1)}, bf16[128,640]{1,0:T(8,128)(2,1)S(1)}, u32[]{:S(2)}, u32[]{:S(2)}) %collective-permute-start.3) | collective-permute-done | bytes 163872 | tf_op jit(solution)/shard_map/ppermute | solution.py:239
  17.6 0.5 %shard_map.91.mine = f32[256,512]{1,0:T(8,128)S(1)} custom-call(bf16[256,640]{1,0:T(8,128)(2,1)S(1)} %bitcast.25, bf16[128,640]{1,0:T(8,128)(2,1)S(1)} %get-tuple-element.26.refs_1_.refs_3_, bf16[128,640]{1,0:T(8,128)(2,1)S(1)} %get-tuple-element.24.refs_2_.refs_4_, bf16[128,640]{1,0:T(8,128)(2,1)S(1)} %collective-permute-done.3.refs_3_.refs_5_, ...), custom_call_target="tpu_custom_call" | custom-call | tf_op jit(solution)/shard_map/pallas_call | solution.py:93
  18.2 0.4 %collective-permute-start.4 = (bf16[128,640]{1,0:T(8,128)(2,1)S(1)}, bf16[128,640]{1,0:T(8,128)(2,1)S(1)}, u32[]{:S(2)}, u32[]{:S(2)}) collective-permute-start(bf16[128,640]{1,0:T(8,128)(2,1)S(1)} %collective-permute-done.refs_4_.refs_6_), channel_id=1, source_target_pairs={{0,4},{4,0},{8,12},{12,8},{1,5},{5,1},{9,13},{13,9},{2,6},{6,2},{1... | collective-permute-start | bytes 491528 | tf_op jit(solution)/shard_map/ppermute | solution.py:239
  18.6 1.5 %collective-permute-start.6 = (bf16[128,640]{1,0:T(8,128)(2,1)S(1)}, bf16[128,640]{1,0:T(8,128)(2,1)S(1)}, u32[]{:S(2)}, u32[]{:S(2)}) collective-permute-start(bf16[128,640]{1,0:T(8,128)(2,1)S(1)} %collective-permute-done.refs_4_.refs_6_), channel_id=1, source_target_pairs={{0,2},{2,0},{1,3},{3,1},{4,6},{6,4},{5,7},{7,5},{8,10},{10,8},{9,1... | collective-permute-start | bytes 491528 | tf_op jit(solution)/shard_map/ppermute | solution.py:242
  20.1 1.7 %collective-permute-start.7 = (bf16[128,640]{1,0:T(8,128)(2,1)S(1)}, bf16[128,640]{1,0:T(8,128)(2,1)S(1)}, u32[]{:S(2)}, u32[]{:S(2)}) collective-permute-start(bf16[128,640]{1,0:T(8,128)(2,1)S(1)} %get-tuple-element.17), channel_id=1, source_target_pairs={{0,4},{4,0},{8,12},{12,8},{1,5},{5,1},{9,13},{13,9},{2,6},{6,2},{1... | collective-permute-start | bytes 491528 | tf_op jit(solution)/shard_map/ppermute | solution.py:239
  21.8 3.5 %collective-permute-done.4.refs_1_.refs_7_ = bf16[128,640]{1,0:T(8,128)(2,1)S(1)} collective-permute-done((bf16[128,640]{1,0:T(8,128)(2,1)S(1)}, bf16[128,640]{1,0:T(8,128)(2,1)S(1)}, u32[]{:S(2)}, u32[]{:S(2)}) %collective-permute-start.4) | collective-permute-done | bytes 163872 | tf_op jit(solution)/shard_map/ppermute | solution.py:239
  25.2 0.2 shard_map.87.mine
  25.7 1.5 %collective-permute-start.10 = (bf16[128,640]{1,0:T(8,128)(2,1)S(1)}, bf16[128,640]{1,0:T(8,128)(2,1)S(1)}, u32[]{:S(2)}, u32[]{:S(2)}) collective-permute-start(bf16[128,640]{1,0:T(8,128)(2,1)S(1)} %collective-permute-done.4.refs_1_.refs_7_), channel_id=1, source_target_pairs={{0,2},{2,0},{1,3},{3,1},{4,6},{6,4},{5,7},{7,5},{8,10},{10,8},{9,1... | collective-permute-start | bytes 491528 | tf_op jit(solution)/shard_map/ppermute | solution.py:242
  28.1 0.5 %shard_map.88.refs_1_ = bf16[256,128]{1,0:T(8,128)(2,1)S(1)} custom-call(f32[8,128]{1,0:T(8,128)S(1)} %broadcast_in_dim.39.len_ref, f32[1,128]{1,0:T(1,128)S(1)} %broadcast_in_dim.40.sharp_ref, f32[256,128]{1,0:T(8,128)S(1)} %shard_map.87.mine, f32[256,128]{1,0:T(8,128)S(1)} %collective-permute-done.5.other), custom_call_target="tpu_custom_call" | custom-call | tf_op jit(solution)/shard_map/pallas_call | solution.py:93
  28.6 0.3 shard_map.89.mine
  29.0 0.2 collective-permute-start.12
  29.2 0.3 collective-permute-start.8
  29.8 0.8 %collective-permute-done.8.refs_2_ = f32[2,1280]{1,0:T(2,128)S(1)} collective-permute-done((f32[2,1280]{1,0:T(2,128)S(1)}, f32[2,1280]{1,0:T(2,128)S(1)}, u32[]{:S(2)}, u32[]{:S(2)}) %collective-permute-start.8) | collective-permute-done | bytes 10272 | tf_op jit(solution)/shard_map/ppermute | solution.py:242
  30.6 0.8 %shard_map.90 = (f32[1,8]{1,0:T(1,128)}, f32[8,128]{1,0:T(8,128)S(1)}) custom-call(s32[8,1]{1,0:T(8,128)S(1)} %copy.11.slot_ref, s32[1,28]{1,0:T(1,128)S(1)} %copy-done.5, f32[1,1280]{1,0:T(1,128)S(1)} %copy-done.4, s32[4,1]{1,0:T(4,128)S(1)} %copy.12.owner_ref, f32[2,1280]{1,0:T(2,128)S(1)} %copy-done.3, f32[2,1280]{1,0:T(2,128)S(1)} %collective-permute-done.1.refs_1_, ...), custom_call_target="tpu_custom_call" | custom-call | tf_op jit(solution)/shard_map/pallas_call | solution.py:93
  31.4 1.7 %shard_map.92.refs_0_ = bf16[256,512]{1,0:T(8,128)(2,1)S(1)} custom-call(f32[8,128]{1,0:T(8,128)S(1)} %broadcast_in_dim.39.len_ref, f32[1,128]{1,0:T(1,128)S(1)} %broadcast_in_dim.40.sharp_ref, f32[256,512]{1,0:T(8,128)S(1)} %shard_map.91.mine, f32[256,512]{1,0:T(8,128)S(1)} %collective-permute-done.9.other), custom_call_target="tpu_custom_call" | custom-call | tf_op jit(solution)/shard_map/pallas_call | solution.py:93
  33.4 0.3 collective-permute-start.11
  33.7 0.8 %shard_map.94.refs_2_ = bf16[256,256]{1,0:T(8,128)(2,1)S(1)} custom-call(f32[8,128]{1,0:T(8,128)S(1)} %broadcast_in_dim.39.len_ref, f32[1,128]{1,0:T(1,128)S(1)} %broadcast_in_dim.40.sharp_ref, f32[256,256]{1,0:T(8,128)S(1)} %shard_map.89.mine, f32[256,256]{1,0:T(8,128)S(1)} %collective-permute-done.12.other), custom_call_target="tpu_custom_call" | custom-call | tf_op jit(solution)/shard_map/pallas_call | solution.py:93
  34.5 0.8 %shard_map.95.acc = f32[256,640]{1,0:T(8,128)S(1)} custom-call(f32[8,128]{1,0:T(8,128)S(1)} %get-tuple-element.19.weight_ref, bf16[256,512]{1,0:T(8,128)(2,1)S(1)} %shard_map.92.refs_0_, bf16[256,128]{1,0:T(8,128)(2,1)S(1)} %shard_map.88.refs_1_, bf16[256,256]{1,0:T(8,128)(2,1)S(1)} %shard_map.94.refs_2_, ...), custom_call_target="tpu_custom_call" | custom-call | tf_op jit(solution)/shard_map/pallas_call | solution.py:93
  35.3 1.6 %shard_map.96 = bf16[256,640]{1,0:T(8,128)(2,1)} custom-call(f32[8,128]{1,0:T(8,128)S(1)} %broadcast_in_dim.39.len_ref, f32[1,128]{1,0:T(1,128)S(1)} %broadcast_in_dim.40.sharp_ref, f32[8,128]{1,0:T(8,128)S(1)} %get-tuple-element.19.weight_ref, f32[256,128]{1,0:T(8,128)S(1)} %shard_map.93.mine, f32[256,128]{1,0:T(8,128)S(1)} %collective-permute-done.11.other, ...), custom_call_target="tpu_custom_call" | custom-call | tf_op jit(solution)/shard_map/pallas_call | solution.py:93
  (36 shorter events, 1.4 us)
Async XLA Ops:
  0.6 8.8 %collective-permute-start.1 = (f32[2,1280]{1,0:T(2,128)}, f32[2,1280]{1,0:T(2,128)S(1)}, u32[]{:S(2)}, u32[]{:S(2)}) collective-permute-start(f32[2,1280]{1,0:T(2,128)} %refs_0_.1), channel_id=1, source_target_pairs={{0,4},{1,9},{4,0},{5,13},{8,12},{9,1},{12,8},{13,5},{2,6},{3,11},{... | collective-permute-start | bytes 30728 | tf_op jit(solution)/shard_map/ppermute | solution.py:248
  3.7 5.7 %collective-permute-start.2 = (f32[2,1280]{1,0:T(2,128)}, f32[2,1280]{1,0:T(2,128)S(1)}, u32[]{:S(2)}, u32[]{:S(2)}) collective-permute-start(f32[2,1280]{1,0:T(2,128)} %refs_0_.1), channel_id=1, source_target_pairs={{0,12},{4,8},{8,4},{12,0},{1,13},{5,9},{9,5},{13,1},{2,14},{6,10},... | collective-permute-start | bytes 30728 | tf_op jit(solution)/shard_map/ppermute | solution.py:239
  6.2 1.0 %copy-start.1 = (bf16[2,128,640]{2,1,0:T(8,128)(2,1)S(1)}, bf16[2,128,640]{2,1,0:T(8,128)(2,1)}, u32[]{:S(2)}) copy-start(bf16[2,128,640]{2,1,0:T(8,128)(2,1)} %blocks_ref.1) | copy-start | bytes 983044
  7.2 2.2 %copy-start.2 = (bf16[2,128,640]{2,1,0:T(8,128)(2,1)S(1)}, bf16[2,128,640]{2,1,0:T(8,128)(2,1)}, u32[]{:S(2)}) copy-start(bf16[2,128,640]{2,1,0:T(8,128)(2,1)} %blocks_ref.1) | copy-start | bytes 983044
  7.4 9.7 %collective-permute-start = (bf16[128,640]{1,0:T(8,128)(2,1)S(1)}, bf16[128,640]{1,0:T(8,128)(2,1)S(1)}, u32[]{:S(2)}, u32[]{:S(2)}) collective-permute-start(bf16[128,640]{1,0:T(8,128)(2,1)S(1)} %shard_map.86), channel_id=1, source_target_pairs={{0,8},{4,12},{8,0},{12,4},{1,9},{5,13},{9,1},{13,5},{2,10},{6,14},... | collective-permute-start | bytes 491528 | tf_op jit(solution)/shard_map/ppermute | solution.py:239
  7.6 10.0 %collective-permute-start.3 = (bf16[128,640]{1,0:T(8,128)(2,1)S(1)}, bf16[128,640]{1,0:T(8,128)(2,1)S(1)}, u32[]{:S(2)}, u32[]{:S(2)}) collective-permute-start(bf16[128,640]{1,0:T(8,128)(2,1)S(1)} %shard_map.86), channel_id=1, source_target_pairs={{0,4},{4,0},{8,12},{12,8},{1,5},{5,1},{9,13},{13,9},{2,6},{6,2},{1... | collective-permute-start | bytes 491528 | tf_op jit(solution)/shard_map/ppermute | solution.py:239
  9.4 8.2 %copy-start = (bf16[1,256,640]{2,1,0:T(8,128)(2,1)S(1)}, bf16[1,256,640]{2,1,0:T(8,128)(2,1)}, u32[]{:S(2)}) copy-start(bf16[1,256,640]{2,1,0:T(8,128)(2,1)} %param.7) | copy-start | bytes 983044
  18.1 13.3 %collective-permute-start.9 = (f32[256,512]{1,0:T(8,128)S(1)}, f32[256,512]{1,0:T(8,128)S(1)}, u32[]{:S(2)}, u32[]{:S(2)}) collective-permute-start(f32[256,512]{1,0:T(8,128)S(1)} %shard_map.91.mine), channel_id=1, source_target_pairs={{0,1},{1,0},{2,3},{3,2},{4,5},{5,4},{6,7},{7,6},{8,9},{9,8},{10,11... | collective-permute-start | bytes 1572872 | tf_op jit(solution)/shard_map/ppermute | solution.py:242
  18.2 7.1 %collective-permute-start.4 = (bf16[128,640]{1,0:T(8,128)(2,1)S(1)}, bf16[128,640]{1,0:T(8,128)(2,1)S(1)}, u32[]{:S(2)}, u32[]{:S(2)}) collective-permute-start(bf16[128,640]{1,0:T(8,128)(2,1)S(1)} %collective-permute-done.refs_4_.refs_6_), channel_id=1, source_target_pairs={{0,4},{4,0},{8,12},{12,8},{1,5},{5,1},{9,13},{13,9},{2,6},{6,2},{1... | collective-permute-start | bytes 491528 | tf_op jit(solution)/shard_map/ppermute | solution.py:239
  18.6 10.0 %collective-permute-start.6 = (bf16[128,640]{1,0:T(8,128)(2,1)S(1)}, bf16[128,640]{1,0:T(8,128)(2,1)S(1)}, u32[]{:S(2)}, u32[]{:S(2)}) collective-permute-start(bf16[128,640]{1,0:T(8,128)(2,1)S(1)} %collective-permute-done.refs_4_.refs_6_), channel_id=1, source_target_pairs={{0,2},{2,0},{1,3},{3,1},{4,6},{6,4},{5,7},{7,5},{8,10},{10,8},{9,1... | collective-permute-start | bytes 491528 | tf_op jit(solution)/shard_map/ppermute | solution.py:242
  20.1 8.5 %collective-permute-start.7 = (bf16[128,640]{1,0:T(8,128)(2,1)S(1)}, bf16[128,640]{1,0:T(8,128)(2,1)S(1)}, u32[]{:S(2)}, u32[]{:S(2)}) collective-permute-start(bf16[128,640]{1,0:T(8,128)(2,1)S(1)} %get-tuple-element.17), channel_id=1, source_target_pairs={{0,4},{4,0},{8,12},{12,8},{1,5},{5,1},{9,13},{13,9},{2,6},{6,2},{1... | collective-permute-start | bytes 491528 | tf_op jit(solution)/shard_map/ppermute | solution.py:239
  25.5 2.5 %collective-permute-start.5 = (f32[256,128]{1,0:T(8,128)S(1)}, f32[256,128]{1,0:T(8,128)S(1)}, u32[]{:S(2)}, u32[]{:S(2)}) collective-permute-start(f32[256,128]{1,0:T(8,128)S(1)} %shard_map.87.mine), channel_id=1, source_target_pairs={{0,1},{1,0},{2,3},{3,2},{4,5},{5,4},{6,7},{7,6},{8,9},{9,8},{10,11... | collective-permute-start | bytes 393224 | tf_op jit(solution)/shard_map/ppermute | solution.py:242
  25.6 1.6 %copy-start.6 = (s32[8]{0:T(128)S(1)}, s32[8]{0:T(128)}, u32[]{:S(2)}) copy-start(s32[8]{0:T(128)} %param.9) | copy-start | bytes 100
  25.7 7.5 %collective-permute-start.10 = (bf16[128,640]{1,0:T(8,128)(2,1)S(1)}, bf16[128,640]{1,0:T(8,128)(2,1)S(1)}, u32[]{:S(2)}, u32[]{:S(2)}) collective-permute-start(bf16[128,640]{1,0:T(8,128)(2,1)S(1)} %collective-permute-done.4.refs_1_.refs_7_), channel_id=1, source_target_pairs={{0,2},{2,0},{1,3},{3,1},{4,6},{6,4},{5,7},{7,5},{8,10},{10,8},{9,1... | collective-permute-start | bytes 491528 | tf_op jit(solution)/shard_map/ppermute | solution.py:242
  29.0 4.7 %collective-permute-start.12 = (f32[256,256]{1,0:T(8,128)S(1)}, f32[256,256]{1,0:T(8,128)S(1)}, u32[]{:S(2)}, u32[]{:S(2)}) collective-permute-start(f32[256,256]{1,0:T(8,128)S(1)} %shard_map.89.mine), channel_id=1, source_target_pairs={{0,1},{1,0},{2,3},{3,2},{4,5},{5,4},{6,7},{7,6},{8,9},{9,8},{10,11... | collective-permute-start | bytes 786440 | tf_op jit(solution)/shard_map/ppermute | solution.py:242
  29.2 1.4 %copy-start.3 = (f32[2,1280]{1,0:T(2,128)S(1)}, f32[2,1280]{1,0:T(2,128)}, u32[]{:S(2)}) copy-start(f32[2,1280]{1,0:T(2,128)} %refs_0_.1) | copy-start | bytes 30724
  29.2 1.4 %collective-permute-start.8 = (f32[2,1280]{1,0:T(2,128)S(1)}, f32[2,1280]{1,0:T(2,128)S(1)}, u32[]{:S(2)}, u32[]{:S(2)}) collective-permute-start(f32[2,1280]{1,0:T(2,128)S(1)} %collective-permute-done.1.refs_1_), channel_id=1, source_target_pairs={{0,1},{1,0},{2,3},{3,2},{4,5},{5,4},{6,7},{7,6},{8,9},{9,8},{10,11... | collective-permute-start | bytes 30728 | tf_op jit(solution)/shard_map/ppermute | solution.py:242
  29.6 1.0 %copy-start.4 = (f32[1,1280]{1,0:T(1,128)S(1)}, f32[1,1280]{1,0:T(1,128)}, u32[]{:S(2)}) copy-start(f32[1,1280]{1,0:T(1,128)} %pool_ref.1) | copy-start | bytes 15364
  29.7 0.9 %copy-start.5 = (s32[1,28]{1,0:T(1,128)S(1)}, s32[1,28]{1,0:T(1,128)}, u32[]{:S(2)}) copy-start(s32[1,28]{1,0:T(1,128)} %hits_ref) | copy-start | bytes 340
  33.4 1.9 %collective-permute-start.11 = (f32[256,128]{1,0:T(8,128)S(1)}, f32[256,128]{1,0:T(8,128)S(1)}, u32[]{:S(2)}, u32[]{:S(2)}) collective-permute-start(f32[256,128]{1,0:T(8,128)S(1)} %shard_map.93.mine), channel_id=1, source_target_pairs={{0,1},{1,0},{2,3},{3,2},{4,5},{5,4},{6,7},{7,6},{8,9},{9,8},{10,11... | collective-permute-start | bytes 393224 | tf_op jit(solution)/shard_map/ppermute | solution.py:242

commit v8 on v7

--- a/solution.py
+++ b/solution.py
@@ -99,24 +99,6 @@
         cost_estimate=pl.CostEstimate(flops=flops, bytes_accessed=0, transcendentals=0),
         compiler_params=pltpu.CompilerParams(vmem_limit_bytes=VMEM_BYTES),
     )(*operands)
-
-
-def share_kernel(at_ref, blocks_ref, out_ref, done):
-    copy = pltpu.make_async_copy(blocks_ref.at[at_ref[0]], out_ref, done)
-    copy.start()
-    copy.wait()
-
-
-def take_share(blocks, at):
-    return pl.pallas_call(
-        share_kernel,
-        out_shape=jax.ShapeDtypeStruct(blocks.shape[1:], blocks.dtype),
-        in_specs=[pl.BlockSpec(memory_space=pltpu.SMEM), pl.BlockSpec(memory_space=pl.ANY)],
-        out_specs=pl.BlockSpec(memory_space=pl.ANY),
-        scratch_shapes=[pltpu.SemaphoreType.DMA],
-        cost_estimate=pl.CostEstimate(flops=0, bytes_accessed=0, transcendentals=0),
-        compiler_params=pltpu.CompilerParams(vmem_limit_bytes=VMEM_BYTES),
-    )(at.astype(jnp.int32)[None], blocks)
 
 
 def weigh_kernel(slot_ref, hits_ref, pool_ref, owner_ref, *refs):
@@ -250,7 +232,7 @@
     pool_other = across(pool_split, "rep")
     owners = jnp.stack([at_tgt, at_tgt ^ (1 + at_rep), at_tgt ^ (2 - at_rep), at_tgt ^ 3])
 
-    share = take_share(target_res, at_qry)
+    share = lax.dynamic_index_in_dim(target_res, at_qry, 0, keepdims=False)
     rest = lax.dynamic_index_in_dim(target_res, 1 - at_qry, 0, keepdims=False)
     far = from_peer(share, 2)
     near = from_peer(share, 1)
@@ -278,6 +260,8 @@
     one_blocks = [target_res[0], target_res[1], near, far]
     one = partial_similar(query, one_blocks)
     one_other = across(one, "rep")
+    one_aligned = aligned((0, 1, 2, 4), one, one_other)
+    last = after(last, one_aligned)
 
     last_rest = across(last, "qry")
     three = partial_similar(query, [last])
@@ -301,8 +285,7 @@
         pool_other,
         pool_last,
     )
-    one_aligned = aligned((0, 1, 2, 4), after(one, four), one_other)
-    five = partial_similar(after(query, weights, one_aligned), [last_rest])
+    five = partial_similar(after(query, weights), [last_rest])
     five_other = across(five, "rep")
     four_aligned = aligned((5, 3), after(four, five), four_other)
     acc = call_kernel(

time: 37.1 us -> 33.7 us (0.908)
  waiting for transfers between devices: 12.4 us -> 9.11 us
    ppermute x5, waiting for transfers between devices: 11.6 us -> 2.24 us  [from_peer(): return lax.ppermute(array, 'tgt', [(i, i ^ k) for i in range(4)])]
    ppermute x1, waiting for transfers between devices: 0.01 us -> 4.96 us  [per_device_by_target(): pool_split = lax.ppermute(target_pool, ('tgt', 'rep'), split)]
    ppermute x1, starting transfers between devices: 3.09 us -> 0.45 us  [per_device_by_target(): pool_split = lax.ppermute(target_pool, ('tgt', 'rep'), split)]
    ppermute x5, starting transfers between devices: 6.54 us -> 9.12 us  [from_peer(): return lax.ppermute(array, 'tgt', [(i, i ^ k) for i in range(4)])]
    squeeze x1, local copies, waits for them, and re-layouts: 0.04 us -> 1.26 us  [per_device_by_target(): rest = lax.dynamic_index_in_dim(target_res, 1 - at_qry, 0, keepdims=False)]
    ppermute x7, waiting for transfers between devices: 0.8 us -> 1.91 us  [across(): return lax.ppermute(array, axis, [(0, 1), (1, 0)])]
    unnamed x14 -> x10, local copies, waits for them, and re-layouts: 1 us -> 0.02 us
  transfers between devices with their start and end apart: 13 -> 13, of which waited for: 4 -> 6; matrix products, arithmetic and copies ran while one was open for 2% -> 2% of each run, Pallas kernels for 15% -> 16%
where the time goes in v8:
time: 33.7 us; the launch traced here: 33.5 us
  starting transfers between devices  13.4 us (40%)
  waiting for transfers between devices  9.11 us (27%)
  Pallas kernels  7.62 us (23%)
  local copies, waits for them, and re-layouts  1.61 us (5%)
  between operations  1.45 us (4%)
    ppermute x5, starting transfers between devices, from_peer(): return lax.ppermute(array, 'tgt', [(i, i ^ k) for i in range(4)])  9.12 us
    pallas_call x10, Pallas kernels, call_kernel(): pl.pallas_call(kernel, out_shape=out_shape, in_specs=[VMEM] * len(operand...  7.62 us
    ppermute x1, waiting for transfers between devices, per_device_by_target(): pool_split = lax.ppermute(target_pool, ('tgt', 'rep'), split)  4.96 us
    ppermute x7, starting transfers between devices, across(): return lax.ppermute(array, axis, [(0, 1), (1, 0)])  3.86 us
    ppermute x5, waiting for transfers between devices, from_peer(): return lax.ppermute(array, 'tgt', [(i, i ^ k) for i in range(4)])  2.24 us
    ppermute x7, waiting for transfers between devices, across(): return lax.ppermute(array, axis, [(0, 1), (1, 0)])  1.91 us
    squeeze x1, local copies, waits for them, and re-layouts, per_device_by_target(): rest = lax.dynamic_index_in_dim(target_res, 1 - at_qry, 0, keepdims=False)  1.26 us
  transfers between devices with their start and end apart: 13, of which 6 were waited for; matrix products, arithmetic and copies ran while one was open for 2% of the time, Pallas kernels for 16%

profile of v8, /device:TPU:0, one launch (start us, length us, event | category | flops | bytes accessed | tf_op | source)
XLA Modules:
  0.0 33.5 jit_solution(5752700477041523117)
XLA Ops:
  0.7 1.3 %dynamic-slice_bitcast_fusion = (bf16[128,640]{1,0:T(8,128)(2,1)S(1)}, bf16[128,640]{1,0:T(8,128)(2,1)S(1)}, bf16[128,640]{1,0:T(8,128)(2,1)S(1)}, bf16[128,640]{1,0:T(8,128)(2,1)S(1)}) fusion(bf16[2,128,640]{2,1,0:T(8,128)(2,1)} %param.8, s32[]{:T(128)S(6)} %select_n.13, s32[]{:T(128)S(6)} %select_n.12), kind=kLoop, calls=%fused_computation | loop fusion | bytes 1310728 | tf_op jit(solution)/shard_map/jit(dynamic_index_in_dim)/squeeze | solution.py:236
  1.9 4.1 %collective-permute-start = (bf16[128,640]{1,0:T(8,128)(2,1)S(1)}, bf16[128,640]{1,0:T(8,128)(2,1)S(1)}, u32[]{:S(2)}, u32[]{:S(2)}) collective-permute-start(bf16[128,640]{1,0:T(8,128)(2,1)S(1)} %get-tuple-element.26), channel_id=1, source_target_pairs={{0,8},{4,12},{8,0},{12,4},{1,9},{5,13},{9,1},{13,5},{2,10},{6,14},... | collective-permute-start | bytes 491528 | tf_op jit(solution)/shard_map/ppermute | solution.py:221
  6.0 1.6 %collective-permute-start.3 = (bf16[128,640]{1,0:T(8,128)(2,1)S(1)}, bf16[128,640]{1,0:T(8,128)(2,1)S(1)}, u32[]{:S(2)}, u32[]{:S(2)}) collective-permute-start(bf16[128,640]{1,0:T(8,128)(2,1)S(1)} %get-tuple-element.26), channel_id=1, source_target_pairs={{0,4},{4,0},{8,12},{12,8},{1,5},{5,1},{9,13},{13,9},{2,6},{6,2},{1... | collective-permute-start | bytes 491528 | tf_op jit(solution)/shard_map/ppermute | solution.py:221
  7.6 0.4 %collective-permute-start.1 = (f32[2,1280]{1,0:T(2,128)S(1)}, f32[2,1280]{1,0:T(2,128)S(1)}, u32[]{:S(2)}, u32[]{:S(2)}) collective-permute-start(f32[2,1280]{1,0:T(2,128)S(1)} %copy-done.1), channel_id=1, source_target_pairs={{0,4},{1,9},{4,0},{5,13},{8,12},{9,1},{12,8},{13,5},{2,6},{3,11},{... | collective-permute-start | bytes 30728 | tf_op jit(solution)/shard_map/ppermute | solution.py:230
  8.1 1.3 %collective-permute-start.2 = (f32[2,1280]{1,0:T(2,128)S(1)}, f32[2,1280]{1,0:T(2,128)S(1)}, u32[]{:S(2)}, u32[]{:S(2)}) collective-permute-start(f32[2,1280]{1,0:T(2,128)S(1)} %copy-done.1), channel_id=1, source_target_pairs={{0,12},{4,8},{8,4},{12,0},{1,13},{5,9},{9,5},{13,1},{2,14},{6,10},... | collective-permute-start | bytes 30728 | tf_op jit(solution)/shard_map/ppermute | solution.py:221
  9.4 5.0 %collective-permute-done.1.refs_1_ = f32[2,1280]{1,0:T(2,128)S(1)} collective-permute-done((f32[2,1280]{1,0:T(2,128)S(1)}, f32[2,1280]{1,0:T(2,128)S(1)}, u32[]{:S(2)}, u32[]{:S(2)}) %collective-permute-start.1) | collective-permute-done | bytes 10272 | tf_op jit(solution)/shard_map/ppermute | solution.py:230
  14.4 0.9 %collective-permute-done.2.refs_3_ = f32[2,1280]{1,0:T(2,128)S(1)} collective-permute-done((f32[2,1280]{1,0:T(2,128)S(1)}, f32[2,1280]{1,0:T(2,128)S(1)}, u32[]{:S(2)}, u32[]{:S(2)}) %collective-permute-start.2) | collective-permute-done | bytes 10272 | tf_op jit(solution)/shard_map/ppermute | solution.py:221
  15.3 0.5 %shard_map.86.mine = f32[256,512]{1,0:T(8,128)S(1)} custom-call(bf16[256,640]{1,0:T(8,128)(2,1)S(1)} %bitcast.26, bf16[128,640]{1,0:T(8,128)(2,1)S(1)} %get-tuple-element.25.refs_1_.refs_3_, bf16[128,640]{1,0:T(8,128)(2,1)S(1)} %get-tuple-element.27.refs_2_.refs_4_, bf16[128,640]{1,0:T(8,128)(2,1)S(1)} %collective-permute-done.3.refs_3_.refs_5_, ...), custom_call_target="tpu_custom_call" | custom-call | tf_op jit(solution)/shard_map/pallas_call | solution.py:93
  15.9 0.6 %collective-permute-start.4 = (bf16[128,640]{1,0:T(8,128)(2,1)S(1)}, bf16[128,640]{1,0:T(8,128)(2,1)S(1)}, u32[]{:S(2)}, u32[]{:S(2)}) collective-permute-start(bf16[128,640]{1,0:T(8,128)(2,1)S(1)} %collective-permute-done.refs_4_.refs_6_), channel_id=1, source_target_pairs={{0,4},{4,0},{8,12},{12,8},{1,5},{5,1},{9,13},{13,9},{2,6},{6,2},{1... | collective-permute-start | bytes 491528 | tf_op jit(solution)/shard_map/ppermute | solution.py:221
  16.6 1.5 %collective-permute-start.7 = (bf16[128,640]{1,0:T(8,128)(2,1)S(1)}, bf16[128,640]{1,0:T(8,128)(2,1)S(1)}, u32[]{:S(2)}, u32[]{:S(2)}) collective-permute-start(bf16[128,640]{1,0:T(8,128)(2,1)S(1)} %collective-permute-done.refs_4_.refs_6_), channel_id=1, source_target_pairs={{0,2},{2,0},{1,3},{3,1},{4,6},{6,4},{5,7},{7,5},{8,10},{10,8},{9,1... | collective-permute-start | bytes 491528 | tf_op jit(solution)/shard_map/ppermute | solution.py:224
  18.1 1.5 %collective-permute-start.8 = (bf16[128,640]{1,0:T(8,128)(2,1)S(1)}, bf16[128,640]{1,0:T(8,128)(2,1)S(1)}, u32[]{:S(2)}, u32[]{:S(2)}) collective-permute-start(bf16[128,640]{1,0:T(8,128)(2,1)S(1)} %get-tuple-element.18), channel_id=1, source_target_pairs={{0,4},{4,0},{8,12},{12,8},{1,5},{5,1},{9,13},{13,9},{2,6},{6,2},{1... | collective-permute-start | bytes 491528 | tf_op jit(solution)/shard_map/ppermute | solution.py:221
  20.5 1.7 %shard_map.87.refs_0_ = bf16[256,512]{1,0:T(8,128)(2,1)S(1)} custom-call(f32[8,128]{1,0:T(8,128)S(1)} %broadcast_in_dim.36.len_ref, f32[1,128]{1,0:T(1,128)S(1)} %broadcast_in_dim.37.sharp_ref, f32[256,512]{1,0:T(8,128)S(1)} %shard_map.86.mine, f32[256,512]{1,0:T(8,128)S(1)} %collective-permute-done.5.other), custom_call_target="tpu_custom_call" | custom-call | tf_op jit(solution)/shard_map/pallas_call | solution.py:93
  22.3 0.7 %collective-permute-done.4.refs_1_.refs_7_ = bf16[128,640]{1,0:T(8,128)(2,1)S(1)} collective-permute-done((bf16[128,640]{1,0:T(8,128)(2,1)S(1)}, bf16[128,640]{1,0:T(8,128)(2,1)S(1)}, u32[]{:S(2)}, u32[]{:S(2)}) %collective-permute-start.4) | collective-permute-done | bytes 163872 | tf_op jit(solution)/shard_map/ppermute | solution.py:221
  23.3 1.6 %collective-permute-start.10 = (bf16[128,640]{1,0:T(8,128)(2,1)S(1)}, bf16[128,640]{1,0:T(8,128)(2,1)S(1)}, u32[]{:S(2)}, u32[]{:S(2)}) collective-permute-start(bf16[128,640]{1,0:T(8,128)(2,1)S(1)} %collective-permute-done.4.refs_1_.refs_7_), channel_id=1, source_target_pairs={{0,2},{2,0},{1,3},{3,1},{4,6},{6,4},{5,7},{7,5},{8,10},{10,8},{9,1... | collective-permute-start | bytes 491528 | tf_op jit(solution)/shard_map/ppermute | solution.py:224
  24.8 0.5 %shard_map.89.refs_1_ = bf16[256,128]{1,0:T(8,128)(2,1)S(1)} custom-call(f32[8,128]{1,0:T(8,128)S(1)} %broadcast_in_dim.36.len_ref, f32[1,128]{1,0:T(1,128)S(1)} %broadcast_in_dim.37.sharp_ref, f32[256,128]{1,0:T(8,128)S(1)} %shard_map.88.mine, f32[256,128]{1,0:T(8,128)S(1)} %collective-permute-done.6.other), custom_call_target="tpu_custom_call" | custom-call | tf_op jit(solution)/shard_map/pallas_call | solution.py:93
  25.4 0.6 %collective-permute-done.8.refs_2_.refs_9_ = bf16[128,640]{1,0:T(8,128)(2,1)S(1)} collective-permute-done((bf16[128,640]{1,0:T(8,128)(2,1)S(1)}, bf16[128,640]{1,0:T(8,128)(2,1)S(1)}, u32[]{:S(2)}, u32[]{:S(2)}) %collective-permute-start.8) | collective-permute-done | bytes 163872 | tf_op jit(solution)/shard_map/ppermute | solution.py:221
  26.0 0.3 shard_map.90.mine
  26.4 0.5 %collective-permute-start.9 = (f32[2,1280]{1,0:T(2,128)S(1)}, f32[2,1280]{1,0:T(2,128)S(1)}, u32[]{:S(2)}, u32[]{:S(2)}) collective-permute-start(f32[2,1280]{1,0:T(2,128)S(1)} %collective-permute-done.1.refs_1_), channel_id=1, source_target_pairs={{0,1},{1,0},{2,3},{3,2},{4,5},{5,4},{6,7},{7,6},{8,9},{9,8},{10,11... | collective-permute-start | bytes 30728 | tf_op jit(solution)/shard_map/ppermute | solution.py:224
  27.2 0.8 %collective-permute-done.9.refs_2_ = f32[2,1280]{1,0:T(2,128)S(1)} collective-permute-done((f32[2,1280]{1,0:T(2,128)S(1)}, f32[2,1280]{1,0:T(2,128)S(1)}, u32[]{:S(2)}, u32[]{:S(2)}) %collective-permute-start.9) | collective-permute-done | bytes 10272 | tf_op jit(solution)/shard_map/ppermute | solution.py:224
  28.0 0.8 %shard_map.91 = (f32[1,8]{1,0:T(1,128)}, f32[8,128]{1,0:T(8,128)S(1)}) custom-call(s32[8,1]{1,0:T(8,128)S(1)} %copy.11.slot_ref, s32[1,28]{1,0:T(1,128)S(1)} %copy-done.3, f32[1,1280]{1,0:T(1,128)S(1)} %copy-done.2, s32[4,1]{1,0:T(4,128)S(1)} %copy.12.owner_ref, f32[2,1280]{1,0:T(2,128)S(1)} %copy-done.1, f32[2,1280]{1,0:T(2,128)S(1)} %collective-permute-done.1.refs_1_, ...), custom_call_target="tpu_custom_call" | custom-call | tf_op jit(solution)/shard_map/pallas_call | solution.py:93
  28.8 1.1 %collective-permute-done.10.refs_1_.block = bf16[128,640]{1,0:T(8,128)(2,1)S(1)} collective-permute-done((bf16[128,640]{1,0:T(8,128)(2,1)S(1)}, bf16[128,640]{1,0:T(8,128)(2,1)S(1)}, u32[]{:S(2)}, u32[]{:S(2)}) %collective-permute-start.10) | collective-permute-done | bytes 163872 | tf_op jit(solution)/shard_map/ppermute | solution.py:224
  30.2 0.8 %shard_map.93.refs_2_ = bf16[256,256]{1,0:T(8,128)(2,1)S(1)} custom-call(f32[8,128]{1,0:T(8,128)S(1)} %broadcast_in_dim.36.len_ref, f32[1,128]{1,0:T(1,128)S(1)} %broadcast_in_dim.37.sharp_ref, f32[256,256]{1,0:T(8,128)S(1)} %shard_map.90.mine, f32[256,256]{1,0:T(8,128)S(1)} %collective-permute-done.12.other), custom_call_target="tpu_custom_call" | custom-call | tf_op jit(solution)/shard_map/pallas_call | solution.py:93
  31.0 0.8 %shard_map.94.acc = f32[256,640]{1,0:T(8,128)S(1)} custom-call(f32[8,128]{1,0:T(8,128)S(1)} %get-tuple-element.20.weight_ref, bf16[256,512]{1,0:T(8,128)(2,1)S(1)} %shard_map.87.refs_0_, bf16[256,128]{1,0:T(8,128)(2,1)S(1)} %shard_map.89.refs_1_, bf16[256,256]{1,0:T(8,128)(2,1)S(1)} %shard_map.93.refs_2_, ...), custom_call_target="tpu_custom_call" | custom-call | tf_op jit(solution)/shard_map/pallas_call | solution.py:93
  31.8 1.6 %shard_map.95 = bf16[256,640]{1,0:T(8,128)(2,1)} custom-call(f32[8,128]{1,0:T(8,128)S(1)} %broadcast_in_dim.36.len_ref, f32[1,128]{1,0:T(1,128)S(1)} %broadcast_in_dim.37.sharp_ref, f32[8,128]{1,0:T(8,128)S(1)} %get-tuple-element.20.weight_ref, f32[256,128]{1,0:T(8,128)S(1)} %shard_map.92.mine, f32[256,128]{1,0:T(8,128)S(1)} %collective-permute-done.11.other, ...), custom_call_target="tpu_custom_call" | custom-call | tf_op jit(solution)/shard_map/pallas_call | solution.py:93
  (31 shorter events, 1.4 us)
Async XLA Ops:
  0.6 7.0 %copy-start.1 = (f32[2,1280]{1,0:T(2,128)S(1)}, f32[2,1280]{1,0:T(2,128)}, u32[]{:S(2)}) copy-start(f32[2,1280]{1,0:T(2,128)} %refs_0_.1) | copy-start | bytes 30724
  0.6 14.6 %copy-start = (bf16[1,256,640]{2,1,0:T(8,128)(2,1)S(1)}, bf16[1,256,640]{2,1,0:T(8,128)(2,1)}, u32[]{:S(2)}) copy-start(bf16[1,256,640]{2,1,0:T(8,128)(2,1)} %param.7) | copy-start | bytes 983044
  1.9 13.4 %collective-permute-start = (bf16[128,640]{1,0:T(8,128)(2,1)S(1)}, bf16[128,640]{1,0:T(8,128)(2,1)S(1)}, u32[]{:S(2)}, u32[]{:S(2)}) collective-permute-start(bf16[128,640]{1,0:T(8,128)(2,1)S(1)} %get-tuple-element.26), channel_id=1, source_target_pairs={{0,8},{4,12},{8,0},{12,4},{1,9},{5,13},{9,1},{13,5},{2,10},{6,14},... | collective-permute-start | bytes 491528 | tf_op jit(solution)/shard_map/ppermute | solution.py:221
  6.0 9.3 %collective-permute-start.3 = (bf16[128,640]{1,0:T(8,128)(2,1)S(1)}, bf16[128,640]{1,0:T(8,128)(2,1)S(1)}, u32[]{:S(2)}, u32[]{:S(2)}) collective-permute-start(bf16[128,640]{1,0:T(8,128)(2,1)S(1)} %get-tuple-element.26), channel_id=1, source_target_pairs={{0,4},{4,0},{8,12},{12,8},{1,5},{5,1},{9,13},{13,9},{2,6},{6,2},{1... | collective-permute-start | bytes 491528 | tf_op jit(solution)/shard_map/ppermute | solution.py:221
  7.6 6.8 %collective-permute-start.1 = (f32[2,1280]{1,0:T(2,128)S(1)}, f32[2,1280]{1,0:T(2,128)S(1)}, u32[]{:S(2)}, u32[]{:S(2)}) collective-permute-start(f32[2,1280]{1,0:T(2,128)S(1)} %copy-done.1), channel_id=1, source_target_pairs={{0,4},{1,9},{4,0},{5,13},{8,12},{9,1},{12,8},{13,5},{2,6},{3,11},{... | collective-permute-start | bytes 30728 | tf_op jit(solution)/shard_map/ppermute | solution.py:230
  8.1 7.2 %collective-permute-start.2 = (f32[2,1280]{1,0:T(2,128)S(1)}, f32[2,1280]{1,0:T(2,128)S(1)}, u32[]{:S(2)}, u32[]{:S(2)}) collective-permute-start(f32[2,1280]{1,0:T(2,128)S(1)} %copy-done.1), channel_id=1, source_target_pairs={{0,12},{4,8},{8,4},{12,0},{1,13},{5,9},{9,5},{13,1},{2,14},{6,10},... | collective-permute-start | bytes 30728 | tf_op jit(solution)/shard_map/ppermute | solution.py:221
  15.8 4.6 %collective-permute-start.5 = (f32[256,512]{1,0:T(8,128)S(1)}, f32[256,512]{1,0:T(8,128)S(1)}, u32[]{:S(2)}, u32[]{:S(2)}) collective-permute-start(f32[256,512]{1,0:T(8,128)S(1)} %shard_map.86.mine), channel_id=1, source_target_pairs={{0,1},{1,0},{2,3},{3,2},{4,5},{5,4},{6,7},{7,6},{8,9},{9,8},{10,11... | collective-permute-start | bytes 1572872 | tf_op jit(solution)/shard_map/ppermute | solution.py:224
  15.9 7.1 %collective-permute-start.4 = (bf16[128,640]{1,0:T(8,128)(2,1)S(1)}, bf16[128,640]{1,0:T(8,128)(2,1)S(1)}, u32[]{:S(2)}, u32[]{:S(2)}) collective-permute-start(bf16[128,640]{1,0:T(8,128)(2,1)S(1)} %collective-permute-done.refs_4_.refs_6_), channel_id=1, source_target_pairs={{0,4},{4,0},{8,12},{12,8},{1,5},{5,1},{9,13},{13,9},{2,6},{6,2},{1... | collective-permute-start | bytes 491528 | tf_op jit(solution)/shard_map/ppermute | solution.py:221
  16.6 3.0 %copy-start.4 = (s32[8]{0:T(128)S(1)}, s32[8]{0:T(128)}, u32[]{:S(2)}) copy-start(s32[8]{0:T(128)} %param.9) | copy-start | bytes 100
  16.6 9.4 %collective-permute-start.7 = (bf16[128,640]{1,0:T(8,128)(2,1)S(1)}, bf16[128,640]{1,0:T(8,128)(2,1)S(1)}, u32[]{:S(2)}, u32[]{:S(2)}) collective-permute-start(bf16[128,640]{1,0:T(8,128)(2,1)S(1)} %collective-permute-done.refs_4_.refs_6_), channel_id=1, source_target_pairs={{0,2},{2,0},{1,3},{3,1},{4,6},{6,4},{5,7},{7,5},{8,10},{10,8},{9,1... | collective-permute-start | bytes 491528 | tf_op jit(solution)/shard_map/ppermute | solution.py:224
  18.1 7.9 %collective-permute-start.8 = (bf16[128,640]{1,0:T(8,128)(2,1)S(1)}, bf16[128,640]{1,0:T(8,128)(2,1)S(1)}, u32[]{:S(2)}, u32[]{:S(2)}) collective-permute-start(bf16[128,640]{1,0:T(8,128)(2,1)S(1)} %get-tuple-element.18), channel_id=1, source_target_pairs={{0,4},{4,0},{8,12},{12,8},{1,5},{5,1},{9,13},{13,9},{2,6},{6,2},{1... | collective-permute-start | bytes 491528 | tf_op jit(solution)/shard_map/ppermute | solution.py:221
  23.2 1.6 %collective-permute-start.6 = (f32[256,128]{1,0:T(8,128)S(1)}, f32[256,128]{1,0:T(8,128)S(1)}, u32[]{:S(2)}, u32[]{:S(2)}) collective-permute-start(f32[256,128]{1,0:T(8,128)S(1)} %shard_map.88.mine), channel_id=1, source_target_pairs={{0,1},{1,0},{2,3},{3,2},{4,5},{5,4},{6,7},{7,6},{8,9},{9,8},{10,11... | collective-permute-start | bytes 393224 | tf_op jit(solution)/shard_map/ppermute | solution.py:224
  23.3 6.6 %collective-permute-start.10 = (bf16[128,640]{1,0:T(8,128)(2,1)S(1)}, bf16[128,640]{1,0:T(8,128)(2,1)S(1)}, u32[]{:S(2)}, u32[]{:S(2)}) collective-permute-start(bf16[128,640]{1,0:T(8,128)(2,1)S(1)} %collective-permute-done.4.refs_1_.refs_7_), channel_id=1, source_target_pairs={{0,2},{2,0},{1,3},{3,1},{4,6},{6,4},{5,7},{7,5},{8,10},{10,8},{9,1... | collective-permute-start | bytes 491528 | tf_op jit(solution)/shard_map/ppermute | solution.py:224
  26.3 3.9 %collective-permute-start.12 = (f32[256,256]{1,0:T(8,128)S(1)}, f32[256,256]{1,0:T(8,128)S(1)}, u32[]{:S(2)}, u32[]{:S(2)}) collective-permute-start(f32[256,256]{1,0:T(8,128)S(1)} %shard_map.90.mine), channel_id=1, source_target_pairs={{0,1},{1,0},{2,3},{3,2},{4,5},{5,4},{6,7},{7,6},{8,9},{9,8},{10,11... | collective-permute-start | bytes 786440 | tf_op jit(solution)/shard_map/ppermute | solution.py:224
  26.4 1.5 %collective-permute-start.9 = (f32[2,1280]{1,0:T(2,128)S(1)}, f32[2,1280]{1,0:T(2,128)S(1)}, u32[]{:S(2)}, u32[]{:S(2)}) collective-permute-start(f32[2,1280]{1,0:T(2,128)S(1)} %collective-permute-done.1.refs_1_), channel_id=1, source_target_pairs={{0,1},{1,0},{2,3},{3,2},{4,5},{5,4},{6,7},{7,6},{8,9},{9,8},{10,11... | collective-permute-start | bytes 30728 | tf_op jit(solution)/shard_map/ppermute | solution.py:224
  27.0 1.0 %copy-start.2 = (f32[1,1280]{1,0:T(1,128)S(1)}, f32[1,1280]{1,0:T(1,128)}, u32[]{:S(2)}) copy-start(f32[1,1280]{1,0:T(1,128)} %pool_ref.1) | copy-start | bytes 15364
  27.1 0.9 %copy-start.3 = (s32[1,28]{1,0:T(1,128)S(1)}, s32[1,28]{1,0:T(1,128)}, u32[]{:S(2)}) copy-start(s32[1,28]{1,0:T(1,128)} %hits_ref) | copy-start | bytes 340
  30.1 1.7 %collective-permute-start.11 = (f32[256,128]{1,0:T(8,128)S(1)}, f32[256,128]{1,0:T(8,128)S(1)}, u32[]{:S(2)}, u32[]{:S(2)}) collective-permute-start(f32[256,128]{1,0:T(8,128)S(1)} %shard_map.92.mine), channel_id=1, source_target_pairs={{0,1},{1,0},{2,3},{3,2},{4,5},{5,4},{6,7},{7,6},{8,9},{9,8},{10,11... | collective-permute-start | bytes 393224 | tf_op jit(solution)/shard_map/ppermute | solution.py:224

commit v9 on v6

--- a/solution.py
+++ b/solution.py
@@ -126,22 +126,6 @@
     weight_ref[...] = jnp.broadcast_to(weights, weight_ref.shape)
 
 
-def partial_kernel(*refs):
-    query, blocks, out = refs[0], refs[1:-1], refs[-1]
-    rows = 0
-    for block in blocks:
-        out[:, rows : rows + block.shape[0]] = lax.dot_general(
-            query[...], block[...], (((1,), (1,)), ((), ())), preferred_element_type=jnp.float32
-        )
-        rows += block.shape[0]
-
-
-def partial_similar(query, blocks):
-    rows = sum(block.shape[0] for block in blocks)
-    shape = jax.ShapeDtypeStruct((query.shape[0], rows), jnp.float32)
-    return call_kernel(partial_kernel, shape, query, *blocks)
-
-
 def align_block(similar, length, half_sharp):
     column = lax.broadcasted_iota(jnp.int32, (1, similar.shape[1]), 1).astype(jnp.float32)
     inside = column < length
@@ -162,58 +146,68 @@
     return raised / jnp.sum(raised, axis=1, keepdims=True)
 
 
-def align_kernel(model_width, slots, len_ref, sharp_ref, mine, other, out_ref):
-    scale = 1.0 / math.sqrt(model_width)
-    rows = mine.shape[1] // len(slots)
-    for at, slot in enumerate(slots):
-        part = pl.ds(at * rows, rows)
-        similar = (mine[:, part] + other[:, part]) * scale
+def similar_block(query, query_other, mine, other, model_width):
+    total = 0.0
+    for rows, blocks in ((query, mine), (query_other, other)):
+        target = jnp.concatenate([block[...] for block in blocks])
+        total += lax.dot_general(
+            rows[...], target, (((1,), (1,)), ((), ())), preferred_element_type=jnp.float32
+        )
+    return total * (1.0 / math.sqrt(model_width))
+
+
+def take_blocks(refs, count):
+    return refs[:count], refs[count : 2 * count], refs[2 * count :]
+
+
+def align_kernel(model_width, targets, len_ref, sharp_ref, query, query_other, *refs):
+    out_ref = refs[-1]
+    rows = out_ref.shape[1] // len(targets)
+    for at, (slot, count) in enumerate(targets):
+        mine, other, refs = take_blocks(refs, count)
+        similar = similar_block(query, query_other, mine, other, model_width)
         alignment = align_block(similar, len_ref[slot : slot + 1, :rows], sharp_ref[:, 0:1])
-        out_ref[:, part] = alignment.astype(out_ref.dtype)
-
-
-def align(model_width, slots, lengths, half_sharp, mine, other):
-    return call_kernel(
-        functools.partial(align_kernel, model_width, slots),
-        jax.ShapeDtypeStruct(mine.shape, jnp.bfloat16),
-        lengths,
-        half_sharp,
-        mine,
-        other,
-    )
+        out_ref[:, at * rows : (at + 1) * rows] = alignment.astype(out_ref.dtype)
+
+
+def weighted_term(weight, alignment, blocks):
+    target = jnp.concatenate([block[...] for block in blocks])
+    return weight * jnp.dot(alignment, target, preferred_element_type=jnp.float32)
 
 
 def profile_kernel(groups, weight_ref, *refs):
     aligned, blocks, out_ref = refs[: len(groups)], refs[len(groups) : -1], refs[-1]
-    rows = blocks[0].shape[0]
-    acc, at = None, 0
-    for group, slots in zip(aligned, groups):
-        for i, slot in enumerate(slots):
-            term = weight_ref[slot : slot + 1, 0:1] * jnp.dot(
-                group[:, i * rows : (i + 1) * rows],
-                blocks[at][...],
-                preferred_element_type=jnp.float32,
+    acc = None
+    for group, targets in zip(aligned, groups):
+        rows = group.shape[1] // len(targets)
+        for at, (slot, count) in enumerate(targets):
+            term = weighted_term(
+                weight_ref[slot : slot + 1, 0:1],
+                group[:, at * rows : (at + 1) * rows],
+                blocks[:count],
             )
             acc = term if acc is None else acc + term
-            at += 1
+            blocks = blocks[count:]
     out_ref[...] = acc
 
 
-def last_kernel(model_width, slot, len_ref, sharp_ref, weight_ref, mine, other, block, acc, out_ref):
-    rows = block.shape[0]
-    similar = (mine[...] + other[...]) * (1.0 / math.sqrt(model_width))
-    alignment = align_block(similar, len_ref[slot : slot + 1, :rows], sharp_ref[:, 0:1])
-    term = weight_ref[slot : slot + 1, 0:1] * jnp.dot(
-        alignment.astype(jnp.bfloat16), block[...], preferred_element_type=jnp.float32
-    )
-    out_ref[...] = (acc[...] + term).astype(out_ref.dtype)
+def last_kernel(model_width, target, len_ref, sharp_ref, query, query_other, weight_ref, *refs):
+    slot, count = target
+    mine, other, (acc_ref, out_ref) = take_blocks(refs, count)
+    similar = similar_block(query, query_other, mine, other, model_width)
+    lengths = len_ref[slot : slot + 1, : similar.shape[1]]
+    alignment = align_block(similar, lengths, sharp_ref[:, 0:1])
+    term = weighted_term(
+        weight_ref[slot : slot + 1, 0:1], alignment.astype(jnp.bfloat16), mine
+    )
+    out_ref[...] = (acc_ref[...] + term).astype(out_ref.dtype)
 
 
 def per_device_by_target(
     query_res, target_res, target_len, hits, sharpness, query_pool, target_pool
 ):
     model_width = query_pool.shape[1]
-    target_rows = target_res.shape[1]
+    target_rows, width = target_res.shape[1:]
     query = query_res[0]
     at_tgt, at_qry, at_rep = (lax.axis_index(name) for name in ("tgt", "qry", "rep"))
 
@@ -227,15 +221,17 @@
         return lax.optimization_barrier((array, *done))[0]
 
     split = [(2 * i + c, 2 * (i ^ (1 + c)) + c) for i in range(4) for c in range(2)]
-    pool_split = lax.ppermute(target_pool, ("tgt", "rep"), split)
-    pool_last = from_peer(target_pool, 3)
-    pool_other = across(pool_split, "rep")
     owners = jnp.stack([at_tgt, at_tgt ^ (1 + at_rep), at_tgt ^ (2 - at_rep), at_tgt ^ 3])
 
     share = lax.dynamic_index_in_dim(target_res, at_qry, 0, keepdims=False)
     rest = lax.dynamic_index_in_dim(target_res, 1 - at_qry, 0, keepdims=False)
     far = from_peer(share, 2)
     near = from_peer(share, 1)
+    query_other = across(after(query, share), "rep")
+    own_other = across(after(target_res, share), "rep")
+    pool = after(target_pool, query_other, own_other)
+    pool_split = lax.ppermute(pool, ("tgt", "rep"), split)
+    pool_last = from_peer(pool, 3)
 
     bases = [2 * (at_tgt ^ k) for k in range(4)]
     slots = [bases[0], bases[0] + 1]
@@ -247,16 +243,30 @@
     lengths = jnp.broadcast_to(lengths.astype(jnp.float32), (len(target_len), target_rows))
     half_sharp = jnp.broadcast_to(0.5 * sharpness, (1, target_rows))
 
-    def aligned(slots, mine, other):
-        return align(model_width, slots, lengths, half_sharp, mine, other)
+    def aligned(slots, blocks, *done):
+        return call_kernel(
+            functools.partial(align_kernel, model_width, [(slot, 1) for slot in slots]),
+            jax.ShapeDtypeStruct((query.shape[0], len(slots) * target_rows), jnp.bfloat16),
+            lengths,
+            half_sharp,
+            after(query, *done) if done else query,
+            query_other,
+            *blocks,
+        )
 
     far = after(far, pool_split, pool_last)
     near = after(near, far)
-    far = after(far, near)
     last = from_peer(far, 1)
-    far_rest = across(far, "qry")
     near_rest = from_peer(after(rest, far), 1)
-
+    near_other = across(near, "rep")
+    far_other = across(far, "rep")
+    far_rest = across(after(far, near_other), "qry")
+
+    one = [target_res[0], own_other[0], target_res[1], own_other[1]]
+    one += [near, near_other, far, far_other]
+    one_aligned = aligned((0, 1, 2, 4), one)
+
+    pool_other = across(after(pool_split, near_other, far_other), "rep")
     posterior, weights = call_kernel(
         weigh_kernel,
         (
@@ -264,7 +274,7 @@
             jax.ShapeDtypeStruct((len(target_len), target_rows), jnp.float32),
         ),
         slots,
-        hits,
+        after(hits, one_aligned),
         query_pool,
         owners.astype(jnp.int32)[:, None],
         target_pool,
@@ -273,46 +283,41 @@
         pool_last,
     )
 
-    one_blocks = [target_res[0], target_res[1], near, far]
-    one = partial_similar(query, one_blocks)
-    one_other = across(one, "rep")
-    one_aligned = aligned((0, 1, 2, 4), one, one_other)
-
-    last = after(last, weights, one_aligned)
+    last = after(last, weights)
     last_rest = across(last, "qry")
-    three = partial_similar(query, [last])
-    three_other = across(three, "rep")
-    three_aligned = aligned((6,), three, three_other)
-    four_blocks = [far_rest, near_rest]
-    four = partial_similar(after(query, three_aligned), four_blocks)
-    four_other = across(four, "rep")
-    five = partial_similar(after(query, four), [last_rest])
-    five_other = across(five, "rep")
-    four_aligned = aligned((5, 3), after(four, five), four_other)
+    two = [last, across(last, "rep")]
+    two_aligned = aligned((6,), two)
+    last_rest = after(last_rest, two_aligned)
+    last_rest_other = across(last_rest, "rep")
+    three = [far_rest, across(far_rest, "rep"), near_rest, across(near_rest, "rep")]
+    three_aligned = aligned((5, 3), three, last_rest)
     acc = call_kernel(
-        functools.partial(profile_kernel, ((0, 1, 2, 4), (6,), (5, 3))),
+        functools.partial(
+            profile_kernel,
+            (((0, 1), (1, 1), (2, 1), (4, 1)), ((6, 1),), ((5, 1), (3, 1))),
+        ),
         jax.ShapeDtypeStruct(query.shape, jnp.float32),
         weights,
         one_aligned,
+        two_aligned,
         three_aligned,
-        four_aligned,
-        *one_blocks,
-        last,
-        *four_blocks,
+        *one[::2],
+        *two[::2],
+        *three[::2],
     )
     profile = call_kernel(
-        functools.partial(last_kernel, model_width, 7),
+        functools.partial(last_kernel, model_width, (7, 1)),
         jax.ShapeDtypeStruct(query.shape, jnp.bfloat16),
         lengths,
         half_sharp,
+        query,
+        query_other,
         weights,
-        five,
-        five_other,
         last_rest,
+        last_rest_other,
         acc,
     )
     return (profile[None], posterior)
-
 
 def solution(mesh):
     placed = (

time: 35 us -> 35.4 us (1.011)
  starting transfers between devices: 12.3 us -> 14.2 us
  local copies, waits for them, and re-layouts: 2.26 us -> 1.66 us
  waiting for transfers between devices: 10.8 us -> 10.4 us
  Pallas kernels: 7.64 us -> 7.28 us
    ppermute x5, waiting for transfers between devices: 0.93 us -> 7.38 us  [from_peer(): return lax.ppermute(array, 'tgt', [(i, i ^ k) for i in range(4)])]
    ppermute x1, waiting for transfers between devices: 4.96 us -> 0.26 us  [per_device_by_target(): pool_split = lax.ppermute(pool, ('tgt', 'rep'), split)]
    ppermute x7 -> x11, waiting for transfers between devices: 4.93 us -> 2.75 us  [across(): return lax.ppermute(array, axis, [(0, 1), (1, 0)])]
    ppermute x7 -> x11, starting transfers between devices: 3.04 us -> 4.61 us  [across(): return lax.ppermute(array, axis, [(0, 1), (1, 0)])]
    unnamed x10 -> x12, local copies, waits for them, and re-layouts: 0.67 us -> 0.02 us
    pallas_call x10 -> x6, Pallas kernels: 7.64 us -> 7.28 us  [call_kernel(): pl.pallas_call(kernel, out_shape=out_shape, in_specs=[VMEM] * len(operand...]
  transfers between devices with their start and end apart: 13 -> 17, of which waited for: 4 -> 6; matrix products, arithmetic and copies ran while one was open for 2% -> 2% of each run, Pallas kernels for 16% -> 16%
where the time goes in v9:
time: 35.4 us; the launch traced here: 35.2 us
  starting transfers between devices  14.2 us (40%)
  waiting for transfers between devices  10.4 us (29%)
  Pallas kernels  7.28 us (21%)
  local copies, waits for them, and re-layouts  1.66 us (5%)
  between operations  1.43 us (4%)
    ppermute x5, starting transfers between devices, from_peer(): return lax.ppermute(array, 'tgt', [(i, i ^ k) for i in range(4)])  9.03 us
    ppermute x5, waiting for transfers between devices, from_peer(): return lax.ppermute(array, 'tgt', [(i, i ^ k) for i in range(4)])  7.38 us
    pallas_call x6, Pallas kernels, call_kernel(): pl.pallas_call(kernel, out_shape=out_shape, in_specs=[VMEM] * len(operand...  7.28 us
    ppermute x11, starting transfers between devices, across(): return lax.ppermute(array, axis, [(0, 1), (1, 0)])  4.61 us
    ppermute x11, waiting for transfers between devices, across(): return lax.ppermute(array, axis, [(0, 1), (1, 0)])  2.75 us
    squeeze x1, local copies, waits for them, and re-layouts, per_device_by_target(): rest = lax.dynamic_index_in_dim(target_res, 1 - at_qry, 0, keepdims=False)  1.28 us
  transfers between devices with their start and end apart: 17, of which 6 were waited for; matrix products, arithmetic and copies ran while one was open for 2% of the time, Pallas kernels for 16%

profile of v9, /device:TPU:0, one launch (start us, length us, event | category | flops | bytes accessed | tf_op | source)
XLA Modules:
  0.0 35.2 jit_solution(16774584575551987426)
XLA Ops:
  0.7 1.3 %dynamic-slice_bitcast_fusion = (bf16[128,640]{1,0:T(8,128)(2,1)S(1)}, bf16[128,640]{1,0:T(8,128)(2,1)S(1)}, bf16[128,640]{1,0:T(8,128)(2,1)S(1)}, bf16[128,640]{1,0:T(8,128)(2,1)S(1)}) fusion(bf16[2,128,640]{2,1,0:T(8,128)(2,1)} %param.8, s32[]{:T(128)S(6)} %select_n.13, s32[]{:T(128)S(6)} %select_n.12), kind=kLoop, calls=%fused_computation.2 | loop fusion | bytes 1310728 | tf_op jit(solution)/shard_map/jit(dynamic_index_in_dim)/squeeze | solution.py:227
  2.0 0.5 %collective-permute-start = (bf16[256,640]{1,0:T(8,128)(2,1)S(1)}, bf16[256,640]{1,0:T(8,128)(2,1)S(1)}, u32[]{:S(2)}, u32[]{:S(2)}) collective-permute-start(bf16[256,640]{1,0:T(8,128)(2,1)S(1)} %bitcast.30), channel_id=1, source_target_pairs={{0,1},{1,0},{2,3},{3,2},{4,5},{5,4},{6,7},{7,6},{8,9},{9,8},{10,11... | collective-permute-start | bytes 983048 | tf_op jit(solution)/shard_map/ppermute | solution.py:218
  2.6 4.0 %collective-permute-start.3 = (bf16[128,640]{1,0:T(8,128)(2,1)S(1)}, bf16[128,640]{1,0:T(8,128)(2,1)S(1)}, u32[]{:S(2)}, u32[]{:S(2)}) collective-permute-start(bf16[128,640]{1,0:T(8,128)(2,1)S(1)} %get-tuple-element.32), channel_id=1, source_target_pairs={{0,8},{4,12},{8,0},{12,4},{1,9},{5,13},{9,1},{13,5},{2,10},{6,14},... | collective-permute-start | bytes 491528 | tf_op jit(solution)/shard_map/ppermute | solution.py:215
  6.6 1.6 %collective-permute-start.2 = (bf16[128,640]{1,0:T(8,128)(2,1)S(1)}, bf16[128,640]{1,0:T(8,128)(2,1)S(1)}, u32[]{:S(2)}, u32[]{:S(2)}) collective-permute-start(bf16[128,640]{1,0:T(8,128)(2,1)S(1)} %get-tuple-element.32), channel_id=1, source_target_pairs={{0,4},{4,0},{8,12},{12,8},{1,5},{5,1},{9,13},{13,9},{2,6},{6,2},{1... | collective-permute-start | bytes 491528 | tf_op jit(solution)/shard_map/ppermute | solution.py:215
  8.2 0.5 %collective-permute-start.4 = (f32[2,1280]{1,0:T(2,128)S(1)}, f32[2,1280]{1,0:T(2,128)S(1)}, u32[]{:S(2)}, u32[]{:S(2)}) collective-permute-start(f32[2,1280]{1,0:T(2,128)S(1)} %copy-done.1), channel_id=1, source_target_pairs={{0,4},{1,9},{4,0},{5,13},{8,12},{9,1},{12,8},{13,5},{2,6},{3,11},{... | collective-permute-start | bytes 30728 | tf_op jit(solution)/shard_map/ppermute | solution.py:233
  8.7 1.3 %collective-permute-start.5 = (f32[2,1280]{1,0:T(2,128)S(1)}, f32[2,1280]{1,0:T(2,128)S(1)}, u32[]{:S(2)}, u32[]{:S(2)}) collective-permute-start(f32[2,1280]{1,0:T(2,128)S(1)} %copy-done.1), channel_id=1, source_target_pairs={{0,12},{4,8},{8,4},{12,0},{1,13},{5,9},{9,5},{13,1},{2,14},{6,10},... | collective-permute-start | bytes 30728 | tf_op jit(solution)/shard_map/ppermute | solution.py:215
  10.1 4.7 %collective-permute-done.3.refs_6_ = bf16[128,640]{1,0:T(8,128)(2,1)S(1)} collective-permute-done((bf16[128,640]{1,0:T(8,128)(2,1)S(1)}, bf16[128,640]{1,0:T(8,128)(2,1)S(1)}, u32[]{:S(2)}, u32[]{:S(2)}) %collective-permute-start.3) | collective-permute-done | bytes 163872 | tf_op jit(solution)/shard_map/ppermute | solution.py:215
  14.8 0.3 collective-permute-done.4.refs_1_
  15.1 1.0 %collective-permute-done.5.refs_3_ = f32[2,1280]{1,0:T(2,128)S(1)} collective-permute-done((f32[2,1280]{1,0:T(2,128)S(1)}, f32[2,1280]{1,0:T(2,128)S(1)}, u32[]{:S(2)}, u32[]{:S(2)}) %collective-permute-start.5) | collective-permute-done | bytes 10272 | tf_op jit(solution)/shard_map/ppermute | solution.py:215
  16.1 0.5 %collective-permute-start.6 = (bf16[128,640]{1,0:T(8,128)(2,1)S(1)}, bf16[128,640]{1,0:T(8,128)(2,1)S(1)}, u32[]{:S(2)}, u32[]{:S(2)}) collective-permute-start(bf16[128,640]{1,0:T(8,128)(2,1)S(1)} %collective-permute-done.2.refs_4_.refs_5_), channel_id=1, source_target_pairs={{0,1},{1,0},{2,3},{3,2},{4,5},{5,4},{6,7},{7,6},{8,9},{9,8},{10,11... | collective-permute-start | bytes 491528 | tf_op jit(solution)/shard_map/ppermute | solution.py:218
  17.7 0.6 %collective-permute-start.9 = (bf16[128,640]{1,0:T(8,128)(2,1)S(1)}, bf16[128,640]{1,0:T(8,128)(2,1)S(1)}, u32[]{:S(2)}, u32[]{:S(2)}) collective-permute-start(bf16[128,640]{1,0:T(8,128)(2,1)S(1)} %collective-permute-done.3.refs_6_), channel_id=1, source_target_pairs={{0,4},{4,0},{8,12},{12,8},{1,5},{5,1},{9,13},{13,9},{2,6},{6,2},{1... | collective-permute-start | bytes 491528 | tf_op jit(solution)/shard_map/ppermute | solution.py:215
  18.3 1.5 %collective-permute-start.15 = (bf16[128,640]{1,0:T(8,128)(2,1)S(1)}, bf16[128,640]{1,0:T(8,128)(2,1)S(1)}, u32[]{:S(2)}, u32[]{:S(2)}) collective-permute-start(bf16[128,640]{1,0:T(8,128)(2,1)S(1)} %get-tuple-element.28), channel_id=1, source_target_pairs={{0,4},{4,0},{8,12},{12,8},{1,5},{5,1},{9,13},{13,9},{2,6},{6,2},{1... | collective-permute-start | bytes 491528 | tf_op jit(solution)/shard_map/ppermute | solution.py:215
  19.8 1.5 %collective-permute-start.13 = (bf16[128,640]{1,0:T(8,128)(2,1)S(1)}, bf16[128,640]{1,0:T(8,128)(2,1)S(1)}, u32[]{:S(2)}, u32[]{:S(2)}) collective-permute-start(bf16[128,640]{1,0:T(8,128)(2,1)S(1)} %collective-permute-done.3.refs_6_), channel_id=1, source_target_pairs={{0,2},{2,0},{1,3},{3,1},{4,6},{6,4},{5,7},{7,5},{8,10},{10,8},{9,1... | collective-permute-start | bytes 491528 | tf_op jit(solution)/shard_map/ppermute | solution.py:218
  21.4 1.9 %shard_map.86.refs_0_ = bf16[256,512]{1,0:T(8,128)(2,1)S(1)} custom-call(f32[8,128]{1,0:T(8,128)S(1)} %broadcast_in_dim.36.len_ref, f32[1,128]{1,0:T(1,128)S(1)} %broadcast_in_dim.37.sharp_ref, bf16[256,640]{1,0:T(8,128)(2,1)S(1)} %bitcast.31, bf16[256,640]{1,0:T(8,128)(2,1)S(1)} %collective-permute-done.query_other, ...), custom_call_target="tpu_custom_call" | custom-call | tf_op jit(solution)/shard_map/pallas_call | solution.py:93
  23.3 0.8 %shard_map.87 = (f32[1,8]{1,0:T(1,128)}, f32[8,128]{1,0:T(8,128)S(1)}) custom-call(s32[8,1]{1,0:T(8,128)S(1)} %copy.11.slot_ref, s32[1,28]{1,0:T(1,128)S(1)} %copy-done.3, f32[1,1280]{1,0:T(1,128)S(1)} %copy-done.2, s32[4,1]{1,0:T(4,128)S(1)} %copy.12.owner_ref, f32[2,1280]{1,0:T(2,128)S(1)} %copy-done.1, f32[2,1280]{1,0:T(2,128)S(1)} %collective-permute-done.4.refs_1_, ...), custom_call_target="tpu_custom_call" | custom-call | tf_op jit(solution)/shard_map/pallas_call | solution.py:93
  24.2 0.6 %collective-permute-done.9.refs_0_.refs_7_ = bf16[128,640]{1,0:T(8,128)(2,1)S(1)} collective-permute-done((bf16[128,640]{1,0:T(8,128)(2,1)S(1)}, bf16[128,640]{1,0:T(8,128)(2,1)S(1)}, u32[]{:S(2)}, u32[]{:S(2)}) %collective-permute-start.9) | collective-permute-done | bytes 163872 | tf_op jit(solution)/shard_map/ppermute | solution.py:215
  24.8 1.5 %collective-permute-start.10 = (bf16[128,640]{1,0:T(8,128)(2,1)S(1)}, bf16[128,640]{1,0:T(8,128)(2,1)S(1)}, u32[]{:S(2)}, u32[]{:S(2)}) collective-permute-start(bf16[128,640]{1,0:T(8,128)(2,1)S(1)} %collective-permute-done.9.refs_0_.refs_7_), channel_id=1, source_target_pairs={{0,2},{2,0},{1,3},{3,1},{4,6},{6,4},{5,7},{7,5},{8,10},{10,8},{9,1... | collective-permute-start | bytes 491528 | tf_op jit(solution)/shard_map/ppermute | solution.py:218
  26.3 1.1 %collective-permute-done.15.refs_2_.refs_9_ = bf16[128,640]{1,0:T(8,128)(2,1)S(1)} collective-permute-done((bf16[128,640]{1,0:T(8,128)(2,1)S(1)}, bf16[128,640]{1,0:T(8,128)(2,1)S(1)}, u32[]{:S(2)}, u32[]{:S(2)}) %collective-permute-start.15) | collective-permute-done | bytes 163872 | tf_op jit(solution)/shard_map/ppermute | solution.py:215
  27.3 0.5 %collective-permute-start.14 = (bf16[128,640]{1,0:T(8,128)(2,1)S(1)}, bf16[128,640]{1,0:T(8,128)(2,1)S(1)}, u32[]{:S(2)}, u32[]{:S(2)}) collective-permute-start(bf16[128,640]{1,0:T(8,128)(2,1)S(1)} %collective-permute-done.13.refs_0_.refs_8_), channel_id=1, source_target_pairs={{0,1},{1,0},{2,3},{3,2},{4,5},{5,4},{6,7},{7,6},{8,9},{9,8},{10,11... | collective-permute-start | bytes 491528 | tf_op jit(solution)/shard_map/ppermute | solution.py:218
  27.8 0.8 %shard_map.88.refs_1_ = bf16[256,128]{1,0:T(8,128)(2,1)S(1)} custom-call(f32[8,128]{1,0:T(8,128)S(1)} %broadcast_in_dim.36.len_ref, f32[1,128]{1,0:T(1,128)S(1)} %broadcast_in_dim.37.sharp_ref, bf16[256,640]{1,0:T(8,128)(2,1)S(1)} %bitcast.32, bf16[256,640]{1,0:T(8,128)(2,1)S(1)} %collective-permute-done.query_other, ...), custom_call_target="tpu_custom_call" | custom-call | tf_op jit(solution)/shard_map/pallas_call | solution.py:93
  28.6 2.7 %collective-permute-done.10.refs_0_ = bf16[128,640]{1,0:T(8,128)(2,1)S(1)} collective-permute-done((bf16[128,640]{1,0:T(8,128)(2,1)S(1)}, bf16[128,640]{1,0:T(8,128)(2,1)S(1)}, u32[]{:S(2)}, u32[]{:S(2)}) %collective-permute-start.10) | collective-permute-done | bytes 163872 | tf_op jit(solution)/shard_map/ppermute | solution.py:218
  31.4 1.1 %shard_map.89.refs_2_ = bf16[256,256]{1,0:T(8,128)(2,1)S(1)} custom-call(f32[8,128]{1,0:T(8,128)S(1)} %broadcast_in_dim.36.len_ref, f32[1,128]{1,0:T(1,128)S(1)} %broadcast_in_dim.37.sharp_ref, bf16[256,640]{1,0:T(8,128)(2,1)S(1)} %bitcast.33, bf16[256,640]{1,0:T(8,128)(2,1)S(1)} %collective-permute-done.query_other, ...), custom_call_target="tpu_custom_call" | custom-call | tf_op jit(solution)/shard_map/pallas_call | solution.py:93
  32.5 0.8 %shard_map.90.refs_2_ = f32[256,640]{1,0:T(8,128)S(1)} custom-call(f32[8,128]{1,0:T(8,128)S(1)} %get-tuple-element.23.weight_ref, bf16[256,512]{1,0:T(8,128)(2,1)S(1)} %shard_map.86.refs_0_, bf16[256,128]{1,0:T(8,128)(2,1)S(1)} %shard_map.88.refs_1_, bf16[256,256]{1,0:T(8,128)(2,1)S(1)} %shard_map.89.refs_2_, ...), custom_call_target="tpu_custom_call" | custom-call | tf_op jit(solution)/shard_map/pallas_call | solution.py:93
  33.4 1.8 %shard_map.91 = bf16[256,640]{1,0:T(8,128)(2,1)} custom-call(f32[8,128]{1,0:T(8,128)S(1)} %broadcast_in_dim.36.len_ref, f32[1,128]{1,0:T(1,128)S(1)} %broadcast_in_dim.37.sharp_ref, bf16[256,640]{1,0:T(8,128)(2,1)S(1)} %bitcast.34, bf16[256,640]{1,0:T(8,128)(2,1)S(1)} %collective-permute-done.query_other, f32[8,128]{1,0:T(8,128)S(1)} %get-tuple-element.23.weight_ref, ...), custom_call_target="tpu_custom_call" | custom-call | tf_op jit(solution)/shard_map/pallas_call | solution.py:93
  (38 shorter events, 0.8 us)
Async XLA Ops:
  0.6 1.3 %copy-start = (bf16[1,256,640]{2,1,0:T(8,128)(2,1)S(1)}, bf16[1,256,640]{2,1,0:T(8,128)(2,1)}, u32[]{:S(2)}) copy-start(bf16[1,256,640]{2,1,0:T(8,128)(2,1)} %param.7) | copy-start | bytes 983044
  0.6 1.8 %copy-start.4 = (bf16[2,128,640]{2,1,0:T(8,128)(2,1)S(1)}, bf16[2,128,640]{2,1,0:T(8,128)(2,1)}, u32[]{:S(2)}) copy-start(bf16[2,128,640]{2,1,0:T(8,128)(2,1)} %param.8) | copy-start | bytes 983044
  0.7 7.5 %copy-start.1 = (f32[2,1280]{1,0:T(2,128)S(1)}, f32[2,1280]{1,0:T(2,128)}, u32[]{:S(2)}) copy-start(f32[2,1280]{1,0:T(2,128)} %refs_0_.1) | copy-start | bytes 30724
  2.0 6.2 %collective-permute-start = (bf16[256,640]{1,0:T(8,128)(2,1)S(1)}, bf16[256,640]{1,0:T(8,128)(2,1)S(1)}, u32[]{:S(2)}, u32[]{:S(2)}) collective-permute-start(bf16[256,640]{1,0:T(8,128)(2,1)S(1)} %bitcast.30), channel_id=1, source_target_pairs={{0,1},{1,0},{2,3},{3,2},{4,5},{5,4},{6,7},{7,6},{8,9},{9,8},{10,11... | collective-permute-start | bytes 983048 | tf_op jit(solution)/shard_map/ppermute | solution.py:218
  2.5 5.7 %collective-permute-start.1 = (bf16[2,128,640]{2,1,0:T(8,128)(2,1)S(1)}, bf16[2,128,640]{2,1,0:T(8,128)(2,1)S(1)}, u32[]{:S(2)}, u32[]{:S(2)}) collective-permute-start(bf16[2,128,640]{2,1,0:T(8,128)(2,1)S(1)} %copy-done.4), channel_id=1, source_target_pairs={{0,1},{1,0},{2,3},{3,2},{4,5},{5,4},{6,7},{7,6},{8,9},{9,8},{10,11... | collective-permute-start | bytes 983048 | tf_op jit(solution)/shard_map/ppermute | solution.py:218
  2.6 12.3 %collective-permute-start.3 = (bf16[128,640]{1,0:T(8,128)(2,1)S(1)}, bf16[128,640]{1,0:T(8,128)(2,1)S(1)}, u32[]{:S(2)}, u32[]{:S(2)}) collective-permute-start(bf16[128,640]{1,0:T(8,128)(2,1)S(1)} %get-tuple-element.32), channel_id=1, source_target_pairs={{0,8},{4,12},{8,0},{12,4},{1,9},{5,13},{9,1},{13,5},{2,10},{6,14},... | collective-permute-start | bytes 491528 | tf_op jit(solution)/shard_map/ppermute | solution.py:215
  6.6 9.5 %collective-permute-start.2 = (bf16[128,640]{1,0:T(8,128)(2,1)S(1)}, bf16[128,640]{1,0:T(8,128)(2,1)S(1)}, u32[]{:S(2)}, u32[]{:S(2)}) collective-permute-start(bf16[128,640]{1,0:T(8,128)(2,1)S(1)} %get-tuple-element.32), channel_id=1, source_target_pairs={{0,4},{4,0},{8,12},{12,8},{1,5},{5,1},{9,13},{13,9},{2,6},{6,2},{1... | collective-permute-start | bytes 491528 | tf_op jit(solution)/shard_map/ppermute | solution.py:215
  8.2 6.9 %collective-permute-start.4 = (f32[2,1280]{1,0:T(2,128)S(1)}, f32[2,1280]{1,0:T(2,128)S(1)}, u32[]{:S(2)}, u32[]{:S(2)}) collective-permute-start(f32[2,1280]{1,0:T(2,128)S(1)} %copy-done.1), channel_id=1, source_target_pairs={{0,4},{1,9},{4,0},{5,13},{8,12},{9,1},{12,8},{13,5},{2,6},{3,11},{... | collective-permute-start | bytes 30728 | tf_op jit(solution)/shard_map/ppermute | solution.py:233
  8.7 7.4 %collective-permute-start.5 = (f32[2,1280]{1,0:T(2,128)S(1)}, f32[2,1280]{1,0:T(2,128)S(1)}, u32[]{:S(2)}, u32[]{:S(2)}) collective-permute-start(f32[2,1280]{1,0:T(2,128)S(1)} %copy-done.1), channel_id=1, source_target_pairs={{0,12},{4,8},{8,4},{12,0},{1,13},{5,9},{9,5},{13,1},{2,14},{6,10},... | collective-permute-start | bytes 30728 | tf_op jit(solution)/shard_map/ppermute | solution.py:215
  10.0 6.6 %copy-start.5 = (s32[8]{0:T(128)S(1)}, s32[8]{0:T(128)}, u32[]{:S(2)}) copy-start(s32[8]{0:T(128)} %param.9) | copy-start | bytes 100
  16.1 2.2 %collective-permute-start.7 = (bf16[128,640]{1,0:T(8,128)(2,1)S(1)}, bf16[128,640]{1,0:T(8,128)(2,1)S(1)}, u32[]{:S(2)}, u32[]{:S(2)}) collective-permute-start(bf16[128,640]{1,0:T(8,128)(2,1)S(1)} %collective-permute-done.3.refs_6_), channel_id=1, source_target_pairs={{0,1},{1,0},{2,3},{3,2},{4,5},{5,4},{6,7},{7,6},{8,9},{9,8},{10,11... | collective-permute-start | bytes 491528 | tf_op jit(solution)/shard_map/ppermute | solution.py:218
  16.1 2.2 %collective-permute-start.6 = (bf16[128,640]{1,0:T(8,128)(2,1)S(1)}, bf16[128,640]{1,0:T(8,128)(2,1)S(1)}, u32[]{:S(2)}, u32[]{:S(2)}) collective-permute-start(bf16[128,640]{1,0:T(8,128)(2,1)S(1)} %collective-permute-done.2.refs_4_.refs_5_), channel_id=1, source_target_pairs={{0,1},{1,0},{2,3},{3,2},{4,5},{5,4},{6,7},{7,6},{8,9},{9,8},{10,11... | collective-permute-start | bytes 491528 | tf_op jit(solution)/shard_map/ppermute | solution.py:218
  17.7 7.1 %collective-permute-start.9 = (bf16[128,640]{1,0:T(8,128)(2,1)S(1)}, bf16[128,640]{1,0:T(8,128)(2,1)S(1)}, u32[]{:S(2)}, u32[]{:S(2)}) collective-permute-start(bf16[128,640]{1,0:T(8,128)(2,1)S(1)} %collective-permute-done.3.refs_6_), channel_id=1, source_target_pairs={{0,4},{4,0},{8,12},{12,8},{1,5},{5,1},{9,13},{13,9},{2,6},{6,2},{1... | collective-permute-start | bytes 491528 | tf_op jit(solution)/shard_map/ppermute | solution.py:215
  18.3 5.0 %collective-permute-start.8 = (f32[2,1280]{1,0:T(2,128)S(1)}, f32[2,1280]{1,0:T(2,128)S(1)}, u32[]{:S(2)}, u32[]{:S(2)}) collective-permute-start(f32[2,1280]{1,0:T(2,128)S(1)} %collective-permute-done.4.refs_1_), channel_id=1, source_target_pairs={{0,1},{1,0},{2,3},{3,2},{4,5},{5,4},{6,7},{7,6},{8,9},{9,8},{10,11... | collective-permute-start | bytes 30728 | tf_op jit(solution)/shard_map/ppermute | solution.py:218
  18.3 9.0 %collective-permute-start.15 = (bf16[128,640]{1,0:T(8,128)(2,1)S(1)}, bf16[128,640]{1,0:T(8,128)(2,1)S(1)}, u32[]{:S(2)}, u32[]{:S(2)}) collective-permute-start(bf16[128,640]{1,0:T(8,128)(2,1)S(1)} %get-tuple-element.28), channel_id=1, source_target_pairs={{0,4},{4,0},{8,12},{12,8},{1,5},{5,1},{9,13},{13,9},{2,6},{6,2},{1... | collective-permute-start | bytes 491528 | tf_op jit(solution)/shard_map/ppermute | solution.py:215
  19.8 7.5 %collective-permute-start.13 = (bf16[128,640]{1,0:T(8,128)(2,1)S(1)}, bf16[128,640]{1,0:T(8,128)(2,1)S(1)}, u32[]{:S(2)}, u32[]{:S(2)}) collective-permute-start(bf16[128,640]{1,0:T(8,128)(2,1)S(1)} %collective-permute-done.3.refs_6_), channel_id=1, source_target_pairs={{0,2},{2,0},{1,3},{3,1},{4,6},{6,4},{5,7},{7,5},{8,10},{10,8},{9,1... | collective-permute-start | bytes 491528 | tf_op jit(solution)/shard_map/ppermute | solution.py:218
  21.4 1.9 %copy-start.2 = (f32[1,1280]{1,0:T(1,128)S(1)}, f32[1,1280]{1,0:T(1,128)}, u32[]{:S(2)}) copy-start(f32[1,1280]{1,0:T(1,128)} %pool_ref.1) | copy-start | bytes 15364
  21.4 1.9 %copy-start.3 = (s32[1,28]{1,0:T(1,128)S(1)}, s32[1,28]{1,0:T(1,128)}, u32[]{:S(2)}) copy-start(s32[1,28]{1,0:T(1,128)} %hits_ref) | copy-start | bytes 340
  24.8 3.1 %collective-permute-start.11 = (bf16[128,640]{1,0:T(8,128)(2,1)S(1)}, bf16[128,640]{1,0:T(8,128)(2,1)S(1)}, u32[]{:S(2)}, u32[]{:S(2)}) collective-permute-start(bf16[128,640]{1,0:T(8,128)(2,1)S(1)} %collective-permute-done.9.refs_0_.refs_7_), channel_id=1, source_target_pairs={{0,1},{1,0},{2,3},{3,2},{4,5},{5,4},{6,7},{7,6},{8,9},{9,8},{10,11... | collective-permute-start | bytes 491528 | tf_op jit(solution)/shard_map/ppermute | solution.py:218
  24.8 6.6 %collective-permute-start.10 = (bf16[128,640]{1,0:T(8,128)(2,1)S(1)}, bf16[128,640]{1,0:T(8,128)(2,1)S(1)}, u32[]{:S(2)}, u32[]{:S(2)}) collective-permute-start(bf16[128,640]{1,0:T(8,128)(2,1)S(1)} %collective-permute-done.9.refs_0_.refs_7_), channel_id=1, source_target_pairs={{0,2},{2,0},{1,3},{3,1},{4,6},{6,4},{5,7},{7,5},{8,10},{10,8},{9,1... | collective-permute-start | bytes 491528 | tf_op jit(solution)/shard_map/ppermute | solution.py:218
  27.3 4.1 %collective-permute-start.16 = (bf16[128,640]{1,0:T(8,128)(2,1)S(1)}, bf16[128,640]{1,0:T(8,128)(2,1)S(1)}, u32[]{:S(2)}, u32[]{:S(2)}) collective-permute-start(bf16[128,640]{1,0:T(8,128)(2,1)S(1)} %collective-permute-done.15.refs_2_.refs_9_), channel_id=1, source_target_pairs={{0,1},{1,0},{2,3},{3,2},{4,5},{5,4},{6,7},{7,6},{8,9},{9,8},{10,11... | collective-permute-start | bytes 491528 | tf_op jit(solution)/shard_map/ppermute | solution.py:218
  27.3 4.1 %collective-permute-start.14 = (bf16[128,640]{1,0:T(8,128)(2,1)S(1)}, bf16[128,640]{1,0:T(8,128)(2,1)S(1)}, u32[]{:S(2)}, u32[]{:S(2)}) collective-permute-start(bf16[128,640]{1,0:T(8,128)(2,1)S(1)} %collective-permute-done.13.refs_0_.refs_8_), channel_id=1, source_target_pairs={{0,1},{1,0},{2,3},{3,2},{4,5},{5,4},{6,7},{7,6},{8,9},{9,8},{10,11... | collective-permute-start | bytes 491528 | tf_op jit(solution)/shard_map/ppermute | solution.py:218
  31.4 2.0 %collective-permute-start.12 = (bf16[128,640]{1,0:T(8,128)(2,1)S(1)}, bf16[128,640]{1,0:T(8,128)(2,1)S(1)}, u32[]{:S(2)}, u32[]{:S(2)}) collective-permute-start(bf16[128,640]{1,0:T(8,128)(2,1)S(1)} %collective-permute-done.10.refs_0_), channel_id=1, source_target_pairs={{0,1},{1,0},{2,3},{3,2},{4,5},{5,4},{6,7},{7,6},{8,9},{9,8},{10,11... | collective-permute-start | bytes 491528 | tf_op jit(solution)/shard_map/ppermute | solution.py:218

commit v10 on v8

--- a/solution.py
+++ b/solution.py
@@ -128,12 +128,12 @@
 
 def partial_kernel(*refs):
     query, blocks, out = refs[0], refs[1:-1], refs[-1]
-    rows = 0
-    for block in blocks:
-        out[:, rows : rows + block.shape[0]] = lax.dot_general(
-            query[...], block[...], (((1,), (1,)), ((), ())), preferred_element_type=jnp.float32
-        )
-        rows += block.shape[0]
+    out[...] = lax.dot_general(
+        query[...],
+        jnp.concatenate([block[...] for block in blocks]),
+        (((1,), (1,)), ((), ())),
+        preferred_element_type=jnp.float32,
+    )
 
 
 def partial_similar(query, blocks):
@@ -183,30 +183,41 @@
     )
 
 
-def profile_kernel(groups, weight_ref, *refs):
+def weighted_term(weight, alignment, blocks):
+    target = blocks[0][...] if len(blocks) == 1 else jnp.concatenate([b[...] for b in blocks])
+    return weight * jnp.dot(alignment, target, preferred_element_type=jnp.float32)
+
+
+def profile_kernel(groups, pieces, weight_ref, *refs):
     aligned, blocks, out_ref = refs[: len(groups)], refs[len(groups) : -1], refs[-1]
-    rows = blocks[0].shape[0]
     acc, at = None, 0
     for group, slots in zip(aligned, groups):
+        rows = group.shape[1] // len(slots)
         for i, slot in enumerate(slots):
-            term = weight_ref[slot : slot + 1, 0:1] * jnp.dot(
+            count = pieces.get(slot, 1)
+            term = weighted_term(
+                weight_ref[slot : slot + 1, 0:1],
                 group[:, i * rows : (i + 1) * rows],
-                blocks[at][...],
-                preferred_element_type=jnp.float32,
+                blocks[at : at + count],
             )
             acc = term if acc is None else acc + term
-            at += 1
+            at += count
     out_ref[...] = acc
 
 
-def last_kernel(model_width, slot, len_ref, sharp_ref, weight_ref, mine, other, block, acc, out_ref):
-    rows = block.shape[0]
-    similar = (mine[...] + other[...]) * (1.0 / math.sqrt(model_width))
-    alignment = align_block(similar, len_ref[slot : slot + 1, :rows], sharp_ref[:, 0:1])
-    term = weight_ref[slot : slot + 1, 0:1] * jnp.dot(
-        alignment.astype(jnp.bfloat16), block[...], preferred_element_type=jnp.float32
-    )
-    out_ref[...] = (acc[...] + term).astype(out_ref.dtype)
+def last_kernel(model_width, targets, len_ref, sharp_ref, weight_ref, mine, other, *refs):
+    blocks, (acc_ref, out_ref) = refs[:-2], refs[-2:]
+    rows = mine.shape[1] // len(targets)
+    acc = acc_ref[...]
+    for at, (slot, count) in enumerate(targets):
+        part = pl.ds(at * rows, rows)
+        similar = (mine[:, part] + other[:, part]) * (1.0 / math.sqrt(model_width))
+        alignment = align_block(similar, len_ref[slot : slot + 1, :rows], sharp_ref[:, 0:1])
+        acc += weighted_term(
+            weight_ref[slot : slot + 1, 0:1], alignment.astype(jnp.bfloat16), blocks[:count]
+        )
+        blocks = blocks[count:]
+    out_ref[...] = acc.astype(out_ref.dtype)
 
 
 def per_device_by_target(
@@ -253,23 +264,21 @@
     far = after(far, pool_split, pool_last)
     near = after(near, far)
     far = after(far, near)
-    last = from_peer(far, 1)
-    far_rest = across(far, "qry")
+    half = target_rows // 2
+    last = [from_peer(far[:half], 1), from_peer(far[half:], 1)]
     near_rest = from_peer(after(rest, far), 1)
 
     one_blocks = [target_res[0], target_res[1], near, far]
     one = partial_similar(query, one_blocks)
     one_other = across(one, "rep")
-    one_aligned = aligned((0, 1, 2, 4), one, one_other)
-    last = after(last, one_aligned)
-
-    last_rest = across(last, "qry")
-    three = partial_similar(query, [last])
-    three_other = across(three, "rep")
-    three_aligned = aligned((6,), three, three_other)
-    four_blocks = [far_rest, near_rest]
-    four = partial_similar(after(query, three_aligned), four_blocks)
-    four_other = across(four, "rep")
+    far_rest = across(after(far, one_other), "qry")
+
+    last_rest = [across(piece, "qry") for piece in last]
+    two_blocks = [far_rest, *last]
+    two = partial_similar(query, two_blocks)
+    two_other = across(two, "rep")
+    one_aligned = aligned((0, 1, 2, 4), after(one, two), one_other)
+
     posterior, weights = call_kernel(
         weigh_kernel,
         (
@@ -277,7 +286,7 @@
             jax.ShapeDtypeStruct((len(target_len), target_rows), jnp.float32),
         ),
         slots,
-        after(hits, four),
+        after(hits, two),
         query_pool,
         owners.astype(jnp.int32)[:, None],
         target_pool,
@@ -285,29 +294,31 @@
         pool_other,
         pool_last,
     )
-    five = partial_similar(after(query, weights), [last_rest])
-    five_other = across(five, "rep")
-    four_aligned = aligned((5, 3), after(four, five), four_other)
+
+    three_blocks = [near_rest, *last_rest]
+    three = partial_similar(after(query, weights, one_aligned), three_blocks)
+    three_other = across(three, "rep")
+    two_aligned = aligned((5, 6), after(two, three), two_other)
     acc = call_kernel(
-        functools.partial(profile_kernel, ((0, 1, 2, 4), (6,), (5, 3))),
+        functools.partial(
+            profile_kernel, ((0, 1, 2, 4), (5, 6)), {6: 2}
+        ),
         jax.ShapeDtypeStruct(query.shape, jnp.float32),
         weights,
         one_aligned,
-        three_aligned,
-        four_aligned,
+        two_aligned,
         *one_blocks,
-        last,
-        *four_blocks,
+        *two_blocks,
     )
     profile = call_kernel(
-        functools.partial(last_kernel, model_width, 7),
+        functools.partial(last_kernel, model_width, ((3, 1), (7, 2))),
         jax.ShapeDtypeStruct(query.shape, jnp.bfloat16),
         lengths,
         half_sharp,
         weights,
-        five,
-        five_other,
-        last_rest,
+        three,
+        three_other,
+        *three_blocks,
         acc,
     )
     return (profile[None], posterior)

time: 33.7 us -> 32.9 us (0.976)
  waiting for transfers between devices: 9.11 us -> 7.04 us
  starting transfers between devices: 13.4 us -> 15.4 us
  Pallas kernels: 7.62 us -> 7 us
    ppermute x7, waiting for transfers between devices: 1.91 us -> 0.02 us  [across(): return lax.ppermute(array, axis, [(0, 1), (1, 0)])]
    ppermute x7, starting transfers between devices: 3.86 us -> 5.25 us  [across(): return lax.ppermute(array, axis, [(0, 1), (1, 0)])]
    pallas_call x10 -> x8, Pallas kernels: 7.62 us -> 7 us  [call_kernel(): pl.pallas_call(kernel, out_shape=out_shape, in_specs=[VMEM] * len(operand...]
    ppermute x5 -> x6, starting transfers between devices: 9.12 us -> 9.7 us  [from_peer(): return lax.ppermute(array, 'tgt', [(i, i ^ k) for i in range(4)])]
    ppermute x5 -> x6, waiting for transfers between devices: 2.24 us -> 2.07 us  [from_peer(): return lax.ppermute(array, 'tgt', [(i, i ^ k) for i in range(4)])]
  transfers between devices with their start and end apart: 13 -> 14, of which waited for: 6 -> 4; matrix products, arithmetic and copies ran while one was open for 2% -> 2% of each run, Pallas kernels for 16% -> 14%
where the time goes in v10:
time: 32.9 us; the launch traced here: 32.8 us
  starting transfers between devices  15.4 us (47%)
  waiting for transfers between devices  7.04 us (21%)
  Pallas kernels  7 us (21%)
  local copies, waits for them, and re-layouts  1.63 us (5%)
  between operations  1.46 us (4%)
    ppermute x6, starting transfers between devices, from_peer(): return lax.ppermute(array, 'tgt', [(i, i ^ k) for i in range(4)])  9.7 us
    pallas_call x8, Pallas kernels, call_kernel(): pl.pallas_call(kernel, out_shape=out_shape, in_specs=[VMEM] * len(operand...  7 us
    ppermute x7, starting transfers between devices, across(): return lax.ppermute(array, axis, [(0, 1), (1, 0)])  5.25 us
    ppermute x1, waiting for transfers between devices, per_device_by_target(): pool_split = lax.ppermute(target_pool, ('tgt', 'rep'), split)  4.96 us
    ppermute x6, waiting for transfers between devices, from_peer(): return lax.ppermute(array, 'tgt', [(i, i ^ k) for i in range(4)])  2.07 us
    squeeze x1, local copies, waits for them, and re-layouts, per_device_by_target(): rest = lax.dynamic_index_in_dim(target_res, 1 - at_qry, 0, keepdims=False)  1.26 us
  transfers between devices with their start and end apart: 14, of which 4 were waited for; matrix products, arithmetic and copies ran while one was open for 2% of the time, Pallas kernels for 14%

profile of v10, /device:TPU:0, one launch (start us, length us, event | category | flops | bytes accessed | tf_op | source)
XLA Modules:
  0.0 32.8 jit_solution(5012588467151718719)
XLA Ops:
  0.7 1.3 %dynamic-slice_bitcast_fusion = (bf16[128,640]{1,0:T(8,128)(2,1)S(1)}, bf16[128,640]{1,0:T(8,128)(2,1)S(1)}, bf16[128,640]{1,0:T(8,128)(2,1)S(1)}, bf16[128,640]{1,0:T(8,128)(2,1)S(1)}) fusion(bf16[2,128,640]{2,1,0:T(8,128)(2,1)} %param.8, s32[]{:T(128)S(6)} %select_n.13, s32[]{:T(128)S(6)} %select_n.12), kind=kLoop, calls=%fused_computation | loop fusion | bytes 1310728 | tf_op jit(solution)/shard_map/jit(dynamic_index_in_dim)/squeeze | solution.py:247
  1.9 4.1 %collective-permute-start = (bf16[128,640]{1,0:T(8,128)(2,1)S(1)}, bf16[128,640]{1,0:T(8,128)(2,1)S(1)}, u32[]{:S(2)}, u32[]{:S(2)}) collective-permute-start(bf16[128,640]{1,0:T(8,128)(2,1)S(1)} %get-tuple-element.26), channel_id=1, source_target_pairs={{0,8},{4,12},{8,0},{12,4},{1,9},{5,13},{9,1},{13,5},{2,10},{6,14},... | collective-permute-start | bytes 491528 | tf_op jit(solution)/shard_map/ppermute | solution.py:232
  6.0 1.6 %collective-permute-start.3 = (bf16[128,640]{1,0:T(8,128)(2,1)S(1)}, bf16[128,640]{1,0:T(8,128)(2,1)S(1)}, u32[]{:S(2)}, u32[]{:S(2)}) collective-permute-start(bf16[128,640]{1,0:T(8,128)(2,1)S(1)} %get-tuple-element.26), channel_id=1, source_target_pairs={{0,4},{4,0},{8,12},{12,8},{1,5},{5,1},{9,13},{13,9},{2,6},{6,2},{1... | collective-permute-start | bytes 491528 | tf_op jit(solution)/shard_map/ppermute | solution.py:232
  7.6 0.4 %collective-permute-start.1 = (f32[2,1280]{1,0:T(2,128)S(1)}, f32[2,1280]{1,0:T(2,128)S(1)}, u32[]{:S(2)}, u32[]{:S(2)}) collective-permute-start(f32[2,1280]{1,0:T(2,128)S(1)} %copy-done.1), channel_id=1, source_target_pairs={{0,4},{1,9},{4,0},{5,13},{8,12},{9,1},{12,8},{13,5},{2,6},{3,11},{... | collective-permute-start | bytes 30728 | tf_op jit(solution)/shard_map/ppermute | solution.py:241
  8.1 1.3 %collective-permute-start.2 = (f32[2,1280]{1,0:T(2,128)S(1)}, f32[2,1280]{1,0:T(2,128)S(1)}, u32[]{:S(2)}, u32[]{:S(2)}) collective-permute-start(f32[2,1280]{1,0:T(2,128)S(1)} %copy-done.1), channel_id=1, source_target_pairs={{0,12},{4,8},{8,4},{12,0},{1,13},{5,9},{9,5},{13,1},{2,14},{6,10},... | collective-permute-start | bytes 30728 | tf_op jit(solution)/shard_map/ppermute | solution.py:232
  9.4 5.0 %collective-permute-done.1.refs_1_ = f32[2,1280]{1,0:T(2,128)S(1)} collective-permute-done((f32[2,1280]{1,0:T(2,128)S(1)}, f32[2,1280]{1,0:T(2,128)S(1)}, u32[]{:S(2)}, u32[]{:S(2)}) %collective-permute-start.1) | collective-permute-done | bytes 10272 | tf_op jit(solution)/shard_map/ppermute | solution.py:241
  14.4 0.9 %collective-permute-done.2.refs_3_ = f32[2,1280]{1,0:T(2,128)S(1)} collective-permute-done((f32[2,1280]{1,0:T(2,128)S(1)}, f32[2,1280]{1,0:T(2,128)S(1)}, u32[]{:S(2)}, u32[]{:S(2)}) %collective-permute-start.2) | collective-permute-done | bytes 10272 | tf_op jit(solution)/shard_map/ppermute | solution.py:232
  15.3 0.4 %shard_map.86.mine = f32[256,512]{1,0:T(8,128)S(1)} custom-call(bf16[256,640]{1,0:T(8,128)(2,1)S(1)} %bitcast.26, bf16[128,640]{1,0:T(8,128)(2,1)S(1)} %get-tuple-element.25.refs_1_.refs_2_, bf16[128,640]{1,0:T(8,128)(2,1)S(1)} %get-tuple-element.27.refs_2_.refs_3_, bf16[128,640]{1,0:T(8,128)(2,1)S(1)} %collective-permute-done.3.refs_3_.refs_4_, ...), custom_call_target="tpu_custom_call" | custom-call | tf_op jit(solution)/shard_map/pallas_call | solution.py:93
  15.9 0.6 %collective-permute-start.6 = (bf16[64,640]{1,0:T(8,128)(2,1)S(1)}, bf16[64,640]{1,0:T(8,128)(2,1)S(1)}, u32[]{:S(2)}, u32[]{:S(2)}) collective-permute-start(bf16[64,640]{1,0:T(8,128)(2,1)S(1)} %get-tuple-element.29), channel_id=1, source_target_pairs={{0,4},{4,0},{8,12},{12,8},{1,5},{5,1},{9,13},{13,9},{2,6},{6,2},{1... | collective-permute-start | bytes 245768 | tf_op jit(solution)/shard_map/ppermute | solution.py:232
  16.5 1.4 %collective-permute-start.7 = (bf16[64,640]{1,0:T(8,128)(2,1)S(1)}, bf16[64,640]{1,0:T(8,128)(2,1)S(1)}, u32[]{:S(2)}, u32[]{:S(2)}) collective-permute-start(bf16[64,640]{1,0:T(8,128)(2,1)S(1)} %get-tuple-element.28), channel_id=1, source_target_pairs={{0,4},{4,0},{8,12},{12,8},{1,5},{5,1},{9,13},{13,9},{2,6},{6,2},{1... | collective-permute-start | bytes 245768 | tf_op jit(solution)/shard_map/ppermute | solution.py:232
  18.0 0.6 %collective-permute-start.9 = (bf16[128,640]{1,0:T(8,128)(2,1)S(1)}, bf16[128,640]{1,0:T(8,128)(2,1)S(1)}, u32[]{:S(2)}, u32[]{:S(2)}) collective-permute-start(bf16[128,640]{1,0:T(8,128)(2,1)S(1)} %get-tuple-element.21), channel_id=1, source_target_pairs={{0,4},{4,0},{8,12},{12,8},{1,5},{5,1},{9,13},{13,9},{2,6},{6,2},{1... | collective-permute-start | bytes 491528 | tf_op jit(solution)/shard_map/ppermute | solution.py:232
  18.6 1.5 %collective-permute-start.5 = (bf16[128,640]{1,0:T(8,128)(2,1)S(1)}, bf16[128,640]{1,0:T(8,128)(2,1)S(1)}, u32[]{:S(2)}, u32[]{:S(2)}) collective-permute-start(bf16[128,640]{1,0:T(8,128)(2,1)S(1)} %collective-permute-done.refs_4_.refs_5_), channel_id=1, source_target_pairs={{0,2},{2,0},{1,3},{3,1},{4,6},{6,4},{5,7},{7,5},{8,10},{10,8},{9,1... | collective-permute-start | bytes 491528 | tf_op jit(solution)/shard_map/ppermute | solution.py:235
  20.3 0.9 %collective-permute-done.6.refs_2_.refs_7_ = bf16[64,640]{1,0:T(8,128)(2,1)S(1)} collective-permute-done((bf16[64,640]{1,0:T(8,128)(2,1)S(1)}, bf16[64,640]{1,0:T(8,128)(2,1)S(1)}, u32[]{:S(2)}, u32[]{:S(2)}) %collective-permute-start.6) | collective-permute-done | bytes 81952 | tf_op jit(solution)/shard_map/ppermute | solution.py:232
  21.2 1.5 %collective-permute-start.10 = (bf16[64,640]{1,0:T(8,128)(2,1)S(1)}, bf16[64,640]{1,0:T(8,128)(2,1)S(1)}, u32[]{:S(2)}, u32[]{:S(2)}) collective-permute-start(bf16[64,640]{1,0:T(8,128)(2,1)S(1)} %collective-permute-done.6.refs_2_.refs_7_), channel_id=1, source_target_pairs={{0,2},{2,0},{1,3},{3,1},{4,6},{6,4},{5,7},{7,5},{8,10},{10,8},{9,1... | collective-permute-start | bytes 245768 | tf_op jit(solution)/shard_map/ppermute | solution.py:235
  22.7 0.3 collective-permute-done.7.refs_3_.refs_8_
  23.0 1.5 %collective-permute-start.11 = (bf16[64,640]{1,0:T(8,128)(2,1)S(1)}, bf16[64,640]{1,0:T(8,128)(2,1)S(1)}, u32[]{:S(2)}, u32[]{:S(2)}) collective-permute-start(bf16[64,640]{1,0:T(8,128)(2,1)S(1)} %collective-permute-done.7.refs_3_.refs_8_), channel_id=1, source_target_pairs={{0,2},{2,0},{1,3},{3,1},{4,6},{6,4},{5,7},{7,5},{8,10},{10,8},{9,1... | collective-permute-start | bytes 245768 | tf_op jit(solution)/shard_map/ppermute | solution.py:235
  25.4 0.3 shard_map.87.mine
  25.8 1.7 %shard_map.89.refs_0_ = bf16[256,512]{1,0:T(8,128)(2,1)S(1)} custom-call(f32[8,128]{1,0:T(8,128)S(1)} %broadcast_in_dim.36.len_ref, f32[1,128]{1,0:T(1,128)S(1)} %broadcast_in_dim.37.sharp_ref, f32[256,512]{1,0:T(8,128)S(1)} %shard_map.86.mine, f32[256,512]{1,0:T(8,128)S(1)} %collective-permute-done.4.other), custom_call_target="tpu_custom_call" | custom-call | tf_op jit(solution)/shard_map/pallas_call | solution.py:93
  27.6 0.8 %shard_map.88 = (f32[1,8]{1,0:T(1,128)}, f32[8,128]{1,0:T(8,128)S(1)}) custom-call(s32[8,1]{1,0:T(8,128)S(1)} %copy.11.slot_ref, s32[1,28]{1,0:T(1,128)S(1)} %copy-done.3, f32[1,1280]{1,0:T(1,128)S(1)} %copy-done.2, s32[4,1]{1,0:T(4,128)S(1)} %copy.12.owner_ref, f32[2,1280]{1,0:T(2,128)S(1)} %copy-done.1, f32[2,1280]{1,0:T(2,128)S(1)} %collective-permute-done.1.refs_1_, ...), custom_call_target="tpu_custom_call" | custom-call | tf_op jit(solution)/shard_map/pallas_call | solution.py:93
  28.4 0.3 shard_map.90.mine
  28.7 0.6 %collective-permute-start.12 = (f32[256,256]{1,0:T(8,128)S(1)}, f32[256,256]{1,0:T(8,128)S(1)}, u32[]{:S(2)}, u32[]{:S(2)}) collective-permute-start(f32[256,256]{1,0:T(8,128)S(1)} %shard_map.90.mine), channel_id=1, source_target_pairs={{0,1},{1,0},{2,3},{3,2},{4,5},{5,4},{6,7},{7,6},{8,9},{9,8},{10,11... | collective-permute-start | bytes 786440 | tf_op jit(solution)/shard_map/ppermute | solution.py:235
  29.3 0.8 %shard_map.91.refs_1_ = bf16[256,256]{1,0:T(8,128)(2,1)S(1)} custom-call(f32[8,128]{1,0:T(8,128)S(1)} %broadcast_in_dim.36.len_ref, f32[1,128]{1,0:T(1,128)S(1)} %broadcast_in_dim.37.sharp_ref, f32[256,256]{1,0:T(8,128)S(1)} %shard_map.87.mine, f32[256,256]{1,0:T(8,128)S(1)} %collective-permute-done.13.other), custom_call_target="tpu_custom_call" | custom-call | tf_op jit(solution)/shard_map/pallas_call | solution.py:93
  30.1 0.7 %shard_map.92.refs_3_ = f32[256,640]{1,0:T(8,128)S(1)} custom-call(f32[8,128]{1,0:T(8,128)S(1)} %get-tuple-element.18.weight_ref, bf16[256,512]{1,0:T(8,128)(2,1)S(1)} %shard_map.89.refs_0_, bf16[256,256]{1,0:T(8,128)(2,1)S(1)} %shard_map.91.refs_1_, bf16[128,640]{1,0:T(8,128)(2,1)S(1)} %get-tuple-element.25.refs_1_.refs_2_, ...), custom_call_target="tpu_custom_call" | custom-call | tf_op jit(solution)/shard_map/pallas_call | solution.py:93
  30.8 2.0 %shard_map.93 = bf16[256,640]{1,0:T(8,128)(2,1)} custom-call(f32[8,128]{1,0:T(8,128)S(1)} %broadcast_in_dim.36.len_ref, f32[1,128]{1,0:T(1,128)S(1)} %broadcast_in_dim.37.sharp_ref, f32[8,128]{1,0:T(8,128)S(1)} %get-tuple-element.18.weight_ref, f32[256,256]{1,0:T(8,128)S(1)} %shard_map.90.mine, f32[256,256]{1,0:T(8,128)S(1)} %collective-permute-done.12.other, ...), custom_call_target="tpu_custom_call" | custom-call | tf_op jit(solution)/shard_map/pallas_call | solution.py:93
  (32 shorter events, 0.9 us)
Async XLA Ops:
  0.6 7.0 %copy-start.1 = (f32[2,1280]{1,0:T(2,128)S(1)}, f32[2,1280]{1,0:T(2,128)}, u32[]{:S(2)}) copy-start(f32[2,1280]{1,0:T(2,128)} %refs_0_.1) | copy-start | bytes 30724
  0.6 14.6 %copy-start = (bf16[1,256,640]{2,1,0:T(8,128)(2,1)S(1)}, bf16[1,256,640]{2,1,0:T(8,128)(2,1)}, u32[]{:S(2)}) copy-start(bf16[1,256,640]{2,1,0:T(8,128)(2,1)} %param.7) | copy-start | bytes 983044
  1.9 13.4 %collective-permute-start = (bf16[128,640]{1,0:T(8,128)(2,1)S(1)}, bf16[128,640]{1,0:T(8,128)(2,1)S(1)}, u32[]{:S(2)}, u32[]{:S(2)}) collective-permute-start(bf16[128,640]{1,0:T(8,128)(2,1)S(1)} %get-tuple-element.26), channel_id=1, source_target_pairs={{0,8},{4,12},{8,0},{12,4},{1,9},{5,13},{9,1},{13,5},{2,10},{6,14},... | collective-permute-start | bytes 491528 | tf_op jit(solution)/shard_map/ppermute | solution.py:232
  6.0 9.3 %collective-permute-start.3 = (bf16[128,640]{1,0:T(8,128)(2,1)S(1)}, bf16[128,640]{1,0:T(8,128)(2,1)S(1)}, u32[]{:S(2)}, u32[]{:S(2)}) collective-permute-start(bf16[128,640]{1,0:T(8,128)(2,1)S(1)} %get-tuple-element.26), channel_id=1, source_target_pairs={{0,4},{4,0},{8,12},{12,8},{1,5},{5,1},{9,13},{13,9},{2,6},{6,2},{1... | collective-permute-start | bytes 491528 | tf_op jit(solution)/shard_map/ppermute | solution.py:232
  7.6 6.8 %collective-permute-start.1 = (f32[2,1280]{1,0:T(2,128)S(1)}, f32[2,1280]{1,0:T(2,128)S(1)}, u32[]{:S(2)}, u32[]{:S(2)}) collective-permute-start(f32[2,1280]{1,0:T(2,128)S(1)} %copy-done.1), channel_id=1, source_target_pairs={{0,4},{1,9},{4,0},{5,13},{8,12},{9,1},{12,8},{13,5},{2,6},{3,11},{... | collective-permute-start | bytes 30728 | tf_op jit(solution)/shard_map/ppermute | solution.py:241
  8.1 7.2 %collective-permute-start.2 = (f32[2,1280]{1,0:T(2,128)S(1)}, f32[2,1280]{1,0:T(2,128)S(1)}, u32[]{:S(2)}, u32[]{:S(2)}) collective-permute-start(f32[2,1280]{1,0:T(2,128)S(1)} %copy-done.1), channel_id=1, source_target_pairs={{0,12},{4,8},{8,4},{12,0},{1,13},{5,9},{9,5},{13,1},{2,14},{6,10},... | collective-permute-start | bytes 30728 | tf_op jit(solution)/shard_map/ppermute | solution.py:232
  15.7 2.9 %collective-permute-start.4 = (f32[256,512]{1,0:T(8,128)S(1)}, f32[256,512]{1,0:T(8,128)S(1)}, u32[]{:S(2)}, u32[]{:S(2)}) collective-permute-start(f32[256,512]{1,0:T(8,128)S(1)} %shard_map.86.mine), channel_id=1, source_target_pairs={{0,1},{1,0},{2,3},{3,2},{4,5},{5,4},{6,7},{7,6},{8,9},{9,8},{10,11... | collective-permute-start | bytes 1572872 | tf_op jit(solution)/shard_map/ppermute | solution.py:235
  15.9 5.3 %collective-permute-start.6 = (bf16[64,640]{1,0:T(8,128)(2,1)S(1)}, bf16[64,640]{1,0:T(8,128)(2,1)S(1)}, u32[]{:S(2)}, u32[]{:S(2)}) collective-permute-start(bf16[64,640]{1,0:T(8,128)(2,1)S(1)} %get-tuple-element.29), channel_id=1, source_target_pairs={{0,4},{4,0},{8,12},{12,8},{1,5},{5,1},{9,13},{13,9},{2,6},{6,2},{1... | collective-permute-start | bytes 245768 | tf_op jit(solution)/shard_map/ppermute | solution.py:232
  16.5 3.5 %copy-start.4 = (s32[8]{0:T(128)S(1)}, s32[8]{0:T(128)}, u32[]{:S(2)}) copy-start(s32[8]{0:T(128)} %param.9) | copy-start | bytes 100
  16.5 6.4 %collective-permute-start.7 = (bf16[64,640]{1,0:T(8,128)(2,1)S(1)}, bf16[64,640]{1,0:T(8,128)(2,1)S(1)}, u32[]{:S(2)}, u32[]{:S(2)}) collective-permute-start(bf16[64,640]{1,0:T(8,128)(2,1)S(1)} %get-tuple-element.28), channel_id=1, source_target_pairs={{0,4},{4,0},{8,12},{12,8},{1,5},{5,1},{9,13},{13,9},{2,6},{6,2},{1... | collective-permute-start | bytes 245768 | tf_op jit(solution)/shard_map/ppermute | solution.py:232
  18.0 10.4 %collective-permute-start.9 = (bf16[128,640]{1,0:T(8,128)(2,1)S(1)}, bf16[128,640]{1,0:T(8,128)(2,1)S(1)}, u32[]{:S(2)}, u32[]{:S(2)}) collective-permute-start(bf16[128,640]{1,0:T(8,128)(2,1)S(1)} %get-tuple-element.21), channel_id=1, source_target_pairs={{0,4},{4,0},{8,12},{12,8},{1,5},{5,1},{9,13},{13,9},{2,6},{6,2},{1... | collective-permute-start | bytes 491528 | tf_op jit(solution)/shard_map/ppermute | solution.py:232
  18.6 6.8 %collective-permute-start.5 = (bf16[128,640]{1,0:T(8,128)(2,1)S(1)}, bf16[128,640]{1,0:T(8,128)(2,1)S(1)}, u32[]{:S(2)}, u32[]{:S(2)}) collective-permute-start(bf16[128,640]{1,0:T(8,128)(2,1)S(1)} %collective-permute-done.refs_4_.refs_5_), channel_id=1, source_target_pairs={{0,2},{2,0},{1,3},{3,1},{4,6},{6,4},{5,7},{7,5},{8,10},{10,8},{9,1... | collective-permute-start | bytes 491528 | tf_op jit(solution)/shard_map/ppermute | solution.py:235
  20.2 7.3 %collective-permute-start.8 = (f32[2,1280]{1,0:T(2,128)S(1)}, f32[2,1280]{1,0:T(2,128)S(1)}, u32[]{:S(2)}, u32[]{:S(2)}) collective-permute-start(f32[2,1280]{1,0:T(2,128)S(1)} %collective-permute-done.1.refs_1_), channel_id=1, source_target_pairs={{0,1},{1,0},{2,3},{3,2},{4,5},{5,4},{6,7},{7,6},{8,9},{9,8},{10,11... | collective-permute-start | bytes 30728 | tf_op jit(solution)/shard_map/ppermute | solution.py:235
  21.2 7.2 %collective-permute-start.10 = (bf16[64,640]{1,0:T(8,128)(2,1)S(1)}, bf16[64,640]{1,0:T(8,128)(2,1)S(1)}, u32[]{:S(2)}, u32[]{:S(2)}) collective-permute-start(bf16[64,640]{1,0:T(8,128)(2,1)S(1)} %collective-permute-done.6.refs_2_.refs_7_), channel_id=1, source_target_pairs={{0,2},{2,0},{1,3},{3,1},{4,6},{6,4},{5,7},{7,5},{8,10},{10,8},{9,1... | collective-permute-start | bytes 245768 | tf_op jit(solution)/shard_map/ppermute | solution.py:235
  23.0 5.5 %collective-permute-start.11 = (bf16[64,640]{1,0:T(8,128)(2,1)S(1)}, bf16[64,640]{1,0:T(8,128)(2,1)S(1)}, u32[]{:S(2)}, u32[]{:S(2)}) collective-permute-start(bf16[64,640]{1,0:T(8,128)(2,1)S(1)} %collective-permute-done.7.refs_3_.refs_8_), channel_id=1, source_target_pairs={{0,2},{2,0},{1,3},{3,1},{4,6},{6,4},{5,7},{7,5},{8,10},{10,8},{9,1... | collective-permute-start | bytes 245768 | tf_op jit(solution)/shard_map/ppermute | solution.py:235
  25.7 3.6 %collective-permute-start.13 = (f32[256,256]{1,0:T(8,128)S(1)}, f32[256,256]{1,0:T(8,128)S(1)}, u32[]{:S(2)}, u32[]{:S(2)}) collective-permute-start(f32[256,256]{1,0:T(8,128)S(1)} %shard_map.87.mine), channel_id=1, source_target_pairs={{0,1},{1,0},{2,3},{3,2},{4,5},{5,4},{6,7},{7,6},{8,9},{9,8},{10,11... | collective-permute-start | bytes 786440 | tf_op jit(solution)/shard_map/ppermute | solution.py:235
  25.8 1.8 %copy-start.2 = (f32[1,1280]{1,0:T(1,128)S(1)}, f32[1,1280]{1,0:T(1,128)}, u32[]{:S(2)}) copy-start(f32[1,1280]{1,0:T(1,128)} %pool_ref.1) | copy-start | bytes 15364
  25.8 1.8 %copy-start.3 = (s32[1,28]{1,0:T(1,128)S(1)}, s32[1,28]{1,0:T(1,128)}, u32[]{:S(2)}) copy-start(s32[1,28]{1,0:T(1,128)} %hits_ref) | copy-start | bytes 340
  28.7 2.1 %collective-permute-start.12 = (f32[256,256]{1,0:T(8,128)S(1)}, f32[256,256]{1,0:T(8,128)S(1)}, u32[]{:S(2)}, u32[]{:S(2)}) collective-permute-start(f32[256,256]{1,0:T(8,128)S(1)} %shard_map.90.mine), channel_id=1, source_target_pairs={{0,1},{1,0},{2,3},{3,2},{4,5},{5,4},{6,7},{7,6},{8,9},{9,8},{10,11... | collective-permute-start | bytes 786440 | tf_op jit(solution)/shard_map/ppermute | solution.py:235

commit v11 on v10

--- a/solution.py
+++ b/solution.py
@@ -105,24 +105,24 @@
     libs, (posterior_ref, weight_ref) = refs[:-2], refs[-2:]
     owned, width = libs[0].shape
     target_count = posterior_ref.shape[1]
+    target = lax.broadcasted_iota(jnp.int32, (target_count, 1), 0)
+    counts = jnp.sum(jnp.where(hits_ref[...] == target, 1.0, 0.0), axis=1, keepdims=True)
+    logits = jnp.zeros((target_count, 1), jnp.float32)
+    for at, lib in enumerate(libs):
+        products = jnp.sum(lib[...] * pool_ref[...], axis=1, keepdims=True) / math.sqrt(width)
+        first = owner_ref[at : at + 1, 0:1] * owned
+        for a in range(owned):
+            logits = jnp.where(target == first + a, products[a : a + 1, :], logits)
+    raised = jnp.exp(logits - jnp.max(logits, axis=0, keepdims=True))
+    posterior = raised / jnp.sum(raised, axis=0, keepdims=True)
+    shown = jnp.where(counts > 0.0, logits, -jnp.inf)
+    parts = counts * jnp.exp(shown - jnp.max(shown, axis=0, keepdims=True))
+    weights = parts / jnp.sum(parts, axis=0, keepdims=True)
     lane = lax.broadcasted_iota(jnp.int32, (1, target_count), 1)
-    pool, hits = pool_ref[...], hits_ref[...]
-    logits = jnp.zeros((1, target_count), jnp.float32)
-    counts = jnp.zeros((1, target_count), jnp.float32)
-    for at, lib in enumerate(libs):
-        products = jnp.sum(lib[...] * pool, axis=1, keepdims=True) / math.sqrt(width)
-        first = owner_ref[at : at + 1, :] * owned
-        for a in range(owned):
-            logits = jnp.where(lane == first + a, products[a : a + 1, :], logits)
-    for t in range(target_count):
-        named = jnp.sum(jnp.where(hits == t, 1.0, 0.0), axis=1, keepdims=True)
-        counts = jnp.where(lane == t, named, counts)
-    raised = jnp.exp(logits - jnp.max(logits, axis=1, keepdims=True))
-    posterior_ref[...] = raised / jnp.sum(raised, axis=1, keepdims=True)
-    shown = jnp.where(counts > 0.0, logits, -jnp.inf)
-    parts = counts * jnp.exp(shown - jnp.max(shown, axis=1, keepdims=True))
-    weights = parts / jnp.sum(parts, axis=1, keepdims=True)
-    weights = jnp.sum(jnp.where(slot_ref[...] == lane, weights, 0.0), axis=1, keepdims=True)
+    posterior_ref[...] = jnp.sum(jnp.where(target == lane, posterior, 0.0), axis=0, keepdims=True)
+    weights = jnp.sum(jnp.where(target == lane, weights, 0.0), axis=0, keepdims=True)
+    weights = jnp.where(slot_ref[:, 0:1] == lane, weights, 0.0)
+    weights = jnp.sum(weights, axis=1, keepdims=True)
     weight_ref[...] = jnp.broadcast_to(weights, weight_ref.shape)
 
 
@@ -188,35 +188,31 @@
     return weight * jnp.dot(alignment, target, preferred_element_type=jnp.float32)
 
 
-def profile_kernel(groups, pieces, weight_ref, *refs):
-    aligned, blocks, out_ref = refs[: len(groups)], refs[len(groups) : -1], refs[-1]
-    acc, at = None, 0
-    for group, slots in zip(aligned, groups):
-        rows = group.shape[1] // len(slots)
-        for i, slot in enumerate(slots):
-            count = pieces.get(slot, 1)
-            term = weighted_term(
-                weight_ref[slot : slot + 1, 0:1],
-                group[:, i * rows : (i + 1) * rows],
-                blocks[at : at + count],
-            )
-            acc = term if acc is None else acc + term
-            at += count
-    out_ref[...] = acc
-
-
-def last_kernel(model_width, targets, len_ref, sharp_ref, weight_ref, mine, other, *refs):
-    blocks, (acc_ref, out_ref) = refs[:-2], refs[-2:]
-    rows = mine.shape[1] // len(targets)
-    acc = acc_ref[...]
-    for at, (slot, count) in enumerate(targets):
-        part = pl.ds(at * rows, rows)
-        similar = (mine[:, part] + other[:, part]) * (1.0 / math.sqrt(model_width))
-        alignment = align_block(similar, len_ref[slot : slot + 1, :rows], sharp_ref[:, 0:1])
-        acc += weighted_term(
-            weight_ref[slot : slot + 1, 0:1], alignment.astype(jnp.bfloat16), blocks[:count]
-        )
-        blocks = blocks[count:]
+def profile_kernel(model_width, groups, targets, *refs):
+    weight_ref, aligned, refs = refs[0], refs[1 : 1 + len(groups)], refs[1 + len(groups) :]
+    blocks, out_ref = refs[:-1], refs[-1]
+    acc = None
+
+    def add(acc, target, alignment, blocks):
+        slot, count = target
+        term = weighted_term(weight_ref[slot : slot + 1, 0:1], alignment, blocks[:count])
+        return (term if acc is None else acc + term), blocks[count:]
+
+    for group, members in zip(aligned, groups):
+        rows = group.shape[1] // len(members)
+        for at, target in enumerate(members):
+            acc, blocks = add(acc, target, group[:, at * rows : (at + 1) * rows], blocks)
+    if targets:
+        len_ref, sharp_ref, mine, other, *blocks = blocks
+        rows = mine.shape[1] // len(targets)
+        for at, target in enumerate(targets):
+            part = pl.ds(at * rows, rows)
+            similar = (mine[:, part] + other[:, part]) * (1.0 / math.sqrt(model_width))
+            lengths = len_ref[target[0] : target[0] + 1, :rows]
+            alignment = align_block(similar, lengths, sharp_ref[:, 0:1])
+            acc, blocks = add(acc, target, alignment.astype(jnp.bfloat16), blocks)
+    if len(blocks):
+        acc += blocks[0][...]
     out_ref[...] = acc.astype(out_ref.dtype)
 
 
@@ -240,82 +236,104 @@
     split = [(2 * i + c, 2 * (i ^ (1 + c)) + c) for i in range(4) for c in range(2)]
     pool_split = lax.ppermute(target_pool, ("tgt", "rep"), split)
     pool_last = from_peer(target_pool, 3)
-    pool_other = across(pool_split, "rep")
-    owners = jnp.stack([at_tgt, at_tgt ^ (1 + at_rep), at_tgt ^ (2 - at_rep), at_tgt ^ 3])
 
     share = lax.dynamic_index_in_dim(target_res, at_qry, 0, keepdims=False)
     rest = lax.dynamic_index_in_dim(target_res, 1 - at_qry, 0, keepdims=False)
     far = from_peer(share, 2)
     near = from_peer(share, 1)
 
+    cross = [(2 * i + x, 2 * (i ^ 1) + 1 - x) for i in range(4) for x in range(2)]
+
     bases = [2 * (at_tgt ^ k) for k in range(4)]
     slots = [bases[0], bases[0] + 1]
     for base in bases[1:]:
         slots += [base + at_qry, base + 1 - at_qry]
-    slots = jnp.stack(slots).astype(jnp.int32)[:, None]
-    named = slots == jnp.arange(len(target_len))[None]
+    owners = [at_tgt, at_tgt ^ (1 + at_rep), at_tgt ^ (2 - at_rep), at_tgt ^ 3]
+    table = (len(target_len), target_rows)
+    slots = jnp.broadcast_to(jnp.stack(slots)[:, None], table)
+    owners = jnp.broadcast_to(jnp.stack(owners + owners)[:, None], table)
+    named = slots[:, : table[0]] == jnp.arange(table[0])[None]
     lengths = jnp.sum(jnp.where(named, target_len[None], 0), axis=1, keepdims=True)
-    lengths = jnp.broadcast_to(lengths.astype(jnp.float32), (len(target_len), target_rows))
+    lengths = jnp.broadcast_to(lengths.astype(jnp.float32), table)
     half_sharp = jnp.broadcast_to(0.5 * sharpness, (1, target_rows))
 
     def aligned(slots, mine, other):
         return align(model_width, slots, lengths, half_sharp, mine, other)
 
-    far = after(far, pool_split, pool_last)
+    def add_up(groups, targets, dtype, *operands):
+        return call_kernel(
+            functools.partial(profile_kernel, model_width, groups, targets),
+            jax.ShapeDtypeStruct(query.shape, dtype),
+            weights,
+            *operands,
+        )
+
+    own_blocks = [target_res[0], target_res[1]]
+    own = partial_similar(after(query, share), own_blocks)
+    own_other = across(own, "rep")
+    own_aligned = aligned((0, 1), own, own_other)
+
+    far = after(far, pool_split, pool_last, own_aligned, slots, owners)
     near = after(near, far)
     far = after(far, near)
-    half = target_rows // 2
-    last = [from_peer(far[:half], 1), from_peer(far[half:], 1)]
+    last_rest = lax.ppermute(far, ("tgt", "qry"), cross)
+    last = from_peer(far, 1)
+    far_rest = across(far, "qry")
     near_rest = from_peer(after(rest, far), 1)
 
-    one_blocks = [target_res[0], target_res[1], near, far]
+    one_blocks = [near, far]
     one = partial_similar(query, one_blocks)
     one_other = across(one, "rep")
-    far_rest = across(after(far, one_other), "qry")
-
-    last_rest = [across(piece, "qry") for piece in last]
-    two_blocks = [far_rest, *last]
-    two = partial_similar(query, two_blocks)
-    two_other = across(two, "rep")
-    one_aligned = aligned((0, 1, 2, 4), after(one, two), one_other)
-
+    one_aligned = aligned((2, 4), one, one_other)
+    pool_other = across(pool_split, "rep")
     posterior, weights = call_kernel(
         weigh_kernel,
         (
-            jax.ShapeDtypeStruct((1, len(target_len)), jnp.float32),
-            jax.ShapeDtypeStruct((len(target_len), target_rows), jnp.float32),
+            jax.ShapeDtypeStruct((1, table[0]), jnp.float32),
+            jax.ShapeDtypeStruct(table, jnp.float32),
         ),
         slots,
-        after(hits, two),
+        after(hits, one_aligned),
         query_pool,
-        owners.astype(jnp.int32)[:, None],
+        owners,
         target_pool,
         pool_split,
         pool_other,
         pool_last,
     )
-
-    three_blocks = [near_rest, *last_rest]
-    three = partial_similar(after(query, weights, one_aligned), three_blocks)
+    acc = add_up(
+        (((0, 1), (1, 1)), ((2, 1), (4, 1))),
+        (),
+        jnp.float32,
+        own_aligned,
+        one_aligned,
+        *own_blocks,
+        *one_blocks,
+    )
+
+    two_blocks = [far_rest, near_rest]
+    two = partial_similar(after(query, acc), two_blocks)
+    two_other = across(two, "rep")
+    three_blocks = [last, last_rest]
+    three = partial_similar(after(query, two), three_blocks)
     three_other = across(three, "rep")
-    two_aligned = aligned((5, 6), after(two, three), two_other)
-    acc = call_kernel(
-        functools.partial(
-            profile_kernel, ((0, 1, 2, 4), (5, 6)), {6: 2}
-        ),
-        jax.ShapeDtypeStruct(query.shape, jnp.float32),
-        weights,
-        one_aligned,
-        two_aligned,
-        *one_blocks,
-        *two_blocks,
-    )
-    profile = call_kernel(
-        functools.partial(last_kernel, model_width, ((3, 1), (7, 2))),
-        jax.ShapeDtypeStruct(query.shape, jnp.bfloat16),
+    acc = add_up(
+        (),
+        ((5, 1), (3, 1)),
+        jnp.float32,
         lengths,
         half_sharp,
-        weights,
+        after(two, three),
+        two_other,
+        *two_blocks,
+        acc,
+    )
+    profile = add_up(
+        (),
+        ((6, 1), (7, 1)),
+        jnp.bfloat16,
+        lengths,
+        half_sharp,
         three,
         three_other,
         *three_blocks,

time: 32.9 us -> 34.5 us (1.049)
  waiting for transfers between devices: 7.04 us -> 11.4 us
  starting transfers between devices: 15.4 us -> 11.9 us
  local copies, waits for them, and re-layouts: 1.63 us -> 2.24 us
    ppermute x7 -> x6, starting transfers between devices: 5.25 us -> 2.23 us  [across(): return lax.ppermute(array, axis, [(0, 1), (1, 0)])]
    ppermute x7 -> x6, waiting for transfers between devices: 0.02 us -> 2.66 us  [across(): return lax.ppermute(array, axis, [(0, 1), (1, 0)])]
    ppermute x0 -> x1, waiting for transfers between devices: none -> 2.06 us  [per_device_by_target(): last_rest = lax.ppermute(far, ('tgt', 'qry'), cross)]
    ppermute x1, waiting for transfers between devices: 4.96 us -> 2.98 us  [per_device_by_target(): pool_split = lax.ppermute(target_pool, ('tgt', 'rep'), split)]
    ppermute x6 -> x5, starting transfers between devices: 9.7 us -> 7.78 us  [from_peer(): return lax.ppermute(array, 'tgt', [(i, i ^ k) for i in range(4)])]
    ppermute x6 -> x5, waiting for transfers between devices: 2.07 us -> 3.69 us  [from_peer(): return lax.ppermute(array, 'tgt', [(i, i ^ k) for i in range(4)])]
    ppermute x0 -> x1, starting transfers between devices: none -> 1.42 us  [per_device_by_target(): last_rest = lax.ppermute(far, ('tgt', 'qry'), cross)]
    unnamed x10, local copies, waits for them, and re-layouts: 0.02 us -> 0.6 us
  transfers between devices with their start and end apart: 14 -> 13, of which waited for: 4 -> 8; matrix products, arithmetic and copies ran while one was open for 2% -> 2% of each run, Pallas kernels for 14% -> 14%
where the time goes in v11:
time: 34.5 us; the launch traced here: 34.4 us
  starting transfers between devices  11.9 us (34%)
  waiting for transfers between devices  11.4 us (33%)
  Pallas kernels  7.24 us (21%)
  local copies, waits for them, and re-layouts  2.24 us (6%)
  between operations  1.44 us (4%)
    ppermute x5, starting transfers between devices, from_peer(): return lax.ppermute(array, 'tgt', [(i, i ^ k) for i in range(4)])  7.78 us
    pallas_call x10, Pallas kernels, call_kernel(): pl.pallas_call(kernel, out_shape=out_shape, in_specs=[VMEM] * len(operand...  7.24 us
    ppermute x5, waiting for transfers between devices, from_peer(): return lax.ppermute(array, 'tgt', [(i, i ^ k) for i in range(4)])  3.69 us
    ppermute x1, waiting for transfers between devices, per_device_by_target(): pool_split = lax.ppermute(target_pool, ('tgt', 'rep'), split)  2.98 us
    ppermute x6, waiting for transfers between devices, across(): return lax.ppermute(array, axis, [(0, 1), (1, 0)])  2.66 us
    ppermute x6, starting transfers between devices, across(): return lax.ppermute(array, axis, [(0, 1), (1, 0)])  2.23 us
    ppermute x1, waiting for transfers between devices, per_device_by_target(): last_rest = lax.ppermute(far, ('tgt', 'qry'), cross)  2.06 us
    ppermute x1, starting transfers between devices, per_device_by_target(): last_rest = lax.ppermute(far, ('tgt', 'qry'), cross)  1.42 us
  transfers between devices with their start and end apart: 13, of which 8 were waited for; matrix products, arithmetic and copies ran while one was open for 2% of the time, Pallas kernels for 14%

profile of v11, /device:TPU:0, one launch (start us, length us, event | category | flops | bytes accessed | tf_op | source)
XLA Modules:
  0.0 34.4 jit_solution(1323281776015858159)
XLA Ops:
  0.6 1.3 %dynamic-slice_bitcast_fusion = (bf16[128,640]{1,0:T(8,128)(2,1)S(1)}, bf16[128,640]{1,0:T(8,128)(2,1)S(1)}, bf16[128,640]{1,0:T(8,128)(2,1)S(1)}, bf16[128,640]{1,0:T(8,128)(2,1)S(1)}) fusion(bf16[2,128,640]{2,1,0:T(8,128)(2,1)} %param.8, s32[]{:T(128)S(6)} %select_n.13, s32[]{:T(128)S(6)} %select_n.12), kind=kLoop, calls=%fused_computation | loop fusion | bytes 1310728 | tf_op jit(solution)/shard_map/jit(dynamic_index_in_dim)/squeeze | solution.py:241
  2.2 0.5 %collective-permute-start.4 = (f32[256,256]{1,0:T(8,128)S(1)}, f32[256,256]{1,0:T(8,128)S(1)}, u32[]{:S(2)}, u32[]{:S(2)}) collective-permute-start(f32[256,256]{1,0:T(8,128)S(1)} %shard_map.86.mine), channel_id=1, source_target_pairs={{0,1},{1,0},{2,3},{3,2},{4,5},{5,4},{6,7},{7,6},{8,9},{9,8},{10,11... | collective-permute-start | bytes 786440 | tf_op jit(solution)/shard_map/ppermute | solution.py:231
  2.8 3.7 %collective-permute-start.1 = (bf16[128,640]{1,0:T(8,128)(2,1)S(1)}, bf16[128,640]{1,0:T(8,128)(2,1)S(1)}, u32[]{:S(2)}, u32[]{:S(2)}) collective-permute-start(bf16[128,640]{1,0:T(8,128)(2,1)S(1)} %get-tuple-element.26), channel_id=1, source_target_pairs={{0,8},{4,12},{8,0},{12,4},{1,9},{5,13},{9,1},{13,5},{2,10},{6,14},... | collective-permute-start | bytes 491528 | tf_op jit(solution)/shard_map/ppermute | solution.py:228
  6.4 1.6 %collective-permute-start = (bf16[128,640]{1,0:T(8,128)(2,1)S(1)}, bf16[128,640]{1,0:T(8,128)(2,1)S(1)}, u32[]{:S(2)}, u32[]{:S(2)}) collective-permute-start(bf16[128,640]{1,0:T(8,128)(2,1)S(1)} %get-tuple-element.26), channel_id=1, source_target_pairs={{0,4},{4,0},{8,12},{12,8},{1,5},{5,1},{9,13},{13,9},{2,6},{6,2},{1... | collective-permute-start | bytes 491528 | tf_op jit(solution)/shard_map/ppermute | solution.py:228
  8.0 0.5 %collective-permute-start.2 = (f32[2,1280]{1,0:T(2,128)S(1)}, f32[2,1280]{1,0:T(2,128)S(1)}, u32[]{:S(2)}, u32[]{:S(2)}) collective-permute-start(f32[2,1280]{1,0:T(2,128)S(1)} %copy-done.1), channel_id=1, source_target_pairs={{0,4},{1,9},{4,0},{5,13},{8,12},{9,1},{12,8},{13,5},{2,6},{3,11},{... | collective-permute-start | bytes 30728 | tf_op jit(solution)/shard_map/ppermute | solution.py:237
  8.4 1.3 %collective-permute-start.3 = (f32[2,1280]{1,0:T(2,128)S(1)}, f32[2,1280]{1,0:T(2,128)S(1)}, u32[]{:S(2)}, u32[]{:S(2)}) collective-permute-start(f32[2,1280]{1,0:T(2,128)S(1)} %copy-done.1), channel_id=1, source_target_pairs={{0,12},{4,8},{8,4},{12,0},{1,13},{5,9},{9,5},{13,1},{2,14},{6,10},... | collective-permute-start | bytes 30728 | tf_op jit(solution)/shard_map/ppermute | solution.py:228
  9.9 0.6 %copy-done.4 = s32[8]{0:T(128)S(1)} copy-done((s32[8]{0:T(128)S(1)}, s32[8]{0:T(128)}, u32[]{:S(2)}) %copy-start.4) | copy-done | bytes 56
  11.5 0.8 %shard_map.87.refs_1_ = bf16[256,256]{1,0:T(8,128)(2,1)S(1)} custom-call(f32[8,128]{1,0:T(8,128)S(1)} %broadcast_in_dim.25.len_ref.refs_1_, f32[1,128]{1,0:T(1,128)S(1)} %broadcast_in_dim.44.sharp_ref.refs_2_, f32[256,256]{1,0:T(8,128)S(1)} %shard_map.86.mine, f32[256,256]{1,0:T(8,128)S(1)} %collective-permute-done.4.other), custom_call_target="tpu_custom_call" | custom-call | tf_op jit(solution)/shard_map/pallas_call | solution.py:93
  12.3 3.0 %collective-permute-done.2.refs_1_ = f32[2,1280]{1,0:T(2,128)S(1)} collective-permute-done((f32[2,1280]{1,0:T(2,128)S(1)}, f32[2,1280]{1,0:T(2,128)S(1)}, u32[]{:S(2)}, u32[]{:S(2)}) %collective-permute-start.2) | collective-permute-done | bytes 10272 | tf_op jit(solution)/shard_map/ppermute | solution.py:237
  15.2 1.0 %collective-permute-done.3.refs_3_ = f32[2,1280]{1,0:T(2,128)S(1)} collective-permute-done((f32[2,1280]{1,0:T(2,128)S(1)}, f32[2,1280]{1,0:T(2,128)S(1)}, u32[]{:S(2)}, u32[]{:S(2)}) %collective-permute-start.3) | collective-permute-done | bytes 10272 | tf_op jit(solution)/shard_map/ppermute | solution.py:228
  16.8 0.6 %collective-permute-start.8 = (bf16[128,640]{1,0:T(8,128)(2,1)S(1)}, bf16[128,640]{1,0:T(8,128)(2,1)S(1)}, u32[]{:S(2)}, u32[]{:S(2)}) collective-permute-start(bf16[128,640]{1,0:T(8,128)(2,1)S(1)} %get-tuple-element.20), channel_id=1, source_target_pairs={{0,4},{4,0},{8,12},{12,8},{1,5},{5,1},{9,13},{13,9},{2,6},{6,2},{1... | collective-permute-start | bytes 491528 | tf_op jit(solution)/shard_map/ppermute | solution.py:228
  17.5 1.5 %collective-permute-start.7 = (bf16[128,640]{1,0:T(8,128)(2,1)S(1)}, bf16[128,640]{1,0:T(8,128)(2,1)S(1)}, u32[]{:S(2)}, u32[]{:S(2)}) collective-permute-start(bf16[128,640]{1,0:T(8,128)(2,1)S(1)} %collective-permute-done.1.refs_2_.refs_6_), channel_id=1, source_target_pairs={{0,2},{2,0},{1,3},{3,1},{4,6},{6,4},{5,7},{7,5},{8,10},{10,8},{9,1... | collective-permute-start | bytes 491528 | tf_op jit(solution)/shard_map/ppermute | solution.py:231
  19.0 1.4 %collective-permute-start.10 = (bf16[128,640]{1,0:T(8,128)(2,1)S(1)}, bf16[128,640]{1,0:T(8,128)(2,1)S(1)}, u32[]{:S(2)}, u32[]{:S(2)}) collective-permute-start(bf16[128,640]{1,0:T(8,128)(2,1)S(1)} %collective-permute-done.1.refs_2_.refs_6_), channel_id=1, source_target_pairs={{0,6},{2,4},{4,2},{6,0},{8,14},{10,12},{12,10},{14,8},{1,7},{3,5},... | collective-permute-start | bytes 491528 | tf_op jit(solution)/shard_map/ppermute | solution.py:279
  20.4 0.6 %collective-permute-start.9 = (bf16[128,640]{1,0:T(8,128)(2,1)S(1)}, bf16[128,640]{1,0:T(8,128)(2,1)S(1)}, u32[]{:S(2)}, u32[]{:S(2)}) collective-permute-start(bf16[128,640]{1,0:T(8,128)(2,1)S(1)} %collective-permute-done.1.refs_2_.refs_6_), channel_id=1, source_target_pairs={{0,4},{4,0},{8,12},{12,8},{1,5},{5,1},{9,13},{13,9},{2,6},{6,2},{1... | collective-permute-start | bytes 491528 | tf_op jit(solution)/shard_map/ppermute | solution.py:228
  21.0 0.8 %shard_map.89.refs_2_ = bf16[256,256]{1,0:T(8,128)(2,1)S(1)} custom-call(f32[8,128]{1,0:T(8,128)S(1)} %broadcast_in_dim.25.len_ref.refs_1_, f32[1,128]{1,0:T(1,128)S(1)} %broadcast_in_dim.44.sharp_ref.refs_2_, f32[256,256]{1,0:T(8,128)S(1)} %shard_map.88.mine, f32[256,256]{1,0:T(8,128)S(1)} %collective-permute-done.5.other), custom_call_target="tpu_custom_call" | custom-call | tf_op jit(solution)/shard_map/pallas_call | solution.py:93
  21.8 0.4 %collective-permute-done.6.refs_2_ = f32[2,1280]{1,0:T(2,128)S(1)} collective-permute-done((f32[2,1280]{1,0:T(2,128)S(1)}, f32[2,1280]{1,0:T(2,128)S(1)}, u32[]{:S(2)}, u32[]{:S(2)}) %collective-permute-start.6) | collective-permute-done | bytes 10272 | tf_op jit(solution)/shard_map/ppermute | solution.py:231
  22.1 0.7 %shard_map.90 = (f32[1,8]{1,0:T(1,128)}, f32[8,128]{1,0:T(8,128)S(1)}) custom-call(s32[8,128]{1,0:T(8,128)S(1)} %broadcast_in_dim.22.slot_ref, s32[1,28]{1,0:T(1,128)S(1)} %copy-done.3, f32[1,1280]{1,0:T(1,128)S(1)} %copy-done.2, s32[8,128]{1,0:T(8,128)S(1)} %broadcast_in_dim.45.owner_ref, f32[2,1280]{1,0:T(2,128)S(1)} %copy-done.1, ...), custom_call_target="tpu_custom_call" | custom-call | tf_op jit(solution)/shard_map/pallas_call | solution.py:93
  22.9 0.5 %shard_map.91.refs_7_ = f32[256,640]{1,0:T(8,128)S(1)} custom-call(f32[8,128]{1,0:T(8,128)S(1)} %get-tuple-element.18.refs_0_, bf16[256,256]{1,0:T(8,128)(2,1)S(1)} %shard_map.87.refs_1_, bf16[256,256]{1,0:T(8,128)(2,1)S(1)} %shard_map.89.refs_2_, bf16[128,640]{1,0:T(8,128)(2,1)S(1)} %get-tuple-element.25.refs_1_.refs_3_, ...), custom_call_target="tpu_custom_call" | custom-call | tf_op jit(solution)/shard_map/pallas_call | solution.py:93
  23.4 0.5 %collective-permute-done.8.refs_2_.refs_6_ = bf16[128,640]{1,0:T(8,128)(2,1)S(1)} collective-permute-done((bf16[128,640]{1,0:T(8,128)(2,1)S(1)}, bf16[128,640]{1,0:T(8,128)(2,1)S(1)}, u32[]{:S(2)}, u32[]{:S(2)}) %collective-permute-start.8) | collective-permute-done | bytes 163872 | tf_op jit(solution)/shard_map/ppermute | solution.py:228
  23.9 2.0 %collective-permute-done.7.refs_1_.refs_5_ = bf16[128,640]{1,0:T(8,128)(2,1)S(1)} collective-permute-done((bf16[128,640]{1,0:T(8,128)(2,1)S(1)}, bf16[128,640]{1,0:T(8,128)(2,1)S(1)}, u32[]{:S(2)}, u32[]{:S(2)}) %collective-permute-start.7) | collective-permute-done | bytes 163872 | tf_op jit(solution)/shard_map/ppermute | solution.py:231
  26.3 2.1 %collective-permute-done.10.refs_2_.refs_6_ = bf16[128,640]{1,0:T(8,128)(2,1)S(1)} collective-permute-done((bf16[128,640]{1,0:T(8,128)(2,1)S(1)}, bf16[128,640]{1,0:T(8,128)(2,1)S(1)}, u32[]{:S(2)}, u32[]{:S(2)}) %collective-permute-start.10) | collective-permute-done | bytes 163872 | tf_op jit(solution)/shard_map/ppermute | solution.py:279
  28.3 2.2 %collective-permute-done.9.refs_1_.refs_5_ = bf16[128,640]{1,0:T(8,128)(2,1)S(1)} collective-permute-done((bf16[128,640]{1,0:T(8,128)(2,1)S(1)}, bf16[128,640]{1,0:T(8,128)(2,1)S(1)}, u32[]{:S(2)}, u32[]{:S(2)}) %collective-permute-start.9) | collective-permute-done | bytes 163872 | tf_op jit(solution)/shard_map/ppermute | solution.py:228
  30.9 1.2 %shard_map.94.refs_7_ = f32[256,640]{1,0:T(8,128)S(1)} custom-call(f32[8,128]{1,0:T(8,128)S(1)} %get-tuple-element.18.refs_0_, f32[8,128]{1,0:T(8,128)S(1)} %broadcast_in_dim.25.len_ref.refs_1_, f32[1,128]{1,0:T(1,128)S(1)} %broadcast_in_dim.44.sharp_ref.refs_2_, f32[256,256]{1,0:T(8,128)S(1)} %shard_map.92.refs_3_, ...), custom_call_target="tpu_custom_call" | custom-call | tf_op jit(solution)/shard_map/pallas_call | solution.py:93
  32.4 2.0 %shard_map.95 = bf16[256,640]{1,0:T(8,128)(2,1)} custom-call(f32[8,128]{1,0:T(8,128)S(1)} %get-tuple-element.18.refs_0_, f32[8,128]{1,0:T(8,128)S(1)} %broadcast_in_dim.25.len_ref.refs_1_, f32[1,128]{1,0:T(1,128)S(1)} %broadcast_in_dim.44.sharp_ref.refs_2_, f32[256,256]{1,0:T(8,128)S(1)} %shard_map.93.refs_3_, ...), custom_call_target="tpu_custom_call" | custom-call | tf_op jit(solution)/shard_map/pallas_call | solution.py:93
  (31 shorter events, 2.3 us)
Async XLA Ops:
  0.6 1.3 %copy-start = (bf16[1,256,640]{2,1,0:T(8,128)(2,1)S(1)}, bf16[1,256,640]{2,1,0:T(8,128)(2,1)}, u32[]{:S(2)}) copy-start(bf16[1,256,640]{2,1,0:T(8,128)(2,1)} %param.7) | copy-start | bytes 983044
  1.9 6.1 %copy-start.1 = (f32[2,1280]{1,0:T(2,128)S(1)}, f32[2,1280]{1,0:T(2,128)}, u32[]{:S(2)}) copy-start(f32[2,1280]{1,0:T(2,128)} %refs_0_.1) | copy-start | bytes 30724
  2.2 9.2 %collective-permute-start.4 = (f32[256,256]{1,0:T(8,128)S(1)}, f32[256,256]{1,0:T(8,128)S(1)}, u32[]{:S(2)}, u32[]{:S(2)}) collective-permute-start(f32[256,256]{1,0:T(8,128)S(1)} %shard_map.86.mine), channel_id=1, source_target_pairs={{0,1},{1,0},{2,3},{3,2},{4,5},{5,4},{6,7},{7,6},{8,9},{9,8},{10,11... | collective-permute-start | bytes 786440 | tf_op jit(solution)/shard_map/ppermute | solution.py:231
  2.8 13.5 %collective-permute-start.1 = (bf16[128,640]{1,0:T(8,128)(2,1)S(1)}, bf16[128,640]{1,0:T(8,128)(2,1)S(1)}, u32[]{:S(2)}, u32[]{:S(2)}) collective-permute-start(bf16[128,640]{1,0:T(8,128)(2,1)S(1)} %get-tuple-element.26), channel_id=1, source_target_pairs={{0,8},{4,12},{8,0},{12,4},{1,9},{5,13},{9,1},{13,5},{2,10},{6,14},... | collective-permute-start | bytes 491528 | tf_op jit(solution)/shard_map/ppermute | solution.py:228
  6.4 10.0 %collective-permute-start = (bf16[128,640]{1,0:T(8,128)(2,1)S(1)}, bf16[128,640]{1,0:T(8,128)(2,1)S(1)}, u32[]{:S(2)}, u32[]{:S(2)}) collective-permute-start(bf16[128,640]{1,0:T(8,128)(2,1)S(1)} %get-tuple-element.26), channel_id=1, source_target_pairs={{0,4},{4,0},{8,12},{12,8},{1,5},{5,1},{9,13},{13,9},{2,6},{6,2},{1... | collective-permute-start | bytes 491528 | tf_op jit(solution)/shard_map/ppermute | solution.py:228
  8.0 7.2 %collective-permute-start.2 = (f32[2,1280]{1,0:T(2,128)S(1)}, f32[2,1280]{1,0:T(2,128)S(1)}, u32[]{:S(2)}, u32[]{:S(2)}) collective-permute-start(f32[2,1280]{1,0:T(2,128)S(1)} %copy-done.1), channel_id=1, source_target_pairs={{0,4},{1,9},{4,0},{5,13},{8,12},{9,1},{12,8},{13,5},{2,6},{3,11},{... | collective-permute-start | bytes 30728 | tf_op jit(solution)/shard_map/ppermute | solution.py:237
  8.4 7.8 %collective-permute-start.3 = (f32[2,1280]{1,0:T(2,128)S(1)}, f32[2,1280]{1,0:T(2,128)S(1)}, u32[]{:S(2)}, u32[]{:S(2)}) collective-permute-start(f32[2,1280]{1,0:T(2,128)S(1)} %copy-done.1), channel_id=1, source_target_pairs={{0,12},{4,8},{8,4},{12,0},{1,13},{5,9},{9,5},{13,1},{2,14},{6,10},... | collective-permute-start | bytes 30728 | tf_op jit(solution)/shard_map/ppermute | solution.py:228
  9.8 0.7 %copy-start.4 = (s32[8]{0:T(128)S(1)}, s32[8]{0:T(128)}, u32[]{:S(2)}) copy-start(s32[8]{0:T(128)} %param.9) | copy-start | bytes 100
  16.7 4.2 %collective-permute-start.5 = (f32[256,256]{1,0:T(8,128)S(1)}, f32[256,256]{1,0:T(8,128)S(1)}, u32[]{:S(2)}, u32[]{:S(2)}) collective-permute-start(f32[256,256]{1,0:T(8,128)S(1)} %shard_map.88.mine), channel_id=1, source_target_pairs={{0,1},{1,0},{2,3},{3,2},{4,5},{5,4},{6,7},{7,6},{8,9},{9,8},{10,11... | collective-permute-start | bytes 786440 | tf_op jit(solution)/shard_map/ppermute | solution.py:231
  16.8 5.3 %copy-start.2 = (f32[1,1280]{1,0:T(1,128)S(1)}, f32[1,1280]{1,0:T(1,128)}, u32[]{:S(2)}) copy-start(f32[1,1280]{1,0:T(1,128)} %pool_ref.1) | copy-start | bytes 15364
  16.8 5.3 %copy-start.3 = (s32[1,28]{1,0:T(1,128)S(1)}, s32[1,28]{1,0:T(1,128)}, u32[]{:S(2)}) copy-start(s32[1,28]{1,0:T(1,128)} %hits_ref) | copy-start | bytes 340
  16.8 7.1 %collective-permute-start.8 = (bf16[128,640]{1,0:T(8,128)(2,1)S(1)}, bf16[128,640]{1,0:T(8,128)(2,1)S(1)}, u32[]{:S(2)}, u32[]{:S(2)}) collective-permute-start(bf16[128,640]{1,0:T(8,128)(2,1)S(1)} %get-tuple-element.20), channel_id=1, source_target_pairs={{0,4},{4,0},{8,12},{12,8},{1,5},{5,1},{9,13},{13,9},{2,6},{6,2},{1... | collective-permute-start | bytes 491528 | tf_op jit(solution)/shard_map/ppermute | solution.py:228
  17.5 8.4 %collective-permute-start.7 = (bf16[128,640]{1,0:T(8,128)(2,1)S(1)}, bf16[128,640]{1,0:T(8,128)(2,1)S(1)}, u32[]{:S(2)}, u32[]{:S(2)}) collective-permute-start(bf16[128,640]{1,0:T(8,128)(2,1)S(1)} %collective-permute-done.1.refs_2_.refs_6_), channel_id=1, source_target_pairs={{0,2},{2,0},{1,3},{3,1},{4,6},{6,4},{5,7},{7,5},{8,10},{10,8},{9,1... | collective-permute-start | bytes 491528 | tf_op jit(solution)/shard_map/ppermute | solution.py:231
  19.0 9.4 %collective-permute-start.10 = (bf16[128,640]{1,0:T(8,128)(2,1)S(1)}, bf16[128,640]{1,0:T(8,128)(2,1)S(1)}, u32[]{:S(2)}, u32[]{:S(2)}) collective-permute-start(bf16[128,640]{1,0:T(8,128)(2,1)S(1)} %collective-permute-done.1.refs_2_.refs_6_), channel_id=1, source_target_pairs={{0,6},{2,4},{4,2},{6,0},{8,14},{10,12},{12,10},{14,8},{1,7},{3,5},... | collective-permute-start | bytes 491528 | tf_op jit(solution)/shard_map/ppermute | solution.py:279
  20.4 10.1 %collective-permute-start.9 = (bf16[128,640]{1,0:T(8,128)(2,1)S(1)}, bf16[128,640]{1,0:T(8,128)(2,1)S(1)}, u32[]{:S(2)}, u32[]{:S(2)}) collective-permute-start(bf16[128,640]{1,0:T(8,128)(2,1)S(1)} %collective-permute-done.1.refs_2_.refs_6_), channel_id=1, source_target_pairs={{0,4},{4,0},{8,12},{12,8},{1,5},{5,1},{9,13},{13,9},{2,6},{6,2},{1... | collective-permute-start | bytes 491528 | tf_op jit(solution)/shard_map/ppermute | solution.py:228
  21.0 1.2 %collective-permute-start.6 = (f32[2,1280]{1,0:T(2,128)S(1)}, f32[2,1280]{1,0:T(2,128)S(1)}, u32[]{:S(2)}, u32[]{:S(2)}) collective-permute-start(f32[2,1280]{1,0:T(2,128)S(1)} %collective-permute-done.2.refs_1_), channel_id=1, source_target_pairs={{0,1},{1,0},{2,3},{3,2},{4,5},{5,4},{6,7},{7,6},{8,9},{9,8},{10,11... | collective-permute-start | bytes 30728 | tf_op jit(solution)/shard_map/ppermute | solution.py:231
  26.2 4.7 %collective-permute-start.12 = (f32[256,256]{1,0:T(8,128)S(1)}, f32[256,256]{1,0:T(8,128)S(1)}, u32[]{:S(2)}, u32[]{:S(2)}) collective-permute-start(f32[256,256]{1,0:T(8,128)S(1)} %shard_map.92.refs_3_), channel_id=1, source_target_pairs={{0,1},{1,0},{2,3},{3,2},{4,5},{5,4},{6,7},{7,6},{8,9},{9,8},{10,11... | collective-permute-start | bytes 786440 | tf_op jit(solution)/shard_map/ppermute | solution.py:231
  30.8 1.6 %collective-permute-start.11 = (f32[256,256]{1,0:T(8,128)S(1)}, f32[256,256]{1,0:T(8,128)S(1)}, u32[]{:S(2)}, u32[]{:S(2)}) collective-permute-start(f32[256,256]{1,0:T(8,128)S(1)} %shard_map.93.refs_3_), channel_id=1, source_target_pairs={{0,1},{1,0},{2,3},{3,2},{4,5},{5,4},{6,7},{7,6},{8,9},{9,8},{10,11... | collective-permute-start | bytes 786440 | tf_op jit(solution)/shard_map/ppermute | solution.py:231

commit v12 on v11

--- a/solution.py
+++ b/solution.py
@@ -236,13 +236,12 @@
     split = [(2 * i + c, 2 * (i ^ (1 + c)) + c) for i in range(4) for c in range(2)]
     pool_split = lax.ppermute(target_pool, ("tgt", "rep"), split)
     pool_last = from_peer(target_pool, 3)
+    pool_split = after(pool_split, pool_last)
 
     share = lax.dynamic_index_in_dim(target_res, at_qry, 0, keepdims=False)
     rest = lax.dynamic_index_in_dim(target_res, 1 - at_qry, 0, keepdims=False)
     far = from_peer(share, 2)
     near = from_peer(share, 1)
-
-    cross = [(2 * i + x, 2 * (i ^ 1) + 1 - x) for i in range(4) for x in range(2)]
 
     bases = [2 * (at_tgt ^ k) for k in range(4)]
     slots = [bases[0], bases[0] + 1]
@@ -268,24 +267,19 @@
             *operands,
         )
 
-    own_blocks = [target_res[0], target_res[1]]
-    own = partial_similar(after(query, share), own_blocks)
-    own_other = across(own, "rep")
-    own_aligned = aligned((0, 1), own, own_other)
-
-    far = after(far, pool_split, pool_last, own_aligned, slots, owners)
+    far = after(far, pool_split, pool_last, slots, owners, lengths, half_sharp)
     near = after(near, far)
     far = after(far, near)
-    last_rest = lax.ppermute(far, ("tgt", "qry"), cross)
-    last = from_peer(far, 1)
-    far_rest = across(far, "qry")
+    half = target_rows // 2
+    last = [from_peer(far[:half], 1), from_peer(far[half:], 1)]
+    pool_other = across(pool_split, "rep")
     near_rest = from_peer(after(rest, far), 1)
 
-    one_blocks = [near, far]
+    one_blocks = [target_res[0], target_res[1], near, far]
     one = partial_similar(query, one_blocks)
     one_other = across(one, "rep")
-    one_aligned = aligned((2, 4), one, one_other)
-    pool_other = across(pool_split, "rep")
+    far_rest = across(after(far, one_other), "qry")
+    last_rest = [across(piece, "qry") for piece in last]
     posterior, weights = call_kernel(
         weigh_kernel,
         (
@@ -293,33 +287,35 @@
             jax.ShapeDtypeStruct(table, jnp.float32),
         ),
         slots,
-        after(hits, one_aligned),
+        after(hits, last[1]),
         query_pool,
         owners,
         target_pool,
         pool_split,
         pool_other,
         pool_last,
-    )
+        flops=1_000_000_000,
+    )
+    far_rest = after(far_rest, weights)
+    two_blocks = [far_rest, *last]
+    two = partial_similar(query, two_blocks)
+    two_other = across(two, "rep")
+    one_aligned = aligned((0, 1, 2, 4), after(one, two), one_other)
+
     acc = add_up(
-        (((0, 1), (1, 1)), ((2, 1), (4, 1))),
+        (((0, 1), (1, 1), (2, 1), (4, 1)),),
         (),
         jnp.float32,
-        own_aligned,
         one_aligned,
-        *own_blocks,
         *one_blocks,
     )
 
-    two_blocks = [far_rest, near_rest]
-    two = partial_similar(after(query, acc), two_blocks)
-    two_other = across(two, "rep")
-    three_blocks = [last, last_rest]
-    three = partial_similar(after(query, two), three_blocks)
+    three_blocks = [near_rest, *last_rest]
+    three = partial_similar(after(query, acc), three_blocks)
     three_other = across(three, "rep")
     acc = add_up(
         (),
-        ((5, 1), (3, 1)),
+        ((5, 1), (6, 2)),
         jnp.float32,
         lengths,
         half_sharp,
@@ -330,7 +326,7 @@
     )
     profile = add_up(
         (),
-        ((6, 1), (7, 1)),
+        ((3, 1), (7, 2)),
         jnp.bfloat16,
         lengths,
         half_sharp,

time: 34.5 us -> 32.1 us (0.930)
  waiting for transfers between devices: 11.4 us -> 6.3 us
  starting transfers between devices: 11.9 us -> 14.6 us
    ppermute x1, waiting for transfers between devices: 2.98 us -> 0.01 us  [per_device_by_target(): pool_split = lax.ppermute(target_pool, ('tgt', 'rep'), split)]
    ppermute x6 -> x7, starting transfers between devices: 2.23 us -> 5.17 us  [across(): return lax.ppermute(array, axis, [(0, 1), (1, 0)])]
    ppermute x6 -> x7, waiting for transfers between devices: 2.66 us -> 0.02 us  [across(): return lax.ppermute(array, axis, [(0, 1), (1, 0)])]
    ppermute x5 -> x6, waiting for transfers between devices: 3.69 us -> 6.28 us  [from_peer(): return lax.ppermute(array, 'tgt', [(i, i ^ k) for i in range(4)])]
    ppermute x1 -> x0, waiting for transfers between devices: 2.06 us -> none  [per_device_by_target(): last_rest = lax.ppermute(far, ('tgt', 'qry'), cross)]
    ppermute x1 -> x0, starting transfers between devices: 1.42 us -> none  [per_device_by_target(): last_rest = lax.ppermute(far, ('tgt', 'qry'), cross)]
    ppermute x5 -> x6, starting transfers between devices: 7.78 us -> 8.55 us  [from_peer(): return lax.ppermute(array, 'tgt', [(i, i ^ k) for i in range(4)])]
    ppermute x1, starting transfers between devices: 0.45 us -> 0.9 us  [per_device_by_target(): pool_split = lax.ppermute(target_pool, ('tgt', 'rep'), split)]
  transfers between devices with their start and end apart: 13 -> 14, of which waited for: 8 -> 3; matrix products, arithmetic and copies ran while one was open for 2% -> 2% of each run, Pallas kernels for 14% -> 15%
where the time goes in v12:
time: 32.1 us; the launch traced here: 32 us
  starting transfers between devices  14.6 us (45%)
  Pallas kernels  7.19 us (22%)
  waiting for transfers between devices  6.3 us (20%)
  local copies, waits for them, and re-layouts  2.25 us (7%)
  between operations  1.44 us (4%)
    ppermute x6, starting transfers between devices, from_peer(): return lax.ppermute(array, 'tgt', [(i, i ^ k) for i in range(4)])  8.55 us
    pallas_call x8, Pallas kernels, call_kernel(): pl.pallas_call(kernel, out_shape=out_shape, in_specs=[VMEM] * len(operand...  7.19 us
    ppermute x6, waiting for transfers between devices, from_peer(): return lax.ppermute(array, 'tgt', [(i, i ^ k) for i in range(4)])  6.28 us
    ppermute x7, starting transfers between devices, across(): return lax.ppermute(array, axis, [(0, 1), (1, 0)])  5.17 us
    squeeze x1, local copies, waits for them, and re-layouts, per_device_by_target(): rest = lax.dynamic_index_in_dim(target_res, 1 - at_qry, 0, keepdims=False)  1.26 us
    ppermute x1, starting transfers between devices, per_device_by_target(): pool_split = lax.ppermute(target_pool, ('tgt', 'rep'), split)  0.9 us
  transfers between devices with their start and end apart: 14, of which 3 were waited for; matrix products, arithmetic and copies ran while one was open for 2% of the time, Pallas kernels for 15%

profile of v12, /device:TPU:0, one launch (start us, length us, event | category | flops | bytes accessed | tf_op | source)
XLA Modules:
  0.0 32.0 jit_solution(13916971574543685558)
XLA Ops:
  0.7 1.3 %dynamic-slice_bitcast_fusion = (bf16[128,640]{1,0:T(8,128)(2,1)S(1)}, bf16[128,640]{1,0:T(8,128)(2,1)S(1)}, bf16[128,640]{1,0:T(8,128)(2,1)S(1)}, bf16[128,640]{1,0:T(8,128)(2,1)S(1)}) fusion(bf16[2,128,640]{2,1,0:T(8,128)(2,1)} %param.8, s32[]{:T(128)S(6)} %select_n.13, s32[]{:T(128)S(6)} %select_n.11), kind=kLoop, calls=%fused_computation | loop fusion | bytes 1310728 | tf_op jit(solution)/shard_map/jit(dynamic_index_in_dim)/squeeze | solution.py:242
  1.9 4.1 %collective-permute-start = (bf16[128,640]{1,0:T(8,128)(2,1)S(1)}, bf16[128,640]{1,0:T(8,128)(2,1)S(1)}, u32[]{:S(2)}, u32[]{:S(2)}) collective-permute-start(bf16[128,640]{1,0:T(8,128)(2,1)S(1)} %get-tuple-element.30), channel_id=1, source_target_pairs={{0,8},{4,12},{8,0},{12,4},{1,9},{5,13},{9,1},{13,5},{2,10},{6,14},... | collective-permute-start | bytes 491528 | tf_op jit(solution)/shard_map/ppermute | solution.py:228
  6.0 1.6 %collective-permute-start.3 = (bf16[128,640]{1,0:T(8,128)(2,1)S(1)}, bf16[128,640]{1,0:T(8,128)(2,1)S(1)}, u32[]{:S(2)}, u32[]{:S(2)}) collective-permute-start(bf16[128,640]{1,0:T(8,128)(2,1)S(1)} %get-tuple-element.30), channel_id=1, source_target_pairs={{0,4},{4,0},{8,12},{12,8},{1,5},{5,1},{9,13},{13,9},{2,6},{6,2},{1... | collective-permute-start | bytes 491528 | tf_op jit(solution)/shard_map/ppermute | solution.py:228
  7.6 0.9 %collective-permute-start.1 = (f32[2,1280]{1,0:T(2,128)S(1)}, f32[2,1280]{1,0:T(2,128)S(1)}, u32[]{:S(2)}, u32[]{:S(2)}) collective-permute-start(f32[2,1280]{1,0:T(2,128)S(1)} %copy-done.1), channel_id=1, source_target_pairs={{0,4},{1,9},{4,0},{5,13},{8,12},{9,1},{12,8},{13,5},{2,6},{3,11},{... | collective-permute-start | bytes 30728 | tf_op jit(solution)/shard_map/ppermute | solution.py:237
  8.6 0.6 %copy-done.4 = s32[8]{0:T(128)S(1)} copy-done((s32[8]{0:T(128)S(1)}, s32[8]{0:T(128)}, u32[]{:S(2)}) %copy-start.4) | copy-done | bytes 56
  9.2 0.2 select_reduce_fusion
  10.1 5.1 %collective-permute-done.2.refs_3_ = f32[2,1280]{1,0:T(2,128)S(1)} collective-permute-done((f32[2,1280]{1,0:T(2,128)S(1)}, f32[2,1280]{1,0:T(2,128)S(1)}, u32[]{:S(2)}, u32[]{:S(2)}) %collective-permute-start.2) | collective-permute-done | bytes 10272 | tf_op jit(solution)/shard_map/ppermute | solution.py:228
  15.4 0.4 %shard_map.87.mine = f32[256,512]{1,0:T(8,128)S(1)} custom-call(bf16[256,640]{1,0:T(8,128)(2,1)S(1)} %bitcast.23, bf16[128,640]{1,0:T(8,128)(2,1)S(1)} %get-tuple-element.29.refs_1_.refs_2_, bf16[128,640]{1,0:T(8,128)(2,1)S(1)} %get-tuple-element.31.refs_2_.refs_3_, bf16[128,640]{1,0:T(8,128)(2,1)S(1)} %collective-permute-done.3.refs_3_.refs_4_, ...), custom_call_target="tpu_custom_call" | custom-call | tf_op jit(solution)/shard_map/pallas_call | solution.py:93
  15.9 0.8 %collective-permute-start.4 = (bf16[64,640]{1,0:T(8,128)(2,1)S(1)}, bf16[64,640]{1,0:T(8,128)(2,1)S(1)}, u32[]{:S(2)}, u32[]{:S(2)}) collective-permute-start(bf16[64,640]{1,0:T(8,128)(2,1)S(1)} %get-tuple-element.33), channel_id=1, source_target_pairs={{0,4},{4,0},{8,12},{12,8},{1,5},{5,1},{9,13},{13,9},{2,6},{6,2},{1... | collective-permute-start | bytes 245768 | tf_op jit(solution)/shard_map/ppermute | solution.py:228
  16.8 1.2 %collective-permute-start.8 = (bf16[64,640]{1,0:T(8,128)(2,1)S(1)}, bf16[64,640]{1,0:T(8,128)(2,1)S(1)}, u32[]{:S(2)}, u32[]{:S(2)}) collective-permute-start(bf16[64,640]{1,0:T(8,128)(2,1)S(1)} %get-tuple-element.32), channel_id=1, source_target_pairs={{0,4},{4,0},{8,12},{12,8},{1,5},{5,1},{9,13},{13,9},{2,6},{6,2},{1... | collective-permute-start | bytes 245768 | tf_op jit(solution)/shard_map/ppermute | solution.py:228
  18.0 1.5 %collective-permute-start.7 = (bf16[128,640]{1,0:T(8,128)(2,1)S(1)}, bf16[128,640]{1,0:T(8,128)(2,1)S(1)}, u32[]{:S(2)}, u32[]{:S(2)}) collective-permute-start(bf16[128,640]{1,0:T(8,128)(2,1)S(1)} %collective-permute-done.refs_4_.refs_5_), channel_id=1, source_target_pairs={{0,2},{2,0},{1,3},{3,1},{4,6},{6,4},{5,7},{7,5},{8,10},{10,8},{9,1... | collective-permute-start | bytes 491528 | tf_op jit(solution)/shard_map/ppermute | solution.py:231
  19.5 0.8 %collective-permute-start.9 = (bf16[128,640]{1,0:T(8,128)(2,1)S(1)}, bf16[128,640]{1,0:T(8,128)(2,1)S(1)}, u32[]{:S(2)}, u32[]{:S(2)}) collective-permute-start(bf16[128,640]{1,0:T(8,128)(2,1)S(1)} %get-tuple-element.25), channel_id=1, source_target_pairs={{0,4},{4,0},{8,12},{12,8},{1,5},{5,1},{9,13},{13,9},{2,6},{6,2},{1... | collective-permute-start | bytes 491528 | tf_op jit(solution)/shard_map/ppermute | solution.py:228
  20.3 0.9 %collective-permute-done.4.refs_3_.refs_7_ = bf16[64,640]{1,0:T(8,128)(2,1)S(1)} collective-permute-done((bf16[64,640]{1,0:T(8,128)(2,1)S(1)}, bf16[64,640]{1,0:T(8,128)(2,1)S(1)}, u32[]{:S(2)}, u32[]{:S(2)}) %collective-permute-start.4) | collective-permute-done | bytes 81952 | tf_op jit(solution)/shard_map/ppermute | solution.py:228
  21.2 1.5 %collective-permute-start.11 = (bf16[64,640]{1,0:T(8,128)(2,1)S(1)}, bf16[64,640]{1,0:T(8,128)(2,1)S(1)}, u32[]{:S(2)}, u32[]{:S(2)}) collective-permute-start(bf16[64,640]{1,0:T(8,128)(2,1)S(1)} %collective-permute-done.4.refs_3_.refs_7_), channel_id=1, source_target_pairs={{0,2},{2,0},{1,3},{3,1},{4,6},{6,4},{5,7},{7,5},{8,10},{10,8},{9,1... | collective-permute-start | bytes 245768 | tf_op jit(solution)/shard_map/ppermute | solution.py:231
  22.7 0.3 collective-permute-done.8.refs_2_.refs_6_
  23.0 1.5 %collective-permute-start.10 = (bf16[64,640]{1,0:T(8,128)(2,1)S(1)}, bf16[64,640]{1,0:T(8,128)(2,1)S(1)}, u32[]{:S(2)}, u32[]{:S(2)}) collective-permute-start(bf16[64,640]{1,0:T(8,128)(2,1)S(1)} %collective-permute-done.8.refs_2_.refs_6_), channel_id=1, source_target_pairs={{0,2},{2,0},{1,3},{3,1},{4,6},{6,4},{5,7},{7,5},{8,10},{10,8},{9,1... | collective-permute-start | bytes 245768 | tf_op jit(solution)/shard_map/ppermute | solution.py:231
  24.5 0.8 %shard_map.86 = (f32[1,8]{1,0:T(1,128)}, f32[8,128]{1,0:T(8,128)S(1)}) custom-call(s32[8,128]{1,0:T(8,128)S(1)} %broadcast_in_dim.22.slot_ref, s32[1,28]{1,0:T(1,128)S(1)} %copy-done.3, f32[1,1280]{1,0:T(1,128)S(1)} %copy-done.2, s32[8,128]{1,0:T(8,128)S(1)} %broadcast_in_dim.23.owner_ref, f32[2,1280]{1,0:T(2,128)S(1)} %copy-done.1, ...), custom_call_target="tpu_custom_call" | custom-call | flops 1000000000 | tf_op jit(solution)/shard_map/pallas_call | solution.py:93
  25.2 0.3 shard_map.88.refs_3_
  25.6 1.7 %shard_map.89.refs_1_ = bf16[256,512]{1,0:T(8,128)(2,1)S(1)} custom-call(f32[8,128]{1,0:T(8,128)S(1)} %broadcast_in_dim.44.len_ref.refs_1_, f32[1,128]{1,0:T(1,128)S(1)} %broadcast_in_dim.45.sharp_ref.refs_2_, f32[256,512]{1,0:T(8,128)S(1)} %shard_map.87.mine, f32[256,512]{1,0:T(8,128)S(1)} %collective-permute-done.6.other), custom_call_target="tpu_custom_call" | custom-call | tf_op jit(solution)/shard_map/pallas_call | solution.py:93
  27.4 0.5 %shard_map.90.refs_8_ = f32[256,640]{1,0:T(8,128)S(1)} custom-call(f32[8,128]{1,0:T(8,128)S(1)} %get-tuple-element.20.refs_0_, bf16[256,512]{1,0:T(8,128)(2,1)S(1)} %shard_map.89.refs_1_, bf16[128,640]{1,0:T(8,128)(2,1)S(1)} %get-tuple-element.29.refs_1_.refs_2_, bf16[128,640]{1,0:T(8,128)(2,1)S(1)} %get-tuple-element.31.refs_2_.refs_3_, ...), custom_call_target="tpu_custom_call" | custom-call | tf_op jit(solution)/shard_map/pallas_call | solution.py:93
  27.9 0.3 shard_map.91.refs_3_
  28.2 0.6 %collective-permute-start.12 = (f32[256,256]{1,0:T(8,128)S(1)}, f32[256,256]{1,0:T(8,128)S(1)}, u32[]{:S(2)}, u32[]{:S(2)}) collective-permute-start(f32[256,256]{1,0:T(8,128)S(1)} %shard_map.91.refs_3_), channel_id=1, source_target_pairs={{0,1},{1,0},{2,3},{3,2},{4,5},{5,4},{6,7},{7,6},{8,9},{9,8},{10,11... | collective-permute-start | bytes 786440 | tf_op jit(solution)/shard_map/ppermute | solution.py:231
  28.8 1.2 %shard_map.92.refs_8_ = f32[256,640]{1,0:T(8,128)S(1)} custom-call(f32[8,128]{1,0:T(8,128)S(1)} %get-tuple-element.20.refs_0_, f32[8,128]{1,0:T(8,128)S(1)} %broadcast_in_dim.44.len_ref.refs_1_, f32[1,128]{1,0:T(1,128)S(1)} %broadcast_in_dim.45.sharp_ref.refs_2_, f32[256,256]{1,0:T(8,128)S(1)} %shard_map.88.refs_3_, ...), custom_call_target="tpu_custom_call" | custom-call | tf_op jit(solution)/shard_map/pallas_call | solution.py:93
  30.0 2.0 %shard_map.93 = bf16[256,640]{1,0:T(8,128)(2,1)} custom-call(f32[8,128]{1,0:T(8,128)S(1)} %get-tuple-element.20.refs_0_, f32[8,128]{1,0:T(8,128)S(1)} %broadcast_in_dim.44.len_ref.refs_1_, f32[1,128]{1,0:T(1,128)S(1)} %broadcast_in_dim.45.sharp_ref.refs_2_, f32[256,256]{1,0:T(8,128)S(1)} %shard_map.91.refs_3_, ...), custom_call_target="tpu_custom_call" | custom-call | tf_op jit(solution)/shard_map/pallas_call | solution.py:93
  (32 shorter events, 0.6 us)
Async XLA Ops:
  0.6 7.0 %copy-start.1 = (f32[2,1280]{1,0:T(2,128)S(1)}, f32[2,1280]{1,0:T(2,128)}, u32[]{:S(2)}) copy-start(f32[2,1280]{1,0:T(2,128)} %refs_0_.1) | copy-start | bytes 30724
  0.6 14.7 %copy-start = (bf16[1,256,640]{2,1,0:T(8,128)(2,1)S(1)}, bf16[1,256,640]{2,1,0:T(8,128)(2,1)}, u32[]{:S(2)}) copy-start(bf16[1,256,640]{2,1,0:T(8,128)(2,1)} %param.7) | copy-start | bytes 983044
  1.9 13.3 %collective-permute-start = (bf16[128,640]{1,0:T(8,128)(2,1)S(1)}, bf16[128,640]{1,0:T(8,128)(2,1)S(1)}, u32[]{:S(2)}, u32[]{:S(2)}) collective-permute-start(bf16[128,640]{1,0:T(8,128)(2,1)S(1)} %get-tuple-element.30), channel_id=1, source_target_pairs={{0,8},{4,12},{8,0},{12,4},{1,9},{5,13},{9,1},{13,5},{2,10},{6,14},... | collective-permute-start | bytes 491528 | tf_op jit(solution)/shard_map/ppermute | solution.py:228
  6.0 9.4 %collective-permute-start.3 = (bf16[128,640]{1,0:T(8,128)(2,1)S(1)}, bf16[128,640]{1,0:T(8,128)(2,1)S(1)}, u32[]{:S(2)}, u32[]{:S(2)}) collective-permute-start(bf16[128,640]{1,0:T(8,128)(2,1)S(1)} %get-tuple-element.30), channel_id=1, source_target_pairs={{0,4},{4,0},{8,12},{12,8},{1,5},{5,1},{9,13},{13,9},{2,6},{6,2},{1... | collective-permute-start | bytes 491528 | tf_op jit(solution)/shard_map/ppermute | solution.py:228
  7.6 7.6 %collective-permute-start.2 = (f32[2,1280]{1,0:T(2,128)S(1)}, f32[2,1280]{1,0:T(2,128)S(1)}, u32[]{:S(2)}, u32[]{:S(2)}) collective-permute-start(f32[2,1280]{1,0:T(2,128)S(1)} %copy-done.1), channel_id=1, source_target_pairs={{0,12},{4,8},{8,4},{12,0},{1,13},{5,9},{9,5},{13,1},{2,14},{6,10},... | collective-permute-start | bytes 30728 | tf_op jit(solution)/shard_map/ppermute | solution.py:228
  7.6 7.6 %collective-permute-start.1 = (f32[2,1280]{1,0:T(2,128)S(1)}, f32[2,1280]{1,0:T(2,128)S(1)}, u32[]{:S(2)}, u32[]{:S(2)}) collective-permute-start(f32[2,1280]{1,0:T(2,128)S(1)} %copy-done.1), channel_id=1, source_target_pairs={{0,4},{1,9},{4,0},{5,13},{8,12},{9,1},{12,8},{13,5},{2,6},{3,11},{... | collective-permute-start | bytes 30728 | tf_op jit(solution)/shard_map/ppermute | solution.py:237
  8.5 0.7 %copy-start.4 = (s32[8]{0:T(128)S(1)}, s32[8]{0:T(128)}, u32[]{:S(2)}) copy-start(s32[8]{0:T(128)} %param.9) | copy-start | bytes 100
  15.8 2.2 %collective-permute-start.6 = (f32[256,512]{1,0:T(8,128)S(1)}, f32[256,512]{1,0:T(8,128)S(1)}, u32[]{:S(2)}, u32[]{:S(2)}) collective-permute-start(f32[256,512]{1,0:T(8,128)S(1)} %shard_map.87.mine), channel_id=1, source_target_pairs={{0,1},{1,0},{2,3},{3,2},{4,5},{5,4},{6,7},{7,6},{8,9},{9,8},{10,11... | collective-permute-start | bytes 1572872 | tf_op jit(solution)/shard_map/ppermute | solution.py:231
  15.9 8.6 %copy-start.2 = (f32[1,1280]{1,0:T(1,128)S(1)}, f32[1,1280]{1,0:T(1,128)}, u32[]{:S(2)}) copy-start(f32[1,1280]{1,0:T(1,128)} %pool_ref.1) | copy-start | bytes 15364
  15.9 5.3 %collective-permute-start.4 = (bf16[64,640]{1,0:T(8,128)(2,1)S(1)}, bf16[64,640]{1,0:T(8,128)(2,1)S(1)}, u32[]{:S(2)}, u32[]{:S(2)}) collective-permute-start(bf16[64,640]{1,0:T(8,128)(2,1)S(1)} %get-tuple-element.33), channel_id=1, source_target_pairs={{0,4},{4,0},{8,12},{12,8},{1,5},{5,1},{9,13},{13,9},{2,6},{6,2},{1... | collective-permute-start | bytes 245768 | tf_op jit(solution)/shard_map/ppermute | solution.py:228
  16.8 7.7 %copy-start.3 = (s32[1,28]{1,0:T(1,128)S(1)}, s32[1,28]{1,0:T(1,128)}, u32[]{:S(2)}) copy-start(s32[1,28]{1,0:T(1,128)} %hits_ref) | copy-start | bytes 340
  16.8 6.2 %collective-permute-start.8 = (bf16[64,640]{1,0:T(8,128)(2,1)S(1)}, bf16[64,640]{1,0:T(8,128)(2,1)S(1)}, u32[]{:S(2)}, u32[]{:S(2)}) collective-permute-start(bf16[64,640]{1,0:T(8,128)(2,1)S(1)} %get-tuple-element.32), channel_id=1, source_target_pairs={{0,4},{4,0},{8,12},{12,8},{1,5},{5,1},{9,13},{13,9},{2,6},{6,2},{1... | collective-permute-start | bytes 245768 | tf_op jit(solution)/shard_map/ppermute | solution.py:228
  18.0 7.2 %collective-permute-start.7 = (bf16[128,640]{1,0:T(8,128)(2,1)S(1)}, bf16[128,640]{1,0:T(8,128)(2,1)S(1)}, u32[]{:S(2)}, u32[]{:S(2)}) collective-permute-start(bf16[128,640]{1,0:T(8,128)(2,1)S(1)} %collective-permute-done.refs_4_.refs_5_), channel_id=1, source_target_pairs={{0,2},{2,0},{1,3},{3,1},{4,6},{6,4},{5,7},{7,5},{8,10},{10,8},{9,1... | collective-permute-start | bytes 491528 | tf_op jit(solution)/shard_map/ppermute | solution.py:231
  19.5 8.4 %collective-permute-start.9 = (bf16[128,640]{1,0:T(8,128)(2,1)S(1)}, bf16[128,640]{1,0:T(8,128)(2,1)S(1)}, u32[]{:S(2)}, u32[]{:S(2)}) collective-permute-start(bf16[128,640]{1,0:T(8,128)(2,1)S(1)} %get-tuple-element.25), channel_id=1, source_target_pairs={{0,4},{4,0},{8,12},{12,8},{1,5},{5,1},{9,13},{13,9},{2,6},{6,2},{1... | collective-permute-start | bytes 491528 | tf_op jit(solution)/shard_map/ppermute | solution.py:228
  20.3 4.2 %collective-permute-start.5 = (f32[2,1280]{1,0:T(2,128)S(1)}, f32[2,1280]{1,0:T(2,128)S(1)}, u32[]{:S(2)}, u32[]{:S(2)}) collective-permute-start(f32[2,1280]{1,0:T(2,128)S(1)} %collective-permute-done.1.refs_1_), channel_id=1, source_target_pairs={{0,1},{1,0},{2,3},{3,2},{4,5},{5,4},{6,7},{7,6},{8,9},{9,8},{10,11... | collective-permute-start | bytes 30728 | tf_op jit(solution)/shard_map/ppermute | solution.py:231
  21.2 6.7 %collective-permute-start.11 = (bf16[64,640]{1,0:T(8,128)(2,1)S(1)}, bf16[64,640]{1,0:T(8,128)(2,1)S(1)}, u32[]{:S(2)}, u32[]{:S(2)}) collective-permute-start(bf16[64,640]{1,0:T(8,128)(2,1)S(1)} %collective-permute-done.4.refs_3_.refs_7_), channel_id=1, source_target_pairs={{0,2},{2,0},{1,3},{3,1},{4,6},{6,4},{5,7},{7,5},{8,10},{10,8},{9,1... | collective-permute-start | bytes 245768 | tf_op jit(solution)/shard_map/ppermute | solution.py:231
  23.0 4.9 %collective-permute-start.10 = (bf16[64,640]{1,0:T(8,128)(2,1)S(1)}, bf16[64,640]{1,0:T(8,128)(2,1)S(1)}, u32[]{:S(2)}, u32[]{:S(2)}) collective-permute-start(bf16[64,640]{1,0:T(8,128)(2,1)S(1)} %collective-permute-done.8.refs_2_.refs_6_), channel_id=1, source_target_pairs={{0,2},{2,0},{1,3},{3,1},{4,6},{6,4},{5,7},{7,5},{8,10},{10,8},{9,1... | collective-permute-start | bytes 245768 | tf_op jit(solution)/shard_map/ppermute | solution.py:231
  25.5 3.2 %collective-permute-start.13 = (f32[256,256]{1,0:T(8,128)S(1)}, f32[256,256]{1,0:T(8,128)S(1)}, u32[]{:S(2)}, u32[]{:S(2)}) collective-permute-start(f32[256,256]{1,0:T(8,128)S(1)} %shard_map.88.refs_3_), channel_id=1, source_target_pairs={{0,1},{1,0},{2,3},{3,2},{4,5},{5,4},{6,7},{7,6},{8,9},{9,8},{10,11... | collective-permute-start | bytes 786440 | tf_op jit(solution)/shard_map/ppermute | solution.py:231
  28.2 1.8 %collective-permute-start.12 = (f32[256,256]{1,0:T(8,128)S(1)}, f32[256,256]{1,0:T(8,128)S(1)}, u32[]{:S(2)}, u32[]{:S(2)}) collective-permute-start(f32[256,256]{1,0:T(8,128)S(1)} %shard_map.91.refs_3_), channel_id=1, source_target_pairs={{0,1},{1,0},{2,3},{3,2},{4,5},{5,4},{6,7},{7,6},{8,9},{9,8},{10,11... | collective-permute-start | bytes 786440 | tf_op jit(solution)/shard_map/ppermute | solution.py:231

commit v13 on v12

--- a/solution.py
+++ b/solution.py
@@ -104,7 +104,7 @@
 def weigh_kernel(slot_ref, hits_ref, pool_ref, owner_ref, *refs):
     libs, (posterior_ref, weight_ref) = refs[:-2], refs[-2:]
     owned, width = libs[0].shape
-    target_count = posterior_ref.shape[1]
+    target_count = posterior_ref.shape[0]
     target = lax.broadcasted_iota(jnp.int32, (target_count, 1), 0)
     counts = jnp.sum(jnp.where(hits_ref[...] == target, 1.0, 0.0), axis=1, keepdims=True)
     logits = jnp.zeros((target_count, 1), jnp.float32)
@@ -119,7 +119,7 @@
     parts = counts * jnp.exp(shown - jnp.max(shown, axis=0, keepdims=True))
     weights = parts / jnp.sum(parts, axis=0, keepdims=True)
     lane = lax.broadcasted_iota(jnp.int32, (1, target_count), 1)
-    posterior_ref[...] = jnp.sum(jnp.where(target == lane, posterior, 0.0), axis=0, keepdims=True)
+    posterior_ref[...] = jnp.broadcast_to(posterior, posterior_ref.shape)
     weights = jnp.sum(jnp.where(target == lane, weights, 0.0), axis=0, keepdims=True)
     weights = jnp.where(slot_ref[:, 0:1] == lane, weights, 0.0)
     weights = jnp.sum(weights, axis=1, keepdims=True)
@@ -162,56 +162,33 @@
     return raised / jnp.sum(raised, axis=1, keepdims=True)
 
 
-def align_kernel(model_width, slots, len_ref, sharp_ref, mine, other, out_ref):
-    scale = 1.0 / math.sqrt(model_width)
-    rows = mine.shape[1] // len(slots)
-    for at, slot in enumerate(slots):
-        part = pl.ds(at * rows, rows)
-        similar = (mine[:, part] + other[:, part]) * scale
-        alignment = align_block(similar, len_ref[slot : slot + 1, :rows], sharp_ref[:, 0:1])
-        out_ref[:, part] = alignment.astype(out_ref.dtype)
-
-
-def align(model_width, slots, lengths, half_sharp, mine, other):
-    return call_kernel(
-        functools.partial(align_kernel, model_width, slots),
-        jax.ShapeDtypeStruct(mine.shape, jnp.bfloat16),
-        lengths,
-        half_sharp,
-        mine,
-        other,
-    )
-
-
 def weighted_term(weight, alignment, blocks):
     target = blocks[0][...] if len(blocks) == 1 else jnp.concatenate([b[...] for b in blocks])
     return weight * jnp.dot(alignment, target, preferred_element_type=jnp.float32)
 
 
-def profile_kernel(model_width, groups, targets, *refs):
-    weight_ref, aligned, refs = refs[0], refs[1 : 1 + len(groups)], refs[1 + len(groups) :]
-    blocks, out_ref = refs[:-1], refs[-1]
+def profile_kernel(model_width, targets, last, weight_ref, len_ref, sharp_ref, mine, other, *refs):
+    blocks, out_ref = list(refs[:-1]), refs[-1]
+    if last:
+        posterior_ref, out_ref, posterior_out = blocks[-2], blocks[-1], out_ref
+        blocks = blocks[:-2]
+        count = posterior_out.shape[1]
+        row = lax.broadcasted_iota(jnp.int32, (count, 1), 0)
+        lane = lax.broadcasted_iota(jnp.int32, (1, count), 1)
+        chosen = jnp.where(row == lane, posterior_ref[:, 0:1], 0.0)
+        posterior_out[...] = jnp.sum(chosen, axis=0, keepdims=True)
+    rows = mine.shape[1] // len(targets)
     acc = None
-
-    def add(acc, target, alignment, blocks):
-        slot, count = target
-        term = weighted_term(weight_ref[slot : slot + 1, 0:1], alignment, blocks[:count])
-        return (term if acc is None else acc + term), blocks[count:]
-
-    for group, members in zip(aligned, groups):
-        rows = group.shape[1] // len(members)
-        for at, target in enumerate(members):
-            acc, blocks = add(acc, target, group[:, at * rows : (at + 1) * rows], blocks)
-    if targets:
-        len_ref, sharp_ref, mine, other, *blocks = blocks
-        rows = mine.shape[1] // len(targets)
-        for at, target in enumerate(targets):
-            part = pl.ds(at * rows, rows)
-            similar = (mine[:, part] + other[:, part]) * (1.0 / math.sqrt(model_width))
-            lengths = len_ref[target[0] : target[0] + 1, :rows]
-            alignment = align_block(similar, lengths, sharp_ref[:, 0:1])
-            acc, blocks = add(acc, target, alignment.astype(jnp.bfloat16), blocks)
-    if len(blocks):
+    for at, (slot, count) in enumerate(targets):
+        part = pl.ds(at * rows, rows)
+        similar = (mine[:, part] + other[:, part]) * (1.0 / math.sqrt(model_width))
+        alignment = align_block(similar, len_ref[slot : slot + 1, :rows], sharp_ref[:, 0:1])
+        term = weighted_term(
+            weight_ref[slot : slot + 1, 0:1], alignment.astype(jnp.bfloat16), blocks[:count]
+        )
+        acc = term if acc is None else acc + term
+        blocks = blocks[count:]
+    if blocks:
         acc += blocks[0][...]
     out_ref[...] = acc.astype(out_ref.dtype)
 
@@ -256,17 +233,17 @@
     lengths = jnp.broadcast_to(lengths.astype(jnp.float32), table)
     half_sharp = jnp.broadcast_to(0.5 * sharpness, (1, target_rows))
 
-    def aligned(slots, mine, other):
-        return align(model_width, slots, lengths, half_sharp, mine, other)
-
-    def add_up(groups, targets, dtype, *operands):
+    def add_up(targets, out_shape, *operands):
         return call_kernel(
-            functools.partial(profile_kernel, model_width, groups, targets),
-            jax.ShapeDtypeStruct(query.shape, dtype),
+            functools.partial(profile_kernel, model_width, targets, isinstance(out_shape, tuple)),
+            out_shape,
             weights,
+            lengths,
+            half_sharp,
             *operands,
         )
 
+    acc_shape = jax.ShapeDtypeStruct(query.shape, jnp.float32)
     far = after(far, pool_split, pool_last, slots, owners, lengths, half_sharp)
     near = after(near, far)
     far = after(far, near)
@@ -283,7 +260,7 @@
     posterior, weights = call_kernel(
         weigh_kernel,
         (
-            jax.ShapeDtypeStruct((1, table[0]), jnp.float32),
+            jax.ShapeDtypeStruct(table, jnp.float32),
             jax.ShapeDtypeStruct(table, jnp.float32),
         ),
         slots,
@@ -300,40 +277,26 @@
     two_blocks = [far_rest, *last]
     two = partial_similar(query, two_blocks)
     two_other = across(two, "rep")
-    one_aligned = aligned((0, 1, 2, 4), after(one, two), one_other)
 
     acc = add_up(
-        (((0, 1), (1, 1), (2, 1), (4, 1)),),
-        (),
-        jnp.float32,
-        one_aligned,
-        *one_blocks,
+        ((0, 1), (1, 1), (2, 1), (4, 1)), acc_shape, after(one, two), one_other, *one_blocks
     )
 
     three_blocks = [near_rest, *last_rest]
     three = partial_similar(after(query, acc), three_blocks)
     three_other = across(three, "rep")
-    acc = add_up(
-        (),
-        ((5, 1), (6, 2)),
-        jnp.float32,
-        lengths,
-        half_sharp,
-        after(two, three),
-        two_other,
-        *two_blocks,
-        acc,
-    )
-    profile = add_up(
-        (),
+    acc = add_up(((5, 1), (6, 2)), acc_shape, after(two, three), two_other, *two_blocks, acc)
+    profile, posterior = add_up(
         ((3, 1), (7, 2)),
-        jnp.bfloat16,
-        lengths,
-        half_sharp,
+        (
+            jax.ShapeDtypeStruct(query.shape, jnp.bfloat16),
+            jax.ShapeDtypeStruct((1, table[0]), jnp.float32),
+        ),
         three,
         three_other,
         *three_blocks,
         acc,
+        posterior,
     )
     return (profile[None], posterior)
 

time: 32.1 us -> 31.6 us (0.984)
  Pallas kernels: 7.19 us -> 6.49 us
  waiting for transfers between devices: 6.3 us -> 6.8 us
    pallas_call x8 -> x7, Pallas kernels: 7.19 us -> 6.49 us  [call_kernel(): pl.pallas_call(kernel, out_shape=out_shape, in_specs=[VMEM] * len(operand...]
    ppermute x7, waiting for transfers between devices: 0.02 us -> 0.52 us  [across(): return lax.ppermute(array, axis, [(0, 1), (1, 0)])]
    ppermute x7, starting transfers between devices: 5.17 us -> 4.84 us  [across(): return lax.ppermute(array, axis, [(0, 1), (1, 0)])]
  transfers between devices with their start and end apart: 14 -> 14, of which waited for: 3 -> 5; matrix products, arithmetic and copies ran while one was open for 2% -> 2% of each run, Pallas kernels for 15% -> 13%
where the time goes in v13:
time: 31.6 us; the launch traced here: 31.4 us
  starting transfers between devices  14.3 us (45%)
  waiting for transfers between devices  6.8 us (22%)
  Pallas kernels  6.49 us (21%)
  local copies, waits for them, and re-layouts  2.25 us (7%)
  between operations  1.41 us (4%)
    ppermute x6, starting transfers between devices, from_peer(): return lax.ppermute(array, 'tgt', [(i, i ^ k) for i in range(4)])  8.55 us
    pallas_call x7, Pallas kernels, call_kernel(): pl.pallas_call(kernel, out_shape=out_shape, in_specs=[VMEM] * len(operand...  6.49 us
    ppermute x6, waiting for transfers between devices, from_peer(): return lax.ppermute(array, 'tgt', [(i, i ^ k) for i in range(4)])  6.28 us
    ppermute x7, starting transfers between devices, across(): return lax.ppermute(array, axis, [(0, 1), (1, 0)])  4.84 us
    squeeze x1, local copies, waits for them, and re-layouts, per_device_by_target(): rest = lax.dynamic_index_in_dim(target_res, 1 - at_qry, 0, keepdims=False)  1.26 us
    ppermute x1, starting transfers between devices, per_device_by_target(): pool_split = lax.ppermute(target_pool, ('tgt', 'rep'), split)  0.9 us
  transfers between devices with their start and end apart: 14, of which 5 were waited for; matrix products, arithmetic and copies ran while one was open for 2% of the time, Pallas kernels for 13%

profile of v13, /device:TPU:0, one launch (start us, length us, event | category | flops | bytes accessed | tf_op | source)
XLA Modules:
  0.0 31.4 jit_solution(2958362466208075292)
XLA Ops:
  0.7 1.3 %dynamic-slice_bitcast_fusion = (bf16[128,640]{1,0:T(8,128)(2,1)S(1)}, bf16[128,640]{1,0:T(8,128)(2,1)S(1)}, bf16[128,640]{1,0:T(8,128)(2,1)S(1)}, bf16[128,640]{1,0:T(8,128)(2,1)S(1)}) fusion(bf16[2,128,640]{2,1,0:T(8,128)(2,1)} %param.8, s32[]{:T(128)S(6)} %select_n.13, s32[]{:T(128)S(6)} %select_n.11), kind=kLoop, calls=%fused_computation | loop fusion | bytes 1310728 | tf_op jit(solution)/shard_map/jit(dynamic_index_in_dim)/squeeze | solution.py:219
  1.9 4.1 %collective-permute-start = (bf16[128,640]{1,0:T(8,128)(2,1)S(1)}, bf16[128,640]{1,0:T(8,128)(2,1)S(1)}, u32[]{:S(2)}, u32[]{:S(2)}) collective-permute-start(bf16[128,640]{1,0:T(8,128)(2,1)S(1)} %get-tuple-element.34), channel_id=1, source_target_pairs={{0,8},{4,12},{8,0},{12,4},{1,9},{5,13},{9,1},{13,5},{2,10},{6,14},... | collective-permute-start | bytes 491528 | tf_op jit(solution)/shard_map/ppermute | solution.py:205
  6.0 1.6 %collective-permute-start.3 = (bf16[128,640]{1,0:T(8,128)(2,1)S(1)}, bf16[128,640]{1,0:T(8,128)(2,1)S(1)}, u32[]{:S(2)}, u32[]{:S(2)}) collective-permute-start(bf16[128,640]{1,0:T(8,128)(2,1)S(1)} %get-tuple-element.34), channel_id=1, source_target_pairs={{0,4},{4,0},{8,12},{12,8},{1,5},{5,1},{9,13},{13,9},{2,6},{6,2},{1... | collective-permute-start | bytes 491528 | tf_op jit(solution)/shard_map/ppermute | solution.py:205
  7.6 0.9 %collective-permute-start.1 = (f32[2,1280]{1,0:T(2,128)S(1)}, f32[2,1280]{1,0:T(2,128)S(1)}, u32[]{:S(2)}, u32[]{:S(2)}) collective-permute-start(f32[2,1280]{1,0:T(2,128)S(1)} %copy-done.1), channel_id=1, source_target_pairs={{0,4},{1,9},{4,0},{5,13},{8,12},{9,1},{12,8},{13,5},{2,6},{3,11},{... | collective-permute-start | bytes 30728 | tf_op jit(solution)/shard_map/ppermute | solution.py:214
  8.6 0.6 %copy-done.4 = s32[8]{0:T(128)S(1)} copy-done((s32[8]{0:T(128)S(1)}, s32[8]{0:T(128)}, u32[]{:S(2)}) %copy-start.4) | copy-done | bytes 56
  9.2 0.2 select_reduce_fusion
  10.1 5.1 %collective-permute-done.2.refs_3_ = f32[2,1280]{1,0:T(2,128)S(1)} collective-permute-done((f32[2,1280]{1,0:T(2,128)S(1)}, f32[2,1280]{1,0:T(2,128)S(1)}, u32[]{:S(2)}, u32[]{:S(2)}) %collective-permute-start.2) | collective-permute-done | bytes 10272 | tf_op jit(solution)/shard_map/ppermute | solution.py:205
  15.4 0.4 %shard_map.87.mine = f32[256,512]{1,0:T(8,128)S(1)} custom-call(bf16[256,640]{1,0:T(8,128)(2,1)S(1)} %bitcast.23, bf16[128,640]{1,0:T(8,128)(2,1)S(1)} %get-tuple-element.33.refs_1_.refs_0_, bf16[128,640]{1,0:T(8,128)(2,1)S(1)} %get-tuple-element.35.refs_2_.refs_1_, bf16[128,640]{1,0:T(8,128)(2,1)S(1)} %collective-permute-done.3.refs_3_.refs_2_, ...), custom_call_target="tpu_custom_call" | custom-call | tf_op jit(solution)/shard_map/pallas_call | solution.py:93
  15.9 0.8 %collective-permute-start.4 = (bf16[64,640]{1,0:T(8,128)(2,1)S(1)}, bf16[64,640]{1,0:T(8,128)(2,1)S(1)}, u32[]{:S(2)}, u32[]{:S(2)}) collective-permute-start(bf16[64,640]{1,0:T(8,128)(2,1)S(1)} %get-tuple-element.37), channel_id=1, source_target_pairs={{0,4},{4,0},{8,12},{12,8},{1,5},{5,1},{9,13},{13,9},{2,6},{6,2},{1... | collective-permute-start | bytes 245768 | tf_op jit(solution)/shard_map/ppermute | solution.py:205
  16.8 1.2 %collective-permute-start.8 = (bf16[64,640]{1,0:T(8,128)(2,1)S(1)}, bf16[64,640]{1,0:T(8,128)(2,1)S(1)}, u32[]{:S(2)}, u32[]{:S(2)}) collective-permute-start(bf16[64,640]{1,0:T(8,128)(2,1)S(1)} %get-tuple-element.36), channel_id=1, source_target_pairs={{0,4},{4,0},{8,12},{12,8},{1,5},{5,1},{9,13},{13,9},{2,6},{6,2},{1... | collective-permute-start | bytes 245768 | tf_op jit(solution)/shard_map/ppermute | solution.py:205
  18.0 1.5 %collective-permute-start.7 = (bf16[128,640]{1,0:T(8,128)(2,1)S(1)}, bf16[128,640]{1,0:T(8,128)(2,1)S(1)}, u32[]{:S(2)}, u32[]{:S(2)}) collective-permute-start(bf16[128,640]{1,0:T(8,128)(2,1)S(1)} %collective-permute-done.refs_4_.refs_3_), channel_id=1, source_target_pairs={{0,2},{2,0},{1,3},{3,1},{4,6},{6,4},{5,7},{7,5},{8,10},{10,8},{9,1... | collective-permute-start | bytes 491528 | tf_op jit(solution)/shard_map/ppermute | solution.py:208
  19.5 0.8 %collective-permute-start.9 = (bf16[128,640]{1,0:T(8,128)(2,1)S(1)}, bf16[128,640]{1,0:T(8,128)(2,1)S(1)}, u32[]{:S(2)}, u32[]{:S(2)}) collective-permute-start(bf16[128,640]{1,0:T(8,128)(2,1)S(1)} %get-tuple-element.27), channel_id=1, source_target_pairs={{0,4},{4,0},{8,12},{12,8},{1,5},{5,1},{9,13},{13,9},{2,6},{6,2},{1... | collective-permute-start | bytes 491528 | tf_op jit(solution)/shard_map/ppermute | solution.py:205
  20.3 0.9 %collective-permute-done.4.refs_3_.refs_2_ = bf16[64,640]{1,0:T(8,128)(2,1)S(1)} collective-permute-done((bf16[64,640]{1,0:T(8,128)(2,1)S(1)}, bf16[64,640]{1,0:T(8,128)(2,1)S(1)}, u32[]{:S(2)}, u32[]{:S(2)}) %collective-permute-start.4) | collective-permute-done | bytes 81952 | tf_op jit(solution)/shard_map/ppermute | solution.py:205
  21.2 1.5 %collective-permute-start.11 = (bf16[64,640]{1,0:T(8,128)(2,1)S(1)}, bf16[64,640]{1,0:T(8,128)(2,1)S(1)}, u32[]{:S(2)}, u32[]{:S(2)}) collective-permute-start(bf16[64,640]{1,0:T(8,128)(2,1)S(1)} %collective-permute-done.4.refs_3_.refs_2_), channel_id=1, source_target_pairs={{0,2},{2,0},{1,3},{3,1},{4,6},{6,4},{5,7},{7,5},{8,10},{10,8},{9,1... | collective-permute-start | bytes 245768 | tf_op jit(solution)/shard_map/ppermute | solution.py:208
  22.7 0.3 collective-permute-done.8.refs_2_.refs_1_
  23.0 1.5 %collective-permute-start.10 = (bf16[64,640]{1,0:T(8,128)(2,1)S(1)}, bf16[64,640]{1,0:T(8,128)(2,1)S(1)}, u32[]{:S(2)}, u32[]{:S(2)}) collective-permute-start(bf16[64,640]{1,0:T(8,128)(2,1)S(1)} %collective-permute-done.8.refs_2_.refs_1_), channel_id=1, source_target_pairs={{0,2},{2,0},{1,3},{3,1},{4,6},{6,4},{5,7},{7,5},{8,10},{10,8},{9,1... | collective-permute-start | bytes 245768 | tf_op jit(solution)/shard_map/ppermute | solution.py:208
  24.5 0.3 shard_map.86
  24.8 0.3 shard_map.88.mine
  25.2 2.0 %shard_map.89.refs_3_ = f32[256,640]{1,0:T(8,128)S(1)} custom-call(f32[8,128]{1,0:T(8,128)S(1)} %get-tuple-element.22.weight_ref, f32[8,128]{1,0:T(8,128)S(1)} %broadcast_in_dim.44.len_ref, f32[1,128]{1,0:T(1,128)S(1)} %broadcast_in_dim.45.sharp_ref, f32[256,512]{1,0:T(8,128)S(1)} %shard_map.87.mine, f32[256,512]{1,0:T(8,128)S(1)} %collective-permute-done.6.other, ...), custom_call_target="tpu_custom_call" | custom-call | tf_op jit(solution)/shard_map/pallas_call | solution.py:93
  27.2 0.4 %collective-permute-done.10.refs_2_.refs_1_ = bf16[64,640]{1,0:T(8,128)(2,1)S(1)} collective-permute-done((bf16[64,640]{1,0:T(8,128)(2,1)S(1)}, bf16[64,640]{1,0:T(8,128)(2,1)S(1)}, u32[]{:S(2)}, u32[]{:S(2)}) %collective-permute-start.10) | collective-permute-done | bytes 81952 | tf_op jit(solution)/shard_map/ppermute | solution.py:208
  27.6 0.3 shard_map.90.mine
  27.9 0.2 collective-permute-start.12
  28.1 1.2 %shard_map.91.refs_3_ = f32[256,640]{1,0:T(8,128)S(1)} custom-call(f32[8,128]{1,0:T(8,128)S(1)} %get-tuple-element.22.weight_ref, f32[8,128]{1,0:T(8,128)S(1)} %broadcast_in_dim.44.len_ref, f32[1,128]{1,0:T(1,128)S(1)} %broadcast_in_dim.45.sharp_ref, f32[256,256]{1,0:T(8,128)S(1)} %shard_map.88.mine, f32[256,256]{1,0:T(8,128)S(1)} %collective-permute-done.13.other, ...), custom_call_target="tpu_custom_call" | custom-call | tf_op jit(solution)/shard_map/pallas_call | solution.py:93
  29.5 2.0 %shard_map.92 = (bf16[256,640]{1,0:T(8,128)(2,1)}, f32[1,8]{1,0:T(1,128)}) custom-call(f32[8,128]{1,0:T(8,128)S(1)} %get-tuple-element.22.weight_ref, f32[8,128]{1,0:T(8,128)S(1)} %broadcast_in_dim.44.len_ref, f32[1,128]{1,0:T(1,128)S(1)} %broadcast_in_dim.45.sharp_ref, f32[256,256]{1,0:T(8,128)S(1)} %shard_map.90.mine, ...), custom_call_target="tpu_custom_call" | custom-call | tf_op jit(solution)/shard_map/pallas_call | solution.py:93
  (31 shorter events, 0.7 us)
Async XLA Ops:
  0.6 7.0 %copy-start.1 = (f32[2,1280]{1,0:T(2,128)S(1)}, f32[2,1280]{1,0:T(2,128)}, u32[]{:S(2)}) copy-start(f32[2,1280]{1,0:T(2,128)} %refs_0_.1) | copy-start | bytes 30724
  0.6 14.7 %copy-start = (bf16[1,256,640]{2,1,0:T(8,128)(2,1)S(1)}, bf16[1,256,640]{2,1,0:T(8,128)(2,1)}, u32[]{:S(2)}) copy-start(bf16[1,256,640]{2,1,0:T(8,128)(2,1)} %param.7) | copy-start | bytes 983044
  1.9 13.3 %collective-permute-start = (bf16[128,640]{1,0:T(8,128)(2,1)S(1)}, bf16[128,640]{1,0:T(8,128)(2,1)S(1)}, u32[]{:S(2)}, u32[]{:S(2)}) collective-permute-start(bf16[128,640]{1,0:T(8,128)(2,1)S(1)} %get-tuple-element.34), channel_id=1, source_target_pairs={{0,8},{4,12},{8,0},{12,4},{1,9},{5,13},{9,1},{13,5},{2,10},{6,14},... | collective-permute-start | bytes 491528 | tf_op jit(solution)/shard_map/ppermute | solution.py:205
  6.0 9.4 %collective-permute-start.3 = (bf16[128,640]{1,0:T(8,128)(2,1)S(1)}, bf16[128,640]{1,0:T(8,128)(2,1)S(1)}, u32[]{:S(2)}, u32[]{:S(2)}) collective-permute-start(bf16[128,640]{1,0:T(8,128)(2,1)S(1)} %get-tuple-element.34), channel_id=1, source_target_pairs={{0,4},{4,0},{8,12},{12,8},{1,5},{5,1},{9,13},{13,9},{2,6},{6,2},{1... | collective-permute-start | bytes 491528 | tf_op jit(solution)/shard_map/ppermute | solution.py:205
  7.6 7.6 %collective-permute-start.2 = (f32[2,1280]{1,0:T(2,128)S(1)}, f32[2,1280]{1,0:T(2,128)S(1)}, u32[]{:S(2)}, u32[]{:S(2)}) collective-permute-start(f32[2,1280]{1,0:T(2,128)S(1)} %copy-done.1), channel_id=1, source_target_pairs={{0,12},{4,8},{8,4},{12,0},{1,13},{5,9},{9,5},{13,1},{2,14},{6,10},... | collective-permute-start | bytes 30728 | tf_op jit(solution)/shard_map/ppermute | solution.py:205
  7.6 7.6 %collective-permute-start.1 = (f32[2,1280]{1,0:T(2,128)S(1)}, f32[2,1280]{1,0:T(2,128)S(1)}, u32[]{:S(2)}, u32[]{:S(2)}) collective-permute-start(f32[2,1280]{1,0:T(2,128)S(1)} %copy-done.1), channel_id=1, source_target_pairs={{0,4},{1,9},{4,0},{5,13},{8,12},{9,1},{12,8},{13,5},{2,6},{3,11},{... | collective-permute-start | bytes 30728 | tf_op jit(solution)/shard_map/ppermute | solution.py:214
  8.5 0.7 %copy-start.4 = (s32[8]{0:T(128)S(1)}, s32[8]{0:T(128)}, u32[]{:S(2)}) copy-start(s32[8]{0:T(128)} %param.9) | copy-start | bytes 100
  15.8 2.2 %collective-permute-start.6 = (f32[256,512]{1,0:T(8,128)S(1)}, f32[256,512]{1,0:T(8,128)S(1)}, u32[]{:S(2)}, u32[]{:S(2)}) collective-permute-start(f32[256,512]{1,0:T(8,128)S(1)} %shard_map.87.mine), channel_id=1, source_target_pairs={{0,1},{1,0},{2,3},{3,2},{4,5},{5,4},{6,7},{7,6},{8,9},{9,8},{10,11... | collective-permute-start | bytes 1572872 | tf_op jit(solution)/shard_map/ppermute | solution.py:208
  15.9 8.6 %copy-start.2 = (f32[1,1280]{1,0:T(1,128)S(1)}, f32[1,1280]{1,0:T(1,128)}, u32[]{:S(2)}) copy-start(f32[1,1280]{1,0:T(1,128)} %pool_ref.1) | copy-start | bytes 15364
  15.9 5.3 %collective-permute-start.4 = (bf16[64,640]{1,0:T(8,128)(2,1)S(1)}, bf16[64,640]{1,0:T(8,128)(2,1)S(1)}, u32[]{:S(2)}, u32[]{:S(2)}) collective-permute-start(bf16[64,640]{1,0:T(8,128)(2,1)S(1)} %get-tuple-element.37), channel_id=1, source_target_pairs={{0,4},{4,0},{8,12},{12,8},{1,5},{5,1},{9,13},{13,9},{2,6},{6,2},{1... | collective-permute-start | bytes 245768 | tf_op jit(solution)/shard_map/ppermute | solution.py:205
  16.8 7.7 %copy-start.3 = (s32[1,28]{1,0:T(1,128)S(1)}, s32[1,28]{1,0:T(1,128)}, u32[]{:S(2)}) copy-start(s32[1,28]{1,0:T(1,128)} %hits_ref) | copy-start | bytes 340
  16.8 6.2 %collective-permute-start.8 = (bf16[64,640]{1,0:T(8,128)(2,1)S(1)}, bf16[64,640]{1,0:T(8,128)(2,1)S(1)}, u32[]{:S(2)}, u32[]{:S(2)}) collective-permute-start(bf16[64,640]{1,0:T(8,128)(2,1)S(1)} %get-tuple-element.36), channel_id=1, source_target_pairs={{0,4},{4,0},{8,12},{12,8},{1,5},{5,1},{9,13},{13,9},{2,6},{6,2},{1... | collective-permute-start | bytes 245768 | tf_op jit(solution)/shard_map/ppermute | solution.py:205
  18.0 6.8 %collective-permute-start.7 = (bf16[128,640]{1,0:T(8,128)(2,1)S(1)}, bf16[128,640]{1,0:T(8,128)(2,1)S(1)}, u32[]{:S(2)}, u32[]{:S(2)}) collective-permute-start(bf16[128,640]{1,0:T(8,128)(2,1)S(1)} %collective-permute-done.refs_4_.refs_3_), channel_id=1, source_target_pairs={{0,2},{2,0},{1,3},{3,1},{4,6},{6,4},{5,7},{7,5},{8,10},{10,8},{9,1... | collective-permute-start | bytes 491528 | tf_op jit(solution)/shard_map/ppermute | solution.py:208
  19.5 7.7 %collective-permute-start.9 = (bf16[128,640]{1,0:T(8,128)(2,1)S(1)}, bf16[128,640]{1,0:T(8,128)(2,1)S(1)}, u32[]{:S(2)}, u32[]{:S(2)}) collective-permute-start(bf16[128,640]{1,0:T(8,128)(2,1)S(1)} %get-tuple-element.27), channel_id=1, source_target_pairs={{0,4},{4,0},{8,12},{12,8},{1,5},{5,1},{9,13},{13,9},{2,6},{6,2},{1... | collective-permute-start | bytes 491528 | tf_op jit(solution)/shard_map/ppermute | solution.py:205
  20.3 4.2 %collective-permute-start.5 = (f32[2,1280]{1,0:T(2,128)S(1)}, f32[2,1280]{1,0:T(2,128)S(1)}, u32[]{:S(2)}, u32[]{:S(2)}) collective-permute-start(f32[2,1280]{1,0:T(2,128)S(1)} %collective-permute-done.1.refs_1_), channel_id=1, source_target_pairs={{0,1},{1,0},{2,3},{3,2},{4,5},{5,4},{6,7},{7,6},{8,9},{9,8},{10,11... | collective-permute-start | bytes 30728 | tf_op jit(solution)/shard_map/ppermute | solution.py:208
  21.2 6.3 %collective-permute-start.11 = (bf16[64,640]{1,0:T(8,128)(2,1)S(1)}, bf16[64,640]{1,0:T(8,128)(2,1)S(1)}, u32[]{:S(2)}, u32[]{:S(2)}) collective-permute-start(bf16[64,640]{1,0:T(8,128)(2,1)S(1)} %collective-permute-done.4.refs_3_.refs_2_), channel_id=1, source_target_pairs={{0,2},{2,0},{1,3},{3,1},{4,6},{6,4},{5,7},{7,5},{8,10},{10,8},{9,1... | collective-permute-start | bytes 245768 | tf_op jit(solution)/shard_map/ppermute | solution.py:208
  23.0 4.6 %collective-permute-start.10 = (bf16[64,640]{1,0:T(8,128)(2,1)S(1)}, bf16[64,640]{1,0:T(8,128)(2,1)S(1)}, u32[]{:S(2)}, u32[]{:S(2)}) collective-permute-start(bf16[64,640]{1,0:T(8,128)(2,1)S(1)} %collective-permute-done.8.refs_2_.refs_1_), channel_id=1, source_target_pairs={{0,2},{2,0},{1,3},{3,1},{4,6},{6,4},{5,7},{7,5},{8,10},{10,8},{9,1... | collective-permute-start | bytes 245768 | tf_op jit(solution)/shard_map/ppermute | solution.py:208
  25.1 3.0 %collective-permute-start.13 = (f32[256,256]{1,0:T(8,128)S(1)}, f32[256,256]{1,0:T(8,128)S(1)}, u32[]{:S(2)}, u32[]{:S(2)}) collective-permute-start(f32[256,256]{1,0:T(8,128)S(1)} %shard_map.88.mine), channel_id=1, source_target_pairs={{0,1},{1,0},{2,3},{3,2},{4,5},{5,4},{6,7},{7,6},{8,9},{9,8},{10,11... | collective-permute-start | bytes 786440 | tf_op jit(solution)/shard_map/ppermute | solution.py:208
  27.9 1.6 %collective-permute-start.12 = (f32[256,256]{1,0:T(8,128)S(1)}, f32[256,256]{1,0:T(8,128)S(1)}, u32[]{:S(2)}, u32[]{:S(2)}) collective-permute-start(f32[256,256]{1,0:T(8,128)S(1)} %shard_map.90.mine), channel_id=1, source_target_pairs={{0,1},{1,0},{2,3},{3,2},{4,5},{5,4},{6,7},{7,6},{8,9},{9,8},{10,11... | collective-permute-start | bytes 786440 | tf_op jit(solution)/shard_map/ppermute | solution.py:208

commit v14 on v13

--- a/solution.py
+++ b/solution.py
@@ -99,6 +99,24 @@
         cost_estimate=pl.CostEstimate(flops=flops, bytes_accessed=0, transcendentals=0),
         compiler_params=pltpu.CompilerParams(vmem_limit_bytes=VMEM_BYTES),
     )(*operands)
+
+
+def share_kernel(at_ref, blocks_ref, share_ref, done):
+    copy = pltpu.make_async_copy(blocks_ref.at[at_ref[0]], share_ref, done)
+    copy.start()
+    copy.wait()
+
+
+def take_share(blocks, at):
+    return pl.pallas_call(
+        share_kernel,
+        out_shape=jax.ShapeDtypeStruct(blocks.shape[1:], blocks.dtype),
+        in_specs=[pl.BlockSpec(memory_space=pltpu.SMEM), pl.BlockSpec(memory_space=pl.ANY)],
+        out_specs=pl.BlockSpec(memory_space=pl.ANY),
+        scratch_shapes=[pltpu.SemaphoreType.DMA],
+        cost_estimate=pl.CostEstimate(flops=0, bytes_accessed=0, transcendentals=0),
+        compiler_params=pltpu.CompilerParams(vmem_limit_bytes=62*1024*1024),
+    )(at.astype(jnp.int32)[None], blocks)
 
 
 def weigh_kernel(slot_ref, hits_ref, pool_ref, owner_ref, *refs):
@@ -211,13 +229,14 @@
         return lax.optimization_barrier((array, *done))[0]
 
     split = [(2 * i + c, 2 * (i ^ (1 + c)) + c) for i in range(4) for c in range(2)]
-    pool_split = lax.ppermute(target_pool, ("tgt", "rep"), split)
-    pool_last = from_peer(target_pool, 3)
+
+    share = take_share(target_res, at_qry)
+    far = from_peer(share, 2)
+    rest = lax.dynamic_index_in_dim(after(target_res, share), 1 - at_qry, 0, keepdims=False)
+    pool = after(target_pool, rest)
+    pool_split = lax.ppermute(pool, ("tgt", "rep"), split)
+    pool_last = from_peer(pool, 3)
     pool_split = after(pool_split, pool_last)
-
-    share = lax.dynamic_index_in_dim(target_res, at_qry, 0, keepdims=False)
-    rest = lax.dynamic_index_in_dim(target_res, 1 - at_qry, 0, keepdims=False)
-    far = from_peer(share, 2)
     near = from_peer(share, 1)
 
     bases = [2 * (at_tgt ^ k) for k in range(4)]
@@ -252,7 +271,8 @@
     pool_other = across(pool_split, "rep")
     near_rest = from_peer(after(rest, far), 1)
 
-    one_blocks = [target_res[0], target_res[1], near, far]
+    own = after(target_res, share)
+    one_blocks = [own[0], own[1], near, far]
     one = partial_similar(query, one_blocks)
     one_other = across(one, "rep")
     far_rest = across(after(far, one_other), "qry")

time: 31.6 us -> 36.7 us (1.16)
  Pallas kernels: 6.49 us -> 12.6 us
  local copies, waits for them, and re-layouts: 2.25 us -> 1.68 us
  waiting for transfers between devices: 6.8 us -> 6.26 us
    pallas_call x0 -> x1, Pallas kernels: none -> 6.07 us  [take_share(): pl.pallas_call(share_kernel, out_shape=jax.ShapeDtypeStruct(blocks.shape[...]
    squeeze x1, local copies, waits for them, and re-layouts: 1.26 us -> 0.04 us  [per_device_by_target(): one_blocks = [own[0], own[1], near, far]]
    unnamed x10 -> x12, local copies, waits for them, and re-layouts: 0.59 us -> 1.24 us
    ppermute x6, waiting for transfers between devices: 6.28 us -> 5.78 us  [from_peer(): return lax.ppermute(array, 'tgt', [(i, i ^ k) for i in range(4)])]
  transfers between devices with their start and end apart: 14 -> 14, of which waited for: 5 -> 5; matrix products, arithmetic and copies ran while one was open for 2% -> 2% of each run, Pallas kernels for 13% -> 11%
where the time goes in v14:
time: 36.7 us; the launch traced here: 36.5 us
  starting transfers between devices  14.3 us (39%)
  Pallas kernels  12.6 us (34%)
  waiting for transfers between devices  6.26 us (17%)
  local copies, waits for them, and re-layouts  1.68 us (5%)
  between operations  1.42 us (4%)
    ppermute x6, starting transfers between devices, from_peer(): return lax.ppermute(array, 'tgt', [(i, i ^ k) for i in range(4)])  8.55 us
    pallas_call x7, Pallas kernels, call_kernel(): pl.pallas_call(kernel, out_shape=out_shape, in_specs=[VMEM] * len(operand...  6.51 us
    pallas_call x1, Pallas kernels, take_share(): pl.pallas_call(share_kernel, out_shape=jax.ShapeDtypeStruct(blocks.shape[...  6.07 us
    ppermute x6, waiting for transfers between devices, from_peer(): return lax.ppermute(array, 'tgt', [(i, i ^ k) for i in range(4)])  5.78 us
    ppermute x7, starting transfers between devices, across(): return lax.ppermute(array, axis, [(0, 1), (1, 0)])  4.87 us
    unnamed x12, local copies, waits for them, and re-layouts  1.24 us
    ppermute x1, starting transfers between devices, per_device_by_target(): pool_split = lax.ppermute(pool, ('tgt', 'rep'), split)  0.9 us
  transfers between devices with their start and end apart: 14, of which 5 were waited for; matrix products, arithmetic and copies ran while one was open for 2% of the time, Pallas kernels for 11%

profile of v14, /device:TPU:0, one launch (start us, length us, event | category | flops | bytes accessed | tf_op | source)
XLA Modules:
  0.0 36.5 jit_solution(16431426136860346694)
XLA Ops:
  0.6 6.1 %shard_map.86 = bf16[128,640]{1,0:T(8,128)(2,1)} custom-call(s32[1]{0:T(128)} %bitcast.8.at_ref, bf16[2,128,640]{2,1,0:T(8,128)(2,1)} %blocks_ref.1), custom_call_target="tpu_custom_call" | custom-call | tf_op jit(solution)/shard_map/pallas_call | solution.py:111
  6.7 4.1 %collective-permute-start = (bf16[128,640]{1,0:T(8,128)(2,1)}, bf16[128,640]{1,0:T(8,128)(2,1)S(1)}, u32[]{:S(2)}, u32[]{:S(2)}) collective-permute-start(bf16[128,640]{1,0:T(8,128)(2,1)} %shard_map.86), channel_id=1, source_target_pairs={{0,8},{4,12},{8,0},{12,4},{1,9},{5,13},{9,1},{13,5},{2,10},{6,14},... | collective-permute-start | bytes 491528 | tf_op jit(solution)/shard_map/ppermute | solution.py:223
  10.8 1.6 %collective-permute-start.3 = (bf16[128,640]{1,0:T(8,128)(2,1)}, bf16[128,640]{1,0:T(8,128)(2,1)S(1)}, u32[]{:S(2)}, u32[]{:S(2)}) collective-permute-start(bf16[128,640]{1,0:T(8,128)(2,1)} %shard_map.86), channel_id=1, source_target_pairs={{0,4},{4,0},{8,12},{12,8},{1,5},{5,1},{9,13},{13,9},{2,6},{6,2},{1... | collective-permute-start | bytes 491528 | tf_op jit(solution)/shard_map/ppermute | solution.py:223
  12.5 0.7 %copy-done.1 = f32[2,1280]{1,0:T(2,128)S(1)} copy-done((f32[2,1280]{1,0:T(2,128)S(1)}, f32[2,1280]{1,0:T(2,128)}, u32[]{:S(2)}) %copy-start.1) | copy-done | bytes 10264
  13.1 0.9 %collective-permute-start.1 = (f32[2,1280]{1,0:T(2,128)S(1)}, f32[2,1280]{1,0:T(2,128)S(1)}, u32[]{:S(2)}, u32[]{:S(2)}) collective-permute-start(f32[2,1280]{1,0:T(2,128)S(1)} %copy-done.1), channel_id=1, source_target_pairs={{0,4},{1,9},{4,0},{5,13},{8,12},{9,1},{12,8},{13,5},{2,6},{3,11},{... | collective-permute-start | bytes 30728 | tf_op jit(solution)/shard_map/ppermute | solution.py:237
  14.1 0.6 %copy-done.5 = s32[8]{0:T(128)S(1)} copy-done((s32[8]{0:T(128)S(1)}, s32[8]{0:T(128)}, u32[]{:S(2)}) %copy-start.5) | copy-done | bytes 56
  15.6 4.6 %collective-permute-done.2.refs_3_ = f32[2,1280]{1,0:T(2,128)S(1)} collective-permute-done((f32[2,1280]{1,0:T(2,128)S(1)}, f32[2,1280]{1,0:T(2,128)S(1)}, u32[]{:S(2)}, u32[]{:S(2)}) %collective-permute-start.2) | collective-permute-done | bytes 10272 | tf_op jit(solution)/shard_map/ppermute | solution.py:223
  20.4 0.4 %shard_map.88.mine = f32[256,512]{1,0:T(8,128)S(1)} custom-call(bf16[256,640]{1,0:T(8,128)(2,1)S(1)} %bitcast.22, bf16[128,640]{1,0:T(8,128)(2,1)S(1)} %get-tuple-element.37.refs_1_.refs_0_, bf16[128,640]{1,0:T(8,128)(2,1)S(1)} %get-tuple-element.36.refs_2_.refs_1_, bf16[128,640]{1,0:T(8,128)(2,1)S(1)} %collective-permute-done.3.refs_3_.refs_2_, ...), custom_call_target="tpu_custom_call" | custom-call | tf_op jit(solution)/shard_map/pallas_call | solution.py:93
  20.9 0.8 %collective-permute-start.4 = (bf16[64,640]{1,0:T(8,128)(2,1)S(1)}, bf16[64,640]{1,0:T(8,128)(2,1)S(1)}, u32[]{:S(2)}, u32[]{:S(2)}) collective-permute-start(bf16[64,640]{1,0:T(8,128)(2,1)S(1)} %get-tuple-element.40), channel_id=1, source_target_pairs={{0,4},{4,0},{8,12},{12,8},{1,5},{5,1},{9,13},{13,9},{2,6},{6,2},{1... | collective-permute-start | bytes 245768 | tf_op jit(solution)/shard_map/ppermute | solution.py:223
  21.8 1.2 %collective-permute-start.8 = (bf16[64,640]{1,0:T(8,128)(2,1)S(1)}, bf16[64,640]{1,0:T(8,128)(2,1)S(1)}, u32[]{:S(2)}, u32[]{:S(2)}) collective-permute-start(bf16[64,640]{1,0:T(8,128)(2,1)S(1)} %get-tuple-element.39), channel_id=1, source_target_pairs={{0,4},{4,0},{8,12},{12,8},{1,5},{5,1},{9,13},{13,9},{2,6},{6,2},{1... | collective-permute-start | bytes 245768 | tf_op jit(solution)/shard_map/ppermute | solution.py:223
  23.0 1.5 %collective-permute-start.7 = (bf16[128,640]{1,0:T(8,128)(2,1)S(1)}, bf16[128,640]{1,0:T(8,128)(2,1)S(1)}, u32[]{:S(2)}, u32[]{:S(2)}) collective-permute-start(bf16[128,640]{1,0:T(8,128)(2,1)S(1)} %collective-permute-done.refs_4_.refs_3_), channel_id=1, source_target_pairs={{0,2},{2,0},{1,3},{3,1},{4,6},{6,4},{5,7},{7,5},{8,10},{10,8},{9,1... | collective-permute-start | bytes 491528 | tf_op jit(solution)/shard_map/ppermute | solution.py:226
  24.5 0.8 %collective-permute-start.9 = (bf16[128,640]{1,0:T(8,128)(2,1)S(1)}, bf16[128,640]{1,0:T(8,128)(2,1)S(1)}, u32[]{:S(2)}, u32[]{:S(2)}) collective-permute-start(bf16[128,640]{1,0:T(8,128)(2,1)S(1)} %get-tuple-element.31), channel_id=1, source_target_pairs={{0,4},{4,0},{8,12},{12,8},{1,5},{5,1},{9,13},{13,9},{2,6},{6,2},{1... | collective-permute-start | bytes 491528 | tf_op jit(solution)/shard_map/ppermute | solution.py:223
  25.3 0.9 %collective-permute-done.4.refs_3_.refs_2_ = bf16[64,640]{1,0:T(8,128)(2,1)S(1)} collective-permute-done((bf16[64,640]{1,0:T(8,128)(2,1)S(1)}, bf16[64,640]{1,0:T(8,128)(2,1)S(1)}, u32[]{:S(2)}, u32[]{:S(2)}) %collective-permute-start.4) | collective-permute-done | bytes 81952 | tf_op jit(solution)/shard_map/ppermute | solution.py:223
  26.2 1.5 %collective-permute-start.11 = (bf16[64,640]{1,0:T(8,128)(2,1)S(1)}, bf16[64,640]{1,0:T(8,128)(2,1)S(1)}, u32[]{:S(2)}, u32[]{:S(2)}) collective-permute-start(bf16[64,640]{1,0:T(8,128)(2,1)S(1)} %collective-permute-done.4.refs_3_.refs_2_), channel_id=1, source_target_pairs={{0,2},{2,0},{1,3},{3,1},{4,6},{6,4},{5,7},{7,5},{8,10},{10,8},{9,1... | collective-permute-start | bytes 245768 | tf_op jit(solution)/shard_map/ppermute | solution.py:226
  27.7 0.3 collective-permute-done.8.refs_2_.refs_1_
  28.0 1.5 %collective-permute-start.10 = (bf16[64,640]{1,0:T(8,128)(2,1)S(1)}, bf16[64,640]{1,0:T(8,128)(2,1)S(1)}, u32[]{:S(2)}, u32[]{:S(2)}) collective-permute-start(bf16[64,640]{1,0:T(8,128)(2,1)S(1)} %collective-permute-done.8.refs_2_.refs_1_), channel_id=1, source_target_pairs={{0,2},{2,0},{1,3},{3,1},{4,6},{6,4},{5,7},{7,5},{8,10},{10,8},{9,1... | collective-permute-start | bytes 245768 | tf_op jit(solution)/shard_map/ppermute | solution.py:226
  29.5 0.3 shard_map.87
  29.8 0.3 shard_map.89.mine
  30.2 2.0 %shard_map.90.refs_3_ = f32[256,640]{1,0:T(8,128)S(1)} custom-call(f32[8,128]{1,0:T(8,128)S(1)} %get-tuple-element.26.weight_ref, f32[8,128]{1,0:T(8,128)S(1)} %broadcast_in_dim.48.len_ref, f32[1,128]{1,0:T(1,128)S(1)} %broadcast_in_dim.49.sharp_ref, f32[256,512]{1,0:T(8,128)S(1)} %shard_map.88.mine, f32[256,512]{1,0:T(8,128)S(1)} %collective-permute-done.6.other, ...), custom_call_target="tpu_custom_call" | custom-call | tf_op jit(solution)/shard_map/pallas_call | solution.py:93
  32.2 0.3 collective-permute-done.10.refs_2_.refs_1_
  32.6 0.3 shard_map.91.mine
  32.9 0.2 collective-permute-start.12
  33.1 1.2 %shard_map.92.refs_3_ = f32[256,640]{1,0:T(8,128)S(1)} custom-call(f32[8,128]{1,0:T(8,128)S(1)} %get-tuple-element.26.weight_ref, f32[8,128]{1,0:T(8,128)S(1)} %broadcast_in_dim.48.len_ref, f32[1,128]{1,0:T(1,128)S(1)} %broadcast_in_dim.49.sharp_ref, f32[256,256]{1,0:T(8,128)S(1)} %shard_map.89.mine, f32[256,256]{1,0:T(8,128)S(1)} %collective-permute-done.13.other, ...), custom_call_target="tpu_custom_call" | custom-call | tf_op jit(solution)/shard_map/pallas_call | solution.py:93
  34.5 2.0 %shard_map.93 = (bf16[256,640]{1,0:T(8,128)(2,1)}, f32[1,8]{1,0:T(1,128)}) custom-call(f32[8,128]{1,0:T(8,128)S(1)} %get-tuple-element.26.weight_ref, f32[8,128]{1,0:T(8,128)S(1)} %broadcast_in_dim.48.len_ref, f32[1,128]{1,0:T(1,128)S(1)} %broadcast_in_dim.49.sharp_ref, f32[256,256]{1,0:T(8,128)S(1)} %shard_map.91.mine, ...), custom_call_target="tpu_custom_call" | custom-call | tf_op jit(solution)/shard_map/pallas_call | solution.py:93
  (34 shorter events, 0.9 us)
Async XLA Ops:
  0.6 11.8 %copy-start.4 = (bf16[2,128,640]{2,1,0:T(8,128)(2,1)S(1)}, bf16[2,128,640]{2,1,0:T(8,128)(2,1)}, u32[]{:S(2)}) copy-start(bf16[2,128,640]{2,1,0:T(8,128)(2,1)} %blocks_ref.1) | copy-start | bytes 983044
  6.7 13.5 %collective-permute-start = (bf16[128,640]{1,0:T(8,128)(2,1)}, bf16[128,640]{1,0:T(8,128)(2,1)S(1)}, u32[]{:S(2)}, u32[]{:S(2)}) collective-permute-start(bf16[128,640]{1,0:T(8,128)(2,1)} %shard_map.86), channel_id=1, source_target_pairs={{0,8},{4,12},{8,0},{12,4},{1,9},{5,13},{9,1},{13,5},{2,10},{6,14},... | collective-permute-start | bytes 491528 | tf_op jit(solution)/shard_map/ppermute | solution.py:223
  10.8 9.6 %collective-permute-start.3 = (bf16[128,640]{1,0:T(8,128)(2,1)}, bf16[128,640]{1,0:T(8,128)(2,1)S(1)}, u32[]{:S(2)}, u32[]{:S(2)}) collective-permute-start(bf16[128,640]{1,0:T(8,128)(2,1)} %shard_map.86), channel_id=1, source_target_pairs={{0,4},{4,0},{8,12},{12,8},{1,5},{5,1},{9,13},{13,9},{2,6},{6,2},{1... | collective-permute-start | bytes 491528 | tf_op jit(solution)/shard_map/ppermute | solution.py:223
  12.4 0.7 %copy-start.1 = (f32[2,1280]{1,0:T(2,128)S(1)}, f32[2,1280]{1,0:T(2,128)}, u32[]{:S(2)}) copy-start(f32[2,1280]{1,0:T(2,128)} %refs_0_.1) | copy-start | bytes 30724
  12.4 8.0 %copy-start = (bf16[1,256,640]{2,1,0:T(8,128)(2,1)S(1)}, bf16[1,256,640]{2,1,0:T(8,128)(2,1)}, u32[]{:S(2)}) copy-start(bf16[1,256,640]{2,1,0:T(8,128)(2,1)} %param.7) | copy-start | bytes 983044
  13.1 7.1 %collective-permute-start.2 = (f32[2,1280]{1,0:T(2,128)S(1)}, f32[2,1280]{1,0:T(2,128)S(1)}, u32[]{:S(2)}, u32[]{:S(2)}) collective-permute-start(f32[2,1280]{1,0:T(2,128)S(1)} %copy-done.1), channel_id=1, source_target_pairs={{0,12},{4,8},{8,4},{12,0},{1,13},{5,9},{9,5},{13,1},{2,14},{6,10},... | collective-permute-start | bytes 30728 | tf_op jit(solution)/shard_map/ppermute | solution.py:223
  13.1 7.1 %collective-permute-start.1 = (f32[2,1280]{1,0:T(2,128)S(1)}, f32[2,1280]{1,0:T(2,128)S(1)}, u32[]{:S(2)}, u32[]{:S(2)}) collective-permute-start(f32[2,1280]{1,0:T(2,128)S(1)} %copy-done.1), channel_id=1, source_target_pairs={{0,4},{1,9},{4,0},{5,13},{8,12},{9,1},{12,8},{13,5},{2,6},{3,11},{... | collective-permute-start | bytes 30728 | tf_op jit(solution)/shard_map/ppermute | solution.py:237
  14.0 0.7 %copy-start.5 = (s32[8]{0:T(128)S(1)}, s32[8]{0:T(128)}, u32[]{:S(2)}) copy-start(s32[8]{0:T(128)} %param.9) | copy-start | bytes 100
  20.8 8.7 %copy-start.2 = (f32[1,1280]{1,0:T(1,128)S(1)}, f32[1,1280]{1,0:T(1,128)}, u32[]{:S(2)}) copy-start(f32[1,1280]{1,0:T(1,128)} %pool_ref.1) | copy-start | bytes 15364
  20.8 2.2 %collective-permute-start.6 = (f32[256,512]{1,0:T(8,128)S(1)}, f32[256,512]{1,0:T(8,128)S(1)}, u32[]{:S(2)}, u32[]{:S(2)}) collective-permute-start(f32[256,512]{1,0:T(8,128)S(1)} %shard_map.88.mine), channel_id=1, source_target_pairs={{0,1},{1,0},{2,3},{3,2},{4,5},{5,4},{6,7},{7,6},{8,9},{9,8},{10,11... | collective-permute-start | bytes 1572872 | tf_op jit(solution)/shard_map/ppermute | solution.py:226
  20.9 8.6 %copy-start.3 = (s32[1,28]{1,0:T(1,128)S(1)}, s32[1,28]{1,0:T(1,128)}, u32[]{:S(2)}) copy-start(s32[1,28]{1,0:T(1,128)} %hits_ref) | copy-start | bytes 340
  20.9 5.3 %collective-permute-start.4 = (bf16[64,640]{1,0:T(8,128)(2,1)S(1)}, bf16[64,640]{1,0:T(8,128)(2,1)S(1)}, u32[]{:S(2)}, u32[]{:S(2)}) collective-permute-start(bf16[64,640]{1,0:T(8,128)(2,1)S(1)} %get-tuple-element.40), channel_id=1, source_target_pairs={{0,4},{4,0},{8,12},{12,8},{1,5},{5,1},{9,13},{13,9},{2,6},{6,2},{1... | collective-permute-start | bytes 245768 | tf_op jit(solution)/shard_map/ppermute | solution.py:223
  21.8 6.2 %collective-permute-start.8 = (bf16[64,640]{1,0:T(8,128)(2,1)S(1)}, bf16[64,640]{1,0:T(8,128)(2,1)S(1)}, u32[]{:S(2)}, u32[]{:S(2)}) collective-permute-start(bf16[64,640]{1,0:T(8,128)(2,1)S(1)} %get-tuple-element.39), channel_id=1, source_target_pairs={{0,4},{4,0},{8,12},{12,8},{1,5},{5,1},{9,13},{13,9},{2,6},{6,2},{1... | collective-permute-start | bytes 245768 | tf_op jit(solution)/shard_map/ppermute | solution.py:223
  23.0 6.8 %collective-permute-start.7 = (bf16[128,640]{1,0:T(8,128)(2,1)S(1)}, bf16[128,640]{1,0:T(8,128)(2,1)S(1)}, u32[]{:S(2)}, u32[]{:S(2)}) collective-permute-start(bf16[128,640]{1,0:T(8,128)(2,1)S(1)} %collective-permute-done.refs_4_.refs_3_), channel_id=1, source_target_pairs={{0,2},{2,0},{1,3},{3,1},{4,6},{6,4},{5,7},{7,5},{8,10},{10,8},{9,1... | collective-permute-start | bytes 491528 | tf_op jit(solution)/shard_map/ppermute | solution.py:226
  24.5 7.7 %collective-permute-start.9 = (bf16[128,640]{1,0:T(8,128)(2,1)S(1)}, bf16[128,640]{1,0:T(8,128)(2,1)S(1)}, u32[]{:S(2)}, u32[]{:S(2)}) collective-permute-start(bf16[128,640]{1,0:T(8,128)(2,1)S(1)} %get-tuple-element.31), channel_id=1, source_target_pairs={{0,4},{4,0},{8,12},{12,8},{1,5},{5,1},{9,13},{13,9},{2,6},{6,2},{1... | collective-permute-start | bytes 491528 | tf_op jit(solution)/shard_map/ppermute | solution.py:223
  25.3 4.2 %collective-permute-start.5 = (f32[2,1280]{1,0:T(2,128)S(1)}, f32[2,1280]{1,0:T(2,128)S(1)}, u32[]{:S(2)}, u32[]{:S(2)}) collective-permute-start(f32[2,1280]{1,0:T(2,128)S(1)} %collective-permute-done.1.refs_1_), channel_id=1, source_target_pairs={{0,1},{1,0},{2,3},{3,2},{4,5},{5,4},{6,7},{7,6},{8,9},{9,8},{10,11... | collective-permute-start | bytes 30728 | tf_op jit(solution)/shard_map/ppermute | solution.py:226
  26.2 6.3 %collective-permute-start.11 = (bf16[64,640]{1,0:T(8,128)(2,1)S(1)}, bf16[64,640]{1,0:T(8,128)(2,1)S(1)}, u32[]{:S(2)}, u32[]{:S(2)}) collective-permute-start(bf16[64,640]{1,0:T(8,128)(2,1)S(1)} %collective-permute-done.4.refs_3_.refs_2_), channel_id=1, source_target_pairs={{0,2},{2,0},{1,3},{3,1},{4,6},{6,4},{5,7},{7,5},{8,10},{10,8},{9,1... | collective-permute-start | bytes 245768 | tf_op jit(solution)/shard_map/ppermute | solution.py:226
  28.0 4.6 %collective-permute-start.10 = (bf16[64,640]{1,0:T(8,128)(2,1)S(1)}, bf16[64,640]{1,0:T(8,128)(2,1)S(1)}, u32[]{:S(2)}, u32[]{:S(2)}) collective-permute-start(bf16[64,640]{1,0:T(8,128)(2,1)S(1)} %collective-permute-done.8.refs_2_.refs_1_), channel_id=1, source_target_pairs={{0,2},{2,0},{1,3},{3,1},{4,6},{6,4},{5,7},{7,5},{8,10},{10,8},{9,1... | collective-permute-start | bytes 245768 | tf_op jit(solution)/shard_map/ppermute | solution.py:226
  30.1 3.0 %collective-permute-start.13 = (f32[256,256]{1,0:T(8,128)S(1)}, f32[256,256]{1,0:T(8,128)S(1)}, u32[]{:S(2)}, u32[]{:S(2)}) collective-permute-start(f32[256,256]{1,0:T(8,128)S(1)} %shard_map.89.mine), channel_id=1, source_target_pairs={{0,1},{1,0},{2,3},{3,2},{4,5},{5,4},{6,7},{7,6},{8,9},{9,8},{10,11... | collective-permute-start | bytes 786440 | tf_op jit(solution)/shard_map/ppermute | solution.py:226
  32.9 1.6 %collective-permute-start.12 = (f32[256,256]{1,0:T(8,128)S(1)}, f32[256,256]{1,0:T(8,128)S(1)}, u32[]{:S(2)}, u32[]{:S(2)}) collective-permute-start(f32[256,256]{1,0:T(8,128)S(1)} %shard_map.91.mine), channel_id=1, source_target_pairs={{0,1},{1,0},{2,3},{3,2},{4,5},{5,4},{6,7},{7,6},{8,9},{9,8},{10,11... | collective-permute-start | bytes 786440 | tf_op jit(solution)/shard_map/ppermute | solution.py:226

commit v15 on v13

--- a/solution.py
+++ b/solution.py
@@ -126,20 +126,26 @@
     weight_ref[...] = jnp.broadcast_to(weights, weight_ref.shape)
 
 
-def partial_kernel(*refs):
-    query, blocks, out = refs[0], refs[1:-1], refs[-1]
-    out[...] = lax.dot_general(
-        query[...],
-        jnp.concatenate([block[...] for block in blocks]),
-        (((1,), (1,)), ((), ())),
-        preferred_element_type=jnp.float32,
-    )
-
-
-def partial_similar(query, blocks):
-    rows = sum(block.shape[0] for block in blocks)
-    shape = jax.ShapeDtypeStruct((query.shape[0], rows), jnp.float32)
-    return call_kernel(partial_kernel, shape, query, *blocks)
+def partial_kernel(groups, *refs):
+    query, blocks, outs = refs[0], refs[1 : -len(groups)], refs[-len(groups) :]
+    for count, out in zip(groups, outs):
+        out[...] = lax.dot_general(
+            query[...],
+            jnp.concatenate([block[...] for block in blocks[:count]]),
+            (((1,), (1,)), ((), ())),
+            preferred_element_type=jnp.float32,
+        )
+        blocks = blocks[count:]
+
+
+def partial_similar(query, *groups, flops=0):
+    shapes = tuple(
+        jax.ShapeDtypeStruct((query.shape[0], sum(b.shape[0] for b in group)), jnp.float32)
+        for group in groups
+    )
+    kernel = functools.partial(partial_kernel, [len(group) for group in groups])
+    blocks = [block for group in groups for block in group]
+    return call_kernel(kernel, shapes, query, *blocks, flops=flops)
 
 
 def align_block(similar, length, half_sharp):
@@ -162,34 +168,33 @@
     return raised / jnp.sum(raised, axis=1, keepdims=True)
 
 
-def weighted_term(weight, alignment, blocks):
-    target = blocks[0][...] if len(blocks) == 1 else jnp.concatenate([b[...] for b in blocks])
-    return weight * jnp.dot(alignment, target, preferred_element_type=jnp.float32)
-
-
-def profile_kernel(model_width, targets, last, weight_ref, len_ref, sharp_ref, mine, other, *refs):
-    blocks, out_ref = list(refs[:-1]), refs[-1]
+def profile_kernel(model_width, groups, last, weight_ref, len_ref, sharp_ref, *refs):
+    acc = None
+    for slots, counts in groups:
+        mine, other, refs = refs[0], refs[1], refs[2:]
+        rows = mine.shape[1] // len(slots)
+        for at, (slot, count) in enumerate(zip(slots, counts)):
+            part = pl.ds(at * rows, rows)
+            similar = (mine[:, part] + other[:, part]) * (1.0 / math.sqrt(model_width))
+            alignment = align_block(similar, len_ref[slot : slot + 1, :rows], sharp_ref[:, 0:1])
+            target = jnp.concatenate([block[...] for block in refs[:count]])
+            term = weight_ref[slot : slot + 1, 0:1] * jnp.dot(
+                alignment.astype(jnp.bfloat16), target, preferred_element_type=jnp.float32
+            )
+            acc = term if acc is None else acc + term
+            refs = refs[count:]
     if last:
-        posterior_ref, out_ref, posterior_out = blocks[-2], blocks[-1], out_ref
-        blocks = blocks[:-2]
+        acc_ref, posterior_ref, out_ref, posterior_out = refs
         count = posterior_out.shape[1]
         row = lax.broadcasted_iota(jnp.int32, (count, 1), 0)
         lane = lax.broadcasted_iota(jnp.int32, (1, count), 1)
         chosen = jnp.where(row == lane, posterior_ref[:, 0:1], 0.0)
         posterior_out[...] = jnp.sum(chosen, axis=0, keepdims=True)
-    rows = mine.shape[1] // len(targets)
-    acc = None
-    for at, (slot, count) in enumerate(targets):
-        part = pl.ds(at * rows, rows)
-        similar = (mine[:, part] + other[:, part]) * (1.0 / math.sqrt(model_width))
-        alignment = align_block(similar, len_ref[slot : slot + 1, :rows], sharp_ref[:, 0:1])
-        term = weighted_term(
-            weight_ref[slot : slot + 1, 0:1], alignment.astype(jnp.bfloat16), blocks[:count]
-        )
-        acc = term if acc is None else acc + term
-        blocks = blocks[count:]
-    if blocks:
-        acc += blocks[0][...]
+        acc += acc_ref[...]
+    else:
+        out_ref = refs[-1]
+        if len(refs) > 1:
+            acc += refs[0][...]
     out_ref[...] = acc.astype(out_ref.dtype)
 
 
@@ -233,9 +238,9 @@
     lengths = jnp.broadcast_to(lengths.astype(jnp.float32), table)
     half_sharp = jnp.broadcast_to(0.5 * sharpness, (1, target_rows))
 
-    def add_up(targets, out_shape, *operands):
+    def add_up(groups, out_shape, *operands):
         return call_kernel(
-            functools.partial(profile_kernel, model_width, targets, isinstance(out_shape, tuple)),
+            functools.partial(profile_kernel, model_width, groups, isinstance(out_shape, tuple)),
             out_shape,
             weights,
             lengths,
@@ -252,8 +257,9 @@
     pool_other = across(pool_split, "rep")
     near_rest = from_peer(after(rest, far), 1)
 
-    one_blocks = [target_res[0], target_res[1], near, far]
-    one = partial_similar(query, one_blocks)
+    own_blocks = [target_res[0], target_res[1]]
+    one_blocks = [near, far]
+    (one,) = partial_similar(query, own_blocks + one_blocks)
     one_other = across(one, "rep")
     far_rest = across(after(far, one_other), "qry")
     last_rest = [across(piece, "qry") for piece in last]
@@ -271,30 +277,49 @@
         pool_split,
         pool_other,
         pool_last,
-        flops=1_000_000_000,
+        flops=1000000000,
     )
     far_rest = after(far_rest, weights)
     two_blocks = [far_rest, *last]
-    two = partial_similar(query, two_blocks)
-    two_other = across(two, "rep")
+    two, two_b = partial_similar(query, [far_rest], last, flops=0)
+    two_other, two_b_other = across(two, "rep"), across(two_b, "rep")
 
     acc = add_up(
-        ((0, 1), (1, 1), (2, 1), (4, 1)), acc_shape, after(one, two), one_other, *one_blocks
-    )
-
-    three_blocks = [near_rest, *last_rest]
-    three = partial_similar(after(query, acc), three_blocks)
+        (((0, 1, 2, 4), (1, 1, 1, 1)),),
+        acc_shape,
+        after(one, two),
+        one_other,
+        *own_blocks,
+        *one_blocks,
+    )
+
+    (three,) = partial_similar(after(query, two), [near_rest])
     three_other = across(three, "rep")
-    acc = add_up(((5, 1), (6, 2)), acc_shape, after(two, three), two_other, *two_blocks, acc)
+    (four,) = partial_similar(after(query, acc, three), last_rest)
+    four_other = across(four, "rep")
+    acc = add_up(
+        (((5,), (1,)), ((6,), (2,)), ((3,), (1,))),
+        acc_shape,
+        after(two, four),
+        two_other,
+        far_rest,
+        two_b,
+        two_b_other,
+        *last,
+        three,
+        three_other,
+        near_rest,
+        acc,
+    )
     profile, posterior = add_up(
-        ((3, 1), (7, 2)),
+        (((7,), (2,)),),
         (
             jax.ShapeDtypeStruct(query.shape, jnp.bfloat16),
             jax.ShapeDtypeStruct((1, table[0]), jnp.float32),
         ),
-        three,
-        three_other,
-        *three_blocks,
+        four,
+        four_other,
+        *last_rest,
         acc,
         posterior,
     )

time: 31.6 us -> 33.4 us (1.057)
  starting transfers between devices: 14.3 us -> 15.5 us
  waiting for transfers between devices: 6.8 us -> 7.24 us
    ppermute x1, waiting for transfers between devices: 0.01 us -> 3.37 us  [per_device_by_target(): pool_split = lax.ppermute(target_pool, ('tgt', 'rep'), split)]
    ppermute x6, waiting for transfers between devices: 6.28 us -> 3.16 us  [from_peer(): return lax.ppermute(array, 'tgt', [(i, i ^ k) for i in range(4)])]
    ppermute x6, starting transfers between devices: 8.55 us -> 9.69 us  [from_peer(): return lax.ppermute(array, 'tgt', [(i, i ^ k) for i in range(4)])]
    ppermute x7 -> x9, starting transfers between devices: 4.84 us -> 5.33 us  [across(): return lax.ppermute(array, axis, [(0, 1), (1, 0)])]
    ppermute x1, starting transfers between devices: 0.9 us -> 0.45 us  [per_device_by_target(): pool_split = lax.ppermute(target_pool, ('tgt', 'rep'), split)]
    pallas_call x7 -> x8, Pallas kernels: 6.49 us -> 6.7 us  [call_kernel(): pl.pallas_call(kernel, out_shape=out_shape, in_specs=[VMEM] * len(operand...]
    ppermute x7 -> x9, waiting for transfers between devices: 0.52 us -> 0.71 us  [across(): return lax.ppermute(array, axis, [(0, 1), (1, 0)])]
  transfers between devices with their start and end apart: 14 -> 16, of which waited for: 5 -> 7; matrix products, arithmetic and copies ran while one was open for 2% -> 2% of each run, Pallas kernels for 13% -> 14%
where the time goes in v15:
time: 33.4 us; the launch traced here: 33.3 us
  starting transfers between devices  15.5 us (46%)
  waiting for transfers between devices  7.24 us (22%)
  Pallas kernels  6.7 us (20%)
  local copies, waits for them, and re-layouts  2.25 us (7%)
  between operations  1.43 us (4%)
    ppermute x6, starting transfers between devices, from_peer(): return lax.ppermute(array, 'tgt', [(i, i ^ k) for i in range(4)])  9.69 us
    pallas_call x8, Pallas kernels, call_kernel(): pl.pallas_call(kernel, out_shape=out_shape, in_specs=[VMEM] * len(operand...  6.7 us
    ppermute x9, starting transfers between devices, across(): return lax.ppermute(array, axis, [(0, 1), (1, 0)])  5.33 us
    ppermute x1, waiting for transfers between devices, per_device_by_target(): pool_split = lax.ppermute(target_pool, ('tgt', 'rep'), split)  3.37 us
    ppermute x6, waiting for transfers between devices, from_peer(): return lax.ppermute(array, 'tgt', [(i, i ^ k) for i in range(4)])  3.16 us
    squeeze x1, local copies, waits for them, and re-layouts, per_device_by_target(): rest = lax.dynamic_index_in_dim(target_res, 1 - at_qry, 0, keepdims=False)  1.26 us
    ppermute x9, waiting for transfers between devices, across(): return lax.ppermute(array, axis, [(0, 1), (1, 0)])  0.71 us
  transfers between devices with their start and end apart: 16, of which 7 were waited for; matrix products, arithmetic and copies ran while one was open for 2% of the time, Pallas kernels for 14%

profile of v15, /device:TPU:0, one launch (start us, length us, event | category | flops | bytes accessed | tf_op | source)
XLA Modules:
  0.0 33.3 jit_solution(13274835963401126428)
XLA Ops:
  0.7 1.3 %dynamic-slice_bitcast_fusion = (bf16[128,640]{1,0:T(8,128)(2,1)S(1)}, bf16[128,640]{1,0:T(8,128)(2,1)S(1)}, bf16[128,640]{1,0:T(8,128)(2,1)S(1)}, bf16[128,640]{1,0:T(8,128)(2,1)S(1)}) fusion(bf16[2,128,640]{2,1,0:T(8,128)(2,1)} %param.8, s32[]{:T(128)S(6)} %select_n.13, s32[]{:T(128)S(6)} %select_n.11), kind=kLoop, calls=%fused_computation | loop fusion | bytes 1310728 | tf_op jit(solution)/shard_map/jit(dynamic_index_in_dim)/squeeze | solution.py:224
  1.9 4.1 %collective-permute-start = (bf16[128,640]{1,0:T(8,128)(2,1)S(1)}, bf16[128,640]{1,0:T(8,128)(2,1)S(1)}, u32[]{:S(2)}, u32[]{:S(2)}) collective-permute-start(bf16[128,640]{1,0:T(8,128)(2,1)S(1)} %get-tuple-element.40), channel_id=1, source_target_pairs={{0,8},{4,12},{8,0},{12,4},{1,9},{5,13},{9,1},{13,5},{2,10},{6,14},... | collective-permute-start | bytes 491528 | tf_op jit(solution)/shard_map/ppermute | solution.py:210
  6.0 1.6 %collective-permute-start.3 = (bf16[128,640]{1,0:T(8,128)(2,1)S(1)}, bf16[128,640]{1,0:T(8,128)(2,1)S(1)}, u32[]{:S(2)}, u32[]{:S(2)}) collective-permute-start(bf16[128,640]{1,0:T(8,128)(2,1)S(1)} %get-tuple-element.40), channel_id=1, source_target_pairs={{0,4},{4,0},{8,12},{12,8},{1,5},{5,1},{9,13},{13,9},{2,6},{6,2},{1... | collective-permute-start | bytes 491528 | tf_op jit(solution)/shard_map/ppermute | solution.py:210
  7.6 0.4 %collective-permute-start.1 = (f32[2,1280]{1,0:T(2,128)S(1)}, f32[2,1280]{1,0:T(2,128)S(1)}, u32[]{:S(2)}, u32[]{:S(2)}) collective-permute-start(f32[2,1280]{1,0:T(2,128)S(1)} %copy-done.1), channel_id=1, source_target_pairs={{0,4},{1,9},{4,0},{5,13},{8,12},{9,1},{12,8},{13,5},{2,6},{3,11},{... | collective-permute-start | bytes 30728 | tf_op jit(solution)/shard_map/ppermute | solution.py:219
  8.1 1.3 %collective-permute-start.2 = (f32[2,1280]{1,0:T(2,128)S(1)}, f32[2,1280]{1,0:T(2,128)S(1)}, u32[]{:S(2)}, u32[]{:S(2)}) collective-permute-start(f32[2,1280]{1,0:T(2,128)S(1)} %copy-done.1), channel_id=1, source_target_pairs={{0,12},{4,8},{8,4},{12,0},{1,13},{5,9},{9,5},{13,1},{2,14},{6,10},... | collective-permute-start | bytes 30728 | tf_op jit(solution)/shard_map/ppermute | solution.py:210
  9.5 0.6 %copy-done.4 = s32[8]{0:T(128)S(1)} copy-done((s32[8]{0:T(128)S(1)}, s32[8]{0:T(128)}, u32[]{:S(2)}) %copy-start.4) | copy-done | bytes 56
  11.0 3.4 %collective-permute-done.1.refs_1_ = f32[2,1280]{1,0:T(2,128)S(1)} collective-permute-done((f32[2,1280]{1,0:T(2,128)S(1)}, f32[2,1280]{1,0:T(2,128)S(1)}, u32[]{:S(2)}, u32[]{:S(2)}) %collective-permute-start.1) | collective-permute-done | bytes 10272 | tf_op jit(solution)/shard_map/ppermute | solution.py:219
  14.4 0.9 %collective-permute-done.2.refs_3_ = f32[2,1280]{1,0:T(2,128)S(1)} collective-permute-done((f32[2,1280]{1,0:T(2,128)S(1)}, f32[2,1280]{1,0:T(2,128)S(1)}, u32[]{:S(2)}, u32[]{:S(2)}) %collective-permute-start.2) | collective-permute-done | bytes 10272 | tf_op jit(solution)/shard_map/ppermute | solution.py:210
  15.5 0.4 %shard_map.87.refs_0_ = f32[256,512]{1,0:T(8,128)S(1)} custom-call(bf16[256,640]{1,0:T(8,128)(2,1)S(1)} %bitcast.23, bf16[128,640]{1,0:T(8,128)(2,1)S(1)} %get-tuple-element.39.refs_1_.refs_2_, bf16[128,640]{1,0:T(8,128)(2,1)S(1)} %get-tuple-element.41.refs_2_.refs_3_, bf16[128,640]{1,0:T(8,128)(2,1)S(1)} %collective-permute-done.3.refs_3_.refs_4_, ...), custom_call_target="tpu_custom_call" | custom-call | tf_op jit(solution)/shard_map/pallas_call | solution.py:93
  16.0 0.6 %collective-permute-start.4 = (bf16[64,640]{1,0:T(8,128)(2,1)S(1)}, bf16[64,640]{1,0:T(8,128)(2,1)S(1)}, u32[]{:S(2)}, u32[]{:S(2)}) collective-permute-start(bf16[64,640]{1,0:T(8,128)(2,1)S(1)} %get-tuple-element.43), channel_id=1, source_target_pairs={{0,4},{4,0},{8,12},{12,8},{1,5},{5,1},{9,13},{13,9},{2,6},{6,2},{1... | collective-permute-start | bytes 245768 | tf_op jit(solution)/shard_map/ppermute | solution.py:210
  16.7 1.5 %collective-permute-start.8 = (bf16[64,640]{1,0:T(8,128)(2,1)S(1)}, bf16[64,640]{1,0:T(8,128)(2,1)S(1)}, u32[]{:S(2)}, u32[]{:S(2)}) collective-permute-start(bf16[64,640]{1,0:T(8,128)(2,1)S(1)} %get-tuple-element.42), channel_id=1, source_target_pairs={{0,4},{4,0},{8,12},{12,8},{1,5},{5,1},{9,13},{13,9},{2,6},{6,2},{1... | collective-permute-start | bytes 245768 | tf_op jit(solution)/shard_map/ppermute | solution.py:210
  18.1 1.5 %collective-permute-start.7 = (bf16[128,640]{1,0:T(8,128)(2,1)S(1)}, bf16[128,640]{1,0:T(8,128)(2,1)S(1)}, u32[]{:S(2)}, u32[]{:S(2)}) collective-permute-start(bf16[128,640]{1,0:T(8,128)(2,1)S(1)} %collective-permute-done.refs_4_.refs_5_), channel_id=1, source_target_pairs={{0,2},{2,0},{1,3},{3,1},{4,6},{6,4},{5,7},{7,5},{8,10},{10,8},{9,1... | collective-permute-start | bytes 491528 | tf_op jit(solution)/shard_map/ppermute | solution.py:213
  19.6 0.6 %collective-permute-start.9 = (bf16[128,640]{1,0:T(8,128)(2,1)S(1)}, bf16[128,640]{1,0:T(8,128)(2,1)S(1)}, u32[]{:S(2)}, u32[]{:S(2)}) collective-permute-start(bf16[128,640]{1,0:T(8,128)(2,1)S(1)} %get-tuple-element.31), channel_id=1, source_target_pairs={{0,4},{4,0},{8,12},{12,8},{1,5},{5,1},{9,13},{13,9},{2,6},{6,2},{1... | collective-permute-start | bytes 491528 | tf_op jit(solution)/shard_map/ppermute | solution.py:210
  20.2 1.1 %collective-permute-done.4.refs_3_.refs_6_ = bf16[64,640]{1,0:T(8,128)(2,1)S(1)} collective-permute-done((bf16[64,640]{1,0:T(8,128)(2,1)S(1)}, bf16[64,640]{1,0:T(8,128)(2,1)S(1)}, u32[]{:S(2)}, u32[]{:S(2)}) %collective-permute-start.4) | collective-permute-done | bytes 81952 | tf_op jit(solution)/shard_map/ppermute | solution.py:210
  21.3 1.5 %collective-permute-start.11 = (bf16[64,640]{1,0:T(8,128)(2,1)S(1)}, bf16[64,640]{1,0:T(8,128)(2,1)S(1)}, u32[]{:S(2)}, u32[]{:S(2)}) collective-permute-start(bf16[64,640]{1,0:T(8,128)(2,1)S(1)} %collective-permute-done.4.refs_3_.refs_6_), channel_id=1, source_target_pairs={{0,2},{2,0},{1,3},{3,1},{4,6},{6,4},{5,7},{7,5},{8,10},{10,8},{9,1... | collective-permute-start | bytes 245768 | tf_op jit(solution)/shard_map/ppermute | solution.py:213
  23.1 1.5 %collective-permute-start.10 = (bf16[64,640]{1,0:T(8,128)(2,1)S(1)}, bf16[64,640]{1,0:T(8,128)(2,1)S(1)}, u32[]{:S(2)}, u32[]{:S(2)}) collective-permute-start(bf16[64,640]{1,0:T(8,128)(2,1)S(1)} %collective-permute-done.8.refs_2_.refs_5_), channel_id=1, source_target_pairs={{0,2},{2,0},{1,3},{3,1},{4,6},{6,4},{5,7},{7,5},{8,10},{10,8},{9,1... | collective-permute-start | bytes 245768 | tf_op jit(solution)/shard_map/ppermute | solution.py:213
  24.6 0.3 shard_map.86
  24.9 0.3 shard_map.88
  25.4 0.8 %collective-permute-done.9.refs_1_.refs_9_ = bf16[128,640]{1,0:T(8,128)(2,1)S(1)} collective-permute-done((bf16[128,640]{1,0:T(8,128)(2,1)S(1)}, bf16[128,640]{1,0:T(8,128)(2,1)S(1)}, u32[]{:S(2)}, u32[]{:S(2)}) %collective-permute-start.9) | collective-permute-done | bytes 163872 | tf_op jit(solution)/shard_map/ppermute | solution.py:210
  26.5 2.0 %shard_map.89.refs_10_ = f32[256,640]{1,0:T(8,128)S(1)} custom-call(f32[8,128]{1,0:T(8,128)S(1)} %get-tuple-element.25.weight_ref, f32[8,128]{1,0:T(8,128)S(1)} %broadcast_in_dim.44.len_ref, f32[1,128]{1,0:T(1,128)S(1)} %broadcast_in_dim.45.sharp_ref, f32[256,512]{1,0:T(8,128)S(1)} %shard_map.87.refs_0_, f32[256,512]{1,0:T(8,128)S(1)} %collective-permute-done.6.refs_1_, ...), custom_call_target="tpu_custom_call" | custom-call | tf_op jit(solution)/shard_map/pallas_call | solution.py:93
  28.5 0.6 %collective-permute-start.14 = (f32[256,128]{1,0:T(8,128)S(1)}, f32[256,128]{1,0:T(8,128)S(1)}, u32[]{:S(2)}, u32[]{:S(2)}) collective-permute-start(f32[256,128]{1,0:T(8,128)S(1)} %get-tuple-element.34.refs_3_), channel_id=1, source_target_pairs={{0,1},{1,0},{2,3},{3,2},{4,5},{5,4},{6,7},{7,6},{8,9},{9,8},{10,11... | collective-permute-start | bytes 393224 | tf_op jit(solution)/shard_map/ppermute | solution.py:213
  29.5 0.6 %collective-permute-done.14.refs_4_ = f32[256,128]{1,0:T(8,128)S(1)} collective-permute-done((f32[256,128]{1,0:T(8,128)S(1)}, f32[256,128]{1,0:T(8,128)S(1)}, u32[]{:S(2)}, u32[]{:S(2)}) %collective-permute-start.14) | collective-permute-done | bytes 131104 | tf_op jit(solution)/shard_map/ppermute | solution.py:213
  30.1 1.5 %shard_map.92.refs_4_ = f32[256,640]{1,0:T(8,128)S(1)} custom-call(f32[8,128]{1,0:T(8,128)S(1)} %get-tuple-element.25.weight_ref, f32[8,128]{1,0:T(8,128)S(1)} %broadcast_in_dim.44.len_ref, f32[1,128]{1,0:T(1,128)S(1)} %broadcast_in_dim.45.sharp_ref, f32[256,128]{1,0:T(8,128)S(1)} %get-tuple-element.33.refs_0_, ...), custom_call_target="tpu_custom_call" | custom-call | tf_op jit(solution)/shard_map/pallas_call | solution.py:93
  31.6 1.6 %shard_map.93 = (bf16[256,640]{1,0:T(8,128)(2,1)}, f32[1,8]{1,0:T(1,128)}) custom-call(f32[8,128]{1,0:T(8,128)S(1)} %get-tuple-element.25.weight_ref, f32[8,128]{1,0:T(8,128)S(1)} %broadcast_in_dim.44.len_ref, f32[1,128]{1,0:T(1,128)S(1)} %broadcast_in_dim.45.sharp_ref, f32[256,128]{1,0:T(8,128)S(1)} %shard_map.91.refs_0_, ...), custom_call_target="tpu_custom_call" | custom-call | tf_op jit(solution)/shard_map/pallas_call | solution.py:93
  (36 shorter events, 1.8 us)
Async XLA Ops:
  0.6 7.0 %copy-start.1 = (f32[2,1280]{1,0:T(2,128)S(1)}, f32[2,1280]{1,0:T(2,128)}, u32[]{:S(2)}) copy-start(f32[2,1280]{1,0:T(2,128)} %refs_0_.1) | copy-start | bytes 30724
  0.6 14.9 %copy-start = (bf16[1,256,640]{2,1,0:T(8,128)(2,1)S(1)}, bf16[1,256,640]{2,1,0:T(8,128)(2,1)}, u32[]{:S(2)}) copy-start(bf16[1,256,640]{2,1,0:T(8,128)(2,1)} %param.7) | copy-start | bytes 983044
  1.9 13.4 %collective-permute-start = (bf16[128,640]{1,0:T(8,128)(2,1)S(1)}, bf16[128,640]{1,0:T(8,128)(2,1)S(1)}, u32[]{:S(2)}, u32[]{:S(2)}) collective-permute-start(bf16[128,640]{1,0:T(8,128)(2,1)S(1)} %get-tuple-element.40), channel_id=1, source_target_pairs={{0,8},{4,12},{8,0},{12,4},{1,9},{5,13},{9,1},{13,5},{2,10},{6,14},... | collective-permute-start | bytes 491528 | tf_op jit(solution)/shard_map/ppermute | solution.py:210
  6.0 9.5 %collective-permute-start.3 = (bf16[128,640]{1,0:T(8,128)(2,1)S(1)}, bf16[128,640]{1,0:T(8,128)(2,1)S(1)}, u32[]{:S(2)}, u32[]{:S(2)}) collective-permute-start(bf16[128,640]{1,0:T(8,128)(2,1)S(1)} %get-tuple-element.40), channel_id=1, source_target_pairs={{0,4},{4,0},{8,12},{12,8},{1,5},{5,1},{9,13},{13,9},{2,6},{6,2},{1... | collective-permute-start | bytes 491528 | tf_op jit(solution)/shard_map/ppermute | solution.py:210
  7.6 6.8 %collective-permute-start.1 = (f32[2,1280]{1,0:T(2,128)S(1)}, f32[2,1280]{1,0:T(2,128)S(1)}, u32[]{:S(2)}, u32[]{:S(2)}) collective-permute-start(f32[2,1280]{1,0:T(2,128)S(1)} %copy-done.1), channel_id=1, source_target_pairs={{0,4},{1,9},{4,0},{5,13},{8,12},{9,1},{12,8},{13,5},{2,6},{3,11},{... | collective-permute-start | bytes 30728 | tf_op jit(solution)/shard_map/ppermute | solution.py:219
  8.1 7.2 %collective-permute-start.2 = (f32[2,1280]{1,0:T(2,128)S(1)}, f32[2,1280]{1,0:T(2,128)S(1)}, u32[]{:S(2)}, u32[]{:S(2)}) collective-permute-start(f32[2,1280]{1,0:T(2,128)S(1)} %copy-done.1), channel_id=1, source_target_pairs={{0,12},{4,8},{8,4},{12,0},{1,13},{5,9},{9,5},{13,1},{2,14},{6,10},... | collective-permute-start | bytes 30728 | tf_op jit(solution)/shard_map/ppermute | solution.py:210
  9.4 0.7 %copy-start.4 = (s32[8]{0:T(128)S(1)}, s32[8]{0:T(128)}, u32[]{:S(2)}) copy-start(s32[8]{0:T(128)} %param.9) | copy-start | bytes 100
  15.9 2.2 %collective-permute-start.6 = (f32[256,512]{1,0:T(8,128)S(1)}, f32[256,512]{1,0:T(8,128)S(1)}, u32[]{:S(2)}, u32[]{:S(2)}) collective-permute-start(f32[256,512]{1,0:T(8,128)S(1)} %shard_map.87.refs_0_), channel_id=1, source_target_pairs={{0,1},{1,0},{2,3},{3,2},{4,5},{5,4},{6,7},{7,6},{8,9},{9,8},{10,11... | collective-permute-start | bytes 1572872 | tf_op jit(solution)/shard_map/ppermute | solution.py:213
  16.0 8.6 %copy-start.2 = (f32[1,1280]{1,0:T(1,128)S(1)}, f32[1,1280]{1,0:T(1,128)}, u32[]{:S(2)}) copy-start(f32[1,1280]{1,0:T(1,128)} %pool_ref.1) | copy-start | bytes 15364
  16.0 5.3 %collective-permute-start.4 = (bf16[64,640]{1,0:T(8,128)(2,1)S(1)}, bf16[64,640]{1,0:T(8,128)(2,1)S(1)}, u32[]{:S(2)}, u32[]{:S(2)}) collective-permute-start(bf16[64,640]{1,0:T(8,128)(2,1)S(1)} %get-tuple-element.43), channel_id=1, source_target_pairs={{0,4},{4,0},{8,12},{12,8},{1,5},{5,1},{9,13},{13,9},{2,6},{6,2},{1... | collective-permute-start | bytes 245768 | tf_op jit(solution)/shard_map/ppermute | solution.py:210
  16.7 7.9 %copy-start.3 = (s32[1,28]{1,0:T(1,128)S(1)}, s32[1,28]{1,0:T(1,128)}, u32[]{:S(2)}) copy-start(s32[1,28]{1,0:T(1,128)} %hits_ref) | copy-start | bytes 340
  16.7 6.4 %collective-permute-start.8 = (bf16[64,640]{1,0:T(8,128)(2,1)S(1)}, bf16[64,640]{1,0:T(8,128)(2,1)S(1)}, u32[]{:S(2)}, u32[]{:S(2)}) collective-permute-start(bf16[64,640]{1,0:T(8,128)(2,1)S(1)} %get-tuple-element.42), channel_id=1, source_target_pairs={{0,4},{4,0},{8,12},{12,8},{1,5},{5,1},{9,13},{13,9},{2,6},{6,2},{1... | collective-permute-start | bytes 245768 | tf_op jit(solution)/shard_map/ppermute | solution.py:210
  18.1 6.8 %collective-permute-start.7 = (bf16[128,640]{1,0:T(8,128)(2,1)S(1)}, bf16[128,640]{1,0:T(8,128)(2,1)S(1)}, u32[]{:S(2)}, u32[]{:S(2)}) collective-permute-start(bf16[128,640]{1,0:T(8,128)(2,1)S(1)} %collective-permute-done.refs_4_.refs_5_), channel_id=1, source_target_pairs={{0,2},{2,0},{1,3},{3,1},{4,6},{6,4},{5,7},{7,5},{8,10},{10,8},{9,1... | collective-permute-start | bytes 491528 | tf_op jit(solution)/shard_map/ppermute | solution.py:213
  19.6 6.6 %collective-permute-start.9 = (bf16[128,640]{1,0:T(8,128)(2,1)S(1)}, bf16[128,640]{1,0:T(8,128)(2,1)S(1)}, u32[]{:S(2)}, u32[]{:S(2)}) collective-permute-start(bf16[128,640]{1,0:T(8,128)(2,1)S(1)} %get-tuple-element.31), channel_id=1, source_target_pairs={{0,4},{4,0},{8,12},{12,8},{1,5},{5,1},{9,13},{13,9},{2,6},{6,2},{1... | collective-permute-start | bytes 491528 | tf_op jit(solution)/shard_map/ppermute | solution.py:210
  20.2 4.4 %collective-permute-start.5 = (f32[2,1280]{1,0:T(2,128)S(1)}, f32[2,1280]{1,0:T(2,128)S(1)}, u32[]{:S(2)}, u32[]{:S(2)}) collective-permute-start(f32[2,1280]{1,0:T(2,128)S(1)} %collective-permute-done.1.refs_1_), channel_id=1, source_target_pairs={{0,1},{1,0},{2,3},{3,2},{4,5},{5,4},{6,7},{7,6},{8,9},{9,8},{10,11... | collective-permute-start | bytes 30728 | tf_op jit(solution)/shard_map/ppermute | solution.py:213
  21.3 7.8 %collective-permute-start.11 = (bf16[64,640]{1,0:T(8,128)(2,1)S(1)}, bf16[64,640]{1,0:T(8,128)(2,1)S(1)}, u32[]{:S(2)}, u32[]{:S(2)}) collective-permute-start(bf16[64,640]{1,0:T(8,128)(2,1)S(1)} %collective-permute-done.4.refs_3_.refs_6_), channel_id=1, source_target_pairs={{0,2},{2,0},{1,3},{3,1},{4,6},{6,4},{5,7},{7,5},{8,10},{10,8},{9,1... | collective-permute-start | bytes 245768 | tf_op jit(solution)/shard_map/ppermute | solution.py:213
  23.1 6.0 %collective-permute-start.10 = (bf16[64,640]{1,0:T(8,128)(2,1)S(1)}, bf16[64,640]{1,0:T(8,128)(2,1)S(1)}, u32[]{:S(2)}, u32[]{:S(2)}) collective-permute-start(bf16[64,640]{1,0:T(8,128)(2,1)S(1)} %collective-permute-done.8.refs_2_.refs_5_), channel_id=1, source_target_pairs={{0,2},{2,0},{1,3},{3,1},{4,6},{6,4},{5,7},{7,5},{8,10},{10,8},{9,1... | collective-permute-start | bytes 245768 | tf_op jit(solution)/shard_map/ppermute | solution.py:213
  25.3 4.2 %collective-permute-start.13 = (f32[256,128]{1,0:T(8,128)S(1)}, f32[256,128]{1,0:T(8,128)S(1)}, u32[]{:S(2)}, u32[]{:S(2)}) collective-permute-start(f32[256,128]{1,0:T(8,128)S(1)} %get-tuple-element.33.refs_0_), channel_id=1, source_target_pairs={{0,1},{1,0},{2,3},{3,2},{4,5},{5,4},{6,7},{7,6},{8,9},{9,8},{10,11... | collective-permute-start | bytes 393224 | tf_op jit(solution)/shard_map/ppermute | solution.py:213
  26.4 3.6 %collective-permute-start.15 = (f32[256,128]{1,0:T(8,128)S(1)}, f32[256,128]{1,0:T(8,128)S(1)}, u32[]{:S(2)}, u32[]{:S(2)}) collective-permute-start(f32[256,128]{1,0:T(8,128)S(1)} %shard_map.90.refs_7_), channel_id=1, source_target_pairs={{0,1},{1,0},{2,3},{3,2},{4,5},{5,4},{6,7},{7,6},{8,9},{9,8},{10,11... | collective-permute-start | bytes 393224 | tf_op jit(solution)/shard_map/ppermute | solution.py:213
  28.5 1.5 %collective-permute-start.14 = (f32[256,128]{1,0:T(8,128)S(1)}, f32[256,128]{1,0:T(8,128)S(1)}, u32[]{:S(2)}, u32[]{:S(2)}) collective-permute-start(f32[256,128]{1,0:T(8,128)S(1)} %get-tuple-element.34.refs_3_), channel_id=1, source_target_pairs={{0,1},{1,0},{2,3},{3,2},{4,5},{5,4},{6,7},{7,6},{8,9},{9,8},{10,11... | collective-permute-start | bytes 393224 | tf_op jit(solution)/shard_map/ppermute | solution.py:213
  29.4 2.3 %collective-permute-start.12 = (f32[256,128]{1,0:T(8,128)S(1)}, f32[256,128]{1,0:T(8,128)S(1)}, u32[]{:S(2)}, u32[]{:S(2)}) collective-permute-start(f32[256,128]{1,0:T(8,128)S(1)} %shard_map.91.refs_0_), channel_id=1, source_target_pairs={{0,1},{1,0},{2,3},{3,2},{4,5},{5,4},{6,7},{7,6},{8,9},{9,8},{10,11... | collective-permute-start | bytes 393224 | tf_op jit(solution)/shard_map/ppermute | solution.py:213

commit v16 on v15

--- a/solution.py
+++ b/solution.py
@@ -101,16 +101,17 @@
     )(*operands)
 
 
-def weigh_kernel(slot_ref, hits_ref, pool_ref, owner_ref, *refs):
+def weigh_kernel(table_ref, hits_ref, pool_ref, *refs):
     libs, (posterior_ref, weight_ref) = refs[:-2], refs[-2:]
     owned, width = libs[0].shape
     target_count = posterior_ref.shape[0]
-    target = lax.broadcasted_iota(jnp.int32, (target_count, 1), 0)
-    counts = jnp.sum(jnp.where(hits_ref[...] == target, 1.0, 0.0), axis=1, keepdims=True)
+    target = lax.broadcasted_iota(jnp.int32, (target_count, 1), 0).astype(jnp.float32)
+    hits = hits_ref[...].astype(jnp.float32)
+    counts = jnp.sum(jnp.where(hits == target, 1.0, 0.0), axis=1, keepdims=True)
     logits = jnp.zeros((target_count, 1), jnp.float32)
     for at, lib in enumerate(libs):
         products = jnp.sum(lib[...] * pool_ref[...], axis=1, keepdims=True) / math.sqrt(width)
-        first = owner_ref[at : at + 1, 0:1] * owned
+        first = table_ref[target_count + at : target_count + at + 1, 0:1] * owned
         for a in range(owned):
             logits = jnp.where(target == first + a, products[a : a + 1, :], logits)
     raised = jnp.exp(logits - jnp.max(logits, axis=0, keepdims=True))
@@ -118,10 +119,10 @@
     shown = jnp.where(counts > 0.0, logits, -jnp.inf)
     parts = counts * jnp.exp(shown - jnp.max(shown, axis=0, keepdims=True))
     weights = parts / jnp.sum(parts, axis=0, keepdims=True)
-    lane = lax.broadcasted_iota(jnp.int32, (1, target_count), 1)
+    lane = lax.broadcasted_iota(jnp.int32, (1, target_count), 1).astype(jnp.float32)
     posterior_ref[...] = jnp.broadcast_to(posterior, posterior_ref.shape)
     weights = jnp.sum(jnp.where(target == lane, weights, 0.0), axis=0, keepdims=True)
-    weights = jnp.where(slot_ref[:, 0:1] == lane, weights, 0.0)
+    weights = jnp.where(table_ref[:target_count, 0:1] == lane, weights, 0.0)
     weights = jnp.sum(weights, axis=1, keepdims=True)
     weight_ref[...] = jnp.broadcast_to(weights, weight_ref.shape)
 
@@ -168,15 +169,16 @@
     return raised / jnp.sum(raised, axis=1, keepdims=True)
 
 
-def profile_kernel(model_width, groups, last, weight_ref, len_ref, sharp_ref, *refs):
-    acc = None
+def profile_kernel(model_width, groups, last, weight_ref, table_ref, sharp_ref, *refs):
+    acc, lengths = None, 2 * weight_ref.shape[0]
     for slots, counts in groups:
         mine, other, refs = refs[0], refs[1], refs[2:]
         rows = mine.shape[1] // len(slots)
         for at, (slot, count) in enumerate(zip(slots, counts)):
             part = pl.ds(at * rows, rows)
             similar = (mine[:, part] + other[:, part]) * (1.0 / math.sqrt(model_width))
-            alignment = align_block(similar, len_ref[slot : slot + 1, :rows], sharp_ref[:, 0:1])
+            length = table_ref[lengths + slot : lengths + slot + 1, :rows]
+            alignment = align_block(similar, length, sharp_ref[:, 0:1])
             target = jnp.concatenate([block[...] for block in refs[:count]])
             term = weight_ref[slot : slot + 1, 0:1] * jnp.dot(
                 alignment.astype(jnp.bfloat16), target, preferred_element_type=jnp.float32
@@ -230,12 +232,12 @@
     for base in bases[1:]:
         slots += [base + at_qry, base + 1 - at_qry]
     owners = [at_tgt, at_tgt ^ (1 + at_rep), at_tgt ^ (2 - at_rep), at_tgt ^ 3]
-    table = (len(target_len), target_rows)
-    slots = jnp.broadcast_to(jnp.stack(slots)[:, None], table)
-    owners = jnp.broadcast_to(jnp.stack(owners + owners)[:, None], table)
-    named = slots[:, : table[0]] == jnp.arange(table[0])[None]
-    lengths = jnp.sum(jnp.where(named, target_len[None], 0), axis=1, keepdims=True)
-    lengths = jnp.broadcast_to(lengths.astype(jnp.float32), table)
+    count = len(target_len)
+    slots = jnp.stack(slots)
+    named = slots[:, None] == jnp.arange(count)[None]
+    lengths = jnp.sum(jnp.where(named, target_len[None], 0), axis=1)
+    table = jnp.concatenate([slots, jnp.stack(owners + owners), lengths]).astype(jnp.float32)
+    table = jnp.broadcast_to(table[:, None], (3 * count, target_rows))
     half_sharp = jnp.broadcast_to(0.5 * sharpness, (1, target_rows))
 
     def add_up(groups, out_shape, *operands):
@@ -243,13 +245,17 @@
             functools.partial(profile_kernel, model_width, groups, isinstance(out_shape, tuple)),
             out_shape,
             weights,
-            lengths,
+            table,
             half_sharp,
             *operands,
         )
 
     acc_shape = jax.ShapeDtypeStruct(query.shape, jnp.float32)
-    far = after(far, pool_split, pool_last, slots, owners, lengths, half_sharp)
+    own_blocks = [target_res[0], target_res[1]]
+    (own,) = partial_similar(after(query, share), own_blocks)
+    own_other = across(own, "rep")
+
+    far = after(far, pool_split, pool_last, table, half_sharp)
     near = after(near, far)
     far = after(far, near)
     half = target_rows // 2
@@ -257,69 +263,58 @@
     pool_other = across(pool_split, "rep")
     near_rest = from_peer(after(rest, far), 1)
 
-    own_blocks = [target_res[0], target_res[1]]
     one_blocks = [near, far]
-    (one,) = partial_similar(query, own_blocks + one_blocks)
+    (one,) = partial_similar(query, one_blocks)
     one_other = across(one, "rep")
     far_rest = across(after(far, one_other), "qry")
+    last = [last[0], after(last[1], pool_other)]
     last_rest = [across(piece, "qry") for piece in last]
     posterior, weights = call_kernel(
         weigh_kernel,
         (
-            jax.ShapeDtypeStruct(table, jnp.float32),
-            jax.ShapeDtypeStruct(table, jnp.float32),
+            jax.ShapeDtypeStruct((count, target_rows), jnp.float32),
+            jax.ShapeDtypeStruct((count, target_rows), jnp.float32),
         ),
-        slots,
+        table,
         after(hits, last[1]),
         query_pool,
-        owners,
         target_pool,
         pool_split,
         pool_other,
         pool_last,
-        flops=1000000000,
+        flops=1500000000,
     )
     far_rest = after(far_rest, weights)
     two_blocks = [far_rest, *last]
-    two, two_b = partial_similar(query, [far_rest], last, flops=0)
-    two_other, two_b_other = across(two, "rep"), across(two_b, "rep")
+    (two,) = partial_similar(query, two_blocks, flops=0)
+    two_other = across(two, "rep")
 
     acc = add_up(
-        (((0, 1, 2, 4), (1, 1, 1, 1)),),
+        (((0, 1), (1, 1)), ((2, 4), (1, 1))),
         acc_shape,
-        after(one, two),
+        after(own, two),
+        own_other,
+        *own_blocks,
+        one,
         one_other,
-        *own_blocks,
         *one_blocks,
     )
 
-    (three,) = partial_similar(after(query, two), [near_rest])
+    three_blocks = [near_rest, *last_rest]
+    (three,) = partial_similar(after(query, acc), three_blocks)
     three_other = across(three, "rep")
-    (four,) = partial_similar(after(query, acc, three), last_rest)
-    four_other = across(four, "rep")
     acc = add_up(
-        (((5,), (1,)), ((6,), (2,)), ((3,), (1,))),
-        acc_shape,
-        after(two, four),
-        two_other,
-        far_rest,
-        two_b,
-        two_b_other,
-        *last,
+        (((5, 6), (1, 2)),), acc_shape, after(two, three), two_other, *two_blocks, acc
+    )
+    profile, posterior = add_up(
+        (((3, 7), (1, 2)),),
+        (
+            jax.ShapeDtypeStruct(query.shape, jnp.bfloat16),
+            jax.ShapeDtypeStruct((1, count), jnp.float32),
+        ),
         three,
         three_other,
-        near_rest,
-        acc,
-    )
-    profile, posterior = add_up(
-        (((7,), (2,)),),
-        (
-            jax.ShapeDtypeStruct(query.shape, jnp.bfloat16),
-            jax.ShapeDtypeStruct((1, table[0]), jnp.float32),
-        ),
-        four,
-        four_other,
-        *last_rest,
+        *three_blocks,
         acc,
         posterior,
     )

time: 33.4 us -> 32 us (0.958)
  starting transfers between devices: 15.5 us -> 14.4 us
  waiting for transfers between devices: 7.24 us -> 6.87 us
    ppermute x1, waiting for transfers between devices: 3.37 us -> 0.01 us  [per_device_by_target(): pool_split = lax.ppermute(target_pool, ('tgt', 'rep'), split)]
    ppermute x6, waiting for transfers between devices: 3.16 us -> 5.64 us  [from_peer(): return lax.ppermute(array, 'tgt', [(i, i ^ k) for i in range(4)])]
    ppermute x6, starting transfers between devices: 9.69 us -> 8.56 us  [from_peer(): return lax.ppermute(array, 'tgt', [(i, i ^ k) for i in range(4)])]
    ppermute x9 -> x8, waiting for transfers between devices: 0.71 us -> 1.23 us  [across(): return lax.ppermute(array, axis, [(0, 1), (1, 0)])]
    ppermute x1, starting transfers between devices: 0.45 us -> 0.9 us  [per_device_by_target(): pool_split = lax.ppermute(target_pool, ('tgt', 'rep'), split)]
    ppermute x9 -> x8, starting transfers between devices: 5.33 us -> 4.96 us  [across(): return lax.ppermute(array, axis, [(0, 1), (1, 0)])]
  transfers between devices with their start and end apart: 16 -> 15, of which waited for: 7 -> 5; matrix products, arithmetic and copies ran while one was open for 2% -> 1% of each run, Pallas kernels for 14% -> 15%
where the time goes in v16:
time: 32 us; the launch traced here: 31.8 us
  starting transfers between devices  14.4 us (45%)
  waiting for transfers between devices  6.87 us (21%)
  Pallas kernels  6.74 us (21%)
  local copies, waits for them, and re-layouts  2.12 us (7%)
  between operations  1.49 us (5%)
    ppermute x6, starting transfers between devices, from_peer(): return lax.ppermute(array, 'tgt', [(i, i ^ k) for i in range(4)])  8.56 us
    pallas_call x8, Pallas kernels, call_kernel(): pl.pallas_call(kernel, out_shape=out_shape, in_specs=[VMEM] * len(operand...  6.74 us
    ppermute x6, waiting for transfers between devices, from_peer(): return lax.ppermute(array, 'tgt', [(i, i ^ k) for i in range(4)])  5.64 us
    ppermute x8, starting transfers between devices, across(): return lax.ppermute(array, axis, [(0, 1), (1, 0)])  4.96 us
    squeeze x1, local copies, waits for them, and re-layouts, per_device_by_target(): rest = lax.dynamic_index_in_dim(target_res, 1 - at_qry, 0, keepdims=False)  1.26 us
    ppermute x8, waiting for transfers between devices, across(): return lax.ppermute(array, axis, [(0, 1), (1, 0)])  1.23 us
    ppermute x1, starting transfers between devices, per_device_by_target(): pool_split = lax.ppermute(target_pool, ('tgt', 'rep'), split)  0.9 us
  transfers between devices with their start and end apart: 15, of which 5 were waited for; matrix products, arithmetic and copies ran while one was open for 1% of the time, Pallas kernels for 15%

profile of v16, /device:TPU:0, one launch (start us, length us, event | category | flops | bytes accessed | tf_op | source)
XLA Modules:
  0.0 31.8 jit_solution(8033010090154280702)
XLA Ops:
  0.7 1.3 %dynamic-slice_bitcast_fusion = (bf16[128,640]{1,0:T(8,128)(2,1)S(1)}, bf16[128,640]{1,0:T(8,128)(2,1)S(1)}, bf16[128,640]{1,0:T(8,128)(2,1)S(1)}, bf16[128,640]{1,0:T(8,128)(2,1)S(1)}) fusion(bf16[2,128,640]{2,1,0:T(8,128)(2,1)} %param.8, s32[]{:T(128)S(6)} %select_n.13, s32[]{:T(128)S(6)} %select_n.12), kind=kLoop, calls=%fused_computation | loop fusion | bytes 1310728 | tf_op jit(solution)/shard_map/jit(dynamic_index_in_dim)/squeeze | solution.py:226
  1.9 4.1 %collective-permute-start = (bf16[128,640]{1,0:T(8,128)(2,1)S(1)}, bf16[128,640]{1,0:T(8,128)(2,1)S(1)}, u32[]{:S(2)}, u32[]{:S(2)}) collective-permute-start(bf16[128,640]{1,0:T(8,128)(2,1)S(1)} %get-tuple-element.38), channel_id=1, source_target_pairs={{0,8},{4,12},{8,0},{12,4},{1,9},{5,13},{9,1},{13,5},{2,10},{6,14},... | collective-permute-start | bytes 491528 | tf_op jit(solution)/shard_map/ppermute | solution.py:212
  6.0 1.6 %collective-permute-start.3 = (bf16[128,640]{1,0:T(8,128)(2,1)S(1)}, bf16[128,640]{1,0:T(8,128)(2,1)S(1)}, u32[]{:S(2)}, u32[]{:S(2)}) collective-permute-start(bf16[128,640]{1,0:T(8,128)(2,1)S(1)} %get-tuple-element.38), channel_id=1, source_target_pairs={{0,4},{4,0},{8,12},{12,8},{1,5},{5,1},{9,13},{13,9},{2,6},{6,2},{1... | collective-permute-start | bytes 491528 | tf_op jit(solution)/shard_map/ppermute | solution.py:212
  7.6 0.9 %collective-permute-start.1 = (f32[2,1280]{1,0:T(2,128)S(1)}, f32[2,1280]{1,0:T(2,128)S(1)}, u32[]{:S(2)}, u32[]{:S(2)}) collective-permute-start(f32[2,1280]{1,0:T(2,128)S(1)} %copy-done.1), channel_id=1, source_target_pairs={{0,4},{1,9},{4,0},{5,13},{8,12},{9,1},{12,8},{13,5},{2,6},{3,11},{... | collective-permute-start | bytes 30728 | tf_op jit(solution)/shard_map/ppermute | solution.py:221
  8.5 0.3 shard_map.87.refs_0_
  9.0 0.6 %copy-done.4 = s32[8]{0:T(128)S(1)} copy-done((s32[8]{0:T(128)S(1)}, s32[8]{0:T(128)}, u32[]{:S(2)}) %copy-start.4) | copy-done | bytes 56
  10.5 4.7 %collective-permute-done.2.refs_3_ = f32[2,1280]{1,0:T(2,128)S(1)} collective-permute-done((f32[2,1280]{1,0:T(2,128)S(1)}, f32[2,1280]{1,0:T(2,128)S(1)}, u32[]{:S(2)}, u32[]{:S(2)}) %collective-permute-start.2) | collective-permute-done | bytes 10272 | tf_op jit(solution)/shard_map/ppermute | solution.py:212
  15.3 0.3 shard_map.88.refs_4_
  15.7 0.8 %collective-permute-start.4 = (bf16[64,640]{1,0:T(8,128)(2,1)S(1)}, bf16[64,640]{1,0:T(8,128)(2,1)S(1)}, u32[]{:S(2)}, u32[]{:S(2)}) collective-permute-start(bf16[64,640]{1,0:T(8,128)(2,1)S(1)} %get-tuple-element.41), channel_id=1, source_target_pairs={{0,4},{4,0},{8,12},{12,8},{1,5},{5,1},{9,13},{13,9},{2,6},{6,2},{1... | collective-permute-start | bytes 245768 | tf_op jit(solution)/shard_map/ppermute | solution.py:212
  16.5 1.2 %collective-permute-start.8 = (bf16[64,640]{1,0:T(8,128)(2,1)S(1)}, bf16[64,640]{1,0:T(8,128)(2,1)S(1)}, u32[]{:S(2)}, u32[]{:S(2)}) collective-permute-start(bf16[64,640]{1,0:T(8,128)(2,1)S(1)} %get-tuple-element.40), channel_id=1, source_target_pairs={{0,4},{4,0},{8,12},{12,8},{1,5},{5,1},{9,13},{13,9},{2,6},{6,2},{1... | collective-permute-start | bytes 245768 | tf_op jit(solution)/shard_map/ppermute | solution.py:212
  17.8 1.5 %collective-permute-start.7 = (bf16[128,640]{1,0:T(8,128)(2,1)S(1)}, bf16[128,640]{1,0:T(8,128)(2,1)S(1)}, u32[]{:S(2)}, u32[]{:S(2)}) collective-permute-start(bf16[128,640]{1,0:T(8,128)(2,1)S(1)} %collective-permute-done.refs_2_.refs_7_), channel_id=1, source_target_pairs={{0,2},{2,0},{1,3},{3,1},{4,6},{6,4},{5,7},{7,5},{8,10},{10,8},{9,1... | collective-permute-start | bytes 491528 | tf_op jit(solution)/shard_map/ppermute | solution.py:215
  19.3 0.8 %collective-permute-start.10 = (bf16[128,640]{1,0:T(8,128)(2,1)S(1)}, bf16[128,640]{1,0:T(8,128)(2,1)S(1)}, u32[]{:S(2)}, u32[]{:S(2)}) collective-permute-start(bf16[128,640]{1,0:T(8,128)(2,1)S(1)} %get-tuple-element.31), channel_id=1, source_target_pairs={{0,4},{4,0},{8,12},{12,8},{1,5},{5,1},{9,13},{13,9},{2,6},{6,2},{1... | collective-permute-start | bytes 491528 | tf_op jit(solution)/shard_map/ppermute | solution.py:212
  20.1 0.9 %collective-permute-done.4.refs_3_.refs_4_ = bf16[64,640]{1,0:T(8,128)(2,1)S(1)} collective-permute-done((bf16[64,640]{1,0:T(8,128)(2,1)S(1)}, bf16[64,640]{1,0:T(8,128)(2,1)S(1)}, u32[]{:S(2)}, u32[]{:S(2)}) %collective-permute-start.4) | collective-permute-done | bytes 81952 | tf_op jit(solution)/shard_map/ppermute | solution.py:212
  21.0 1.5 %collective-permute-start.12 = (bf16[64,640]{1,0:T(8,128)(2,1)S(1)}, bf16[64,640]{1,0:T(8,128)(2,1)S(1)}, u32[]{:S(2)}, u32[]{:S(2)}) collective-permute-start(bf16[64,640]{1,0:T(8,128)(2,1)S(1)} %collective-permute-done.4.refs_3_.refs_4_), channel_id=1, source_target_pairs={{0,2},{2,0},{1,3},{3,1},{4,6},{6,4},{5,7},{7,5},{8,10},{10,8},{9,1... | collective-permute-start | bytes 245768 | tf_op jit(solution)/shard_map/ppermute | solution.py:215
  22.5 1.7 %collective-permute-start.11 = (bf16[64,640]{1,0:T(8,128)(2,1)S(1)}, bf16[64,640]{1,0:T(8,128)(2,1)S(1)}, u32[]{:S(2)}, u32[]{:S(2)}) collective-permute-start(bf16[64,640]{1,0:T(8,128)(2,1)S(1)} %collective-permute-done.8.refs_2_.refs_3_), channel_id=1, source_target_pairs={{0,2},{2,0},{1,3},{3,1},{4,6},{6,4},{5,7},{7,5},{8,10},{10,8},{9,1... | collective-permute-start | bytes 245768 | tf_op jit(solution)/shard_map/ppermute | solution.py:215
  24.2 0.3 shard_map.86
  24.5 0.2 collective-permute-done.7.refs_1_.refs_2_
  24.8 0.3 shard_map.89.refs_0_
  25.2 2.0 %shard_map.90.refs_5_ = f32[256,640]{1,0:T(8,128)S(1)} custom-call(f32[8,128]{1,0:T(8,128)S(1)} %get-tuple-element.25.weight_ref, f32[24,128]{1,0:T(8,128)S(1)} %broadcast_in_dim.31.table_ref, f32[1,128]{1,0:T(1,128)S(1)} %broadcast_in_dim.32.sharp_ref, f32[256,256]{1,0:T(8,128)S(1)} %shard_map.87.refs_0_, f32[256,256]{1,0:T(8,128)S(1)} %collective-permute-done.9.refs_1_, ...), custom_call_target="tpu_custom_call" | custom-call | tf_op jit(solution)/shard_map/pallas_call | solution.py:93
  27.2 0.7 %collective-permute-done.11.refs_2_.refs_3_ = bf16[64,640]{1,0:T(8,128)(2,1)S(1)} collective-permute-done((bf16[64,640]{1,0:T(8,128)(2,1)S(1)}, bf16[64,640]{1,0:T(8,128)(2,1)S(1)}, u32[]{:S(2)}, u32[]{:S(2)}) %collective-permute-start.11) | collective-permute-done | bytes 81952 | tf_op jit(solution)/shard_map/ppermute | solution.py:215
  27.9 0.3 shard_map.91.refs_0_
  28.3 1.2 %shard_map.92.refs_5_ = f32[256,640]{1,0:T(8,128)S(1)} custom-call(f32[8,128]{1,0:T(8,128)S(1)} %get-tuple-element.25.weight_ref, f32[24,128]{1,0:T(8,128)S(1)} %broadcast_in_dim.31.table_ref, f32[1,128]{1,0:T(1,128)S(1)} %broadcast_in_dim.32.sharp_ref, f32[256,256]{1,0:T(8,128)S(1)} %shard_map.89.refs_0_, f32[256,256]{1,0:T(8,128)S(1)} %collective-permute-done.14.refs_1_, ...), custom_call_target="tpu_custom_call" | custom-call | tf_op jit(solution)/shard_map/pallas_call | solution.py:93
  29.5 0.3 collective-permute-done.13.refs_1_
  29.8 2.0 %shard_map.93 = (bf16[256,640]{1,0:T(8,128)(2,1)}, f32[1,8]{1,0:T(1,128)}) custom-call(f32[8,128]{1,0:T(8,128)S(1)} %get-tuple-element.25.weight_ref, f32[24,128]{1,0:T(8,128)S(1)} %broadcast_in_dim.31.table_ref, f32[1,128]{1,0:T(1,128)S(1)} %broadcast_in_dim.32.sharp_ref, f32[256,256]{1,0:T(8,128)S(1)} %shard_map.91.refs_0_, ...), custom_call_target="tpu_custom_call" | custom-call | tf_op jit(solution)/shard_map/pallas_call | solution.py:93
  (32 shorter events, 0.8 us)
Async XLA Ops:
  0.6 7.0 %copy-start.1 = (f32[2,1280]{1,0:T(2,128)S(1)}, f32[2,1280]{1,0:T(2,128)}, u32[]{:S(2)}) copy-start(f32[2,1280]{1,0:T(2,128)} %refs_0_.1) | copy-start | bytes 30724
  0.6 7.9 %copy-start = (bf16[1,256,640]{2,1,0:T(8,128)(2,1)S(1)}, bf16[1,256,640]{2,1,0:T(8,128)(2,1)}, u32[]{:S(2)}) copy-start(bf16[1,256,640]{2,1,0:T(8,128)(2,1)} %param.7) | copy-start | bytes 983044
  1.9 13.3 %collective-permute-start = (bf16[128,640]{1,0:T(8,128)(2,1)S(1)}, bf16[128,640]{1,0:T(8,128)(2,1)S(1)}, u32[]{:S(2)}, u32[]{:S(2)}) collective-permute-start(bf16[128,640]{1,0:T(8,128)(2,1)S(1)} %get-tuple-element.38), channel_id=1, source_target_pairs={{0,8},{4,12},{8,0},{12,4},{1,9},{5,13},{9,1},{13,5},{2,10},{6,14},... | collective-permute-start | bytes 491528 | tf_op jit(solution)/shard_map/ppermute | solution.py:212
  6.0 9.2 %collective-permute-start.3 = (bf16[128,640]{1,0:T(8,128)(2,1)S(1)}, bf16[128,640]{1,0:T(8,128)(2,1)S(1)}, u32[]{:S(2)}, u32[]{:S(2)}) collective-permute-start(bf16[128,640]{1,0:T(8,128)(2,1)S(1)} %get-tuple-element.38), channel_id=1, source_target_pairs={{0,4},{4,0},{8,12},{12,8},{1,5},{5,1},{9,13},{13,9},{2,6},{6,2},{1... | collective-permute-start | bytes 491528 | tf_op jit(solution)/shard_map/ppermute | solution.py:212
  7.6 7.6 %collective-permute-start.2 = (f32[2,1280]{1,0:T(2,128)S(1)}, f32[2,1280]{1,0:T(2,128)S(1)}, u32[]{:S(2)}, u32[]{:S(2)}) collective-permute-start(f32[2,1280]{1,0:T(2,128)S(1)} %copy-done.1), channel_id=1, source_target_pairs={{0,12},{4,8},{8,4},{12,0},{1,13},{5,9},{9,5},{13,1},{2,14},{6,10},... | collective-permute-start | bytes 30728 | tf_op jit(solution)/shard_map/ppermute | solution.py:212
  7.6 7.6 %collective-permute-start.1 = (f32[2,1280]{1,0:T(2,128)S(1)}, f32[2,1280]{1,0:T(2,128)S(1)}, u32[]{:S(2)}, u32[]{:S(2)}) collective-permute-start(f32[2,1280]{1,0:T(2,128)S(1)} %copy-done.1), channel_id=1, source_target_pairs={{0,4},{1,9},{4,0},{5,13},{8,12},{9,1},{12,8},{13,5},{2,6},{3,11},{... | collective-permute-start | bytes 30728 | tf_op jit(solution)/shard_map/ppermute | solution.py:221
  8.8 16.4 %collective-permute-start.9 = (f32[256,256]{1,0:T(8,128)S(1)}, f32[256,256]{1,0:T(8,128)S(1)}, u32[]{:S(2)}, u32[]{:S(2)}) collective-permute-start(f32[256,256]{1,0:T(8,128)S(1)} %shard_map.87.refs_0_), channel_id=1, source_target_pairs={{0,1},{1,0},{2,3},{3,2},{4,5},{5,4},{6,7},{7,6},{8,9},{9,8},{10,11... | collective-permute-start | bytes 786440 | tf_op jit(solution)/shard_map/ppermute | solution.py:215
  8.9 0.7 %copy-start.4 = (s32[8]{0:T(128)S(1)}, s32[8]{0:T(128)}, u32[]{:S(2)}) copy-start(s32[8]{0:T(128)} %param.9) | copy-start | bytes 100
  15.6 2.2 %collective-permute-start.6 = (f32[256,256]{1,0:T(8,128)S(1)}, f32[256,256]{1,0:T(8,128)S(1)}, u32[]{:S(2)}, u32[]{:S(2)}) collective-permute-start(f32[256,256]{1,0:T(8,128)S(1)} %shard_map.88.refs_4_), channel_id=1, source_target_pairs={{0,1},{1,0},{2,3},{3,2},{4,5},{5,4},{6,7},{7,6},{8,9},{9,8},{10,11... | collective-permute-start | bytes 786440 | tf_op jit(solution)/shard_map/ppermute | solution.py:215
  15.7 8.6 %copy-start.2 = (f32[1,1280]{1,0:T(1,128)S(1)}, f32[1,1280]{1,0:T(1,128)}, u32[]{:S(2)}) copy-start(f32[1,1280]{1,0:T(1,128)} %pool_ref.1) | copy-start | bytes 15364
  15.7 5.3 %collective-permute-start.4 = (bf16[64,640]{1,0:T(8,128)(2,1)S(1)}, bf16[64,640]{1,0:T(8,128)(2,1)S(1)}, u32[]{:S(2)}, u32[]{:S(2)}) collective-permute-start(bf16[64,640]{1,0:T(8,128)(2,1)S(1)} %get-tuple-element.41), channel_id=1, source_target_pairs={{0,4},{4,0},{8,12},{12,8},{1,5},{5,1},{9,13},{13,9},{2,6},{6,2},{1... | collective-permute-start | bytes 245768 | tf_op jit(solution)/shard_map/ppermute | solution.py:212
  16.5 7.7 %copy-start.3 = (s32[1,28]{1,0:T(1,128)S(1)}, s32[1,28]{1,0:T(1,128)}, u32[]{:S(2)}) copy-start(s32[1,28]{1,0:T(1,128)} %hits_ref) | copy-start | bytes 340
  16.5 6.0 %collective-permute-start.8 = (bf16[64,640]{1,0:T(8,128)(2,1)S(1)}, bf16[64,640]{1,0:T(8,128)(2,1)S(1)}, u32[]{:S(2)}, u32[]{:S(2)}) collective-permute-start(bf16[64,640]{1,0:T(8,128)(2,1)S(1)} %get-tuple-element.40), channel_id=1, source_target_pairs={{0,4},{4,0},{8,12},{12,8},{1,5},{5,1},{9,13},{13,9},{2,6},{6,2},{1... | collective-permute-start | bytes 245768 | tf_op jit(solution)/shard_map/ppermute | solution.py:212
  17.8 1.5 %collective-permute-start.5 = (f32[2,1280]{1,0:T(2,128)S(1)}, f32[2,1280]{1,0:T(2,128)S(1)}, u32[]{:S(2)}, u32[]{:S(2)}) collective-permute-start(f32[2,1280]{1,0:T(2,128)S(1)} %collective-permute-done.1.refs_1_), channel_id=1, source_target_pairs={{0,1},{1,0},{2,3},{3,2},{4,5},{5,4},{6,7},{7,6},{8,9},{9,8},{10,11... | collective-permute-start | bytes 30728 | tf_op jit(solution)/shard_map/ppermute | solution.py:215
  17.8 7.0 %collective-permute-start.7 = (bf16[128,640]{1,0:T(8,128)(2,1)S(1)}, bf16[128,640]{1,0:T(8,128)(2,1)S(1)}, u32[]{:S(2)}, u32[]{:S(2)}) collective-permute-start(bf16[128,640]{1,0:T(8,128)(2,1)S(1)} %collective-permute-done.refs_2_.refs_7_), channel_id=1, source_target_pairs={{0,2},{2,0},{1,3},{3,1},{4,6},{6,4},{5,7},{7,5},{8,10},{10,8},{9,1... | collective-permute-start | bytes 491528 | tf_op jit(solution)/shard_map/ppermute | solution.py:215
  19.3 7.9 %collective-permute-start.10 = (bf16[128,640]{1,0:T(8,128)(2,1)S(1)}, bf16[128,640]{1,0:T(8,128)(2,1)S(1)}, u32[]{:S(2)}, u32[]{:S(2)}) collective-permute-start(bf16[128,640]{1,0:T(8,128)(2,1)S(1)} %get-tuple-element.31), channel_id=1, source_target_pairs={{0,4},{4,0},{8,12},{12,8},{1,5},{5,1},{9,13},{13,9},{2,6},{6,2},{1... | collective-permute-start | bytes 491528 | tf_op jit(solution)/shard_map/ppermute | solution.py:212
  21.0 6.2 %collective-permute-start.12 = (bf16[64,640]{1,0:T(8,128)(2,1)S(1)}, bf16[64,640]{1,0:T(8,128)(2,1)S(1)}, u32[]{:S(2)}, u32[]{:S(2)}) collective-permute-start(bf16[64,640]{1,0:T(8,128)(2,1)S(1)} %collective-permute-done.4.refs_3_.refs_4_), channel_id=1, source_target_pairs={{0,2},{2,0},{1,3},{3,1},{4,6},{6,4},{5,7},{7,5},{8,10},{10,8},{9,1... | collective-permute-start | bytes 245768 | tf_op jit(solution)/shard_map/ppermute | solution.py:215
  22.5 5.4 %collective-permute-start.11 = (bf16[64,640]{1,0:T(8,128)(2,1)S(1)}, bf16[64,640]{1,0:T(8,128)(2,1)S(1)}, u32[]{:S(2)}, u32[]{:S(2)}) collective-permute-start(bf16[64,640]{1,0:T(8,128)(2,1)S(1)} %collective-permute-done.8.refs_2_.refs_3_), channel_id=1, source_target_pairs={{0,2},{2,0},{1,3},{3,1},{4,6},{6,4},{5,7},{7,5},{8,10},{10,8},{9,1... | collective-permute-start | bytes 245768 | tf_op jit(solution)/shard_map/ppermute | solution.py:215
  25.1 3.2 %collective-permute-start.14 = (f32[256,256]{1,0:T(8,128)S(1)}, f32[256,256]{1,0:T(8,128)S(1)}, u32[]{:S(2)}, u32[]{:S(2)}) collective-permute-start(f32[256,256]{1,0:T(8,128)S(1)} %shard_map.89.refs_0_), channel_id=1, source_target_pairs={{0,1},{1,0},{2,3},{3,2},{4,5},{5,4},{6,7},{7,6},{8,9},{9,8},{10,11... | collective-permute-start | bytes 786440 | tf_op jit(solution)/shard_map/ppermute | solution.py:215
  28.2 1.6 %collective-permute-start.13 = (f32[256,256]{1,0:T(8,128)S(1)}, f32[256,256]{1,0:T(8,128)S(1)}, u32[]{:S(2)}, u32[]{:S(2)}) collective-permute-start(f32[256,256]{1,0:T(8,128)S(1)} %shard_map.91.refs_0_), channel_id=1, source_target_pairs={{0,1},{1,0},{2,3},{3,2},{4,5},{5,4},{6,7},{7,6},{8,9},{9,8},{10,11... | collective-permute-start | bytes 786440 | tf_op jit(solution)/shard_map/ppermute | solution.py:215

commit v17 on v16

--- a/solution.py
+++ b/solution.py
@@ -251,10 +251,6 @@
         )
 
     acc_shape = jax.ShapeDtypeStruct(query.shape, jnp.float32)
-    own_blocks = [target_res[0], target_res[1]]
-    (own,) = partial_similar(after(query, share), own_blocks)
-    own_other = across(own, "rep")
-
     far = after(far, pool_split, pool_last, table, half_sharp)
     near = after(near, far)
     far = after(far, near)
@@ -263,11 +259,11 @@
     pool_other = across(pool_split, "rep")
     near_rest = from_peer(after(rest, far), 1)
 
+    own_blocks = [target_res[0], target_res[1]]
     one_blocks = [near, far]
-    (one,) = partial_similar(query, one_blocks)
+    (one,) = partial_similar(query, own_blocks + one_blocks)
     one_other = across(one, "rep")
     far_rest = across(after(far, one_other), "qry")
-    last = [last[0], after(last[1], pool_other)]
     last_rest = [across(piece, "qry") for piece in last]
     posterior, weights = call_kernel(
         weigh_kernel,
@@ -282,7 +278,7 @@
         pool_split,
         pool_other,
         pool_last,
-        flops=1500000000,
+        flops=1000000000,
     )
     far_rest = after(far_rest, weights)
     two_blocks = [far_rest, *last]
@@ -290,13 +286,11 @@
     two_other = across(two, "rep")
 
     acc = add_up(
-        (((0, 1), (1, 1)), ((2, 4), (1, 1))),
+        (((0, 1, 2, 4), (1, 1, 1, 1)),),
         acc_shape,
-        after(own, two),
-        own_other,
+        after(one, two),
+        one_other,
         *own_blocks,
-        one,
-        one_other,
         *one_blocks,
     )
 

time: 32 us -> 31.5 us (0.984)
    ppermute x8 -> x7, waiting for transfers between devices: 1.23 us -> 0.5 us  [across(): return lax.ppermute(array, axis, [(0, 1), (1, 0)])]
    ppermute x6, waiting for transfers between devices: 5.64 us -> 6.27 us  [from_peer(): return lax.ppermute(array, 'tgt', [(i, i ^ k) for i in range(4)])]
    pallas_call x8 -> x7, Pallas kernels: 6.74 us -> 6.58 us  [call_kernel(): pl.pallas_call(kernel, out_shape=out_shape, in_specs=[VMEM] * len(operand...]
    ppermute x8 -> x7, starting transfers between devices: 4.96 us -> 4.83 us  [across(): return lax.ppermute(array, axis, [(0, 1), (1, 0)])]
  transfers between devices with their start and end apart: 15 -> 14, of which waited for: 5 -> 5; matrix products, arithmetic and copies ran while one was open for 1% -> 1% of each run, Pallas kernels for 15% -> 13%
where the time goes in v17:
time: 31.5 us; the launch traced here: 31.4 us
  starting transfers between devices  14.3 us (45%)
  waiting for transfers between devices  6.77 us (21%)
  Pallas kernels  6.58 us (21%)
  local copies, waits for them, and re-layouts  2.12 us (7%)
  between operations  1.43 us (5%)
    ppermute x6, starting transfers between devices, from_peer(): return lax.ppermute(array, 'tgt', [(i, i ^ k) for i in range(4)])  8.55 us
    pallas_call x7, Pallas kernels, call_kernel(): pl.pallas_call(kernel, out_shape=out_shape, in_specs=[VMEM] * len(operand...  6.58 us
    ppermute x6, waiting for transfers between devices, from_peer(): return lax.ppermute(array, 'tgt', [(i, i ^ k) for i in range(4)])  6.27 us
    ppermute x7, starting transfers between devices, across(): return lax.ppermute(array, axis, [(0, 1), (1, 0)])  4.83 us
    squeeze x1, local copies, waits for them, and re-layouts, per_device_by_target(): rest = lax.dynamic_index_in_dim(target_res, 1 - at_qry, 0, keepdims=False)  1.26 us
    ppermute x1, starting transfers between devices, per_device_by_target(): pool_split = lax.ppermute(target_pool, ('tgt', 'rep'), split)  0.9 us
  transfers between devices with their start and end apart: 14, of which 5 were waited for; matrix products, arithmetic and copies ran while one was open for 1% of the time, Pallas kernels for 13%

profile of v17, /device:TPU:0, one launch (start us, length us, event | category | flops | bytes accessed | tf_op | source)
XLA Modules:
  0.0 31.4 jit_solution(12703095414575830239)
XLA Ops:
  0.7 1.3 %dynamic-slice_bitcast_fusion = (bf16[128,640]{1,0:T(8,128)(2,1)S(1)}, bf16[128,640]{1,0:T(8,128)(2,1)S(1)}, bf16[128,640]{1,0:T(8,128)(2,1)S(1)}, bf16[128,640]{1,0:T(8,128)(2,1)S(1)}) fusion(bf16[2,128,640]{2,1,0:T(8,128)(2,1)} %param.8, s32[]{:T(128)S(6)} %select_n.13, s32[]{:T(128)S(6)} %select_n.12), kind=kLoop, calls=%fused_computation | loop fusion | bytes 1310728 | tf_op jit(solution)/shard_map/jit(dynamic_index_in_dim)/squeeze | solution.py:226
  1.9 4.1 %collective-permute-start = (bf16[128,640]{1,0:T(8,128)(2,1)S(1)}, bf16[128,640]{1,0:T(8,128)(2,1)S(1)}, u32[]{:S(2)}, u32[]{:S(2)}) collective-permute-start(bf16[128,640]{1,0:T(8,128)(2,1)S(1)} %get-tuple-element.34), channel_id=1, source_target_pairs={{0,8},{4,12},{8,0},{12,4},{1,9},{5,13},{9,1},{13,5},{2,10},{6,14},... | collective-permute-start | bytes 491528 | tf_op jit(solution)/shard_map/ppermute | solution.py:212
  6.0 1.6 %collective-permute-start.3 = (bf16[128,640]{1,0:T(8,128)(2,1)S(1)}, bf16[128,640]{1,0:T(8,128)(2,1)S(1)}, u32[]{:S(2)}, u32[]{:S(2)}) collective-permute-start(bf16[128,640]{1,0:T(8,128)(2,1)S(1)} %get-tuple-element.34), channel_id=1, source_target_pairs={{0,4},{4,0},{8,12},{12,8},{1,5},{5,1},{9,13},{13,9},{2,6},{6,2},{1... | collective-permute-start | bytes 491528 | tf_op jit(solution)/shard_map/ppermute | solution.py:212
  7.6 0.9 %collective-permute-start.1 = (f32[2,1280]{1,0:T(2,128)S(1)}, f32[2,1280]{1,0:T(2,128)S(1)}, u32[]{:S(2)}, u32[]{:S(2)}) collective-permute-start(f32[2,1280]{1,0:T(2,128)S(1)} %copy-done.1), channel_id=1, source_target_pairs={{0,4},{1,9},{4,0},{5,13},{8,12},{9,1},{12,8},{13,5},{2,6},{3,11},{... | collective-permute-start | bytes 30728 | tf_op jit(solution)/shard_map/ppermute | solution.py:221
  8.6 0.6 %copy-done.4 = s32[8]{0:T(128)S(1)} copy-done((s32[8]{0:T(128)S(1)}, s32[8]{0:T(128)}, u32[]{:S(2)}) %copy-start.4) | copy-done | bytes 56
  9.2 0.2 select_reduce_fusion
  10.1 5.1 %collective-permute-done.2.refs_3_ = f32[2,1280]{1,0:T(2,128)S(1)} collective-permute-done((f32[2,1280]{1,0:T(2,128)S(1)}, f32[2,1280]{1,0:T(2,128)S(1)}, u32[]{:S(2)}, u32[]{:S(2)}) %collective-permute-start.2) | collective-permute-done | bytes 10272 | tf_op jit(solution)/shard_map/ppermute | solution.py:212
  15.3 0.4 %shard_map.87.refs_0_ = f32[256,512]{1,0:T(8,128)S(1)} custom-call(bf16[256,640]{1,0:T(8,128)(2,1)S(1)} %bitcast.23, bf16[128,640]{1,0:T(8,128)(2,1)S(1)} %get-tuple-element.33.refs_1_.refs_2_, bf16[128,640]{1,0:T(8,128)(2,1)S(1)} %get-tuple-element.35.refs_2_.refs_3_, bf16[128,640]{1,0:T(8,128)(2,1)S(1)} %collective-permute-done.3.refs_3_.refs_4_, ...), custom_call_target="tpu_custom_call" | custom-call | tf_op jit(solution)/shard_map/pallas_call | solution.py:93
  15.8 0.8 %collective-permute-start.4 = (bf16[64,640]{1,0:T(8,128)(2,1)S(1)}, bf16[64,640]{1,0:T(8,128)(2,1)S(1)}, u32[]{:S(2)}, u32[]{:S(2)}) collective-permute-start(bf16[64,640]{1,0:T(8,128)(2,1)S(1)} %get-tuple-element.37), channel_id=1, source_target_pairs={{0,4},{4,0},{8,12},{12,8},{1,5},{5,1},{9,13},{13,9},{2,6},{6,2},{1... | collective-permute-start | bytes 245768 | tf_op jit(solution)/shard_map/ppermute | solution.py:212
  16.6 1.2 %collective-permute-start.8 = (bf16[64,640]{1,0:T(8,128)(2,1)S(1)}, bf16[64,640]{1,0:T(8,128)(2,1)S(1)}, u32[]{:S(2)}, u32[]{:S(2)}) collective-permute-start(bf16[64,640]{1,0:T(8,128)(2,1)S(1)} %get-tuple-element.36), channel_id=1, source_target_pairs={{0,4},{4,0},{8,12},{12,8},{1,5},{5,1},{9,13},{13,9},{2,6},{6,2},{1... | collective-permute-start | bytes 245768 | tf_op jit(solution)/shard_map/ppermute | solution.py:212
  17.9 1.5 %collective-permute-start.7 = (bf16[128,640]{1,0:T(8,128)(2,1)S(1)}, bf16[128,640]{1,0:T(8,128)(2,1)S(1)}, u32[]{:S(2)}, u32[]{:S(2)}) collective-permute-start(bf16[128,640]{1,0:T(8,128)(2,1)S(1)} %collective-permute-done.refs_4_.refs_5_), channel_id=1, source_target_pairs={{0,2},{2,0},{1,3},{3,1},{4,6},{6,4},{5,7},{7,5},{8,10},{10,8},{9,1... | collective-permute-start | bytes 491528 | tf_op jit(solution)/shard_map/ppermute | solution.py:215
  19.4 0.8 %collective-permute-start.9 = (bf16[128,640]{1,0:T(8,128)(2,1)S(1)}, bf16[128,640]{1,0:T(8,128)(2,1)S(1)}, u32[]{:S(2)}, u32[]{:S(2)}) collective-permute-start(bf16[128,640]{1,0:T(8,128)(2,1)S(1)} %get-tuple-element.27), channel_id=1, source_target_pairs={{0,4},{4,0},{8,12},{12,8},{1,5},{5,1},{9,13},{13,9},{2,6},{6,2},{1... | collective-permute-start | bytes 491528 | tf_op jit(solution)/shard_map/ppermute | solution.py:212
  20.2 0.9 %collective-permute-done.4.refs_3_.refs_4_ = bf16[64,640]{1,0:T(8,128)(2,1)S(1)} collective-permute-done((bf16[64,640]{1,0:T(8,128)(2,1)S(1)}, bf16[64,640]{1,0:T(8,128)(2,1)S(1)}, u32[]{:S(2)}, u32[]{:S(2)}) %collective-permute-start.4) | collective-permute-done | bytes 81952 | tf_op jit(solution)/shard_map/ppermute | solution.py:212
  21.1 1.5 %collective-permute-start.11 = (bf16[64,640]{1,0:T(8,128)(2,1)S(1)}, bf16[64,640]{1,0:T(8,128)(2,1)S(1)}, u32[]{:S(2)}, u32[]{:S(2)}) collective-permute-start(bf16[64,640]{1,0:T(8,128)(2,1)S(1)} %collective-permute-done.4.refs_3_.refs_4_), channel_id=1, source_target_pairs={{0,2},{2,0},{1,3},{3,1},{4,6},{6,4},{5,7},{7,5},{8,10},{10,8},{9,1... | collective-permute-start | bytes 245768 | tf_op jit(solution)/shard_map/ppermute | solution.py:215
  22.6 0.3 collective-permute-done.8.refs_2_.refs_3_
  22.8 1.5 %collective-permute-start.10 = (bf16[64,640]{1,0:T(8,128)(2,1)S(1)}, bf16[64,640]{1,0:T(8,128)(2,1)S(1)}, u32[]{:S(2)}, u32[]{:S(2)}) collective-permute-start(bf16[64,640]{1,0:T(8,128)(2,1)S(1)} %collective-permute-done.8.refs_2_.refs_3_), channel_id=1, source_target_pairs={{0,2},{2,0},{1,3},{3,1},{4,6},{6,4},{5,7},{7,5},{8,10},{10,8},{9,1... | collective-permute-start | bytes 245768 | tf_op jit(solution)/shard_map/ppermute | solution.py:215
  24.3 0.3 shard_map.86
  24.6 0.3 shard_map.88.refs_0_
  25.0 2.0 %shard_map.89.refs_5_ = f32[256,640]{1,0:T(8,128)S(1)} custom-call(f32[8,128]{1,0:T(8,128)S(1)} %get-tuple-element.22.weight_ref, f32[24,128]{1,0:T(8,128)S(1)} %broadcast_in_dim.31.table_ref, f32[1,128]{1,0:T(1,128)S(1)} %broadcast_in_dim.32.sharp_ref, f32[256,512]{1,0:T(8,128)S(1)} %shard_map.87.refs_0_, f32[256,512]{1,0:T(8,128)S(1)} %collective-permute-done.6.refs_1_, ...), custom_call_target="tpu_custom_call" | custom-call | tf_op jit(solution)/shard_map/pallas_call | solution.py:93
  27.1 0.4 %collective-permute-done.10.refs_2_.refs_3_ = bf16[64,640]{1,0:T(8,128)(2,1)S(1)} collective-permute-done((bf16[64,640]{1,0:T(8,128)(2,1)S(1)}, bf16[64,640]{1,0:T(8,128)(2,1)S(1)}, u32[]{:S(2)}, u32[]{:S(2)}) %collective-permute-start.10) | collective-permute-done | bytes 81952 | tf_op jit(solution)/shard_map/ppermute | solution.py:215
  27.4 0.3 shard_map.90.refs_0_
  27.7 0.2 collective-permute-start.12
  28.0 1.2 %shard_map.91.refs_5_ = f32[256,640]{1,0:T(8,128)S(1)} custom-call(f32[8,128]{1,0:T(8,128)S(1)} %get-tuple-element.22.weight_ref, f32[24,128]{1,0:T(8,128)S(1)} %broadcast_in_dim.31.table_ref, f32[1,128]{1,0:T(1,128)S(1)} %broadcast_in_dim.32.sharp_ref, f32[256,256]{1,0:T(8,128)S(1)} %shard_map.88.refs_0_, f32[256,256]{1,0:T(8,128)S(1)} %collective-permute-done.13.refs_1_, ...), custom_call_target="tpu_custom_call" | custom-call | tf_op jit(solution)/shard_map/pallas_call | solution.py:93
  29.3 2.0 %shard_map.92 = (bf16[256,640]{1,0:T(8,128)(2,1)}, f32[1,8]{1,0:T(1,128)}) custom-call(f32[8,128]{1,0:T(8,128)S(1)} %get-tuple-element.22.weight_ref, f32[24,128]{1,0:T(8,128)S(1)} %broadcast_in_dim.31.table_ref, f32[1,128]{1,0:T(1,128)S(1)} %broadcast_in_dim.32.sharp_ref, f32[256,256]{1,0:T(8,128)S(1)} %shard_map.90.refs_0_, ...), custom_call_target="tpu_custom_call" | custom-call | tf_op jit(solution)/shard_map/pallas_call | solution.py:93
  (29 shorter events, 0.6 us)
Async XLA Ops:
  0.6 7.0 %copy-start.1 = (f32[2,1280]{1,0:T(2,128)S(1)}, f32[2,1280]{1,0:T(2,128)}, u32[]{:S(2)}) copy-start(f32[2,1280]{1,0:T(2,128)} %refs_0_.1) | copy-start | bytes 30724
  0.6 14.6 %copy-start = (bf16[1,256,640]{2,1,0:T(8,128)(2,1)S(1)}, bf16[1,256,640]{2,1,0:T(8,128)(2,1)}, u32[]{:S(2)}) copy-start(bf16[1,256,640]{2,1,0:T(8,128)(2,1)} %param.7) | copy-start | bytes 983044
  1.9 13.3 %collective-permute-start = (bf16[128,640]{1,0:T(8,128)(2,1)S(1)}, bf16[128,640]{1,0:T(8,128)(2,1)S(1)}, u32[]{:S(2)}, u32[]{:S(2)}) collective-permute-start(bf16[128,640]{1,0:T(8,128)(2,1)S(1)} %get-tuple-element.34), channel_id=1, source_target_pairs={{0,8},{4,12},{8,0},{12,4},{1,9},{5,13},{9,1},{13,5},{2,10},{6,14},... | collective-permute-start | bytes 491528 | tf_op jit(solution)/shard_map/ppermute | solution.py:212
  6.0 9.2 %collective-permute-start.3 = (bf16[128,640]{1,0:T(8,128)(2,1)S(1)}, bf16[128,640]{1,0:T(8,128)(2,1)S(1)}, u32[]{:S(2)}, u32[]{:S(2)}) collective-permute-start(bf16[128,640]{1,0:T(8,128)(2,1)S(1)} %get-tuple-element.34), channel_id=1, source_target_pairs={{0,4},{4,0},{8,12},{12,8},{1,5},{5,1},{9,13},{13,9},{2,6},{6,2},{1... | collective-permute-start | bytes 491528 | tf_op jit(solution)/shard_map/ppermute | solution.py:212
  7.6 7.6 %collective-permute-start.2 = (f32[2,1280]{1,0:T(2,128)S(1)}, f32[2,1280]{1,0:T(2,128)S(1)}, u32[]{:S(2)}, u32[]{:S(2)}) collective-permute-start(f32[2,1280]{1,0:T(2,128)S(1)} %copy-done.1), channel_id=1, source_target_pairs={{0,12},{4,8},{8,4},{12,0},{1,13},{5,9},{9,5},{13,1},{2,14},{6,10},... | collective-permute-start | bytes 30728 | tf_op jit(solution)/shard_map/ppermute | solution.py:212
  7.6 7.6 %collective-permute-start.1 = (f32[2,1280]{1,0:T(2,128)S(1)}, f32[2,1280]{1,0:T(2,128)S(1)}, u32[]{:S(2)}, u32[]{:S(2)}) collective-permute-start(f32[2,1280]{1,0:T(2,128)S(1)} %copy-done.1), channel_id=1, source_target_pairs={{0,4},{1,9},{4,0},{5,13},{8,12},{9,1},{12,8},{13,5},{2,6},{3,11},{... | collective-permute-start | bytes 30728 | tf_op jit(solution)/shard_map/ppermute | solution.py:221
  8.5 0.7 %copy-start.4 = (s32[8]{0:T(128)S(1)}, s32[8]{0:T(128)}, u32[]{:S(2)}) copy-start(s32[8]{0:T(128)} %param.9) | copy-start | bytes 100
  15.7 2.2 %collective-permute-start.6 = (f32[256,512]{1,0:T(8,128)S(1)}, f32[256,512]{1,0:T(8,128)S(1)}, u32[]{:S(2)}, u32[]{:S(2)}) collective-permute-start(f32[256,512]{1,0:T(8,128)S(1)} %shard_map.87.refs_0_), channel_id=1, source_target_pairs={{0,1},{1,0},{2,3},{3,2},{4,5},{5,4},{6,7},{7,6},{8,9},{9,8},{10,11... | collective-permute-start | bytes 1572872 | tf_op jit(solution)/shard_map/ppermute | solution.py:215
  15.8 8.6 %copy-start.2 = (f32[1,1280]{1,0:T(1,128)S(1)}, f32[1,1280]{1,0:T(1,128)}, u32[]{:S(2)}) copy-start(f32[1,1280]{1,0:T(1,128)} %pool_ref.1) | copy-start | bytes 15364
  15.8 5.3 %collective-permute-start.4 = (bf16[64,640]{1,0:T(8,128)(2,1)S(1)}, bf16[64,640]{1,0:T(8,128)(2,1)S(1)}, u32[]{:S(2)}, u32[]{:S(2)}) collective-permute-start(bf16[64,640]{1,0:T(8,128)(2,1)S(1)} %get-tuple-element.37), channel_id=1, source_target_pairs={{0,4},{4,0},{8,12},{12,8},{1,5},{5,1},{9,13},{13,9},{2,6},{6,2},{1... | collective-permute-start | bytes 245768 | tf_op jit(solution)/shard_map/ppermute | solution.py:212
  16.6 7.7 %copy-start.3 = (s32[1,28]{1,0:T(1,128)S(1)}, s32[1,28]{1,0:T(1,128)}, u32[]{:S(2)}) copy-start(s32[1,28]{1,0:T(1,128)} %hits_ref) | copy-start | bytes 340
  16.6 6.2 %collective-permute-start.8 = (bf16[64,640]{1,0:T(8,128)(2,1)S(1)}, bf16[64,640]{1,0:T(8,128)(2,1)S(1)}, u32[]{:S(2)}, u32[]{:S(2)}) collective-permute-start(bf16[64,640]{1,0:T(8,128)(2,1)S(1)} %get-tuple-element.36), channel_id=1, source_target_pairs={{0,4},{4,0},{8,12},{12,8},{1,5},{5,1},{9,13},{13,9},{2,6},{6,2},{1... | collective-permute-start | bytes 245768 | tf_op jit(solution)/shard_map/ppermute | solution.py:212
  17.9 6.8 %collective-permute-start.7 = (bf16[128,640]{1,0:T(8,128)(2,1)S(1)}, bf16[128,640]{1,0:T(8,128)(2,1)S(1)}, u32[]{:S(2)}, u32[]{:S(2)}) collective-permute-start(bf16[128,640]{1,0:T(8,128)(2,1)S(1)} %collective-permute-done.refs_4_.refs_5_), channel_id=1, source_target_pairs={{0,2},{2,0},{1,3},{3,1},{4,6},{6,4},{5,7},{7,5},{8,10},{10,8},{9,1... | collective-permute-start | bytes 491528 | tf_op jit(solution)/shard_map/ppermute | solution.py:215
  19.4 7.7 %collective-permute-start.9 = (bf16[128,640]{1,0:T(8,128)(2,1)S(1)}, bf16[128,640]{1,0:T(8,128)(2,1)S(1)}, u32[]{:S(2)}, u32[]{:S(2)}) collective-permute-start(bf16[128,640]{1,0:T(8,128)(2,1)S(1)} %get-tuple-element.27), channel_id=1, source_target_pairs={{0,4},{4,0},{8,12},{12,8},{1,5},{5,1},{9,13},{13,9},{2,6},{6,2},{1... | collective-permute-start | bytes 491528 | tf_op jit(solution)/shard_map/ppermute | solution.py:212
  20.1 4.2 %collective-permute-start.5 = (f32[2,1280]{1,0:T(2,128)S(1)}, f32[2,1280]{1,0:T(2,128)S(1)}, u32[]{:S(2)}, u32[]{:S(2)}) collective-permute-start(f32[2,1280]{1,0:T(2,128)S(1)} %collective-permute-done.1.refs_1_), channel_id=1, source_target_pairs={{0,1},{1,0},{2,3},{3,2},{4,5},{5,4},{6,7},{7,6},{8,9},{9,8},{10,11... | collective-permute-start | bytes 30728 | tf_op jit(solution)/shard_map/ppermute | solution.py:215
  21.1 6.3 %collective-permute-start.11 = (bf16[64,640]{1,0:T(8,128)(2,1)S(1)}, bf16[64,640]{1,0:T(8,128)(2,1)S(1)}, u32[]{:S(2)}, u32[]{:S(2)}) collective-permute-start(bf16[64,640]{1,0:T(8,128)(2,1)S(1)} %collective-permute-done.4.refs_3_.refs_4_), channel_id=1, source_target_pairs={{0,2},{2,0},{1,3},{3,1},{4,6},{6,4},{5,7},{7,5},{8,10},{10,8},{9,1... | collective-permute-start | bytes 245768 | tf_op jit(solution)/shard_map/ppermute | solution.py:215
  22.8 4.6 %collective-permute-start.10 = (bf16[64,640]{1,0:T(8,128)(2,1)S(1)}, bf16[64,640]{1,0:T(8,128)(2,1)S(1)}, u32[]{:S(2)}, u32[]{:S(2)}) collective-permute-start(bf16[64,640]{1,0:T(8,128)(2,1)S(1)} %collective-permute-done.8.refs_2_.refs_3_), channel_id=1, source_target_pairs={{0,2},{2,0},{1,3},{3,1},{4,6},{6,4},{5,7},{7,5},{8,10},{10,8},{9,1... | collective-permute-start | bytes 245768 | tf_op jit(solution)/shard_map/ppermute | solution.py:215
  25.0 3.0 %collective-permute-start.13 = (f32[256,256]{1,0:T(8,128)S(1)}, f32[256,256]{1,0:T(8,128)S(1)}, u32[]{:S(2)}, u32[]{:S(2)}) collective-permute-start(f32[256,256]{1,0:T(8,128)S(1)} %shard_map.88.refs_0_), channel_id=1, source_target_pairs={{0,1},{1,0},{2,3},{3,2},{4,5},{5,4},{6,7},{7,6},{8,9},{9,8},{10,11... | collective-permute-start | bytes 786440 | tf_op jit(solution)/shard_map/ppermute | solution.py:215
  27.7 1.6 %collective-permute-start.12 = (f32[256,256]{1,0:T(8,128)S(1)}, f32[256,256]{1,0:T(8,128)S(1)}, u32[]{:S(2)}, u32[]{:S(2)}) collective-permute-start(f32[256,256]{1,0:T(8,128)S(1)} %shard_map.90.refs_0_), channel_id=1, source_target_pairs={{0,1},{1,0},{2,3},{3,2},{4,5},{5,4},{6,7},{7,6},{8,9},{9,8},{10,11... | collective-permute-start | bytes 786440 | tf_op jit(solution)/shard_map/ppermute | solution.py:215

commit v18 on v13

--- a/solution.py
+++ b/solution.py
@@ -159,7 +159,7 @@
     )
     scores = jnp.where(inside, scores, -jnp.inf)
     raised = jnp.exp(scores - jnp.max(scores, axis=1, keepdims=True))
-    return raised / jnp.sum(raised, axis=1, keepdims=True)
+    return raised, jnp.sum(raised, axis=1, keepdims=True)
 
 
 def weighted_term(weight, alignment, blocks):
@@ -182,9 +182,9 @@
     for at, (slot, count) in enumerate(targets):
         part = pl.ds(at * rows, rows)
         similar = (mine[:, part] + other[:, part]) * (1.0 / math.sqrt(model_width))
-        alignment = align_block(similar, len_ref[slot : slot + 1, :rows], sharp_ref[:, 0:1])
+        raised, total = align_block(similar, len_ref[slot : slot + 1, :rows], sharp_ref[:, 0:1])
         term = weighted_term(
-            weight_ref[slot : slot + 1, 0:1], alignment.astype(jnp.bfloat16), blocks[:count]
+            weight_ref[slot : slot + 1, 0:1] / total, raised.astype(jnp.bfloat16), blocks[:count]
         )
         acc = term if acc is None else acc + term
         blocks = blocks[count:]

time: 31.6 us -> 32.1 us (1.016)
  Pallas kernels: 6.49 us -> 7.15 us
  waiting for transfers between devices: 6.8 us -> 6.32 us
    pallas_call x7, Pallas kernels: 6.49 us -> 7.15 us  [call_kernel(): pl.pallas_call(kernel, out_shape=out_shape, in_specs=[VMEM] * len(operand...]
    ppermute x7, waiting for transfers between devices: 0.52 us -> 0.04 us  [across(): return lax.ppermute(array, axis, [(0, 1), (1, 0)])]
    ppermute x7, starting transfers between devices: 4.84 us -> 5.17 us  [across(): return lax.ppermute(array, axis, [(0, 1), (1, 0)])]
  transfers between devices with their start and end apart: 14 -> 14, of which waited for: 5 -> 3; matrix products, arithmetic and copies ran while one was open for 2% -> 2% of each run, Pallas kernels for 13% -> 14%
where the time goes in v18:
time: 32.1 us; the launch traced here: 32 us
  starting transfers between devices  14.6 us (45%)
  Pallas kernels  7.15 us (22%)
  waiting for transfers between devices  6.32 us (20%)
  local copies, waits for them, and re-layouts  2.25 us (7%)
  between operations  1.42 us (4%)
    ppermute x6, starting transfers between devices, from_peer(): return lax.ppermute(array, 'tgt', [(i, i ^ k) for i in range(4)])  8.55 us
    pallas_call x7, Pallas kernels, call_kernel(): pl.pallas_call(kernel, out_shape=out_shape, in_specs=[VMEM] * len(operand...  7.15 us
    ppermute x6, waiting for transfers between devices, from_peer(): return lax.ppermute(array, 'tgt', [(i, i ^ k) for i in range(4)])  6.28 us
    ppermute x7, starting transfers between devices, across(): return lax.ppermute(array, axis, [(0, 1), (1, 0)])  5.17 us
    squeeze x1, local copies, waits for them, and re-layouts, per_device_by_target(): rest = lax.dynamic_index_in_dim(target_res, 1 - at_qry, 0, keepdims=False)  1.26 us
    ppermute x1, starting transfers between devices, per_device_by_target(): pool_split = lax.ppermute(target_pool, ('tgt', 'rep'), split)  0.9 us
  transfers between devices with their start and end apart: 14, of which 3 were waited for; matrix products, arithmetic and copies ran while one was open for 2% of the time, Pallas kernels for 14%

profile of v18, /device:TPU:0, one launch (start us, length us, event | category | flops | bytes accessed | tf_op | source)
XLA Modules:
  0.0 32.0 jit_solution(8084953682930616546)
XLA Ops:
  0.7 1.3 %dynamic-slice_bitcast_fusion = (bf16[128,640]{1,0:T(8,128)(2,1)S(1)}, bf16[128,640]{1,0:T(8,128)(2,1)S(1)}, bf16[128,640]{1,0:T(8,128)(2,1)S(1)}, bf16[128,640]{1,0:T(8,128)(2,1)S(1)}) fusion(bf16[2,128,640]{2,1,0:T(8,128)(2,1)} %param.8, s32[]{:T(128)S(6)} %select_n.13, s32[]{:T(128)S(6)} %select_n.11), kind=kLoop, calls=%fused_computation | loop fusion | bytes 1310728 | tf_op jit(solution)/shard_map/jit(dynamic_index_in_dim)/squeeze | solution.py:219
  1.9 4.1 %collective-permute-start = (bf16[128,640]{1,0:T(8,128)(2,1)S(1)}, bf16[128,640]{1,0:T(8,128)(2,1)S(1)}, u32[]{:S(2)}, u32[]{:S(2)}) collective-permute-start(bf16[128,640]{1,0:T(8,128)(2,1)S(1)} %get-tuple-element.34), channel_id=1, source_target_pairs={{0,8},{4,12},{8,0},{12,4},{1,9},{5,13},{9,1},{13,5},{2,10},{6,14},... | collective-permute-start | bytes 491528 | tf_op jit(solution)/shard_map/ppermute | solution.py:205
  6.0 1.6 %collective-permute-start.3 = (bf16[128,640]{1,0:T(8,128)(2,1)S(1)}, bf16[128,640]{1,0:T(8,128)(2,1)S(1)}, u32[]{:S(2)}, u32[]{:S(2)}) collective-permute-start(bf16[128,640]{1,0:T(8,128)(2,1)S(1)} %get-tuple-element.34), channel_id=1, source_target_pairs={{0,4},{4,0},{8,12},{12,8},{1,5},{5,1},{9,13},{13,9},{2,6},{6,2},{1... | collective-permute-start | bytes 491528 | tf_op jit(solution)/shard_map/ppermute | solution.py:205
  7.6 0.9 %collective-permute-start.1 = (f32[2,1280]{1,0:T(2,128)S(1)}, f32[2,1280]{1,0:T(2,128)S(1)}, u32[]{:S(2)}, u32[]{:S(2)}) collective-permute-start(f32[2,1280]{1,0:T(2,128)S(1)} %copy-done.1), channel_id=1, source_target_pairs={{0,4},{1,9},{4,0},{5,13},{8,12},{9,1},{12,8},{13,5},{2,6},{3,11},{... | collective-permute-start | bytes 30728 | tf_op jit(solution)/shard_map/ppermute | solution.py:214
  8.6 0.6 %copy-done.4 = s32[8]{0:T(128)S(1)} copy-done((s32[8]{0:T(128)S(1)}, s32[8]{0:T(128)}, u32[]{:S(2)}) %copy-start.4) | copy-done | bytes 56
  9.2 0.2 select_reduce_fusion
  10.0 0.1 stack.59
  10.1 5.1 %collective-permute-done.2.refs_3_ = f32[2,1280]{1,0:T(2,128)S(1)} collective-permute-done((f32[2,1280]{1,0:T(2,128)S(1)}, f32[2,1280]{1,0:T(2,128)S(1)}, u32[]{:S(2)}, u32[]{:S(2)}) %collective-permute-start.2) | collective-permute-done | bytes 10272 | tf_op jit(solution)/shard_map/ppermute | solution.py:205
  15.4 0.4 %shard_map.87.mine = f32[256,512]{1,0:T(8,128)S(1)} custom-call(bf16[256,640]{1,0:T(8,128)(2,1)S(1)} %bitcast.23, bf16[128,640]{1,0:T(8,128)(2,1)S(1)} %get-tuple-element.33.refs_1_.refs_0_, bf16[128,640]{1,0:T(8,128)(2,1)S(1)} %get-tuple-element.35.refs_2_.refs_1_, bf16[128,640]{1,0:T(8,128)(2,1)S(1)} %collective-permute-done.3.refs_3_.refs_2_, ...), custom_call_target="tpu_custom_call" | custom-call | tf_op jit(solution)/shard_map/pallas_call | solution.py:93
  15.9 0.8 %collective-permute-start.4 = (bf16[64,640]{1,0:T(8,128)(2,1)S(1)}, bf16[64,640]{1,0:T(8,128)(2,1)S(1)}, u32[]{:S(2)}, u32[]{:S(2)}) collective-permute-start(bf16[64,640]{1,0:T(8,128)(2,1)S(1)} %get-tuple-element.37), channel_id=1, source_target_pairs={{0,4},{4,0},{8,12},{12,8},{1,5},{5,1},{9,13},{13,9},{2,6},{6,2},{1... | collective-permute-start | bytes 245768 | tf_op jit(solution)/shard_map/ppermute | solution.py:205
  16.8 1.2 %collective-permute-start.8 = (bf16[64,640]{1,0:T(8,128)(2,1)S(1)}, bf16[64,640]{1,0:T(8,128)(2,1)S(1)}, u32[]{:S(2)}, u32[]{:S(2)}) collective-permute-start(bf16[64,640]{1,0:T(8,128)(2,1)S(1)} %get-tuple-element.36), channel_id=1, source_target_pairs={{0,4},{4,0},{8,12},{12,8},{1,5},{5,1},{9,13},{13,9},{2,6},{6,2},{1... | collective-permute-start | bytes 245768 | tf_op jit(solution)/shard_map/ppermute | solution.py:205
  18.0 1.5 %collective-permute-start.7 = (bf16[128,640]{1,0:T(8,128)(2,1)S(1)}, bf16[128,640]{1,0:T(8,128)(2,1)S(1)}, u32[]{:S(2)}, u32[]{:S(2)}) collective-permute-start(bf16[128,640]{1,0:T(8,128)(2,1)S(1)} %collective-permute-done.refs_4_.refs_3_), channel_id=1, source_target_pairs={{0,2},{2,0},{1,3},{3,1},{4,6},{6,4},{5,7},{7,5},{8,10},{10,8},{9,1... | collective-permute-start | bytes 491528 | tf_op jit(solution)/shard_map/ppermute | solution.py:208
  19.5 0.8 %collective-permute-start.9 = (bf16[128,640]{1,0:T(8,128)(2,1)S(1)}, bf16[128,640]{1,0:T(8,128)(2,1)S(1)}, u32[]{:S(2)}, u32[]{:S(2)}) collective-permute-start(bf16[128,640]{1,0:T(8,128)(2,1)S(1)} %get-tuple-element.27), channel_id=1, source_target_pairs={{0,4},{4,0},{8,12},{12,8},{1,5},{5,1},{9,13},{13,9},{2,6},{6,2},{1... | collective-permute-start | bytes 491528 | tf_op jit(solution)/shard_map/ppermute | solution.py:205
  20.3 0.9 %collective-permute-done.4.refs_3_.refs_2_ = bf16[64,640]{1,0:T(8,128)(2,1)S(1)} collective-permute-done((bf16[64,640]{1,0:T(8,128)(2,1)S(1)}, bf16[64,640]{1,0:T(8,128)(2,1)S(1)}, u32[]{:S(2)}, u32[]{:S(2)}) %collective-permute-start.4) | collective-permute-done | bytes 81952 | tf_op jit(solution)/shard_map/ppermute | solution.py:205
  21.2 1.5 %collective-permute-start.11 = (bf16[64,640]{1,0:T(8,128)(2,1)S(1)}, bf16[64,640]{1,0:T(8,128)(2,1)S(1)}, u32[]{:S(2)}, u32[]{:S(2)}) collective-permute-start(bf16[64,640]{1,0:T(8,128)(2,1)S(1)} %collective-permute-done.4.refs_3_.refs_2_), channel_id=1, source_target_pairs={{0,2},{2,0},{1,3},{3,1},{4,6},{6,4},{5,7},{7,5},{8,10},{10,8},{9,1... | collective-permute-start | bytes 245768 | tf_op jit(solution)/shard_map/ppermute | solution.py:208
  22.7 0.3 collective-permute-done.8.refs_2_.refs_1_
  23.0 1.5 %collective-permute-start.10 = (bf16[64,640]{1,0:T(8,128)(2,1)S(1)}, bf16[64,640]{1,0:T(8,128)(2,1)S(1)}, u32[]{:S(2)}, u32[]{:S(2)}) collective-permute-start(bf16[64,640]{1,0:T(8,128)(2,1)S(1)} %collective-permute-done.8.refs_2_.refs_1_), channel_id=1, source_target_pairs={{0,2},{2,0},{1,3},{3,1},{4,6},{6,4},{5,7},{7,5},{8,10},{10,8},{9,1... | collective-permute-start | bytes 245768 | tf_op jit(solution)/shard_map/ppermute | solution.py:208
  24.5 0.3 shard_map.86
  24.8 0.3 shard_map.88.mine
  25.2 2.3 %shard_map.89.refs_3_ = f32[256,640]{1,0:T(8,128)S(1)} custom-call(f32[8,128]{1,0:T(8,128)S(1)} %get-tuple-element.22.weight_ref, f32[8,128]{1,0:T(8,128)S(1)} %broadcast_in_dim.44.len_ref, f32[1,128]{1,0:T(1,128)S(1)} %broadcast_in_dim.45.sharp_ref, f32[256,512]{1,0:T(8,128)S(1)} %shard_map.87.mine, f32[256,512]{1,0:T(8,128)S(1)} %collective-permute-done.6.other, ...), custom_call_target="tpu_custom_call" | custom-call | tf_op jit(solution)/shard_map/pallas_call | solution.py:93
  27.6 0.3 shard_map.90.mine
  27.9 0.6 %collective-permute-start.12 = (f32[256,256]{1,0:T(8,128)S(1)}, f32[256,256]{1,0:T(8,128)S(1)}, u32[]{:S(2)}, u32[]{:S(2)}) collective-permute-start(f32[256,256]{1,0:T(8,128)S(1)} %shard_map.90.mine), channel_id=1, source_target_pairs={{0,1},{1,0},{2,3},{3,2},{4,5},{5,4},{6,7},{7,6},{8,9},{9,8},{10,11... | collective-permute-start | bytes 786440 | tf_op jit(solution)/shard_map/ppermute | solution.py:208
  28.4 1.4 %shard_map.91.refs_3_ = f32[256,640]{1,0:T(8,128)S(1)} custom-call(f32[8,128]{1,0:T(8,128)S(1)} %get-tuple-element.22.weight_ref, f32[8,128]{1,0:T(8,128)S(1)} %broadcast_in_dim.44.len_ref, f32[1,128]{1,0:T(1,128)S(1)} %broadcast_in_dim.45.sharp_ref, f32[256,256]{1,0:T(8,128)S(1)} %shard_map.88.mine, f32[256,256]{1,0:T(8,128)S(1)} %collective-permute-done.13.other, ...), custom_call_target="tpu_custom_call" | custom-call | tf_op jit(solution)/shard_map/pallas_call | solution.py:93
  29.8 2.1 %shard_map.92 = (bf16[256,640]{1,0:T(8,128)(2,1)}, f32[1,8]{1,0:T(1,128)}) custom-call(f32[8,128]{1,0:T(8,128)S(1)} %get-tuple-element.22.weight_ref, f32[8,128]{1,0:T(8,128)S(1)} %broadcast_in_dim.44.len_ref, f32[1,128]{1,0:T(1,128)S(1)} %broadcast_in_dim.45.sharp_ref, f32[256,256]{1,0:T(8,128)S(1)} %shard_map.90.mine, ...), custom_call_target="tpu_custom_call" | custom-call | tf_op jit(solution)/shard_map/pallas_call | solution.py:93
  (31 shorter events, 0.5 us)
Async XLA Ops:
  0.6 7.0 %copy-start.1 = (f32[2,1280]{1,0:T(2,128)S(1)}, f32[2,1280]{1,0:T(2,128)}, u32[]{:S(2)}) copy-start(f32[2,1280]{1,0:T(2,128)} %refs_0_.1) | copy-start | bytes 30724
  0.6 14.7 %copy-start = (bf16[1,256,640]{2,1,0:T(8,128)(2,1)S(1)}, bf16[1,256,640]{2,1,0:T(8,128)(2,1)}, u32[]{:S(2)}) copy-start(bf16[1,256,640]{2,1,0:T(8,128)(2,1)} %param.7) | copy-start | bytes 983044
  1.9 13.3 %collective-permute-start = (bf16[128,640]{1,0:T(8,128)(2,1)S(1)}, bf16[128,640]{1,0:T(8,128)(2,1)S(1)}, u32[]{:S(2)}, u32[]{:S(2)}) collective-permute-start(bf16[128,640]{1,0:T(8,128)(2,1)S(1)} %get-tuple-element.34), channel_id=1, source_target_pairs={{0,8},{4,12},{8,0},{12,4},{1,9},{5,13},{9,1},{13,5},{2,10},{6,14},... | collective-permute-start | bytes 491528 | tf_op jit(solution)/shard_map/ppermute | solution.py:205
  6.0 9.4 %collective-permute-start.3 = (bf16[128,640]{1,0:T(8,128)(2,1)S(1)}, bf16[128,640]{1,0:T(8,128)(2,1)S(1)}, u32[]{:S(2)}, u32[]{:S(2)}) collective-permute-start(bf16[128,640]{1,0:T(8,128)(2,1)S(1)} %get-tuple-element.34), channel_id=1, source_target_pairs={{0,4},{4,0},{8,12},{12,8},{1,5},{5,1},{9,13},{13,9},{2,6},{6,2},{1... | collective-permute-start | bytes 491528 | tf_op jit(solution)/shard_map/ppermute | solution.py:205
  7.6 7.6 %collective-permute-start.2 = (f32[2,1280]{1,0:T(2,128)S(1)}, f32[2,1280]{1,0:T(2,128)S(1)}, u32[]{:S(2)}, u32[]{:S(2)}) collective-permute-start(f32[2,1280]{1,0:T(2,128)S(1)} %copy-done.1), channel_id=1, source_target_pairs={{0,12},{4,8},{8,4},{12,0},{1,13},{5,9},{9,5},{13,1},{2,14},{6,10},... | collective-permute-start | bytes 30728 | tf_op jit(solution)/shard_map/ppermute | solution.py:205
  7.6 7.6 %collective-permute-start.1 = (f32[2,1280]{1,0:T(2,128)S(1)}, f32[2,1280]{1,0:T(2,128)S(1)}, u32[]{:S(2)}, u32[]{:S(2)}) collective-permute-start(f32[2,1280]{1,0:T(2,128)S(1)} %copy-done.1), channel_id=1, source_target_pairs={{0,4},{1,9},{4,0},{5,13},{8,12},{9,1},{12,8},{13,5},{2,6},{3,11},{... | collective-permute-start | bytes 30728 | tf_op jit(solution)/shard_map/ppermute | solution.py:214
  8.5 0.7 %copy-start.4 = (s32[8]{0:T(128)S(1)}, s32[8]{0:T(128)}, u32[]{:S(2)}) copy-start(s32[8]{0:T(128)} %param.9) | copy-start | bytes 100
  15.8 2.2 %collective-permute-start.6 = (f32[256,512]{1,0:T(8,128)S(1)}, f32[256,512]{1,0:T(8,128)S(1)}, u32[]{:S(2)}, u32[]{:S(2)}) collective-permute-start(f32[256,512]{1,0:T(8,128)S(1)} %shard_map.87.mine), channel_id=1, source_target_pairs={{0,1},{1,0},{2,3},{3,2},{4,5},{5,4},{6,7},{7,6},{8,9},{9,8},{10,11... | collective-permute-start | bytes 1572872 | tf_op jit(solution)/shard_map/ppermute | solution.py:208
  15.9 8.6 %copy-start.2 = (f32[1,1280]{1,0:T(1,128)S(1)}, f32[1,1280]{1,0:T(1,128)}, u32[]{:S(2)}) copy-start(f32[1,1280]{1,0:T(1,128)} %pool_ref.1) | copy-start | bytes 15364
  15.9 5.3 %collective-permute-start.4 = (bf16[64,640]{1,0:T(8,128)(2,1)S(1)}, bf16[64,640]{1,0:T(8,128)(2,1)S(1)}, u32[]{:S(2)}, u32[]{:S(2)}) collective-permute-start(bf16[64,640]{1,0:T(8,128)(2,1)S(1)} %get-tuple-element.37), channel_id=1, source_target_pairs={{0,4},{4,0},{8,12},{12,8},{1,5},{5,1},{9,13},{13,9},{2,6},{6,2},{1... | collective-permute-start | bytes 245768 | tf_op jit(solution)/shard_map/ppermute | solution.py:205
  16.8 7.7 %copy-start.3 = (s32[1,28]{1,0:T(1,128)S(1)}, s32[1,28]{1,0:T(1,128)}, u32[]{:S(2)}) copy-start(s32[1,28]{1,0:T(1,128)} %hits_ref) | copy-start | bytes 340
  16.8 6.2 %collective-permute-start.8 = (bf16[64,640]{1,0:T(8,128)(2,1)S(1)}, bf16[64,640]{1,0:T(8,128)(2,1)S(1)}, u32[]{:S(2)}, u32[]{:S(2)}) collective-permute-start(bf16[64,640]{1,0:T(8,128)(2,1)S(1)} %get-tuple-element.36), channel_id=1, source_target_pairs={{0,4},{4,0},{8,12},{12,8},{1,5},{5,1},{9,13},{13,9},{2,6},{6,2},{1... | collective-permute-start | bytes 245768 | tf_op jit(solution)/shard_map/ppermute | solution.py:205
  18.0 6.8 %collective-permute-start.7 = (bf16[128,640]{1,0:T(8,128)(2,1)S(1)}, bf16[128,640]{1,0:T(8,128)(2,1)S(1)}, u32[]{:S(2)}, u32[]{:S(2)}) collective-permute-start(bf16[128,640]{1,0:T(8,128)(2,1)S(1)} %collective-permute-done.refs_4_.refs_3_), channel_id=1, source_target_pairs={{0,2},{2,0},{1,3},{3,1},{4,6},{6,4},{5,7},{7,5},{8,10},{10,8},{9,1... | collective-permute-start | bytes 491528 | tf_op jit(solution)/shard_map/ppermute | solution.py:208
  19.5 8.0 %collective-permute-start.9 = (bf16[128,640]{1,0:T(8,128)(2,1)S(1)}, bf16[128,640]{1,0:T(8,128)(2,1)S(1)}, u32[]{:S(2)}, u32[]{:S(2)}) collective-permute-start(bf16[128,640]{1,0:T(8,128)(2,1)S(1)} %get-tuple-element.27), channel_id=1, source_target_pairs={{0,4},{4,0},{8,12},{12,8},{1,5},{5,1},{9,13},{13,9},{2,6},{6,2},{1... | collective-permute-start | bytes 491528 | tf_op jit(solution)/shard_map/ppermute | solution.py:205
  20.3 4.2 %collective-permute-start.5 = (f32[2,1280]{1,0:T(2,128)S(1)}, f32[2,1280]{1,0:T(2,128)S(1)}, u32[]{:S(2)}, u32[]{:S(2)}) collective-permute-start(f32[2,1280]{1,0:T(2,128)S(1)} %collective-permute-done.1.refs_1_), channel_id=1, source_target_pairs={{0,1},{1,0},{2,3},{3,2},{4,5},{5,4},{6,7},{7,6},{8,9},{9,8},{10,11... | collective-permute-start | bytes 30728 | tf_op jit(solution)/shard_map/ppermute | solution.py:208
  21.2 6.3 %collective-permute-start.11 = (bf16[64,640]{1,0:T(8,128)(2,1)S(1)}, bf16[64,640]{1,0:T(8,128)(2,1)S(1)}, u32[]{:S(2)}, u32[]{:S(2)}) collective-permute-start(bf16[64,640]{1,0:T(8,128)(2,1)S(1)} %collective-permute-done.4.refs_3_.refs_2_), channel_id=1, source_target_pairs={{0,2},{2,0},{1,3},{3,1},{4,6},{6,4},{5,7},{7,5},{8,10},{10,8},{9,1... | collective-permute-start | bytes 245768 | tf_op jit(solution)/shard_map/ppermute | solution.py:208
  23.0 4.6 %collective-permute-start.10 = (bf16[64,640]{1,0:T(8,128)(2,1)S(1)}, bf16[64,640]{1,0:T(8,128)(2,1)S(1)}, u32[]{:S(2)}, u32[]{:S(2)}) collective-permute-start(bf16[64,640]{1,0:T(8,128)(2,1)S(1)} %collective-permute-done.8.refs_2_.refs_1_), channel_id=1, source_target_pairs={{0,2},{2,0},{1,3},{3,1},{4,6},{6,4},{5,7},{7,5},{8,10},{10,8},{9,1... | collective-permute-start | bytes 245768 | tf_op jit(solution)/shard_map/ppermute | solution.py:208
  25.1 3.3 %collective-permute-start.13 = (f32[256,256]{1,0:T(8,128)S(1)}, f32[256,256]{1,0:T(8,128)S(1)}, u32[]{:S(2)}, u32[]{:S(2)}) collective-permute-start(f32[256,256]{1,0:T(8,128)S(1)} %shard_map.88.mine), channel_id=1, source_target_pairs={{0,1},{1,0},{2,3},{3,2},{4,5},{5,4},{6,7},{7,6},{8,9},{9,8},{10,11... | collective-permute-start | bytes 786440 | tf_op jit(solution)/shard_map/ppermute | solution.py:208
  27.9 2.0 %collective-permute-start.12 = (f32[256,256]{1,0:T(8,128)S(1)}, f32[256,256]{1,0:T(8,128)S(1)}, u32[]{:S(2)}, u32[]{:S(2)}) collective-permute-start(f32[256,256]{1,0:T(8,128)S(1)} %shard_map.90.mine), channel_id=1, source_target_pairs={{0,1},{1,0},{2,3},{3,2},{4,5},{5,4},{6,7},{7,6},{8,9},{9,8},{10,11... | collective-permute-start | bytes 786440 | tf_op jit(solution)/shard_map/ppermute | solution.py:208

commit v19 on v18

--- a/solution.py
+++ b/solution.py
@@ -142,7 +142,7 @@
     return call_kernel(partial_kernel, shape, query, *blocks)
 
 
-def align_block(similar, length, half_sharp):
+def align_block(similar, length, half_sharp, weight):
     column = lax.broadcasted_iota(jnp.int32, (1, similar.shape[1]), 1).astype(jnp.float32)
     inside = column < length
     fraction = 1.0 / length[:, 0:1]
@@ -159,12 +159,7 @@
     )
     scores = jnp.where(inside, scores, -jnp.inf)
     raised = jnp.exp(scores - jnp.max(scores, axis=1, keepdims=True))
-    return raised, jnp.sum(raised, axis=1, keepdims=True)
-
-
-def weighted_term(weight, alignment, blocks):
-    target = blocks[0][...] if len(blocks) == 1 else jnp.concatenate([b[...] for b in blocks])
-    return weight * jnp.dot(alignment, target, preferred_element_type=jnp.float32)
+    return raised * (weight / jnp.sum(raised, axis=1, keepdims=True))
 
 
 def profile_kernel(model_width, targets, last, weight_ref, len_ref, sharp_ref, mine, other, *refs):
@@ -178,16 +173,20 @@
         chosen = jnp.where(row == lane, posterior_ref[:, 0:1], 0.0)
         posterior_out[...] = jnp.sum(chosen, axis=0, keepdims=True)
     rows = mine.shape[1] // len(targets)
-    acc = None
+    weighted, rows_of = [], []
     for at, (slot, count) in enumerate(targets):
         part = pl.ds(at * rows, rows)
         similar = (mine[:, part] + other[:, part]) * (1.0 / math.sqrt(model_width))
-        raised, total = align_block(similar, len_ref[slot : slot + 1, :rows], sharp_ref[:, 0:1])
-        term = weighted_term(
-            weight_ref[slot : slot + 1, 0:1] / total, raised.astype(jnp.bfloat16), blocks[:count]
-        )
-        acc = term if acc is None else acc + term
+        weight = weight_ref[slot : slot + 1, 0:1]
+        aligned = align_block(similar, len_ref[slot : slot + 1, :rows], sharp_ref[:, 0:1], weight)
+        weighted.append(aligned.astype(jnp.bfloat16))
+        rows_of += [block[...] for block in blocks[:count]]
         blocks = blocks[count:]
+    acc = jnp.dot(
+        jnp.concatenate(weighted, axis=1),
+        jnp.concatenate(rows_of),
+        preferred_element_type=jnp.float32,
+    )
     if blocks:
         acc += blocks[0][...]
     out_ref[...] = acc.astype(out_ref.dtype)

time: 32.1 us -> 31.5 us (0.981)
  Pallas kernels: 7.15 us -> 6.41 us
    pallas_call x7, Pallas kernels: 7.15 us -> 6.41 us  [call_kernel(): pl.pallas_call(kernel, out_shape=out_shape, in_specs=[VMEM] * len(operand...]
  transfers between devices with their start and end apart: 14 -> 14, of which waited for: 3 -> 5; matrix products, arithmetic and copies ran while one was open for 2% -> 2% of each run, Pallas kernels for 14% -> 13%
where the time goes in v19:
time: 31.5 us; the launch traced here: 31.3 us
  starting transfers between devices  14.5 us (46%)
  waiting for transfers between devices  6.49 us (21%)
  Pallas kernels  6.41 us (20%)
  local copies, waits for them, and re-layouts  2.25 us (7%)
  between operations  1.41 us (4%)
    ppermute x6, starting transfers between devices, from_peer(): return lax.ppermute(array, 'tgt', [(i, i ^ k) for i in range(4)])  8.55 us
    pallas_call x7, Pallas kernels, call_kernel(): pl.pallas_call(kernel, out_shape=out_shape, in_specs=[VMEM] * len(operand...  6.41 us
    ppermute x6, waiting for transfers between devices, from_peer(): return lax.ppermute(array, 'tgt', [(i, i ^ k) for i in range(4)])  6.28 us
    ppermute x7, starting transfers between devices, across(): return lax.ppermute(array, axis, [(0, 1), (1, 0)])  5.09 us
    squeeze x1, local copies, waits for them, and re-layouts, per_device_by_target(): rest = lax.dynamic_index_in_dim(target_res, 1 - at_qry, 0, keepdims=False)  1.26 us
    ppermute x1, starting transfers between devices, per_device_by_target(): pool_split = lax.ppermute(target_pool, ('tgt', 'rep'), split)  0.9 us
  transfers between devices with their start and end apart: 14, of which 5 were waited for; matrix products, arithmetic and copies ran while one was open for 2% of the time, Pallas kernels for 13%

profile of v19, /device:TPU:0, one launch (start us, length us, event | category | flops | bytes accessed | tf_op | source)
XLA Modules:
  0.0 31.3 jit_solution(15527221294982508677)
XLA Ops:
  0.7 1.3 %dynamic-slice_bitcast_fusion = (bf16[128,640]{1,0:T(8,128)(2,1)S(1)}, bf16[128,640]{1,0:T(8,128)(2,1)S(1)}, bf16[128,640]{1,0:T(8,128)(2,1)S(1)}, bf16[128,640]{1,0:T(8,128)(2,1)S(1)}) fusion(bf16[2,128,640]{2,1,0:T(8,128)(2,1)} %param.8, s32[]{:T(128)S(6)} %select_n.13, s32[]{:T(128)S(6)} %select_n.11), kind=kLoop, calls=%fused_computation | loop fusion | bytes 1310728 | tf_op jit(solution)/shard_map/jit(dynamic_index_in_dim)/squeeze | solution.py:218
  1.9 4.1 %collective-permute-start = (bf16[128,640]{1,0:T(8,128)(2,1)S(1)}, bf16[128,640]{1,0:T(8,128)(2,1)S(1)}, u32[]{:S(2)}, u32[]{:S(2)}) collective-permute-start(bf16[128,640]{1,0:T(8,128)(2,1)S(1)} %get-tuple-element.34), channel_id=1, source_target_pairs={{0,8},{4,12},{8,0},{12,4},{1,9},{5,13},{9,1},{13,5},{2,10},{6,14},... | collective-permute-start | bytes 491528 | tf_op jit(solution)/shard_map/ppermute | solution.py:204
  6.0 1.6 %collective-permute-start.3 = (bf16[128,640]{1,0:T(8,128)(2,1)S(1)}, bf16[128,640]{1,0:T(8,128)(2,1)S(1)}, u32[]{:S(2)}, u32[]{:S(2)}) collective-permute-start(bf16[128,640]{1,0:T(8,128)(2,1)S(1)} %get-tuple-element.34), channel_id=1, source_target_pairs={{0,4},{4,0},{8,12},{12,8},{1,5},{5,1},{9,13},{13,9},{2,6},{6,2},{1... | collective-permute-start | bytes 491528 | tf_op jit(solution)/shard_map/ppermute | solution.py:204
  7.6 0.9 %collective-permute-start.1 = (f32[2,1280]{1,0:T(2,128)S(1)}, f32[2,1280]{1,0:T(2,128)S(1)}, u32[]{:S(2)}, u32[]{:S(2)}) collective-permute-start(f32[2,1280]{1,0:T(2,128)S(1)} %copy-done.1), channel_id=1, source_target_pairs={{0,4},{1,9},{4,0},{5,13},{8,12},{9,1},{12,8},{13,5},{2,6},{3,11},{... | collective-permute-start | bytes 30728 | tf_op jit(solution)/shard_map/ppermute | solution.py:213
  8.6 0.6 %copy-done.4 = s32[8]{0:T(128)S(1)} copy-done((s32[8]{0:T(128)S(1)}, s32[8]{0:T(128)}, u32[]{:S(2)}) %copy-start.4) | copy-done | bytes 56
  9.2 0.2 select_reduce_fusion
  10.1 5.1 %collective-permute-done.2.refs_3_ = f32[2,1280]{1,0:T(2,128)S(1)} collective-permute-done((f32[2,1280]{1,0:T(2,128)S(1)}, f32[2,1280]{1,0:T(2,128)S(1)}, u32[]{:S(2)}, u32[]{:S(2)}) %collective-permute-start.2) | collective-permute-done | bytes 10272 | tf_op jit(solution)/shard_map/ppermute | solution.py:204
  15.4 0.4 %shard_map.87.mine = f32[256,512]{1,0:T(8,128)S(1)} custom-call(bf16[256,640]{1,0:T(8,128)(2,1)S(1)} %bitcast.23, bf16[128,640]{1,0:T(8,128)(2,1)S(1)} %get-tuple-element.33.refs_1_.refs_0_, bf16[128,640]{1,0:T(8,128)(2,1)S(1)} %get-tuple-element.35.refs_2_.refs_1_, bf16[128,640]{1,0:T(8,128)(2,1)S(1)} %collective-permute-done.3.refs_3_.refs_2_, ...), custom_call_target="tpu_custom_call" | custom-call | tf_op jit(solution)/shard_map/pallas_call | solution.py:93
  15.9 0.8 %collective-permute-start.4 = (bf16[64,640]{1,0:T(8,128)(2,1)S(1)}, bf16[64,640]{1,0:T(8,128)(2,1)S(1)}, u32[]{:S(2)}, u32[]{:S(2)}) collective-permute-start(bf16[64,640]{1,0:T(8,128)(2,1)S(1)} %get-tuple-element.37), channel_id=1, source_target_pairs={{0,4},{4,0},{8,12},{12,8},{1,5},{5,1},{9,13},{13,9},{2,6},{6,2},{1... | collective-permute-start | bytes 245768 | tf_op jit(solution)/shard_map/ppermute | solution.py:204
  16.8 1.2 %collective-permute-start.8 = (bf16[64,640]{1,0:T(8,128)(2,1)S(1)}, bf16[64,640]{1,0:T(8,128)(2,1)S(1)}, u32[]{:S(2)}, u32[]{:S(2)}) collective-permute-start(bf16[64,640]{1,0:T(8,128)(2,1)S(1)} %get-tuple-element.36), channel_id=1, source_target_pairs={{0,4},{4,0},{8,12},{12,8},{1,5},{5,1},{9,13},{13,9},{2,6},{6,2},{1... | collective-permute-start | bytes 245768 | tf_op jit(solution)/shard_map/ppermute | solution.py:204
  18.0 1.5 %collective-permute-start.7 = (bf16[128,640]{1,0:T(8,128)(2,1)S(1)}, bf16[128,640]{1,0:T(8,128)(2,1)S(1)}, u32[]{:S(2)}, u32[]{:S(2)}) collective-permute-start(bf16[128,640]{1,0:T(8,128)(2,1)S(1)} %collective-permute-done.refs_4_.refs_3_), channel_id=1, source_target_pairs={{0,2},{2,0},{1,3},{3,1},{4,6},{6,4},{5,7},{7,5},{8,10},{10,8},{9,1... | collective-permute-start | bytes 491528 | tf_op jit(solution)/shard_map/ppermute | solution.py:207
  19.5 0.8 %collective-permute-start.9 = (bf16[128,640]{1,0:T(8,128)(2,1)S(1)}, bf16[128,640]{1,0:T(8,128)(2,1)S(1)}, u32[]{:S(2)}, u32[]{:S(2)}) collective-permute-start(bf16[128,640]{1,0:T(8,128)(2,1)S(1)} %get-tuple-element.27), channel_id=1, source_target_pairs={{0,4},{4,0},{8,12},{12,8},{1,5},{5,1},{9,13},{13,9},{2,6},{6,2},{1... | collective-permute-start | bytes 491528 | tf_op jit(solution)/shard_map/ppermute | solution.py:204
  20.3 0.9 %collective-permute-done.4.refs_3_.refs_2_ = bf16[64,640]{1,0:T(8,128)(2,1)S(1)} collective-permute-done((bf16[64,640]{1,0:T(8,128)(2,1)S(1)}, bf16[64,640]{1,0:T(8,128)(2,1)S(1)}, u32[]{:S(2)}, u32[]{:S(2)}) %collective-permute-start.4) | collective-permute-done | bytes 81952 | tf_op jit(solution)/shard_map/ppermute | solution.py:204
  21.2 1.5 %collective-permute-start.11 = (bf16[64,640]{1,0:T(8,128)(2,1)S(1)}, bf16[64,640]{1,0:T(8,128)(2,1)S(1)}, u32[]{:S(2)}, u32[]{:S(2)}) collective-permute-start(bf16[64,640]{1,0:T(8,128)(2,1)S(1)} %collective-permute-done.4.refs_3_.refs_2_), channel_id=1, source_target_pairs={{0,2},{2,0},{1,3},{3,1},{4,6},{6,4},{5,7},{7,5},{8,10},{10,8},{9,1... | collective-permute-start | bytes 245768 | tf_op jit(solution)/shard_map/ppermute | solution.py:207
  22.7 0.3 collective-permute-done.8.refs_2_.refs_1_
  23.0 1.5 %collective-permute-start.10 = (bf16[64,640]{1,0:T(8,128)(2,1)S(1)}, bf16[64,640]{1,0:T(8,128)(2,1)S(1)}, u32[]{:S(2)}, u32[]{:S(2)}) collective-permute-start(bf16[64,640]{1,0:T(8,128)(2,1)S(1)} %collective-permute-done.8.refs_2_.refs_1_), channel_id=1, source_target_pairs={{0,2},{2,0},{1,3},{3,1},{4,6},{6,4},{5,7},{7,5},{8,10},{10,8},{9,1... | collective-permute-start | bytes 245768 | tf_op jit(solution)/shard_map/ppermute | solution.py:207
  24.5 0.3 shard_map.86
  24.8 0.3 shard_map.88.mine
  25.2 2.3 %shard_map.89.refs_3_ = f32[256,640]{1,0:T(8,128)S(1)} custom-call(f32[8,128]{1,0:T(8,128)S(1)} %get-tuple-element.22.weight_ref, f32[8,128]{1,0:T(8,128)S(1)} %broadcast_in_dim.44.len_ref, f32[1,128]{1,0:T(1,128)S(1)} %broadcast_in_dim.45.sharp_ref, f32[256,512]{1,0:T(8,128)S(1)} %shard_map.87.mine, f32[256,512]{1,0:T(8,128)S(1)} %collective-permute-done.6.other, ...), custom_call_target="tpu_custom_call" | custom-call | tf_op jit(solution)/shard_map/pallas_call | solution.py:93
  27.5 0.1 collective-permute-done.10.refs_2_.refs_1_
  27.6 0.3 shard_map.90.mine
  27.9 0.5 %collective-permute-start.12 = (f32[256,256]{1,0:T(8,128)S(1)}, f32[256,256]{1,0:T(8,128)S(1)}, u32[]{:S(2)}, u32[]{:S(2)}) collective-permute-start(f32[256,256]{1,0:T(8,128)S(1)} %shard_map.90.mine), channel_id=1, source_target_pairs={{0,1},{1,0},{2,3},{3,2},{4,5},{5,4},{6,7},{7,6},{8,9},{9,8},{10,11... | collective-permute-start | bytes 786440 | tf_op jit(solution)/shard_map/ppermute | solution.py:207
  28.3 1.1 %shard_map.91.refs_3_ = f32[256,640]{1,0:T(8,128)S(1)} custom-call(f32[8,128]{1,0:T(8,128)S(1)} %get-tuple-element.22.weight_ref, f32[8,128]{1,0:T(8,128)S(1)} %broadcast_in_dim.44.len_ref, f32[1,128]{1,0:T(1,128)S(1)} %broadcast_in_dim.45.sharp_ref, f32[256,256]{1,0:T(8,128)S(1)} %shard_map.88.mine, f32[256,256]{1,0:T(8,128)S(1)} %collective-permute-done.13.other, ...), custom_call_target="tpu_custom_call" | custom-call | tf_op jit(solution)/shard_map/pallas_call | solution.py:93
  29.5 1.8 %shard_map.92 = (bf16[256,640]{1,0:T(8,128)(2,1)}, f32[1,8]{1,0:T(1,128)}) custom-call(f32[8,128]{1,0:T(8,128)S(1)} %get-tuple-element.22.weight_ref, f32[8,128]{1,0:T(8,128)S(1)} %broadcast_in_dim.44.len_ref, f32[1,128]{1,0:T(1,128)S(1)} %broadcast_in_dim.45.sharp_ref, f32[256,256]{1,0:T(8,128)S(1)} %shard_map.90.mine, ...), custom_call_target="tpu_custom_call" | custom-call | tf_op jit(solution)/shard_map/pallas_call | solution.py:93
  (31 shorter events, 0.7 us)
Async XLA Ops:
  0.6 7.0 %copy-start.1 = (f32[2,1280]{1,0:T(2,128)S(1)}, f32[2,1280]{1,0:T(2,128)}, u32[]{:S(2)}) copy-start(f32[2,1280]{1,0:T(2,128)} %refs_0_.1) | copy-start | bytes 30724
  0.6 14.7 %copy-start = (bf16[1,256,640]{2,1,0:T(8,128)(2,1)S(1)}, bf16[1,256,640]{2,1,0:T(8,128)(2,1)}, u32[]{:S(2)}) copy-start(bf16[1,256,640]{2,1,0:T(8,128)(2,1)} %param.7) | copy-start | bytes 983044
  1.9 13.3 %collective-permute-start = (bf16[128,640]{1,0:T(8,128)(2,1)S(1)}, bf16[128,640]{1,0:T(8,128)(2,1)S(1)}, u32[]{:S(2)}, u32[]{:S(2)}) collective-permute-start(bf16[128,640]{1,0:T(8,128)(2,1)S(1)} %get-tuple-element.34), channel_id=1, source_target_pairs={{0,8},{4,12},{8,0},{12,4},{1,9},{5,13},{9,1},{13,5},{2,10},{6,14},... | collective-permute-start | bytes 491528 | tf_op jit(solution)/shard_map/ppermute | solution.py:204
  6.0 9.4 %collective-permute-start.3 = (bf16[128,640]{1,0:T(8,128)(2,1)S(1)}, bf16[128,640]{1,0:T(8,128)(2,1)S(1)}, u32[]{:S(2)}, u32[]{:S(2)}) collective-permute-start(bf16[128,640]{1,0:T(8,128)(2,1)S(1)} %get-tuple-element.34), channel_id=1, source_target_pairs={{0,4},{4,0},{8,12},{12,8},{1,5},{5,1},{9,13},{13,9},{2,6},{6,2},{1... | collective-permute-start | bytes 491528 | tf_op jit(solution)/shard_map/ppermute | solution.py:204
  7.6 7.6 %collective-permute-start.2 = (f32[2,1280]{1,0:T(2,128)S(1)}, f32[2,1280]{1,0:T(2,128)S(1)}, u32[]{:S(2)}, u32[]{:S(2)}) collective-permute-start(f32[2,1280]{1,0:T(2,128)S(1)} %copy-done.1), channel_id=1, source_target_pairs={{0,12},{4,8},{8,4},{12,0},{1,13},{5,9},{9,5},{13,1},{2,14},{6,10},... | collective-permute-start | bytes 30728 | tf_op jit(solution)/shard_map/ppermute | solution.py:204
  7.6 7.6 %collective-permute-start.1 = (f32[2,1280]{1,0:T(2,128)S(1)}, f32[2,1280]{1,0:T(2,128)S(1)}, u32[]{:S(2)}, u32[]{:S(2)}) collective-permute-start(f32[2,1280]{1,0:T(2,128)S(1)} %copy-done.1), channel_id=1, source_target_pairs={{0,4},{1,9},{4,0},{5,13},{8,12},{9,1},{12,8},{13,5},{2,6},{3,11},{... | collective-permute-start | bytes 30728 | tf_op jit(solution)/shard_map/ppermute | solution.py:213
  8.5 0.7 %copy-start.4 = (s32[8]{0:T(128)S(1)}, s32[8]{0:T(128)}, u32[]{:S(2)}) copy-start(s32[8]{0:T(128)} %param.9) | copy-start | bytes 100
  15.8 2.2 %collective-permute-start.6 = (f32[256,512]{1,0:T(8,128)S(1)}, f32[256,512]{1,0:T(8,128)S(1)}, u32[]{:S(2)}, u32[]{:S(2)}) collective-permute-start(f32[256,512]{1,0:T(8,128)S(1)} %shard_map.87.mine), channel_id=1, source_target_pairs={{0,1},{1,0},{2,3},{3,2},{4,5},{5,4},{6,7},{7,6},{8,9},{9,8},{10,11... | collective-permute-start | bytes 1572872 | tf_op jit(solution)/shard_map/ppermute | solution.py:207
  15.9 8.6 %copy-start.2 = (f32[1,1280]{1,0:T(1,128)S(1)}, f32[1,1280]{1,0:T(1,128)}, u32[]{:S(2)}) copy-start(f32[1,1280]{1,0:T(1,128)} %pool_ref.1) | copy-start | bytes 15364
  15.9 5.3 %collective-permute-start.4 = (bf16[64,640]{1,0:T(8,128)(2,1)S(1)}, bf16[64,640]{1,0:T(8,128)(2,1)S(1)}, u32[]{:S(2)}, u32[]{:S(2)}) collective-permute-start(bf16[64,640]{1,0:T(8,128)(2,1)S(1)} %get-tuple-element.37), channel_id=1, source_target_pairs={{0,4},{4,0},{8,12},{12,8},{1,5},{5,1},{9,13},{13,9},{2,6},{6,2},{1... | collective-permute-start | bytes 245768 | tf_op jit(solution)/shard_map/ppermute | solution.py:204
  16.8 7.7 %copy-start.3 = (s32[1,28]{1,0:T(1,128)S(1)}, s32[1,28]{1,0:T(1,128)}, u32[]{:S(2)}) copy-start(s32[1,28]{1,0:T(1,128)} %hits_ref) | copy-start | bytes 340
  16.8 6.2 %collective-permute-start.8 = (bf16[64,640]{1,0:T(8,128)(2,1)S(1)}, bf16[64,640]{1,0:T(8,128)(2,1)S(1)}, u32[]{:S(2)}, u32[]{:S(2)}) collective-permute-start(bf16[64,640]{1,0:T(8,128)(2,1)S(1)} %get-tuple-element.36), channel_id=1, source_target_pairs={{0,4},{4,0},{8,12},{12,8},{1,5},{5,1},{9,13},{13,9},{2,6},{6,2},{1... | collective-permute-start | bytes 245768 | tf_op jit(solution)/shard_map/ppermute | solution.py:204
  18.0 6.8 %collective-permute-start.7 = (bf16[128,640]{1,0:T(8,128)(2,1)S(1)}, bf16[128,640]{1,0:T(8,128)(2,1)S(1)}, u32[]{:S(2)}, u32[]{:S(2)}) collective-permute-start(bf16[128,640]{1,0:T(8,128)(2,1)S(1)} %collective-permute-done.refs_4_.refs_3_), channel_id=1, source_target_pairs={{0,2},{2,0},{1,3},{3,1},{4,6},{6,4},{5,7},{7,5},{8,10},{10,8},{9,1... | collective-permute-start | bytes 491528 | tf_op jit(solution)/shard_map/ppermute | solution.py:207
  19.5 7.9 %collective-permute-start.9 = (bf16[128,640]{1,0:T(8,128)(2,1)S(1)}, bf16[128,640]{1,0:T(8,128)(2,1)S(1)}, u32[]{:S(2)}, u32[]{:S(2)}) collective-permute-start(bf16[128,640]{1,0:T(8,128)(2,1)S(1)} %get-tuple-element.27), channel_id=1, source_target_pairs={{0,4},{4,0},{8,12},{12,8},{1,5},{5,1},{9,13},{13,9},{2,6},{6,2},{1... | collective-permute-start | bytes 491528 | tf_op jit(solution)/shard_map/ppermute | solution.py:204
  20.3 4.2 %collective-permute-start.5 = (f32[2,1280]{1,0:T(2,128)S(1)}, f32[2,1280]{1,0:T(2,128)S(1)}, u32[]{:S(2)}, u32[]{:S(2)}) collective-permute-start(f32[2,1280]{1,0:T(2,128)S(1)} %collective-permute-done.1.refs_1_), channel_id=1, source_target_pairs={{0,1},{1,0},{2,3},{3,2},{4,5},{5,4},{6,7},{7,6},{8,9},{9,8},{10,11... | collective-permute-start | bytes 30728 | tf_op jit(solution)/shard_map/ppermute | solution.py:207
  21.2 6.3 %collective-permute-start.11 = (bf16[64,640]{1,0:T(8,128)(2,1)S(1)}, bf16[64,640]{1,0:T(8,128)(2,1)S(1)}, u32[]{:S(2)}, u32[]{:S(2)}) collective-permute-start(bf16[64,640]{1,0:T(8,128)(2,1)S(1)} %collective-permute-done.4.refs_3_.refs_2_), channel_id=1, source_target_pairs={{0,2},{2,0},{1,3},{3,1},{4,6},{6,4},{5,7},{7,5},{8,10},{10,8},{9,1... | collective-permute-start | bytes 245768 | tf_op jit(solution)/shard_map/ppermute | solution.py:207
  23.0 4.6 %collective-permute-start.10 = (bf16[64,640]{1,0:T(8,128)(2,1)S(1)}, bf16[64,640]{1,0:T(8,128)(2,1)S(1)}, u32[]{:S(2)}, u32[]{:S(2)}) collective-permute-start(bf16[64,640]{1,0:T(8,128)(2,1)S(1)} %collective-permute-done.8.refs_2_.refs_1_), channel_id=1, source_target_pairs={{0,2},{2,0},{1,3},{3,1},{4,6},{6,4},{5,7},{7,5},{8,10},{10,8},{9,1... | collective-permute-start | bytes 245768 | tf_op jit(solution)/shard_map/ppermute | solution.py:207
  25.1 3.2 %collective-permute-start.13 = (f32[256,256]{1,0:T(8,128)S(1)}, f32[256,256]{1,0:T(8,128)S(1)}, u32[]{:S(2)}, u32[]{:S(2)}) collective-permute-start(f32[256,256]{1,0:T(8,128)S(1)} %shard_map.88.mine), channel_id=1, source_target_pairs={{0,1},{1,0},{2,3},{3,2},{4,5},{5,4},{6,7},{7,6},{8,9},{9,8},{10,11... | collective-permute-start | bytes 786440 | tf_op jit(solution)/shard_map/ppermute | solution.py:207
  27.9 1.6 %collective-permute-start.12 = (f32[256,256]{1,0:T(8,128)S(1)}, f32[256,256]{1,0:T(8,128)S(1)}, u32[]{:S(2)}, u32[]{:S(2)}) collective-permute-start(f32[256,256]{1,0:T(8,128)S(1)} %shard_map.90.mine), channel_id=1, source_target_pairs={{0,1},{1,0},{2,3},{3,2},{4,5},{5,4},{6,7},{7,6},{8,9},{9,8},{10,11... | collective-permute-start | bytes 786440 | tf_op jit(solution)/shard_map/ppermute | solution.py:207

commit v20 on v19

--- a/solution.py
+++ b/solution.py
@@ -173,7 +173,7 @@
         chosen = jnp.where(row == lane, posterior_ref[:, 0:1], 0.0)
         posterior_out[...] = jnp.sum(chosen, axis=0, keepdims=True)
     rows = mine.shape[1] // len(targets)
-    weighted, rows_of = [], []
+    acc, weighted, rows_of = None, [], []
     for at, (slot, count) in enumerate(targets):
         part = pl.ds(at * rows, rows)
         similar = (mine[:, part] + other[:, part]) * (1.0 / math.sqrt(model_width))
@@ -182,11 +182,14 @@
         weighted.append(aligned.astype(jnp.bfloat16))
         rows_of += [block[...] for block in blocks[:count]]
         blocks = blocks[count:]
-    acc = jnp.dot(
-        jnp.concatenate(weighted, axis=1),
-        jnp.concatenate(rows_of),
-        preferred_element_type=jnp.float32,
-    )
+        if at % 2 or at == len(targets) - 1:
+            term = jnp.dot(
+                jnp.concatenate(weighted, axis=1),
+                jnp.concatenate(rows_of),
+                preferred_element_type=jnp.float32,
+            )
+            acc = term if acc is None else acc + term
+            weighted, rows_of = [], []
     if blocks:
         acc += blocks[0][...]
     out_ref[...] = acc.astype(out_ref.dtype)

time: 31.5 us -> 31.4 us (level)
  no operation moved by 1% of the time
where the time goes in v20:
time: 31.4 us; the launch traced here: 31.3 us
  starting transfers between devices  14.4 us (46%)
  waiting for transfers between devices  6.7 us (21%)
  Pallas kernels  6.29 us (20%)
  local copies, waits for them, and re-layouts  2.25 us (7%)
  between operations  1.41 us (4%)
    ppermute x6, starting transfers between devices, from_peer(): return lax.ppermute(array, 'tgt', [(i, i ^ k) for i in range(4)])  8.55 us
    pallas_call x7, Pallas kernels, call_kernel(): pl.pallas_call(kernel, out_shape=out_shape, in_specs=[VMEM] * len(operand...  6.29 us
    ppermute x6, waiting for transfers between devices, from_peer(): return lax.ppermute(array, 'tgt', [(i, i ^ k) for i in range(4)])  6.28 us
    ppermute x7, starting transfers between devices, across(): return lax.ppermute(array, axis, [(0, 1), (1, 0)])  4.97 us
    squeeze x1, local copies, waits for them, and re-layouts, per_device_by_target(): rest = lax.dynamic_index_in_dim(target_res, 1 - at_qry, 0, keepdims=False)  1.26 us
    ppermute x1, starting transfers between devices, per_device_by_target(): pool_split = lax.ppermute(target_pool, ('tgt', 'rep'), split)  0.9 us
  transfers between devices with their start and end apart: 14, of which 5 were waited for; matrix products, arithmetic and copies ran while one was open for 2% of the time, Pallas kernels for 13%

profile of v20, /device:TPU:0, one launch (start us, length us, event | category | flops | bytes accessed | tf_op | source)
XLA Modules:
  0.0 31.3 jit_solution(7228046398735866259)
XLA Ops:
  0.7 1.3 %dynamic-slice_bitcast_fusion = (bf16[128,640]{1,0:T(8,128)(2,1)S(1)}, bf16[128,640]{1,0:T(8,128)(2,1)S(1)}, bf16[128,640]{1,0:T(8,128)(2,1)S(1)}, bf16[128,640]{1,0:T(8,128)(2,1)S(1)}) fusion(bf16[2,128,640]{2,1,0:T(8,128)(2,1)} %param.8, s32[]{:T(128)S(6)} %select_n.13, s32[]{:T(128)S(6)} %select_n.11), kind=kLoop, calls=%fused_computation | loop fusion | bytes 1310728 | tf_op jit(solution)/shard_map/jit(dynamic_index_in_dim)/squeeze | solution.py:221
  1.9 4.1 %collective-permute-start = (bf16[128,640]{1,0:T(8,128)(2,1)S(1)}, bf16[128,640]{1,0:T(8,128)(2,1)S(1)}, u32[]{:S(2)}, u32[]{:S(2)}) collective-permute-start(bf16[128,640]{1,0:T(8,128)(2,1)S(1)} %get-tuple-element.34), channel_id=1, source_target_pairs={{0,8},{4,12},{8,0},{12,4},{1,9},{5,13},{9,1},{13,5},{2,10},{6,14},... | collective-permute-start | bytes 491528 | tf_op jit(solution)/shard_map/ppermute | solution.py:207
  6.0 1.6 %collective-permute-start.3 = (bf16[128,640]{1,0:T(8,128)(2,1)S(1)}, bf16[128,640]{1,0:T(8,128)(2,1)S(1)}, u32[]{:S(2)}, u32[]{:S(2)}) collective-permute-start(bf16[128,640]{1,0:T(8,128)(2,1)S(1)} %get-tuple-element.34), channel_id=1, source_target_pairs={{0,4},{4,0},{8,12},{12,8},{1,5},{5,1},{9,13},{13,9},{2,6},{6,2},{1... | collective-permute-start | bytes 491528 | tf_op jit(solution)/shard_map/ppermute | solution.py:207
  7.6 0.9 %collective-permute-start.1 = (f32[2,1280]{1,0:T(2,128)S(1)}, f32[2,1280]{1,0:T(2,128)S(1)}, u32[]{:S(2)}, u32[]{:S(2)}) collective-permute-start(f32[2,1280]{1,0:T(2,128)S(1)} %copy-done.1), channel_id=1, source_target_pairs={{0,4},{1,9},{4,0},{5,13},{8,12},{9,1},{12,8},{13,5},{2,6},{3,11},{... | collective-permute-start | bytes 30728 | tf_op jit(solution)/shard_map/ppermute | solution.py:216
  8.6 0.6 %copy-done.4 = s32[8]{0:T(128)S(1)} copy-done((s32[8]{0:T(128)S(1)}, s32[8]{0:T(128)}, u32[]{:S(2)}) %copy-start.4) | copy-done | bytes 56
  9.2 0.2 select_reduce_fusion
  10.1 5.1 %collective-permute-done.2.refs_3_ = f32[2,1280]{1,0:T(2,128)S(1)} collective-permute-done((f32[2,1280]{1,0:T(2,128)S(1)}, f32[2,1280]{1,0:T(2,128)S(1)}, u32[]{:S(2)}, u32[]{:S(2)}) %collective-permute-start.2) | collective-permute-done | bytes 10272 | tf_op jit(solution)/shard_map/ppermute | solution.py:207
  15.4 0.4 %shard_map.87.mine = f32[256,512]{1,0:T(8,128)S(1)} custom-call(bf16[256,640]{1,0:T(8,128)(2,1)S(1)} %bitcast.23, bf16[128,640]{1,0:T(8,128)(2,1)S(1)} %get-tuple-element.33.refs_1_.refs_0_, bf16[128,640]{1,0:T(8,128)(2,1)S(1)} %get-tuple-element.35.refs_2_.refs_1_, bf16[128,640]{1,0:T(8,128)(2,1)S(1)} %collective-permute-done.3.refs_3_.refs_2_, ...), custom_call_target="tpu_custom_call" | custom-call | tf_op jit(solution)/shard_map/pallas_call | solution.py:93
  15.9 0.8 %collective-permute-start.4 = (bf16[64,640]{1,0:T(8,128)(2,1)S(1)}, bf16[64,640]{1,0:T(8,128)(2,1)S(1)}, u32[]{:S(2)}, u32[]{:S(2)}) collective-permute-start(bf16[64,640]{1,0:T(8,128)(2,1)S(1)} %get-tuple-element.37), channel_id=1, source_target_pairs={{0,4},{4,0},{8,12},{12,8},{1,5},{5,1},{9,13},{13,9},{2,6},{6,2},{1... | collective-permute-start | bytes 245768 | tf_op jit(solution)/shard_map/ppermute | solution.py:207
  16.8 1.2 %collective-permute-start.8 = (bf16[64,640]{1,0:T(8,128)(2,1)S(1)}, bf16[64,640]{1,0:T(8,128)(2,1)S(1)}, u32[]{:S(2)}, u32[]{:S(2)}) collective-permute-start(bf16[64,640]{1,0:T(8,128)(2,1)S(1)} %get-tuple-element.36), channel_id=1, source_target_pairs={{0,4},{4,0},{8,12},{12,8},{1,5},{5,1},{9,13},{13,9},{2,6},{6,2},{1... | collective-permute-start | bytes 245768 | tf_op jit(solution)/shard_map/ppermute | solution.py:207
  18.0 1.5 %collective-permute-start.7 = (bf16[128,640]{1,0:T(8,128)(2,1)S(1)}, bf16[128,640]{1,0:T(8,128)(2,1)S(1)}, u32[]{:S(2)}, u32[]{:S(2)}) collective-permute-start(bf16[128,640]{1,0:T(8,128)(2,1)S(1)} %collective-permute-done.refs_4_.refs_3_), channel_id=1, source_target_pairs={{0,2},{2,0},{1,3},{3,1},{4,6},{6,4},{5,7},{7,5},{8,10},{10,8},{9,1... | collective-permute-start | bytes 491528 | tf_op jit(solution)/shard_map/ppermute | solution.py:210
  19.5 0.8 %collective-permute-start.9 = (bf16[128,640]{1,0:T(8,128)(2,1)S(1)}, bf16[128,640]{1,0:T(8,128)(2,1)S(1)}, u32[]{:S(2)}, u32[]{:S(2)}) collective-permute-start(bf16[128,640]{1,0:T(8,128)(2,1)S(1)} %get-tuple-element.27), channel_id=1, source_target_pairs={{0,4},{4,0},{8,12},{12,8},{1,5},{5,1},{9,13},{13,9},{2,6},{6,2},{1... | collective-permute-start | bytes 491528 | tf_op jit(solution)/shard_map/ppermute | solution.py:207
  20.3 0.9 %collective-permute-done.4.refs_3_.refs_2_ = bf16[64,640]{1,0:T(8,128)(2,1)S(1)} collective-permute-done((bf16[64,640]{1,0:T(8,128)(2,1)S(1)}, bf16[64,640]{1,0:T(8,128)(2,1)S(1)}, u32[]{:S(2)}, u32[]{:S(2)}) %collective-permute-start.4) | collective-permute-done | bytes 81952 | tf_op jit(solution)/shard_map/ppermute | solution.py:207
  21.2 1.5 %collective-permute-start.11 = (bf16[64,640]{1,0:T(8,128)(2,1)S(1)}, bf16[64,640]{1,0:T(8,128)(2,1)S(1)}, u32[]{:S(2)}, u32[]{:S(2)}) collective-permute-start(bf16[64,640]{1,0:T(8,128)(2,1)S(1)} %collective-permute-done.4.refs_3_.refs_2_), channel_id=1, source_target_pairs={{0,2},{2,0},{1,3},{3,1},{4,6},{6,4},{5,7},{7,5},{8,10},{10,8},{9,1... | collective-permute-start | bytes 245768 | tf_op jit(solution)/shard_map/ppermute | solution.py:210
  22.7 0.3 collective-permute-done.8.refs_2_.refs_1_
  23.0 1.5 %collective-permute-start.10 = (bf16[64,640]{1,0:T(8,128)(2,1)S(1)}, bf16[64,640]{1,0:T(8,128)(2,1)S(1)}, u32[]{:S(2)}, u32[]{:S(2)}) collective-permute-start(bf16[64,640]{1,0:T(8,128)(2,1)S(1)} %collective-permute-done.8.refs_2_.refs_1_), channel_id=1, source_target_pairs={{0,2},{2,0},{1,3},{3,1},{4,6},{6,4},{5,7},{7,5},{8,10},{10,8},{9,1... | collective-permute-start | bytes 245768 | tf_op jit(solution)/shard_map/ppermute | solution.py:210
  24.5 0.3 shard_map.86
  24.8 0.3 shard_map.88.mine
  25.2 2.1 %shard_map.89.refs_3_ = f32[256,640]{1,0:T(8,128)S(1)} custom-call(f32[8,128]{1,0:T(8,128)S(1)} %get-tuple-element.22.weight_ref, f32[8,128]{1,0:T(8,128)S(1)} %broadcast_in_dim.44.len_ref, f32[1,128]{1,0:T(1,128)S(1)} %broadcast_in_dim.45.sharp_ref, f32[256,512]{1,0:T(8,128)S(1)} %shard_map.87.mine, f32[256,512]{1,0:T(8,128)S(1)} %collective-permute-done.6.other, ...), custom_call_target="tpu_custom_call" | custom-call | tf_op jit(solution)/shard_map/pallas_call | solution.py:93
  27.3 0.2 collective-permute-done.10.refs_2_.refs_1_
  27.6 0.3 shard_map.90.mine
  27.9 0.4 %collective-permute-start.12 = (f32[256,256]{1,0:T(8,128)S(1)}, f32[256,256]{1,0:T(8,128)S(1)}, u32[]{:S(2)}, u32[]{:S(2)}) collective-permute-start(f32[256,256]{1,0:T(8,128)S(1)} %shard_map.90.mine), channel_id=1, source_target_pairs={{0,1},{1,0},{2,3},{3,2},{4,5},{5,4},{6,7},{7,6},{8,9},{9,8},{10,11... | collective-permute-start | bytes 786440 | tf_op jit(solution)/shard_map/ppermute | solution.py:210
  28.2 1.1 %shard_map.91.refs_3_ = f32[256,640]{1,0:T(8,128)S(1)} custom-call(f32[8,128]{1,0:T(8,128)S(1)} %get-tuple-element.22.weight_ref, f32[8,128]{1,0:T(8,128)S(1)} %broadcast_in_dim.44.len_ref, f32[1,128]{1,0:T(1,128)S(1)} %broadcast_in_dim.45.sharp_ref, f32[256,256]{1,0:T(8,128)S(1)} %shard_map.88.mine, f32[256,256]{1,0:T(8,128)S(1)} %collective-permute-done.13.other, ...), custom_call_target="tpu_custom_call" | custom-call | tf_op jit(solution)/shard_map/pallas_call | solution.py:93
  29.5 1.8 %shard_map.92 = (bf16[256,640]{1,0:T(8,128)(2,1)}, f32[1,8]{1,0:T(1,128)}) custom-call(f32[8,128]{1,0:T(8,128)S(1)} %get-tuple-element.22.weight_ref, f32[8,128]{1,0:T(8,128)S(1)} %broadcast_in_dim.44.len_ref, f32[1,128]{1,0:T(1,128)S(1)} %broadcast_in_dim.45.sharp_ref, f32[256,256]{1,0:T(8,128)S(1)} %shard_map.90.mine, ...), custom_call_target="tpu_custom_call" | custom-call | tf_op jit(solution)/shard_map/pallas_call | solution.py:93
  (31 shorter events, 0.8 us)
Async XLA Ops:
  0.6 7.0 %copy-start.1 = (f32[2,1280]{1,0:T(2,128)S(1)}, f32[2,1280]{1,0:T(2,128)}, u32[]{:S(2)}) copy-start(f32[2,1280]{1,0:T(2,128)} %refs_0_.1) | copy-start | bytes 30724
  0.6 14.7 %copy-start = (bf16[1,256,640]{2,1,0:T(8,128)(2,1)S(1)}, bf16[1,256,640]{2,1,0:T(8,128)(2,1)}, u32[]{:S(2)}) copy-start(bf16[1,256,640]{2,1,0:T(8,128)(2,1)} %param.7) | copy-start | bytes 983044
  1.9 13.3 %collective-permute-start = (bf16[128,640]{1,0:T(8,128)(2,1)S(1)}, bf16[128,640]{1,0:T(8,128)(2,1)S(1)}, u32[]{:S(2)}, u32[]{:S(2)}) collective-permute-start(bf16[128,640]{1,0:T(8,128)(2,1)S(1)} %get-tuple-element.34), channel_id=1, source_target_pairs={{0,8},{4,12},{8,0},{12,4},{1,9},{5,13},{9,1},{13,5},{2,10},{6,14},... | collective-permute-start | bytes 491528 | tf_op jit(solution)/shard_map/ppermute | solution.py:207
  6.0 9.4 %collective-permute-start.3 = (bf16[128,640]{1,0:T(8,128)(2,1)S(1)}, bf16[128,640]{1,0:T(8,128)(2,1)S(1)}, u32[]{:S(2)}, u32[]{:S(2)}) collective-permute-start(bf16[128,640]{1,0:T(8,128)(2,1)S(1)} %get-tuple-element.34), channel_id=1, source_target_pairs={{0,4},{4,0},{8,12},{12,8},{1,5},{5,1},{9,13},{13,9},{2,6},{6,2},{1... | collective-permute-start | bytes 491528 | tf_op jit(solution)/shard_map/ppermute | solution.py:207
  7.6 7.6 %collective-permute-start.2 = (f32[2,1280]{1,0:T(2,128)S(1)}, f32[2,1280]{1,0:T(2,128)S(1)}, u32[]{:S(2)}, u32[]{:S(2)}) collective-permute-start(f32[2,1280]{1,0:T(2,128)S(1)} %copy-done.1), channel_id=1, source_target_pairs={{0,12},{4,8},{8,4},{12,0},{1,13},{5,9},{9,5},{13,1},{2,14},{6,10},... | collective-permute-start | bytes 30728 | tf_op jit(solution)/shard_map/ppermute | solution.py:207
  7.6 7.6 %collective-permute-start.1 = (f32[2,1280]{1,0:T(2,128)S(1)}, f32[2,1280]{1,0:T(2,128)S(1)}, u32[]{:S(2)}, u32[]{:S(2)}) collective-permute-start(f32[2,1280]{1,0:T(2,128)S(1)} %copy-done.1), channel_id=1, source_target_pairs={{0,4},{1,9},{4,0},{5,13},{8,12},{9,1},{12,8},{13,5},{2,6},{3,11},{... | collective-permute-start | bytes 30728 | tf_op jit(solution)/shard_map/ppermute | solution.py:216
  8.5 0.7 %copy-start.4 = (s32[8]{0:T(128)S(1)}, s32[8]{0:T(128)}, u32[]{:S(2)}) copy-start(s32[8]{0:T(128)} %param.9) | copy-start | bytes 100
  15.8 2.2 %collective-permute-start.6 = (f32[256,512]{1,0:T(8,128)S(1)}, f32[256,512]{1,0:T(8,128)S(1)}, u32[]{:S(2)}, u32[]{:S(2)}) collective-permute-start(f32[256,512]{1,0:T(8,128)S(1)} %shard_map.87.mine), channel_id=1, source_target_pairs={{0,1},{1,0},{2,3},{3,2},{4,5},{5,4},{6,7},{7,6},{8,9},{9,8},{10,11... | collective-permute-start | bytes 1572872 | tf_op jit(solution)/shard_map/ppermute | solution.py:210
  15.9 8.6 %copy-start.2 = (f32[1,1280]{1,0:T(1,128)S(1)}, f32[1,1280]{1,0:T(1,128)}, u32[]{:S(2)}) copy-start(f32[1,1280]{1,0:T(1,128)} %pool_ref.1) | copy-start | bytes 15364
  15.9 5.3 %collective-permute-start.4 = (bf16[64,640]{1,0:T(8,128)(2,1)S(1)}, bf16[64,640]{1,0:T(8,128)(2,1)S(1)}, u32[]{:S(2)}, u32[]{:S(2)}) collective-permute-start(bf16[64,640]{1,0:T(8,128)(2,1)S(1)} %get-tuple-element.37), channel_id=1, source_target_pairs={{0,4},{4,0},{8,12},{12,8},{1,5},{5,1},{9,13},{13,9},{2,6},{6,2},{1... | collective-permute-start | bytes 245768 | tf_op jit(solution)/shard_map/ppermute | solution.py:207
  16.8 7.7 %copy-start.3 = (s32[1,28]{1,0:T(1,128)S(1)}, s32[1,28]{1,0:T(1,128)}, u32[]{:S(2)}) copy-start(s32[1,28]{1,0:T(1,128)} %hits_ref) | copy-start | bytes 340
  16.8 6.2 %collective-permute-start.8 = (bf16[64,640]{1,0:T(8,128)(2,1)S(1)}, bf16[64,640]{1,0:T(8,128)(2,1)S(1)}, u32[]{:S(2)}, u32[]{:S(2)}) collective-permute-start(bf16[64,640]{1,0:T(8,128)(2,1)S(1)} %get-tuple-element.36), channel_id=1, source_target_pairs={{0,4},{4,0},{8,12},{12,8},{1,5},{5,1},{9,13},{13,9},{2,6},{6,2},{1... | collective-permute-start | bytes 245768 | tf_op jit(solution)/shard_map/ppermute | solution.py:207
  18.0 6.8 %collective-permute-start.7 = (bf16[128,640]{1,0:T(8,128)(2,1)S(1)}, bf16[128,640]{1,0:T(8,128)(2,1)S(1)}, u32[]{:S(2)}, u32[]{:S(2)}) collective-permute-start(bf16[128,640]{1,0:T(8,128)(2,1)S(1)} %collective-permute-done.refs_4_.refs_3_), channel_id=1, source_target_pairs={{0,2},{2,0},{1,3},{3,1},{4,6},{6,4},{5,7},{7,5},{8,10},{10,8},{9,1... | collective-permute-start | bytes 491528 | tf_op jit(solution)/shard_map/ppermute | solution.py:210
  19.5 7.8 %collective-permute-start.9 = (bf16[128,640]{1,0:T(8,128)(2,1)S(1)}, bf16[128,640]{1,0:T(8,128)(2,1)S(1)}, u32[]{:S(2)}, u32[]{:S(2)}) collective-permute-start(bf16[128,640]{1,0:T(8,128)(2,1)S(1)} %get-tuple-element.27), channel_id=1, source_target_pairs={{0,4},{4,0},{8,12},{12,8},{1,5},{5,1},{9,13},{13,9},{2,6},{6,2},{1... | collective-permute-start | bytes 491528 | tf_op jit(solution)/shard_map/ppermute | solution.py:207
  20.3 4.2 %collective-permute-start.5 = (f32[2,1280]{1,0:T(2,128)S(1)}, f32[2,1280]{1,0:T(2,128)S(1)}, u32[]{:S(2)}, u32[]{:S(2)}) collective-permute-start(f32[2,1280]{1,0:T(2,128)S(1)} %collective-permute-done.1.refs_1_), channel_id=1, source_target_pairs={{0,1},{1,0},{2,3},{3,2},{4,5},{5,4},{6,7},{7,6},{8,9},{9,8},{10,11... | collective-permute-start | bytes 30728 | tf_op jit(solution)/shard_map/ppermute | solution.py:210
  21.2 6.3 %collective-permute-start.11 = (bf16[64,640]{1,0:T(8,128)(2,1)S(1)}, bf16[64,640]{1,0:T(8,128)(2,1)S(1)}, u32[]{:S(2)}, u32[]{:S(2)}) collective-permute-start(bf16[64,640]{1,0:T(8,128)(2,1)S(1)} %collective-permute-done.4.refs_3_.refs_2_), channel_id=1, source_target_pairs={{0,2},{2,0},{1,3},{3,1},{4,6},{6,4},{5,7},{7,5},{8,10},{10,8},{9,1... | collective-permute-start | bytes 245768 | tf_op jit(solution)/shard_map/ppermute | solution.py:210
  23.0 4.6 %collective-permute-start.10 = (bf16[64,640]{1,0:T(8,128)(2,1)S(1)}, bf16[64,640]{1,0:T(8,128)(2,1)S(1)}, u32[]{:S(2)}, u32[]{:S(2)}) collective-permute-start(bf16[64,640]{1,0:T(8,128)(2,1)S(1)} %collective-permute-done.8.refs_2_.refs_1_), channel_id=1, source_target_pairs={{0,2},{2,0},{1,3},{3,1},{4,6},{6,4},{5,7},{7,5},{8,10},{10,8},{9,1... | collective-permute-start | bytes 245768 | tf_op jit(solution)/shard_map/ppermute | solution.py:210
  25.1 3.1 %collective-permute-start.13 = (f32[256,256]{1,0:T(8,128)S(1)}, f32[256,256]{1,0:T(8,128)S(1)}, u32[]{:S(2)}, u32[]{:S(2)}) collective-permute-start(f32[256,256]{1,0:T(8,128)S(1)} %shard_map.88.mine), channel_id=1, source_target_pairs={{0,1},{1,0},{2,3},{3,2},{4,5},{5,4},{6,7},{7,6},{8,9},{9,8},{10,11... | collective-permute-start | bytes 786440 | tf_op jit(solution)/shard_map/ppermute | solution.py:210
  27.9 1.6 %collective-permute-start.12 = (f32[256,256]{1,0:T(8,128)S(1)}, f32[256,256]{1,0:T(8,128)S(1)}, u32[]{:S(2)}, u32[]{:S(2)}) collective-permute-start(f32[256,256]{1,0:T(8,128)S(1)} %shard_map.90.mine), channel_id=1, source_target_pairs={{0,1},{1,0},{2,3},{3,2},{4,5},{5,4},{6,7},{7,6},{8,9},{9,8},{10,11... | collective-permute-start | bytes 786440 | tf_op jit(solution)/shard_map/ppermute | solution.py:210
